TPU v7x, 32 devices: a whole 2x2x4 slice. The times are simulated.
32 devices in a mesh: pipe: 4 (over z), expert: 8 (over y, x, core).
Axes of the slice: x: 2, y: 2, z: 4, core: 2. Of those that a mesh axis runs over, the one named last changes fastest.
Arguments:
- out_grad: bfloat16 [1024, 5120], P('expert'), may hold values from -0.59765625 to 0.59765625
- saved_inputs: bfloat16 [4, 1024, 5120], P('pipe', 'expert'), may hold values from -6 to 6
- router: bfloat16 [4, 5120, 160], P('pipe'), may hold values from -0.078125 to 0.078125
- routes: int32 [4, 1024, 6], P('pipe', 'expert'), may hold values from 0 to 159, all different within a row; in each aligned block of 128 rows (0 to 127, 128 to 255, ..., all dimensions but the last counted through in order) at most 9 rows name the same one
- hidden_saved: bfloat16 [4, 8, 72, 768], P('pipe', 'expert'), may hold values from -6 to 6
- codes: int32 [4, 8, 2, 768, 640], P('pipe', 'expert'), may hold values from 0 to 255
- codebook: bfloat16 [4, 8, 2, 256, 8], P('pipe', 'expert'), may hold values from -0.29882812 to 0.29882812
- scale: float32 [4, 8, 5120], P('pipe', 'expert'), may hold values from 0.25 to 1
Outputs:
- section_grads: bfloat16 [4, 1024, 5120], P('pipe', 'expert')
- codebook_grad: float32 [4, 8, 2, 256, 8], P('pipe', 'expert')
- scale_grad: float32 [4, 8, 5120], P('pipe', 'expert')
Inputs may be any that keep to these rules, and one draw needn't show every extreme that they name: `routes`: each row names 6 different experts; in each aligned block of 128 rows (one device's tokens of one layer) no expert is named by more than 9 rows.
All inputs are finite; a program needn't handle non-finite values.
Results may differ from a plain program's by a relative error of at most 0.0063.
Values may be sent and summed in bfloat16 or wider, within the bound.
No kernel may reach another device: no remote copies, remote signals or barrier semaphores. Data moves between devices by JAX's collectives and lax.ppermute only.
A program may use at most 192 MiB of HBM per device.

v0:
```python
import jax
import jax.numpy as jnp
from jax import lax
from jax.sharding import PartitionSpec as P

MOST = 9


ROUTE_SCALE = 16.0


def shifted(value, axis, steps):
    count = lax.axis_size(axis)
    leading, last = (max(0, -steps), min(count, count - steps))
    return lax.ppermute(value, axis, [(source, source + steps) for source in range(leading, last)])


def slot_tables(route_ids, experts, most):
    flat_ids = route_ids.reshape(-1)
    hit_table = (flat_ids[:, None] == lax.iota(jnp.int32, experts)[None, :]).astype(jnp.int32)
    position = jnp.sum(hit_table * (jnp.cumsum(hit_table, axis=0) - 1), axis=1)
    slot_index = jnp.where(flat_ids < experts, flat_ids * most + position, -1)
    selector = (slot_index[None, :] == lax.iota(jnp.int32, experts * most)[:, None]).astype(
        jnp.bfloat16
    )
    tok_select = jnp.sum(
        selector.reshape(experts * most, route_ids.shape[0], route_ids.shape[1]), axis=2
    )
    return (selector, tok_select)


def router_back(current, score_pick, softmax_out, route_hits, router_w):
    spread = jnp.einsum("tk,tkr->tr", score_pick, route_hits, preferred_element_type=jnp.float32)
    weighted = jnp.sum(softmax_out * spread, axis=1, keepdims=True)
    dlogit = (ROUTE_SCALE * softmax_out * (spread - weighted)).astype(jnp.bfloat16)
    returned = lax.dot_general(
        dlogit, router_w, (((1,), (1,)), ((), ())), preferred_element_type=jnp.float32
    )
    return (current.astype(jnp.float32) + returned).astype(jnp.bfloat16)


def pass_down(updated):
    return shifted(updated, "pipe", -1)


def on_device(out_grad, saved_inputs, router, routes, hidden_saved, codes, codebook, scale):
    experts = lax.axis_size("expert")
    phases = lax.axis_size("pipe")
    layer_index = lax.axis_index("pipe")
    tok_rows, model_width = out_grad.shape
    expert_count = router.shape[2]
    top_count = routes.shape[2]
    code_rows = codes[0, 0]
    code_book = codebook[0, 0]
    gain_row = scale[0, 0]
    hidden = hidden_saved[0, 0]
    hidden_width = hidden.shape[1]
    book_count = code_rows.shape[0]
    groups = code_rows.shape[2]
    entries = code_book.shape[1]
    group_size = code_book.shape[2]
    row_block = 64
    block_count = hidden_width // row_block

    def one_hot_codes(rows_codes):
        flat_codes = rows_codes.reshape(-1)
        return (flat_codes[:, None] == lax.iota(jnp.int32, entries)[None, :]).astype(jnp.bfloat16)

    def decode_block(block_codes):
        plain_t = jnp.zeros((group_size, row_block * groups), jnp.float32)
        for book_index in range(book_count):
            onehot = one_hot_codes(block_codes[book_index])
            plain_t = plain_t + lax.dot_general(
                code_book[book_index],
                onehot,
                (((0,), (1,)), ((), ())),
                preferred_element_type=jnp.float32,
            )
        plain_part = plain_t.T.reshape(row_block, model_width)
        return (plain_part, (plain_part * gain_row[None, :]).astype(jnp.bfloat16))

    blocked_codes = code_rows.reshape(book_count, block_count, row_block, groups).transpose(
        1, 0, 2, 3
    )
    plain_w, weight = lax.map(decode_block, blocked_codes)
    plain_w = plain_w.reshape(hidden_width, model_width)
    weight = weight.reshape(hidden_width, model_width)
    expert_out = jnp.dot(hidden, weight, preferred_element_type=jnp.float32).astype(jnp.bfloat16)
    inputs = saved_inputs[0]
    router_w = router[0]
    route_ids = routes[0]
    logits = jnp.dot(inputs, router_w, preferred_element_type=jnp.float32)
    raised = jnp.exp(logits)
    softmax_out = raised / jnp.sum(raised, axis=1, keepdims=True)
    route_match = route_ids[:, :, None] == lax.iota(jnp.int32, expert_count)[None, None, :]
    route_hits = route_match.astype(jnp.bfloat16)
    chosen = jnp.sum(jnp.where(route_match, softmax_out[:, None, :], 0.0), axis=2)
    gate_weight = (ROUTE_SCALE * chosen).astype(jnp.bfloat16)
    selector, tok_select = slot_tables(route_ids, experts, MOST)
    gate_slots = (
        jnp.dot(selector, gate_weight.reshape(-1), preferred_element_type=jnp.float32)
        .astype(jnp.bfloat16)
        .reshape(experts, MOST)
    )
    current = out_grad
    result = jnp.zeros_like(out_grad)
    kept_rows = jnp.zeros((experts * MOST, model_width), jnp.bfloat16)
    gates_in = jnp.zeros((experts * MOST,), jnp.bfloat16)
    for step_index in range(phases):
        active = layer_index == phases - 1 - step_index
        outgoing = (
            jnp.dot(tok_select, current, preferred_element_type=jnp.float32)
            .astype(jnp.bfloat16)
            .reshape(experts, MOST, model_width)
        )
        slot_rows, slot_gates = (
            lax.all_to_all(outgoing, "expert", split_axis=0, concat_axis=0, tiled=True),
            lax.all_to_all(gate_slots, "expert", split_axis=0, concat_axis=0, tiled=True),
        )
        slot_rows = slot_rows.reshape(experts * MOST, model_width)
        scores = jnp.sum(
            slot_rows.astype(jnp.float32) * expert_out.astype(jnp.float32), axis=1
        ).astype(jnp.bfloat16)
        returned = lax.all_to_all(
            scores.reshape(experts, MOST), "expert", split_axis=0, concat_axis=0, tiled=True
        )
        picked = jnp.dot(returned.reshape(-1), selector, preferred_element_type=jnp.float32)
        score_pick = picked.astype(jnp.bfloat16).reshape(tok_rows, top_count)
        updated = router_back(current, score_pick, softmax_out, route_hits, router_w)
        kept_rows = jnp.where(active, slot_rows, kept_rows)
        gates_in = slot_gates.reshape(-1)
        result = jnp.where(active, updated, result)
        if step_index + 1 < phases:
            current = pass_down(updated)
    slot_grad = (gates_in.astype(jnp.float32)[:, None] * kept_rows.astype(jnp.float32)).astype(
        jnp.bfloat16
    )

    def grad_block(totals, block_index):
        first_row = block_index * row_block
        hidden_part = lax.dynamic_slice_in_dim(hidden, first_row, row_block, 1)
        rows_codes = lax.dynamic_slice_in_dim(code_rows, first_row, row_block, 1)
        plain_part = lax.dynamic_slice_in_dim(plain_w, first_row, row_block, 0)
        grad_w = lax.dot_general(
            hidden_part, slot_grad, (((0,), (0,)), ((), ())), preferred_element_type=jnp.float32
        )
        scale_part = jnp.sum(grad_w * plain_part, axis=0)
        scaled = (
            (grad_w * gain_row[None, :])
            .astype(jnp.bfloat16)
            .reshape(row_block * groups, group_size)
        )
        book_parts = []
        for book_index in range(book_count):
            onehot = one_hot_codes(rows_codes[book_index])
            book_parts.append(
                lax.dot_general(
                    scaled, onehot, (((0,), (0,)), ((), ())), preferred_element_type=jnp.float32
                )
            )
        return ((totals[0] + scale_part, totals[1] + jnp.stack(book_parts)), None)

    start_totals = (
        jnp.zeros((model_width,), jnp.float32),
        jnp.zeros((book_count, group_size, entries), jnp.float32),
    )
    (scale_total, book_total), _ = lax.scan(
        grad_block, start_totals, jnp.arange(block_count, dtype=jnp.int32)
    )
    book_total = book_total.transpose(0, 2, 1)
    return (result[None], book_total[None, None], scale_total[None, None])


def solution(mesh):
    placed = (
        P("expert", None),
        P("pipe", "expert", None),
        P("pipe", None, None),
        P("pipe", "expert", None),
        P("pipe", "expert", None, None),
        P("pipe", "expert", None, None, None),
        P("pipe", "expert", None, None, None),
        P("pipe", "expert", None),
    )
    return jax.shard_map(
        on_device,
        mesh=mesh,
        in_specs=placed,
        out_specs=(
            P("pipe", "expert", None),
            P("pipe", "expert", None, None, None),
            P("pipe", "expert", None),
        ),
        check_vma=False,
    )
```

profile of v0, /device:TPU:0, one launch (start us, length us, event | category | flops | bytes accessed | tf_op | source)
XLA Modules:
  0.0 1933.5 jit_solution(793089949726911163)
XLA Ops:
  12.8 885.5 %while.25 = (s32[]{:T(128)}, f32[12,64,5120]{2,1,0:T(8,128)}, bf16[12,64,5120]{2,1,0:T(8,128)(2,1)}, s32[12,2,64,640]{3,2,0,1:T(8,128)}, bf16[2,256,8]{1,2,0:T(8...) while((s32[]{:T(128)}, f32[12,64,5120]{2,1,0:T(8,128)}, bf16[12,64,5120]{2,1,0:T(8,128)(2,1)}, ...), condition=%wide.region_6.7_spmd, body=%wide.region_5.6_spmd.sunk | while | flops 357498880 | bytes 16086097 | solution.py:85
  36.7 22.9 %convolution_add_fusion.3 = f32[40960,8]{0,1:T(8,128)S(1)} fusion(f32[40960,8]{0,1:T(8,128)} %fusion.104, s32[40960]{0:T(1024)S(1)} %eq.310, bf16[2,256,8]{1,2,0:T(8,128)(2,1)S(1)} %get-tuple-element.308), kind=kOutput, calls=%fused_computation.clone.1 | convolution fusion | flops 178585600 | bytes 2789376 | tf_op jit(solution)/shard_map/while/body/eval_jaxpr/dot_general | solution.py:73
  553.2 22.9 %convolution_add_fusion.3 = f32[40960,8]{0,1:T(8,128)S(1)} fusion(f32[40960,8]{0,1:T(8,128)} %fusion.104, s32[40960]{0:T(1024)S(1)} %eq.310, bf16[2,256,8]{1,2,0:T(8,128)(2,1)S(1)} %get-tuple-element.308), kind=kOutput, calls=%fused_computation.clone.1 | convolution fusion | flops 178585600 | bytes 2789376 | tf_op jit(solution)/shard_map/while/body/eval_jaxpr/dot_general | solution.py:73
  774.6 22.9 %convolution_add_fusion.3 = f32[40960,8]{0,1:T(8,128)S(1)} fusion(f32[40960,8]{0,1:T(8,128)} %fusion.104, s32[40960]{0:T(1024)S(1)} %eq.310, bf16[2,256,8]{1,2,0:T(8,128)(2,1)S(1)} %get-tuple-element.308), kind=kOutput, calls=%fused_computation.clone.1 | convolution fusion | flops 178585600 | bytes 2789376 | tf_op jit(solution)/shard_map/while/body/eval_jaxpr/dot_general | solution.py:73
  921.6 31.3 %collective-permute-done = bf16[128,5120]{1,0:T(8,128)(2,1)S(1)} collective-permute-done((bf16[128,5120]{1,0:T(8,128)(2,1)S(1)}, bf16[128,5120]{1,0:T(8,128)(2,1)S(1)}, u32[]{:S(2)}, u32[]{:S(2)}) %collective-permute-start) | collective-permute-done | bytes 1310752 | tf_op jit(solution)/shard_map/ppermute | solution.py:15
  995.3 31.1 %collective-permute-done.1 = bf16[128,5120]{1,0:T(8,128)(2,1)S(1)} collective-permute-done((bf16[128,5120]{1,0:T(8,128)(2,1)S(1)}, bf16[128,5120]{1,0:T(8,128)(2,1)S(1)}, u32[]{:S(2)}, u32[]{:S(2)}) %collective-permute-start.1) | collective-permute-done | bytes 1310752 | tf_op jit(solution)/shard_map/ppermute | solution.py:15
  1068.9 31.1 %collective-permute-done.2 = bf16[128,5120]{1,0:T(8,128)(2,1)S(1)} collective-permute-done((bf16[128,5120]{1,0:T(8,128)(2,1)S(1)}, bf16[128,5120]{1,0:T(8,128)(2,1)S(1)}, u32[]{:S(2)}, u32[]{:S(2)}) %collective-permute-start.2) | collective-permute-done | bytes 1310752 | tf_op jit(solution)/shard_map/ppermute | solution.py:15
  1154.1 778.8 %while.26 = (s32[]{:T(128)}, f32[5120]{0:T(1024)S(1)}, f32[2,8,256]{2,1,0:T(8,128)S(1)}, s32[12]{0:T(128)S(1)}, bf16[72,768]{1,0:T(8,128)(2,1)S(1)}, /*index=5*/...) while((s32[]{:T(128)}, f32[5120]{0:T(1024)S(1)}, ...), condition=%wide.region_18.19_spmd.clone, body=%wide.region_16.18_spmd.clone.sunk | while | flops 405029888 | bytes 7150814 | solution.py:167
  1171.6 23.7 %fusion.109 = f32[1,8,256]{2,1,0:T(8,128)S(1)} fusion(bf16[40960,8]{1,0:T(8,128)(2,1)} %reshape.317, s32[40960]{0:T(1024)S(1)} %eq.317), kind=kOutput, calls=%fused_computation.22.clone.1 | convolution fusion | flops 178257920 | bytes 827392 | tf_op jit(solution)/shard_map/while/body/eval_jaxpr/dot_general | solution.py:157
  1195.3 23.7 %fusion.110 = f32[1,8,256]{2,1,0:T(8,128)S(1)} fusion(bf16[40960,8]{1,0:T(8,128)(2,1)} %reshape.317, s32[40960]{0:T(1024)S(1)} %eq.318), kind=kOutput, calls=%fused_computation.23.clone.1 | convolution fusion | flops 178257920 | bytes 827392 | tf_op jit(solution)/shard_map/while/body/eval_jaxpr/dot_general | solution.py:157
  1236.5 23.7 %fusion.109 = f32[1,8,256]{2,1,0:T(8,128)S(1)} fusion(bf16[40960,8]{1,0:T(8,128)(2,1)} %reshape.317, s32[40960]{0:T(1024)S(1)} %eq.317), kind=kOutput, calls=%fused_computation.22.clone.1 | convolution fusion | flops 178257920 | bytes 827392 | tf_op jit(solution)/shard_map/while/body/eval_jaxpr/dot_general | solution.py:157
  1260.2 23.7 %fusion.110 = f32[1,8,256]{2,1,0:T(8,128)S(1)} fusion(bf16[40960,8]{1,0:T(8,128)(2,1)} %reshape.317, s32[40960]{0:T(1024)S(1)} %eq.318), kind=kOutput, calls=%fused_computation.23.clone.1 | convolution fusion | flops 178257920 | bytes 827392 | tf_op jit(solution)/shard_map/while/body/eval_jaxpr/dot_general | solution.py:157
  1301.4 23.7 %fusion.109 = f32[1,8,256]{2,1,0:T(8,128)S(1)} fusion(bf16[40960,8]{1,0:T(8,128)(2,1)} %reshape.317, s32[40960]{0:T(1024)S(1)} %eq.317), kind=kOutput, calls=%fused_computation.22.clone.1 | convolution fusion | flops 178257920 | bytes 827392 | tf_op jit(solution)/shard_map/while/body/eval_jaxpr/dot_general | solution.py:157
  1325.1 23.7 %fusion.110 = f32[1,8,256]{2,1,0:T(8,128)S(1)} fusion(bf16[40960,8]{1,0:T(8,128)(2,1)} %reshape.317, s32[40960]{0:T(1024)S(1)} %eq.318), kind=kOutput, calls=%fused_computation.23.clone.1 | convolution fusion | flops 178257920 | bytes 827392 | tf_op jit(solution)/shard_map/while/body/eval_jaxpr/dot_general | solution.py:157
  1366.3 23.7 %fusion.109 = f32[1,8,256]{2,1,0:T(8,128)S(1)} fusion(bf16[40960,8]{1,0:T(8,128)(2,1)} %reshape.317, s32[40960]{0:T(1024)S(1)} %eq.317), kind=kOutput, calls=%fused_computation.22.clone.1 | convolution fusion | flops 178257920 | bytes 827392 | tf_op jit(solution)/shard_map/while/body/eval_jaxpr/dot_general | solution.py:157
  1390.0 23.7 %fusion.110 = f32[1,8,256]{2,1,0:T(8,128)S(1)} fusion(bf16[40960,8]{1,0:T(8,128)(2,1)} %reshape.317, s32[40960]{0:T(1024)S(1)} %eq.318), kind=kOutput, calls=%fused_computation.23.clone.1 | convolution fusion | flops 178257920 | bytes 827392 | tf_op jit(solution)/shard_map/while/body/eval_jaxpr/dot_general | solution.py:157
  1431.2 23.7 %fusion.109 = f32[1,8,256]{2,1,0:T(8,128)S(1)} fusion(bf16[40960,8]{1,0:T(8,128)(2,1)} %reshape.317, s32[40960]{0:T(1024)S(1)} %eq.317), kind=kOutput, calls=%fused_computation.22.clone.1 | convolution fusion | flops 178257920 | bytes 827392 | tf_op jit(solution)/shard_map/while/body/eval_jaxpr/dot_general | solution.py:157
  1454.9 23.7 %fusion.110 = f32[1,8,256]{2,1,0:T(8,128)S(1)} fusion(bf16[40960,8]{1,0:T(8,128)(2,1)} %reshape.317, s32[40960]{0:T(1024)S(1)} %eq.318), kind=kOutput, calls=%fused_computation.23.clone.1 | convolution fusion | flops 178257920 | bytes 827392 | tf_op jit(solution)/shard_map/while/body/eval_jaxpr/dot_general | solution.py:157
  1496.1 23.7 %fusion.109 = f32[1,8,256]{2,1,0:T(8,128)S(1)} fusion(bf16[40960,8]{1,0:T(8,128)(2,1)} %reshape.317, s32[40960]{0:T(1024)S(1)} %eq.317), kind=kOutput, calls=%fused_computation.22.clone.1 | convolution fusion | flops 178257920 | bytes 827392 | tf_op jit(solution)/shard_map/while/body/eval_jaxpr/dot_general | solution.py:157
  1519.8 23.7 %fusion.110 = f32[1,8,256]{2,1,0:T(8,128)S(1)} fusion(bf16[40960,8]{1,0:T(8,128)(2,1)} %reshape.317, s32[40960]{0:T(1024)S(1)} %eq.318), kind=kOutput, calls=%fused_computation.23.clone.1 | convolution fusion | flops 178257920 | bytes 827392 | tf_op jit(solution)/shard_map/while/body/eval_jaxpr/dot_general | solution.py:157
  1561.0 23.7 %fusion.109 = f32[1,8,256]{2,1,0:T(8,128)S(1)} fusion(bf16[40960,8]{1,0:T(8,128)(2,1)} %reshape.317, s32[40960]{0:T(1024)S(1)} %eq.317), kind=kOutput, calls=%fused_computation.22.clone.1 | convolution fusion | flops 178257920 | bytes 827392 | tf_op jit(solution)/shard_map/while/body/eval_jaxpr/dot_general | solution.py:157
  1584.7 23.7 %fusion.110 = f32[1,8,256]{2,1,0:T(8,128)S(1)} fusion(bf16[40960,8]{1,0:T(8,128)(2,1)} %reshape.317, s32[40960]{0:T(1024)S(1)} %eq.318), kind=kOutput, calls=%fused_computation.23.clone.1 | convolution fusion | flops 178257920 | bytes 827392 | tf_op jit(solution)/shard_map/while/body/eval_jaxpr/dot_general | solution.py:157
  1625.9 23.7 %fusion.109 = f32[1,8,256]{2,1,0:T(8,128)S(1)} fusion(bf16[40960,8]{1,0:T(8,128)(2,1)} %reshape.317, s32[40960]{0:T(1024)S(1)} %eq.317), kind=kOutput, calls=%fused_computation.22.clone.1 | convolution fusion | flops 178257920 | bytes 827392 | tf_op jit(solution)/shard_map/while/body/eval_jaxpr/dot_general | solution.py:157
  1649.6 23.7 %fusion.110 = f32[1,8,256]{2,1,0:T(8,128)S(1)} fusion(bf16[40960,8]{1,0:T(8,128)(2,1)} %reshape.317, s32[40960]{0:T(1024)S(1)} %eq.318), kind=kOutput, calls=%fused_computation.23.clone.1 | convolution fusion | flops 178257920 | bytes 827392 | tf_op jit(solution)/shard_map/while/body/eval_jaxpr/dot_general | solution.py:157
  1690.8 23.7 %fusion.109 = f32[1,8,256]{2,1,0:T(8,128)S(1)} fusion(bf16[40960,8]{1,0:T(8,128)(2,1)} %reshape.317, s32[40960]{0:T(1024)S(1)} %eq.317), kind=kOutput, calls=%fused_computation.22.clone.1 | convolution fusion | flops 178257920 | bytes 827392 | tf_op jit(solution)/shard_map/while/body/eval_jaxpr/dot_general | solution.py:157
  1714.5 23.7 %fusion.110 = f32[1,8,256]{2,1,0:T(8,128)S(1)} fusion(bf16[40960,8]{1,0:T(8,128)(2,1)} %reshape.317, s32[40960]{0:T(1024)S(1)} %eq.318), kind=kOutput, calls=%fused_computation.23.clone.1 | convolution fusion | flops 178257920 | bytes 827392 | tf_op jit(solution)/shard_map/while/body/eval_jaxpr/dot_general | solution.py:157
  1755.7 23.7 %fusion.109 = f32[1,8,256]{2,1,0:T(8,128)S(1)} fusion(bf16[40960,8]{1,0:T(8,128)(2,1)} %reshape.317, s32[40960]{0:T(1024)S(1)} %eq.317), kind=kOutput, calls=%fused_computation.22.clone.1 | convolution fusion | flops 178257920 | bytes 827392 | tf_op jit(solution)/shard_map/while/body/eval_jaxpr/dot_general | solution.py:157
  1779.4 23.7 %fusion.110 = f32[1,8,256]{2,1,0:T(8,128)S(1)} fusion(bf16[40960,8]{1,0:T(8,128)(2,1)} %reshape.317, s32[40960]{0:T(1024)S(1)} %eq.318), kind=kOutput, calls=%fused_computation.23.clone.1 | convolution fusion | flops 178257920 | bytes 827392 | tf_op jit(solution)/shard_map/while/body/eval_jaxpr/dot_general | solution.py:157
  1820.6 23.7 %fusion.109 = f32[1,8,256]{2,1,0:T(8,128)S(1)} fusion(bf16[40960,8]{1,0:T(8,128)(2,1)} %reshape.317, s32[40960]{0:T(1024)S(1)} %eq.317), kind=kOutput, calls=%fused_computation.22.clone.1 | convolution fusion | flops 178257920 | bytes 827392 | tf_op jit(solution)/shard_map/while/body/eval_jaxpr/dot_general | solution.py:157
  1844.3 23.7 %fusion.110 = f32[1,8,256]{2,1,0:T(8,128)S(1)} fusion(bf16[40960,8]{1,0:T(8,128)(2,1)} %reshape.317, s32[40960]{0:T(1024)S(1)} %eq.318), kind=kOutput, calls=%fused_computation.23.clone.1 | convolution fusion | flops 178257920 | bytes 827392 | tf_op jit(solution)/shard_map/while/body/eval_jaxpr/dot_general | solution.py:157
  1885.5 23.7 %fusion.109 = f32[1,8,256]{2,1,0:T(8,128)S(1)} fusion(bf16[40960,8]{1,0:T(8,128)(2,1)} %reshape.317, s32[40960]{0:T(1024)S(1)} %eq.317), kind=kOutput, calls=%fused_computation.22.clone.1 | convolution fusion | flops 178257920 | bytes 827392 | tf_op jit(solution)/shard_map/while/body/eval_jaxpr/dot_general | solution.py:157
  1909.2 23.7 %fusion.110 = f32[1,8,256]{2,1,0:T(8,128)S(1)} fusion(bf16[40960,8]{1,0:T(8,128)(2,1)} %reshape.317, s32[40960]{0:T(1024)S(1)} %eq.318), kind=kOutput, calls=%fused_computation.23.clone.1 | convolution fusion | flops 178257920 | bytes 827392 | tf_op jit(solution)/shard_map/while/body/eval_jaxpr/dot_general | solution.py:157
  (342 shorter events, 1192.8 us)
Async XLA Ops:
  0.6 897.6 %copy-start = (bf16[1,5120,160]{1,2,0:T(8,128)(2,1)S(1)}, bf16[1,5120,160]{1,2,0:T(8,128)(2,1)}, u32[]{:S(2)}) copy-start(bf16[1,5120,160]{1,2,0:T(8,128)(2,1)} %param.14) | copy-start | bytes 4915204
  7.5 5.3 copy-start.3
  7.5 5.3 copy-start.13
  7.5 892.7 %all-to-all-start = ((bf16[8,9,5120]{2,1,0:T(8,128)(2,1)}), bf16[8,9,5120]{2,1,0:T(8,128)(2,1)}, u32[]{:S(2)}, u32[]{:S(2)}) async-start(bf16[8,9,5120]{2,1,0:T(8,128)(2,1)} %reshape.257), calls=%async_computation | async-start | bytes 2621440 | tf_op jit(solution)/shard_map/all_to_all | solution.py:117
  900.2 2.8 copy-start.11
  903.0 10.2 copy-start.12
  908.9 8.8 all-to-all-start.1
  920.2 32.6 %copy-start.6 = (bf16[128,5120]{1,0:T(8,128)(2,1)}, bf16[128,5120]{1,0:T(8,128)(2,1)S(1)}, u32[]{:S(2)}) copy-start(bf16[128,5120]{1,0:T(8,128)(2,1)S(1)} %fusion.17) | copy-start | bytes 3932164
  920.3 32.6 %collective-permute-start = (bf16[128,5120]{1,0:T(8,128)(2,1)S(1)}, bf16[128,5120]{1,0:T(8,128)(2,1)S(1)}, u32[]{:S(2)}, u32[]{:S(2)}) collective-permute-start(bf16[128,5120]{1,0:T(8,128)(2,1)S(1)} %fusion.17), channel_id=1, source_target_pairs={{8,0},{16,8},{24,16},{9,1},{17,9},{25,17},{10,2},{18,10},{26,18},{... | collective-permute-start | bytes 3932168 | tf_op jit(solution)/shard_map/ppermute | solution.py:15
  952.9 1.1 copy-start.1
  994.0 32.4 %copy-start.7 = (bf16[128,5120]{1,0:T(8,128)(2,1)}, bf16[128,5120]{1,0:T(8,128)(2,1)S(1)}, u32[]{:S(2)}) copy-start(bf16[128,5120]{1,0:T(8,128)(2,1)S(1)} %add_convert_fusion.2) | copy-start | bytes 3932164
  994.0 32.4 %collective-permute-start.1 = (bf16[128,5120]{1,0:T(8,128)(2,1)S(1)}, bf16[128,5120]{1,0:T(8,128)(2,1)S(1)}, u32[]{:S(2)}, u32[]{:S(2)}) collective-permute-start(bf16[128,5120]{1,0:T(8,128)(2,1)S(1)} %add_convert_fusion.2), channel_id=1, source_target_pairs={{8,0},{16,8},{24,16},{9,1},{17,9},{25,17},{10,2},{18,10},{26,18},{... | collective-permute-start | bytes 3932168 | tf_op jit(solution)/shard_map/ppermute | solution.py:15
  1026.4 1.1 copy-start.2
  1067.6 32.4 %copy-start.8 = (bf16[128,5120]{1,0:T(8,128)(2,1)}, bf16[128,5120]{1,0:T(8,128)(2,1)S(1)}, u32[]{:S(2)}) copy-start(bf16[128,5120]{1,0:T(8,128)(2,1)S(1)} %add_convert_fusion.1) | copy-start | bytes 3932164
  1067.6 32.4 %collective-permute-start.2 = (bf16[128,5120]{1,0:T(8,128)(2,1)S(1)}, bf16[128,5120]{1,0:T(8,128)(2,1)S(1)}, u32[]{:S(2)}, u32[]{:S(2)}) collective-permute-start(bf16[128,5120]{1,0:T(8,128)(2,1)S(1)} %add_convert_fusion.1), channel_id=1, source_target_pairs={{8,0},{16,8},{24,16},{9,1},{17,9},{25,17},{10,2},{18,10},{26,18},{... | collective-permute-start | bytes 3932168 | tf_op jit(solution)/shard_map/ppermute | solution.py:15
  1100.0 1.1 copy-start.4
  1104.8 22.5 %all-to-all-start.6 = ((bf16[8,9,5120]{2,1,0:T(8,128)(2,1)}), bf16[8,9,5120]{2,1,0:T(8,128)(2,1)}, u32[]{:S(2)}, u32[]{:S(2)}) async-start(bf16[8,9,5120]{2,1,0:T(8,128)(2,1)} %reshape.267), calls=%async_computation.6 | async-start | bytes 2621440 | tf_op jit(solution)/shard_map/all_to_all | solution.py:117
  1132.4 9.6 all-to-all-start.7
  1138.8 9.1 copy-start.5
  1143.7 8.7 all-to-all-start.8
  1932.9 0.6 copy-start.9
  1932.9 0.6 copy-start.10
where the time goes:
time: 1940 us; the launch traced here: 1930 us
  matrix products  1160 us (60%)
  local copies, waits for them, and re-layouts  538 us (28%)
  waiting for transfers between devices  119 us (6%)
  blocking collectives  58.9 us (3%)
  starting transfers between devices  25.1 us (1%)
  other arithmetic  23.5 us (1%)
    dot_general x24, matrix products, grad_block(): lax.dot_general(scaled, onehot, (((0,), (0,)), ((), ())), preferred_eleme...  568 us
    dot_general x24, matrix products, decode_block(): lax.dot_general(code_book[book_index], onehot, (((0,), (1,)), ((), ())),...  549 us
    broadcast_in_dim x12, local copies, waits for them, and re-layouts, on_device(): plain_w, weight = lax.map(decode_block, blocked_codes)  180 us
    reshape x12, local copies, waits for them, and re-layouts, grad_block(): scaled = (grad_w * gain_row[None, :]).astype(jnp.bfloat16).reshape(row_bl...  161 us
    add x12, local copies, waits for them, and re-layouts, decode_block(): plain_t + lax.dot_general(code_book[book_index], onehot, (((0,), (1,)), (...  118 us
    ppermute x3, waiting for transfers between devices, shifted(): lax.ppermute(value, axis, [(source, source + steps) for source in range(l...  93.5 us
    all_to_all x2, blocking collectives, on_device(): lax.all_to_all(outgoing, 'expert', split_axis=0, concat_axis=0, tiled=True)  44.8 us
  transfers between devices with their start and end apart: 8, of which 6 were waited for; matrix products, arithmetic and copies ran while one was open for 46% of the time, Pallas kernels for 0%

commit v1 on v0

v1 whole, which is shorter than its diff:
```python
import functools

import jax
import jax.numpy as jnp
from jax import lax
from jax.experimental import pallas as pl
from jax.experimental.pallas import tpu as pltpu
from jax.sharding import PartitionSpec as P

MOST = 9
ROUTE_SCALE = 16.0
LANES = 128
LOW = 8
F32 = jnp.float32
BF16 = jnp.bfloat16


def params(mib):
    return pltpu.CompilerParams(vmem_limit_bytes=mib << 20)


def dot(a, b):
    return jnp.dot(a, b, preferred_element_type=F32)


def dot_nt(a, b):
    return lax.dot_general(a, b, (((1,), (1,)), ((), ())), preferred_element_type=F32)


def dot_tn(a, b):
    return lax.dot_general(a, b, (((0,), (0,)), ((), ())), preferred_element_type=F32)


def iota(shape, axis):
    return lax.broadcasted_iota(jnp.int32, shape, axis)


def lane_gather(table, index):
    return lax.gather(
        table,
        index[..., None],
        lax.GatherDimensionNumbers(
            offset_dims=(),
            collapsed_slice_dims=(1,),
            start_index_map=(1,),
            operand_batching_dims=(0,),
            start_indices_batching_dims=(0,),
        ),
        slice_sizes=(1, 1),
        mode=lax.GatherScatterMode.PROMISE_IN_BOUNDS,
    )


def slot_expert(rows, columns):
    first = MOST * iota((rows, columns), 1)
    row = iota((rows, columns), 0)
    return (row >= first) & (row < first + MOST)


def prepare_kernel(experts, logits_ref, routes_ref, grad_ref, probs_ref, select_ref, rows_ref):
    tokens, routed = logits_ref.shape
    top = routes_ref.shape[0]
    width = grad_ref.shape[1]
    rows = experts * MOST
    raised = jnp.exp(logits_ref[...])
    probs = raised / jnp.sum(raised, axis=1, keepdims=True)
    probs_ref[...] = probs
    expert = iota((experts, tokens), 0)
    hits = jnp.zeros((experts, tokens), F32)
    for k in range(top):
        hits = hits + (routes_ref[k : k + 1, :] == expert).astype(F32)
    hits = hits.astype(BF16)
    earlier = (iota((tokens, tokens), 0) < iota((tokens, tokens), 1)).astype(F32).astype(BF16)
    position = dot(hits, earlier).astype(BF16)
    owner = slot_expert(rows, experts)
    spread_out = owner.astype(F32).astype(BF16)
    slot_hit = dot(spread_out, hits)
    slot_position = dot(spread_out, position)
    first = jnp.sum(
        jnp.where(owner, (MOST * iota((rows, experts), 1)).astype(F32), 0.0), axis=1, keepdims=True
    )
    place = iota((rows, tokens), 0).astype(F32) - first
    select = jnp.where(
        (slot_hit > 0.5) & (jnp.abs(slot_position - place) < 0.5), 1.0, 0.0
    ).astype(BF16)
    select_ref[...] = select
    gate = (ROUTE_SCALE * probs).astype(BF16)
    slot_gate = jnp.sum(
        jnp.where(slot_expert(rows, routed), dot(select, gate), 0.0), axis=1, keepdims=True
    )
    rows_ref[:, :width] = dot(select, grad_ref[...]).astype(BF16)
    rows_ref[:, width:] = jnp.broadcast_to(slot_gate, (rows, LANES)).astype(BF16)


def decode_kernel(codes_ref, table_ref, hidden_ref, scale_ref, plain_out_ref, out_ref, weight_ref):
    step = pl.program_id(0)
    books, block, groups = codes_ref.shape
    entries = table_ref.shape[1]
    size = table_ref.shape[2]
    rows = hidden_ref.shape[0]

    @pl.when(step == 0)
    def _():
        plain_out_ref[...] = jnp.zeros_like(plain_out_ref)

    for chunk in range(groups // LANES):
        lanes = slice(chunk * LANES, (chunk + 1) * LANES)

        def decode_rows(index, carry):
            values = [[] for _ in range(size)]
            for half in range(2):
                at = pl.ds(pl.multiple_of(index * 16 + 8 * half, 8), 8)
                codes = [codes_ref[b, at, lanes] for b in range(books)]
                low = [c & (LANES - 1) for c in codes]
                part = [c >= LANES for c in codes]
                for i in range(size):
                    total = None
                    for b in range(books):
                        value = jnp.where(
                            part[b],
                            lane_gather(table_ref[b, 1, i], low[b]),
                            lane_gather(table_ref[b, 0, i], low[b]),
                        )
                        total = value if total is None else total + value
                    values[i].append(total)
            at = pl.ds(pl.multiple_of(index * 16, 16), 16)
            for i in range(size):
                weight_ref[at, i * LANES : (i + 1) * LANES] = jnp.concatenate(values[i], 0).astype(
                    BF16
                )
            return carry

        lax.fori_loop(0, block // 16, decode_rows, 0)
        product = dot(hidden_ref[...], weight_ref[...])
        for i in range(size):
            plain_out_ref[i, :, lanes] += product[:, i * LANES : (i + 1) * LANES]

    @pl.when(step == pl.num_programs(0) - 1)
    def _():
        span = size * LANES
        column = iota((span, span), 0)
        source = size * (column & (LANES - 1)) + column // LANES
        back = (source == iota((span, span), 1)).astype(F32).astype(BF16)
        for chunk in range(groups // LANES):
            lanes = slice(chunk * LANES, (chunk + 1) * LANES)
            split = jnp.concatenate(
                [plain_out_ref[i, :, lanes] * scale_ref[i : i + 1, lanes] for i in range(size)], 1
            ).astype(BF16)
            out_ref[:, chunk * span : (chunk + 1) * span] = dot(split, back).astype(BF16)


def score_kernel(out_ref, slots_ref, router_ref, score_ref):
    rows, width = out_ref.shape
    wide = router_ref.shape[1]
    extra = score_ref.shape[1] - wide
    out = out_ref[...]
    base = jnp.sum(slots_ref[:, :width].astype(F32) * out.astype(F32), axis=1, keepdims=True)
    high = base.astype(BF16)
    rest = base - high.astype(F32)
    middle = rest.astype(BF16)
    low = (rest - middle.astype(F32)).astype(BF16)
    score_ref[:, :wide] = dot(out, router_ref[...]).astype(BF16)
    column = iota((rows, extra), 1)
    score_ref[:, wide:] = jnp.where(
        column == 0,
        high.astype(F32),
        jnp.where(
            column == 1, middle.astype(F32), jnp.where(column == 2, low.astype(F32), 0.0)
        ),
    ).astype(BF16)


def chain_kernel(scores_ref, later_ref, probs_ref, select_ref, own_ref, send_ref, picked_ref):
    rows = scores_ref.shape[0]
    tokens, wide = later_ref.shape
    routed = probs_ref.shape[1]
    later = later_ref[...]
    select = select_ref[...]
    picked = dot(select, later)
    picked_ref[...] = picked.astype(BF16)
    score = jnp.sum(picked * scores_ref[:, :wide].astype(F32), axis=1, keepdims=True) + jnp.sum(
        scores_ref[:, wide:].astype(F32), axis=1, keepdims=True
    )
    score = score.astype(BF16).astype(F32)
    placed = jnp.where(slot_expert(rows, routed), score, 0.0).astype(BF16)
    spread = dot_tn(select, placed)
    probs = probs_ref[...]
    weighted = jnp.sum(probs * spread, axis=1, keepdims=True)
    own = (ROUTE_SCALE * probs * (spread - weighted)).astype(BF16)
    own_ref[...] = own
    put = (iota((routed, wide), 0) == iota((routed, wide), 1)).astype(F32).astype(BF16)
    shift = (iota((wide, wide), 0) + routed == iota((wide, wide), 1)).astype(F32).astype(BF16)
    send_ref[...] = (dot(own, put) + dot(later, shift)).astype(BF16)


def add_layers(current, later, router, routed):
    count = later.shape[1] // routed
    column = iota(later.shape, 1)
    for s in range(count - 1, -1, -1):
        part = jnp.where(
            (column >= s * routed) & (column < (s + 1) * routed), later.astype(F32), 0.0
        ).astype(BF16)
        current = (current.astype(F32) + dot_nt(part, router)).astype(BF16)
    return current


def finish_kernel(grad_ref, later_ref, own_ref, routers_ref, router_ref, result_ref):
    current = add_layers(grad_ref[...], later_ref[...], routers_ref[...], own_ref.shape[1])
    added = dot_nt(own_ref[...], router_ref[...])
    result_ref[...] = (current.astype(F32) + added).astype(BF16)


def slots_kernel(
    routed, slots_ref, gates_ref, later_ref, routers_ref, plain_out_ref, split_ref, scale_grad_ref
):
    span = slots_ref.shape[1]
    size = span // LANES
    current = add_layers(slots_ref[...], later_ref[...], routers_ref[...], routed)
    gate = gates_ref[:, :1].astype(F32)
    grad = (gate * current.astype(F32)).astype(BF16)
    column = iota((span, span), 1)
    source = size * (column & (LANES - 1)) + column // LANES
    split = dot(grad, (source == iota((span, span), 0)).astype(F32).astype(BF16))
    for i in range(size):
        part = split[:, i * LANES : (i + 1) * LANES]
        split_ref[i] = part.astype(BF16)
        scale_grad_ref[i : i + 1, :] = jnp.sum(part * plain_out_ref[i], axis=0, keepdims=True)


def book_kernel(
    unroll, hidden_ref, slots_ref, scale_ref, codes_ref, out_ref, grad_ref, high_ref, low_ref
):
    books, block, groups = codes_ref.shape
    size = slots_ref.shape[0]
    high_count = out_ref.shape[1]
    chunks = groups // LANES

    @pl.when(pl.program_id(0) == 0)
    def _():
        out_ref[...] = jnp.zeros_like(out_ref)

    hidden = hidden_ref[...]
    for i in range(size):
        grad = dot(hidden, slots_ref[i]) * scale_ref[i : i + 1, :]
        for c in range(chunks):
            grad_ref[c, pl.ds(i, block, stride=size), :] = grad[:, c * LANES : (c + 1) * LANES]
    for b in range(books):
        codes = codes_ref[b]
        high_ref[b] = (codes >> 3).astype(F32)
        low_ref[b] = (codes & (LOW - 1)).astype(F32)
    row = iota((16, groups), 0)
    high_rows = [(row + 16 * k).astype(F32).astype(BF16) for k in range(high_count // 16)]
    low_rows = [((row >> 3) + 2 * k).astype(F32).astype(BF16) for k in range(LOW // 2)]
    one = jnp.ones((16, groups), BF16)
    zero = jnp.zeros((16, groups), BF16)

    def add_rows(index, totals):
        totals = list(totals)
        for pair in range(unroll // 2):
            left = [[] for _ in range(books)]
            right = [[] for _ in range(books)]
            for member in range(2):
                f = index * unroll + pair * 2 + member
                at = pl.ds(pl.multiple_of(f * size, size), size)
                values = jnp.concatenate([grad_ref[c, at, :] for c in range(chunks)], 1)
                values = jnp.concatenate([values, values], 0).astype(BF16)
                for b in range(books):
                    high = jnp.broadcast_to(high_ref[b, pl.ds(f, 1), :], (16, groups)).astype(BF16)
                    low = jnp.broadcast_to(low_ref[b, pl.ds(f, 1), :], (16, groups)).astype(BF16)
                    left[b].append(
                        jnp.concatenate([jnp.where(high == r, one, zero) for r in high_rows], 0)
                    )
                    right[b].append(
                        jnp.concatenate([jnp.where(low == r, values, zero) for r in low_rows], 0)
                    )
            for b in range(books):
                totals[b] = totals[b] + dot_nt(
                    jnp.concatenate(left[b], 1), jnp.concatenate(right[b], 1)
                )
        return tuple(totals)

    start = tuple(jnp.zeros(out_ref.shape[1:], F32) for _ in range(books))
    totals = lax.fori_loop(0, block // unroll, add_rows, start)
    for b in range(books):
        out_ref[b] += totals[b]


def whole(shape):
    return pl.BlockSpec(shape, lambda s: (0,) * len(shape))


def exchange(value):
    return lax.all_to_all(value, "expert", split_axis=0, concat_axis=0, tiled=True)


def on_device(out_grad, saved_inputs, router, routes, hidden_saved, codes, codebook, scale):
    experts = lax.axis_size("expert")
    layers = lax.axis_size("pipe")
    tokens, width = out_grad.shape
    routed = router.shape[2]
    codes = codes[0, 0]
    codebook = codebook[0, 0]
    hidden = hidden_saved[0, 0]
    router = router[0]
    inner = hidden.shape[1]
    books, _, groups = codes.shape
    entries, size = codebook.shape[1:]
    rows = experts * MOST
    later_count = layers - 1
    wide = later_count * routed
    score_wide = -(-(wide + 3) // LANES) * LANES
    scale_split = scale[0, 0].reshape(groups, size).T

    share = width // experts
    own_share = lax.dynamic_slice_in_dim(router, lax.axis_index("expert") * share, share, 0)
    shares = [
        lax.ppermute(own_share, "pipe", [(p, p - s) for p in range(s, layers)])
        for s in range(1, layers)
    ]
    routers = lax.all_gather(jnp.concatenate(shares, 1), "expert", axis=0, tiled=True)

    logits = dot(saved_inputs[0], router)
    probs, select, outgoing = pl.pallas_call(
        functools.partial(prepare_kernel, experts),
        out_shape=(
            jax.ShapeDtypeStruct((tokens, routed), F32),
            jax.ShapeDtypeStruct((rows, tokens), BF16),
            jax.ShapeDtypeStruct((rows, width + LANES), BF16),
        ),
        compiler_params=params(32),
        name="prepare",
    )(logits, routes[0].T, out_grad)
    slots = exchange(outgoing.reshape(experts, MOST, width + LANES)).reshape(rows, width + LANES)

    halves = entries // LANES
    table = codebook.astype(F32).transpose(0, 2, 1).reshape(books, size, halves, LANES)
    table = jnp.broadcast_to(
        table.transpose(0, 2, 1, 3)[:, :, :, None, :], (books, halves, size, 8, LANES)
    )
    block = 256
    plain_out, expert_out = pl.pallas_call(
        decode_kernel,
        grid=(inner // block,),
        in_specs=[
            pl.BlockSpec((books, block, groups), lambda s: (0, s, 0)),
            whole((books, halves, size, 8, LANES)),
            pl.BlockSpec((rows, block), lambda s: (0, s)),
            whole((size, groups)),
        ],
        out_specs=[whole((size, rows, groups)), whole((rows, width))],
        out_shape=[
            jax.ShapeDtypeStruct((size, rows, groups), F32),
            jax.ShapeDtypeStruct((rows, width), BF16),
        ],
        scratch_shapes=[pltpu.VMEM((block, size * LANES), BF16)],
        compiler_params=params(48),
        cost_estimate=pl.CostEstimate(
            flops=50_000_000_000, bytes_accessed=10_000_000, transcendentals=0
        ),
        name="decode",
    )(codes, table, hidden, scale_split)

    scores = pl.pallas_call(
        score_kernel,
        out_shape=jax.ShapeDtypeStruct((rows, score_wide), BF16),
        compiler_params=params(48),
        name="scores",
    )(expert_out, slots, routers)
    scores = exchange(scores.reshape(experts, MOST, score_wide)).reshape(rows, score_wide)

    chain = pl.pallas_call(
        chain_kernel,
        out_shape=(
            jax.ShapeDtypeStruct((tokens, routed), BF16),
            jax.ShapeDtypeStruct((tokens, wide), BF16),
            jax.ShapeDtypeStruct((rows, wide), BF16),
        ),
        compiler_params=params(32),
        name="chain",
    )
    later = jnp.zeros((tokens, wide), BF16)
    for step in range(layers):
        own, send, picked = chain(scores, later, probs, select)
        if step + 1 < layers:
            later = lax.ppermute(send, "pipe", [(p, p - 1) for p in range(1, layers)])

    slot_later = exchange(picked.reshape(experts, MOST, wide)).reshape(rows, wide)

    span = size * LANES
    result = pl.pallas_call(
        finish_kernel,
        grid=(width // span,),
        in_specs=[
            pl.BlockSpec((tokens, span), lambda s: (0, s)),
            whole((tokens, wide)),
            whole((tokens, routed)),
            pl.BlockSpec((span, wide), lambda s: (s, 0)),
            pl.BlockSpec((span, routed), lambda s: (s, 0)),
        ],
        out_specs=pl.BlockSpec((tokens, span), lambda s: (0, s)),
        out_shape=jax.ShapeDtypeStruct((tokens, width), BF16),
        compiler_params=params(32),
        name="finish",
    )(out_grad, later, own, routers, router)

    slot_split, scale_grad = pl.pallas_call(
        functools.partial(slots_kernel, routed),
        grid=(width // span,),
        in_specs=[
            pl.BlockSpec((rows, span), lambda s: (0, s)),
            pl.BlockSpec((rows, LANES), lambda s: (0, width // LANES)),
            whole((rows, wide)),
            pl.BlockSpec((span, wide), lambda s: (s, 0)),
            pl.BlockSpec((size, rows, LANES), lambda s: (0, 0, s)),
        ],
        out_specs=[
            pl.BlockSpec((size, rows, LANES), lambda s: (0, 0, s)),
            pl.BlockSpec((size, LANES), lambda s: (0, s)),
        ],
        out_shape=[
            jax.ShapeDtypeStruct((size, rows, groups), BF16),
            jax.ShapeDtypeStruct((size, groups), F32),
        ],
        compiler_params=params(48),
        name="slot_grads",
    )(slots, slots, slot_later, routers, plain_out)

    block = 64
    unroll = 16
    high_count = entries // LOW
    book_grad = pl.pallas_call(
        functools.partial(book_kernel, unroll),
        grid=(inner // block,),
        in_specs=[
            pl.BlockSpec((block, rows), lambda s: (s, 0)),
            whole((size, rows, groups)),
            whole((size, groups)),
            pl.BlockSpec((books, block, groups), lambda s: (0, s, 0)),
        ],
        out_specs=whole((books, high_count, LOW * size)),
        out_shape=jax.ShapeDtypeStruct((books, high_count, LOW * size), F32),
        scratch_shapes=[
            pltpu.VMEM((groups // LANES, block * size, LANES), F32),
            pltpu.VMEM((books, block, groups), F32),
            pltpu.VMEM((books, block, groups), F32),
        ],
        compiler_params=params(48),
        name="book_grads",
    )(hidden.T, slot_split, scale_split, codes)

    book_grad = book_grad.reshape(books, entries, size)
    scale_grad = scale_grad.T.reshape(width)
    return (result[None], book_grad[None, None], scale_grad[None, None])


def solution(mesh):
    placed = (
        P("expert", None),
        P("pipe", "expert", None),
        P("pipe", None, None),
        P("pipe", "expert", None),
        P("pipe", "expert", None, None),
        P("pipe", "expert", None, None, None),
        P("pipe", "expert", None, None, None),
        P("pipe", "expert", None),
    )
    return jax.shard_map(
        on_device,
        mesh=mesh,
        in_specs=placed,
        out_specs=(
            P("pipe", "expert", None),
            P("pipe", "expert", None, None, None),
            P("pipe", "expert", None),
        ),
        check_vma=False,
    )
```

time: 1940 us -> 255 us (0.13)
  matrix products: 1160 us -> 2.19 us
  local copies, waits for them, and re-layouts: 538 us -> 30.8 us
  Pallas kernels: 0 us -> 131 us
  waiting for transfers between devices: 119 us -> 46.8 us
  blocking collectives: 58.9 us -> 9.87 us
  other arithmetic: 23.5 us -> 1.91 us
    dot_general x75 -> x1, matrix products: 1160 us -> 2.19 us  [dot(): return jnp.dot(a, b, preferred_element_type=F32)]
    broadcast_in_dim x12 -> x2, local copies, waits for them, and re-layouts: 180 us -> 0.05 us  [the longest x1 0.03 us: on_device(): jnp.broadcast_to(table.transpose(0, 2, 1, 3)[:, :, :, None, :], (books, h...]
    reshape x24 -> x6, local copies, waits for them, and re-layouts: 171 us -> 8.79 us  [the longest x1 1.69 us: on_device(): exchange(outgoing.reshape(experts, MOST, width + LANES))]
    pallas_call x0 -> x10, Pallas kernels: none -> 131 us  [the longest x1 59.9 us: on_device(): pl.pallas_call(decode_kernel, grid=(inner // block,), in_specs=[pl.BlockS...]
    add x12 -> x0, local copies, waits for them, and re-layouts: 118 us -> none  [decode_block(): plain_t + lax.dot_general(code_book[book_index], onehot, (((0,), (1,)), (...]
    all_to_all x4 -> x1, blocking collectives: 58.9 us -> 9.87 us  [exchange(): lax.all_to_all(value, 'expert', split_axis=0, concat_axis=0, tiled=True)]
    ppermute x3 -> x6, waiting for transfers between devices: 93.5 us -> 46.8 us  [the longest x3 24.3 us: on_device(): lax.ppermute(own_share, 'pipe', [(p, p - s) for p in range(s, layers)])]
    all_to_all x5 -> x2, waiting for transfers between devices: 25.4 us -> 0.01 us  [exchange(): lax.all_to_all(value, 'expert', split_axis=0, concat_axis=0, tiled=True)]
  transfers between devices with their start and end apart: 8 -> 9, of which waited for: 6 -> 5; matrix products, arithmetic and copies ran while one was open for 46% -> 5% of each run, Pallas kernels for 0% -> 27%
where the time goes in v1:
time: 255 us; the launch traced here: 254 us
  Pallas kernels  131 us (51%)
  waiting for transfers between devices  46.8 us (18%)
  local copies, waits for them, and re-layouts  30.8 us (12%)
  starting transfers between devices  16.4 us (6%)
  between operations  14.3 us (6%)
  blocking collectives  9.87 us (4%)
    pallas_call x1, Pallas kernels, on_device(): pl.pallas_call(decode_kernel, grid=(inner // block,), in_specs=[pl.BlockS...  59.9 us
    pallas_call x1, Pallas kernels, on_device(): pl.pallas_call(functools.partial(book_kernel, unroll), grid=(inner // blo...  45.8 us
    ppermute x3, waiting for transfers between devices, on_device(): lax.ppermute(own_share, 'pipe', [(p, p - s) for p in range(s, layers)])  24.3 us
    ppermute x3, waiting for transfers between devices, on_device(): later = lax.ppermute(send, 'pipe', [(p, p - 1) for p in range(1, layers)])  22.5 us
    unnamed x47, local copies, waits for them, and re-layouts  19.3 us
    all_to_all x1, blocking collectives, exchange(): lax.all_to_all(value, 'expert', split_axis=0, concat_axis=0, tiled=True)  9.87 us
    pallas_call x1, Pallas kernels, on_device(): pl.pallas_call(functools.partial(slots_kernel, routed), grid=(width // sp...  9.51 us
    all_to_all x2, starting transfers between devices, exchange(): lax.all_to_all(value, 'expert', split_axis=0, concat_axis=0, tiled=True)  8.64 us
  transfers between devices with their start and end apart: 9, of which 5 were waited for; matrix products, arithmetic and copies ran while one was open for 5% of the time, Pallas kernels for 27%

profile of v1, /device:TPU:0, one launch (start us, length us, event | category | flops | bytes accessed | tf_op | source)
XLA Modules:
  0.0 253.8 jit_solution(8755578610904788080)
XLA Ops:
  8.5 1.3 collective-permute-start.2
  9.8 1.3 collective-permute-start.1
  11.1 1.3 collective-permute-start
  12.4 11.1 %collective-permute-done.2 = bf16[640,160]{1,0:T(8,128)(2,1)S(1)} collective-permute-done((bf16[640,160]{1,0:T(8,128)(2,1)S(1)}, bf16[640,160]{1,0:T(8,128)(2,1)S(1)}, u32[]{:S(2)}, u32[]{:S(2)}) %collective-permute-start.2) | collective-permute-done | bytes 204832 | tf_op jit(solution)/shard_map/ppermute | solution.py:317
  23.5 13.2 %collective-permute-done.1 = bf16[640,160]{1,0:T(8,128)(2,1)S(1)} collective-permute-done((bf16[640,160]{1,0:T(8,128)(2,1)S(1)}, bf16[640,160]{1,0:T(8,128)(2,1)S(1)}, u32[]{:S(2)}, u32[]{:S(2)}) %collective-permute-start.1) | collective-permute-done | bytes 204832 | tf_op jit(solution)/shard_map/ppermute | solution.py:317
  36.6 1.2 pad_maximum_fusion
  37.9 2.2 fusion.logits_ref
  40.8 1.4 reshape.33
  42.2 4.5 %all-to-all-start = ((bf16[8,9,5248]{2,1,0:T(8,128)(2,1)}), bf16[8,9,5248]{2,1,0:T(8,128)(2,1)}, u32[]{:S(2)}, u32[]{:S(2)}) async-start(bf16[8,9,5248]{2,1,0:T(8,128)(2,1)} %reshape.33), calls=%async_computation | async-start | bytes 2686976 | tf_op jit(solution)/shard_map/all_to_all | solution.py:293
  48.2 59.9 %decode.1 = (f32[8,72,640]{2,1,0:T(8,128)S(1)}, bf16[72,5120]{1,0:T(8,128)(2,1)S(1)}) custom-call(s32[2,768,640]{2,1,0:T(8,128)} %bitcast.31, f32[2,2,8,8,128]{4,3,2,1,0:T(8,128)S(1)} %broadcast_in_dim.12.table_ref, bf16[72,768]{1,0:T(8,128)(2,1)S(1)} %bitcast.34, f32[8,640]{1,0:T(8,128)S(1)} %bitcast.35), custom_call_target="tpu_custom_call" | custom-call | flops 49999998976 | bytes 10000000 | tf_op jit(solution)/shard_map/decode/pallas_call | solution.py:341
  110.1 1.7 reshape.34.slots_ref.gates_ref
  113.0 3.5 %scores.1 = bf16[72,512]{1,0:T(8,128)(2,1)S(1)} custom-call(bf16[72,5120]{1,0:T(8,128)(2,1)S(1)} %copy-done.10, bf16[72,5248]{1,0:T(8,128)(2,1)S(1)} %reshape.34.slots_ref.gates_ref, bf16[5120,480]{1,0:T(8,128)(2,1)} %all-gather.2.cloned.1.call-done.router_ref.routers_ref), custom_call_target="tpu_custom_call" | custom-call | tf_op jit(solution)/shard_map/scores/pallas_call | solution.py:363
  117.1 1.6 reshape.35
  118.7 9.9 %all_to_all.15 = bf16[8,9,512]{2,1,0:T(8,128)(2,1)} all-to-all(bf16[8,9,512]{2,1,0:T(8,128)(2,1)} %reshape.35), channel_id=1, replica_groups=mesh['pipe'=4,'expert'=8] {'expert'}, dimensions={0} | all-to-all | bytes 147456 | tf_op jit(solution)/shard_map/all_to_all | solution.py:293
  128.6 1.6 reshape.36.scores_ref
  132.2 1.3 collective-permute-start.3
  133.5 11.4 %collective-permute-done.3.later_ref = bf16[128,480]{1,0:T(8,128)(2,1)S(1)} collective-permute-done((bf16[128,480]{1,0:T(8,128)(2,1)S(1)}, bf16[128,480]{1,0:T(8,128)(2,1)S(1)}, u32[]{:S(2)}, u32[]{:S(2)}) %collective-permute-start.3) | collective-permute-done | bytes 122912 | tf_op jit(solution)/shard_map/ppermute | solution.py:385
  146.0 1.3 collective-permute-start.4
  147.3 5.6 %collective-permute-done.4.later_ref = bf16[128,480]{1,0:T(8,128)(2,1)S(1)} collective-permute-done((bf16[128,480]{1,0:T(8,128)(2,1)S(1)}, bf16[128,480]{1,0:T(8,128)(2,1)S(1)}, u32[]{:S(2)}, u32[]{:S(2)}) %collective-permute-start.4) | collective-permute-done | bytes 122912 | tf_op jit(solution)/shard_map/ppermute | solution.py:385
  153.9 1.3 collective-permute-start.5
  155.2 5.6 %collective-permute-done.5.later_ref = bf16[128,480]{1,0:T(8,128)(2,1)S(1)} collective-permute-done((bf16[128,480]{1,0:T(8,128)(2,1)S(1)}, bf16[128,480]{1,0:T(8,128)(2,1)S(1)}, u32[]{:S(2)}, u32[]{:S(2)}) %collective-permute-start.5) | collective-permute-done | bytes 122912 | tf_op jit(solution)/shard_map/ppermute | solution.py:385
  160.8 1.3 chain.7
  163.3 1.6 reshape.37
  164.9 4.2 %all-to-all-start.2 = ((bf16[8,9,480]{2,1,0:T(8,128)(2,1)}), bf16[8,9,480]{2,1,0:T(8,128)(2,1)}, u32[]{:S(2)}, u32[]{:S(2)}) async-start(bf16[8,9,480]{2,1,0:T(8,128)(2,1)} %reshape.37), calls=%async_computation.2 | async-start | bytes 262144 | tf_op jit(solution)/shard_map/all_to_all | solution.py:293
  169.1 1.7 copy.17
  170.8 4.0 %copy.20 = bf16[1,5120,160]{2,1,0:T(8,128)(2,1)} copy(bf16[1,5120,160]{1,2,0:T(8,128)(2,1)} %param.10) | data formatting | bytes 3276800 | tf_op args[2]
  174.8 2.5 copy-done.1
  177.3 1.7 copy-done.2
  179.9 7.5 %finish.1 = bf16[128,5120]{1,0:T(8,128)(2,1)} custom-call(bf16[128,5120]{1,0:T(8,128)(2,1)S(1)} %copy-done.3, bf16[128,480]{1,0:T(8,128)(2,1)S(1)} %copy-done.12, bf16[128,160]{1,0:T(8,128)(2,1)S(1)} %copy-done.17, bf16[5120,480]{1,0:T(8,128)(2,1)S(1)} %copy-done.1, bf16[5120,160]{1,0:T(8,128)(2,1)S(1)} %bitcast.30), custom_call_target="tpu_custom_call" | custom-call | tf_op jit(solution)/shard_map/finish/pallas_call | solution.py:390
  188.4 1.4 copy-done.7
  189.7 9.5 %slot_grads.1 = (bf16[8,72,640]{2,1,0:T(8,128)(2,1)S(1)}, f32[8,640]{1,0:T(8,128)S(1)}) custom-call(bf16[72,5248]{1,0:T(8,128)(2,1)S(1)} %reshape.34.slots_ref.gates_ref, bf16[72,5248]{1,0:T(8,128)(2,1)S(1)} %reshape.34.slots_ref.gates_ref, bf16[72,480]{1,0:T(8,128)(2,1)S(1)} %reshape.38.later_ref, ...), custom_call_target="tpu_custom_call" | custom-call | tf_op jit(solution)/shard_map/slot_grads/pallas_call | solution.py:406
  199.3 45.8 %book_grads.1 = f32[2,32,64]{2,1,0:T(8,128)S(1)} custom-call(bf16[768,72]{1,0:T(8,128)(2,1)S(1)} %bitcast.33, bf16[8,72,640]{2,1,0:T(8,128)(2,1)S(1)} %get-tuple-element.25.slots_ref, f32[8,640]{1,0:T(8,128)S(1)} %bitcast.36, s32[2,768,640]{2,1,0:T(8,128)S(1)} %bitcast.32), custom_call_target="tpu_custom_call" | custom-call | tf_op jit(solution)/shard_map/book_grads/pallas_call | solution.py:431
  (64 shorter events, 16.4 us)
Async XLA Ops:
  7.2 30.7 %copy-start = (bf16[1,128,5120]{2,1,0:T(8,128)(2,1)S(1)}, bf16[1,128,5120]{2,1,0:T(8,128)(2,1)}, u32[]{:S(2)}) copy-start(bf16[1,128,5120]{2,1,0:T(8,128)(2,1)} %param.9) | copy-start | bytes 3932164
  7.2 104.7 %all-gather.2.cloned.1.call-start = ((), (), s32[]{:S(2)}) async-start(), calls=%async_computation.3 | async-start | bytes 5898240 | tf_op jit(solution)/shard_map/all_gather | solution.py:320
  8.3 29.6 %copy-start.20 = (s32[1,128,6]{1,0,2:T(1,128)S(1)}, s32[1,128,6]{1,0,2:T(1,128)}, u32[]{:S(2)}) copy-start(s32[1,128,6]{1,0,2:T(1,128)} %param.11) | copy-start | bytes 9220
  8.5 15.0 %collective-permute-start.2 = (bf16[640,160]{1,0:T(8,128)(2,1)S(1)}, bf16[640,160]{1,0:T(8,128)(2,1)S(1)}, u32[]{:S(2)}, u32[]{:S(2)}) collective-permute-start(bf16[640,160]{1,0:T(8,128)(2,1)S(1)} %bitcast.40), channel_id=1, source_target_pairs={{24,0},{25,1},{26,2},{27,3},{28,4},{29,5},{30,6},{31,7}} | collective-permute-start | bytes 614408 | tf_op jit(solution)/shard_map/ppermute | solution.py:317
  9.8 26.9 %collective-permute-start.1 = (bf16[640,160]{1,0:T(8,128)(2,1)S(1)}, bf16[640,160]{1,0:T(8,128)(2,1)S(1)}, u32[]{:S(2)}, u32[]{:S(2)}) collective-permute-start(bf16[640,160]{1,0:T(8,128)(2,1)S(1)} %bitcast.41), channel_id=1, source_target_pairs={{16,0},{24,8},{17,1},{25,9},{18,2},{26,10},{19,3},{27,11},{20,4},{... | collective-permute-start | bytes 614408 | tf_op jit(solution)/shard_map/ppermute | solution.py:317
  11.1 25.6 %collective-permute-start = (bf16[640,160]{1,0:T(8,128)(2,1)S(1)}, bf16[640,160]{1,0:T(8,128)(2,1)S(1)}, u32[]{:S(2)}, u32[]{:S(2)}) collective-permute-start(bf16[640,160]{1,0:T(8,128)(2,1)S(1)} %bitcast.42), channel_id=1, source_target_pairs={{8,0},{16,8},{24,16},{9,1},{17,9},{25,17},{10,2},{18,10},{26,18},{... | collective-permute-start | bytes 614408 | tf_op jit(solution)/shard_map/ppermute | solution.py:317
  37.9 2.2 copy-start.3
  42.2 5.0 %copy-start.18 = (f32[1,1,5120]{2,1,0:T(1,128)S(1)}, f32[1,1,5120]{2,1,0:T(1,128)}, u32[]{:S(2)}) copy-start(f32[1,1,5120]{2,1,0:T(1,128)} %param.15) | copy-start | bytes 61444
  42.2 6.0 %copy-start.19 = (bf16[1,1,2,256,8]{3,4,2,1,0:T(8,128)(2,1)S(1)}, bf16[1,1,2,256,8]{3,4,2,1,0:T(8,128)(2,1)}, u32[]{:S(2)}) copy-start(bf16[1,1,2,256,8]{3,4,2,1,0:T(8,128)(2,1)} %param.14) | copy-start | bytes 24580
  42.2 6.0 %copy-start.14 = (bf16[1,1,72,768]{3,2,1,0:T(8,128)(2,1)S(1)}, bf16[1,1,72,768]{3,2,1,0:T(8,128)(2,1)}, u32[]{:S(2)}) copy-start(bf16[1,1,72,768]{3,2,1,0:T(8,128)(2,1)} %param.12) | copy-start | bytes 331780
  42.2 67.9 %all-to-all-start = ((bf16[8,9,5248]{2,1,0:T(8,128)(2,1)}), bf16[8,9,5248]{2,1,0:T(8,128)(2,1)}, u32[]{:S(2)}, u32[]{:S(2)}) async-start(bf16[8,9,5248]{2,1,0:T(8,128)(2,1)} %reshape.33), calls=%async_computation | async-start | bytes 2686976 | tf_op jit(solution)/shard_map/all_to_all | solution.py:293
  108.1 1.2 copy-start.6
  109.3 0.9 copy-start.9
  111.9 1.1 copy-start.10
  116.5 0.6 copy-start.13
  130.2 0.9 copy-start.5
  132.2 12.7 %collective-permute-start.3 = (bf16[128,480]{1,0:T(8,128)(2,1)S(1)}, bf16[128,480]{1,0:T(8,128)(2,1)S(1)}, u32[]{:S(2)}, u32[]{:S(2)}) collective-permute-start(bf16[128,480]{1,0:T(8,128)(2,1)S(1)} %get-tuple-element.19), channel_id=1, source_target_pairs={{8,0},{16,8},{24,16},{9,1},{17,9},{25,17},{10,2},{18,10},{26,18},{... | collective-permute-start | bytes 368648 | tf_op jit(solution)/shard_map/ppermute | solution.py:385
  146.0 6.8 %collective-permute-start.4 = (bf16[128,480]{1,0:T(8,128)(2,1)S(1)}, bf16[128,480]{1,0:T(8,128)(2,1)S(1)}, u32[]{:S(2)}, u32[]{:S(2)}) collective-permute-start(bf16[128,480]{1,0:T(8,128)(2,1)S(1)} %get-tuple-element.20), channel_id=1, source_target_pairs={{8,0},{16,8},{24,16},{9,1},{17,9},{25,17},{10,2},{18,10},{26,18},{... | collective-permute-start | bytes 368648 | tf_op jit(solution)/shard_map/ppermute | solution.py:385
  153.9 6.8 %collective-permute-start.5 = (bf16[128,480]{1,0:T(8,128)(2,1)S(1)}, bf16[128,480]{1,0:T(8,128)(2,1)S(1)}, u32[]{:S(2)}, u32[]{:S(2)}) collective-permute-start(bf16[128,480]{1,0:T(8,128)(2,1)S(1)} %get-tuple-element.21), channel_id=1, source_target_pairs={{8,0},{16,8},{24,16},{9,1},{17,9},{25,17},{10,2},{18,10},{26,18},{... | collective-permute-start | bytes 368648 | tf_op jit(solution)/shard_map/ppermute | solution.py:385
  160.8 1.3 copy-start.11
  162.1 0.6 copy-start.15
  162.7 0.6 copy-start.16
  164.9 22.5 %all-to-all-start.2 = ((bf16[8,9,480]{2,1,0:T(8,128)(2,1)}), bf16[8,9,480]{2,1,0:T(8,128)(2,1)}, u32[]{:S(2)}, u32[]{:S(2)}) async-start(bf16[8,9,480]{2,1,0:T(8,128)(2,1)} %reshape.37), calls=%async_computation.2 | async-start | bytes 262144 | tf_op jit(solution)/shard_map/all_to_all | solution.py:293
  170.8 4.0 %copy-start.12 = (bf16[128,480]{1,0:T(8,128)(2,1)S(1)}, bf16[128,480]{1,0:T(8,128)(2,1)}, u32[]{:S(2)}) copy-start(bf16[128,480]{1,0:T(8,128)(2,1)} %copy-done.11) | copy-start | bytes 368644
  174.8 2.5 copy-start.1
  177.3 1.7 copy-start.2
  179.1 0.8 copy-start.17
  188.3 1.4 copy-start.7
  189.7 9.5 %copy-start.4 = (s32[1,1,2,768,640]{4,3,2,1,0:T(8,128)S(1)}, s32[1,1,2,768,640]{4,3,2,1,0:T(8,128)}, u32[]{:S(2)}) copy-start(s32[1,1,2,768,640]{4,3,2,1,0:T(8,128)} %param.13) | copy-start | bytes 11796484
  189.7 9.5 %copy-start.8 = (bf16[1,1,72,768]{2,3,1,0:T(8,128)(2,1)S(1)}, bf16[1,1,72,768]{2,3,1,0:T(8,128)(2,1)}, u32[]{:S(2)}) copy-start(bf16[1,1,72,768]{2,3,1,0:T(8,128)(2,1)} %copy.17) | copy-start | bytes 331780
Sparse Core Ops, SparseCore 0:
  38.0 59.7 all-gather.1

commit v2 on v1

v2 whole, which is shorter than its diff:
```python
import functools
import math

import jax
import jax.numpy as jnp
from jax import lax
from jax.experimental import pallas as pl
from jax.experimental.pallas import tpu as pltpu
from jax.sharding import PartitionSpec as P

MOST = 9
SLOT = 16
ROUTE_SCALE = 16.0
LANES = 128
WIDE = 256
LOW = 8
F32 = jnp.float32
BF16 = jnp.bfloat16


def params(mib):
    return pltpu.CompilerParams(vmem_limit_bytes=mib << 20)


def dot(a, b):
    return jnp.dot(a, b, preferred_element_type=F32)


def dot_nt(a, b):
    return lax.dot_general(a, b, (((1,), (1,)), ((), ())), preferred_element_type=F32)


def dot_tn(a, b):
    return lax.dot_general(a, b, (((0,), (0,)), ((), ())), preferred_element_type=F32)


def iota(shape, axis):
    return lax.broadcasted_iota(jnp.int32, shape, axis)


def lane_gather(table, index):
    return lax.gather(
        table,
        index[..., None],
        lax.GatherDimensionNumbers(
            offset_dims=(),
            collapsed_slice_dims=(1,),
            start_index_map=(1,),
            operand_batching_dims=(0,),
            start_indices_batching_dims=(0,),
        ),
        slice_sizes=(1, 1),
        mode=lax.GatherScatterMode.PROMISE_IN_BOUNDS,
    )


def slot_expert(rows, columns):
    return iota((rows, columns), 0) // SLOT == iota((rows, columns), 1)


def one_hot(mask):
    return mask.astype(F32).astype(BF16)


def prepare_kernel(logits_ref, routes_ref, grad_ref, probs_ref, select_ref, rows_ref):
    tokens, routed = logits_ref.shape
    top = routes_ref.shape[0]
    width = grad_ref.shape[1]
    rows = rows_ref.shape[0]
    experts = rows // SLOT
    raised = jnp.exp(logits_ref[...])
    probs = raised / jnp.sum(raised, axis=1, keepdims=True)
    probs_ref[...] = probs
    expert = iota((experts, tokens), 0)
    hits = jnp.zeros((experts, tokens), F32)
    for k in range(top):
        hits = hits + (routes_ref[k : k + 1, :] == expert).astype(F32)
    hits = hits.astype(BF16)
    earlier = one_hot(iota((tokens, tokens), 0) < iota((tokens, tokens), 1))
    position = dot(hits, earlier).astype(BF16)
    owner = one_hot(slot_expert(rows, experts))
    slot_hit = dot(owner, hits)
    slot_position = dot(owner, position)
    place = (iota((rows, tokens), 0) % SLOT).astype(F32)
    select = one_hot(
        (slot_hit > 0.5) & (jnp.abs(slot_position - place) < 0.5) & (place < MOST - 0.5)
    )
    select_ref[...] = select
    gate = (ROUTE_SCALE * probs).astype(BF16)
    slot_gate = jnp.sum(
        jnp.where(slot_expert(rows, routed), dot(select, gate), 0.0), axis=1, keepdims=True
    )
    rows_ref[:, :width] = dot(select, grad_ref[...]).astype(BF16)
    rows_ref[:, width:] = jnp.broadcast_to(slot_gate, (rows, LANES)).astype(BF16)


def decode_kernel(first, last, codes_ref, table_ref, hidden_ref, *rest):
    if not first:
        before_ref, scale_ref, *rest = rest
    plain_out_ref, *rest = rest
    weight_ref = rest[-1]
    step = pl.program_id(0)
    books, block, groups = codes_ref.shape
    entries = table_ref.shape[1]
    size = table_ref.shape[2]

    @pl.when(step == 0)
    def _():
        plain_out_ref[...] = jnp.zeros_like(plain_out_ref) if first else before_ref[...]

    for chunk in range(groups // LANES):
        lanes = slice(chunk * LANES, (chunk + 1) * LANES)

        def decode_rows(index, carry):
            values = [[] for _ in range(size)]
            for half in range(2):
                at = pl.ds(pl.multiple_of(index * 16 + 8 * half, 8), 8)
                codes = [codes_ref[b, at, lanes] for b in range(books)]
                low = [c & (LANES - 1) for c in codes]
                part = [c >= LANES for c in codes]
                for i in range(size):
                    total = None
                    for b in range(books):
                        value = jnp.where(
                            part[b],
                            lane_gather(table_ref[b, 1, i], low[b]),
                            lane_gather(table_ref[b, 0, i], low[b]),
                        )
                        total = value if total is None else total + value
                    values[i].append(total)
            at = pl.ds(pl.multiple_of(index * 16, 16), 16)
            for i in range(size):
                weight_ref[at, i * LANES : (i + 1) * LANES] = jnp.concatenate(values[i], 0).astype(
                    BF16
                )
            return carry

        lax.fori_loop(0, block // 16, decode_rows, 0)
        product = dot(hidden_ref[...], weight_ref[...])
        for i in range(size):
            plain_out_ref[i, :, lanes] += product[:, i * LANES : (i + 1) * LANES]

    if not last:
        return
    out_ref = rest[0]

    @pl.when(step == pl.num_programs(0) - 1)
    def _():
        span = size * LANES
        column = iota((span, span), 0)
        source = size * (column & (LANES - 1)) + column // LANES
        back = (source == iota((span, span), 1)).astype(F32).astype(BF16)
        for chunk in range(groups // LANES):
            lanes = slice(chunk * LANES, (chunk + 1) * LANES)
            split = jnp.concatenate(
                [plain_out_ref[i, :, lanes] * scale_ref[i : i + 1, lanes] for i in range(size)], 1
            ).astype(BF16)
            out_ref[:, chunk * span : (chunk + 1) * span] = dot(split, back).astype(BF16)


def score_kernel(twist_ref, out_ref, slots_ref, near_ref, far_ref, score_ref, total_ref):
    i, j = pl.program_id(0), pl.program_id(1)
    rows = out_ref.shape[0]
    later_count, routed = near_ref.shape[1:3]

    @pl.when((i == 0) & (j == 0))
    def _():
        total_ref[...] = jnp.zeros_like(total_ref)

    out = out_ref[...]
    base = jnp.sum(slots_ref[...].astype(F32) * out.astype(F32), axis=1, keepdims=True)
    total_ref[:, later_count * WIDE :] += jnp.broadcast_to(base, (rows, LANES))

    def add(router_ref):
        for s in range(later_count):
            total_ref[:, s * WIDE : s * WIDE + routed] += dot_nt(out, router_ref[0, s])

    @pl.when(j == 0)
    def _():
        add(near_ref)

    @pl.when(j == 1)
    def _():
        add(far_ref)

    @pl.when((i == pl.num_programs(0) - 1) & (j == 1))
    def _():
        score_ref[:, : later_count * WIDE] = total_ref[:, : later_count * WIDE].astype(BF16)
        base = total_ref[:, later_count * WIDE :]
        high = base.astype(BF16).astype(F32)
        middle = (base - high).astype(BF16).astype(F32)
        low = base - high - middle
        column = iota((rows, LANES), 1)
        score_ref[:, later_count * WIDE :] = jnp.where(
            column == 0,
            high,
            jnp.where(column == 1, middle, jnp.where(column == 2, low, 0.0)),
        ).astype(BF16)


def chain_kernel(scores_ref, later_ref, probs_ref, select_ref, own_ref, send_ref, picked_ref):
    rows = scores_ref.shape[0]
    tokens, wide = later_ref.shape
    routed = probs_ref.shape[1]
    later = later_ref[...]
    select = select_ref[...]
    picked = dot(select, later)
    picked_ref[...] = picked.astype(BF16)
    score = jnp.sum(picked * scores_ref[:, :wide].astype(F32), axis=1, keepdims=True) + jnp.sum(
        scores_ref[:, wide:].astype(F32), axis=1, keepdims=True
    )
    score = score.astype(BF16).astype(F32)
    placed = jnp.where(slot_expert(rows, routed), score, 0.0).astype(BF16)
    spread = dot_tn(select, placed)
    probs = probs_ref[...]
    weighted = jnp.sum(probs * spread, axis=1, keepdims=True)
    own = (ROUTE_SCALE * probs * (spread - weighted)).astype(BF16)
    own_ref[...] = own
    send_ref[:, :WIDE] = jnp.zeros((tokens, WIDE), BF16)
    send_ref[:, :routed] = own
    send_ref[:, WIDE:] = later[:, : wide - WIDE]


def add_layers(current, later_ref, router_ref):
    later_count, routed = router_ref.shape[1:3]
    for s in range(later_count - 1, -1, -1):
        part = later_ref[:, s * WIDE : s * WIDE + routed]
        current = (current.astype(F32) + dot(part, router_ref[0, s])).astype(BF16)
    return current


def finish_kernel(
    twist_ref, grad_ref, later_ref, own_ref, router_ref, near_ref, far_ref, result_ref
):
    def finish(routers_ref):
        current = add_layers(grad_ref[...], later_ref, routers_ref)
        result_ref[...] = (current.astype(F32) + dot(own_ref[...], router_ref[...])).astype(BF16)

    @pl.when(pl.program_id(1) == 0)
    def _():
        finish(near_ref)

    @pl.when(pl.program_id(1) == 1)
    def _():
        finish(far_ref)


def slots_kernel(
    twist_ref, slots_ref, gates_ref, later_ref, near_ref, far_ref, plain_out_ref, split_ref,
    scale_grad_ref, grad_ref
):
    i, j = pl.program_id(0), pl.program_id(1)
    part_width = slots_ref.shape[1]
    size = plain_out_ref.shape[0]
    groups = plain_out_ref.shape[2]
    span = size * LANES
    at = pl.ds(pl.multiple_of((twist_ref[0] ^ (2 * i + j)) * part_width, LANES), part_width)
    gate = gates_ref[:, :1].astype(F32)

    def put(routers_ref):
        current = add_layers(slots_ref[...], later_ref, routers_ref)
        grad_ref[:, at] = (gate * current.astype(F32)).astype(BF16)

    @pl.when(j == 0)
    def _():
        put(near_ref)

    @pl.when(j == 1)
    def _():
        put(far_ref)

    @pl.when((i == pl.num_programs(0) - 1) & (j == 1))
    def _():
        column = iota((span, span), 1)
        source = size * (column & (LANES - 1)) + column // LANES
        order = one_hot(source == iota((span, span), 0))
        for chunk in range(groups // LANES):
            lanes = slice(chunk * LANES, (chunk + 1) * LANES)
            split = dot(grad_ref[:, chunk * span : (chunk + 1) * span], order)
            for i in range(size):
                part = split[:, i * LANES : (i + 1) * LANES]
                split_ref[i, :, lanes] = part.astype(BF16)
                scale_grad_ref[i : i + 1, lanes] = jnp.sum(
                    part * plain_out_ref[i, :, lanes], axis=0, keepdims=True
                )


def book_kernel(
    unroll, hidden_ref, slots_ref, scale_ref, codes_ref, out_ref, grad_ref, high_ref, low_ref
):
    books, block, groups = codes_ref.shape
    size = slots_ref.shape[0]
    high_count = out_ref.shape[1]
    chunks = groups // LANES

    @pl.when(pl.program_id(0) == 0)
    def _():
        out_ref[...] = jnp.zeros_like(out_ref)

    hidden = hidden_ref[...]
    for i in range(size):
        grad = dot_tn(hidden, slots_ref[i]) * scale_ref[i : i + 1, :]
        for c in range(chunks):
            grad_ref[c, pl.ds(i, block, stride=size), :] = grad[:, c * LANES : (c + 1) * LANES]
    for b in range(books):
        codes = codes_ref[b]
        high_ref[b] = (codes >> 3).astype(F32)
        low_ref[b] = (codes & (LOW - 1)).astype(F32)
    row = iota((16, groups), 0)
    high_rows = [(row + 16 * k).astype(F32).astype(BF16) for k in range(high_count // 16)]
    low_rows = [((row >> 3) + 2 * k).astype(F32).astype(BF16) for k in range(LOW // 2)]
    one = jnp.ones((16, groups), BF16)
    zero = jnp.zeros((16, groups), BF16)

    def add_rows(index, totals):
        totals = list(totals)
        for pair in range(unroll // 2):
            left = [[] for _ in range(books)]
            right = [[] for _ in range(books)]
            for member in range(2):
                f = index * unroll + pair * 2 + member
                at = pl.ds(pl.multiple_of(f * size, size), size)
                values = jnp.concatenate([grad_ref[c, at, :] for c in range(chunks)], 1)
                values = jnp.concatenate([values, values], 0).astype(BF16)
                for b in range(books):
                    high = jnp.broadcast_to(high_ref[b, pl.ds(f, 1), :], (16, groups)).astype(BF16)
                    low = jnp.broadcast_to(low_ref[b, pl.ds(f, 1), :], (16, groups)).astype(BF16)
                    left[b].append(
                        jnp.concatenate([jnp.where(high == r, one, zero) for r in high_rows], 0)
                    )
                    right[b].append(
                        jnp.concatenate([jnp.where(low == r, values, zero) for r in low_rows], 0)
                    )
            for b in range(books):
                totals[b] = totals[b] + dot_nt(
                    jnp.concatenate(left[b], 1), jnp.concatenate(right[b], 1)
                )
        return tuple(totals)

    start = tuple(jnp.zeros(out_ref.shape[1:], F32) for _ in range(books))
    totals = lax.fori_loop(0, block // unroll, add_rows, start)
    for b in range(books):
        out_ref[b] += totals[b]


def whole(shape):
    return pl.BlockSpec(shape, lambda *_: (0,) * len(shape))


def exchange(value):
    return lax.all_to_all(value, "expert", split_axis=0, concat_axis=0, tiled=True)


def swap(value, distance):
    count = lax.axis_size("expert")
    return lax.ppermute(value, "expert", [(i, i ^ distance) for i in range(count)])


def gather_exchange(shares):
    count = lax.axis_size("expert")
    return jnp.stack([shares] + [swap(shares, d) for d in range(2, count, 2)])


def on_device(out_grad, saved_inputs, router, routes, hidden_saved, codes, codebook, scale):
    experts = lax.axis_size("expert")
    layers = lax.axis_size("pipe")
    place = lax.axis_index("expert")
    tokens, width = out_grad.shape
    routed = router.shape[2]
    codes = codes[0, 0]
    codebook = codebook[0, 0]
    hidden = hidden_saved[0, 0]
    inner = hidden.shape[1]
    books, _, groups = codes.shape
    entries, size = codebook.shape[1:]
    rows = experts * SLOT
    later_count = layers - 1
    wide = later_count * WIDE
    grow = max(1, rows // 128)
    router_t = router[0].T
    scale_split = scale[0, 0].reshape(groups, size).T
    hidden = jnp.pad(hidden.reshape(experts, MOST, inner), ((0, 0), (0, SLOT - MOST), (0, 0)))
    hidden = hidden.reshape(rows, inner)

    parts = math.gcd(width // LANES, experts)
    direct = parts == experts
    sharers = experts // parts
    part_width = width // parts
    share_rows = routed // sharers
    own_share = lax.dynamic_slice(
        router_t,
        ((place % sharers) * share_rows, (place // sharers) * part_width),
        (share_rows, part_width),
    )
    shares = jnp.stack(
        [
            lax.ppermute(own_share, "pipe", [(p, p - s) for p in range(s, layers)])
            for s in range(1, layers)
        ]
    )
    twist = jnp.full((1,), place if direct else 0, jnp.int32)

    logits = dot(saved_inputs[0], router[0])
    probs, select, outgoing = pl.pallas_call(
        prepare_kernel,
        out_shape=(
            jax.ShapeDtypeStruct((tokens, routed), F32),
            jax.ShapeDtypeStruct((rows, tokens), BF16),
            jax.ShapeDtypeStruct((rows, width + LANES), BF16),
        ),
        compiler_params=params(12 + 6 * grow),
        name="prepare",
    )(logits, routes[0].T, out_grad)
    slots = exchange(outgoing)
    hidden, outgoing = lax.optimization_barrier((hidden, outgoing))

    halves = entries // LANES
    table = codebook.astype(F32).transpose(0, 2, 1).reshape(books, size, halves, LANES)
    table = jnp.broadcast_to(
        table.transpose(0, 2, 1, 3)[:, :, :, None, :], (books, halves, size, 8, LANES)
    )
    block = 128

    def decode(start, count, before):
        first = before is None
        last = start + count == inner // block
        more = [] if first else [before, scale_split]
        return pl.pallas_call(
            functools.partial(decode_kernel, first, last),
            grid=(count,),
            in_specs=[
                pl.BlockSpec((books, block, groups), lambda s: (0, s + start, 0)),
                whole((books, halves, size, 8, LANES)),
                pl.BlockSpec((rows, block), lambda s: (0, s + start)),
            ]
            + [whole(m.shape) for m in more],
            out_specs=[whole((size, rows, groups))] + [whole((rows, width))] * last,
            out_shape=[jax.ShapeDtypeStruct((size, rows, groups), F32)]
            + [jax.ShapeDtypeStruct((rows, width), BF16)] * last,
            scratch_shapes=[pltpu.VMEM((block, size * LANES), BF16)],
            input_output_aliases={} if first else {3: 0},
            compiler_params=params(60),
            cost_estimate=pl.CostEstimate(
                flops=count * 10_000_000_000, bytes_accessed=2_000_000, transcendentals=0
            ),
            name="decode",
        )(codes, table, hidden, *more)

    blocks = inner // block
    first_part, second_part = blocks // 3, blocks // 2
    (plain_out,) = decode(0, first_part, None)
    plain_out, shares = lax.optimization_barrier((plain_out, shares))
    near = gather_exchange(shares) if direct else None
    (plain_out,) = decode(first_part, second_part, plain_out)
    if direct:
        plain_out, near, slots = lax.optimization_barrier((plain_out, near, slots))
        far = swap(near, 1)
    else:
        routers = lax.all_gather(shares, "expert", axis=0, tiled=False)
        routers = routers.reshape(parts, sharers, later_count, share_rows, part_width)
        routers = routers.transpose(0, 2, 1, 3, 4)
        routers = routers.reshape(parts, later_count, routed, part_width)
        near, far = routers[0::2], routers[1::2]
    done = first_part + second_part
    plain_out, expert_out = decode(done, blocks - done, plain_out)

    grid = (parts // 2, 2)

    def columns(height):
        return pl.BlockSpec((height, part_width), lambda i, j, t: (0, t[0] ^ (2 * i + j)))

    router_spec = pl.BlockSpec(
        (1, later_count, routed, part_width), lambda i, j, t: (i, 0, 0, 0)
    )

    def by_columns(kernel, in_specs, out_specs, out_shape, scratch, mib, name):
        return pl.pallas_call(
            kernel,
            grid_spec=pltpu.PrefetchScalarGridSpec(
                num_scalar_prefetch=1,
                grid=grid,
                in_specs=in_specs,
                out_specs=out_specs,
                scratch_shapes=scratch,
            ),
            out_shape=out_shape,
            compiler_params=params(min(56, mib)),
            name=name,
        )

    scores = by_columns(
        score_kernel,
        [columns(rows), columns(rows), router_spec, router_spec],
        whole((rows, wide + LANES)),
        jax.ShapeDtypeStruct((rows, wide + LANES), BF16),
        [pltpu.VMEM((rows, wide + LANES), F32)],
        8 + 4 * grow,
        "scores",
    )(twist, expert_out, slots, near, far)
    scores = exchange(scores)

    chain = pl.pallas_call(
        chain_kernel,
        out_shape=(
            jax.ShapeDtypeStruct((tokens, routed), BF16),
            jax.ShapeDtypeStruct((tokens, wide), BF16),
            jax.ShapeDtypeStruct((rows, wide), BF16),
        ),
        compiler_params=params(8 + 4 * grow),
        name="chain",
    )
    later = jnp.zeros((tokens, wide), BF16)
    for step in range(layers):
        own, send, picked = chain(scores, later, probs, select)
        if step + 1 < layers:
            later = lax.ppermute(send, "pipe", [(p, p - 1) for p in range(1, layers)])

    slot_later = exchange(picked)

    result = by_columns(
        finish_kernel,
        [
            columns(tokens),
            whole((tokens, wide)),
            whole((tokens, routed)),
            columns(routed),
            router_spec,
            router_spec,
        ],
        columns(tokens),
        jax.ShapeDtypeStruct((tokens, width), BF16),
        [],
        12,
        "finish",
    )(twist, out_grad, later, own, router_t, near, far)

    slot_split, scale_grad = by_columns(
        slots_kernel,
        [
            columns(rows),
            pl.BlockSpec((rows, LANES), lambda *_: (0, width // LANES)),
            whole((rows, wide)),
            router_spec,
            router_spec,
            whole((size, rows, groups)),
        ],
        [whole((size, rows, groups)), whole((size, groups))],
        [
            jax.ShapeDtypeStruct((size, rows, groups), BF16),
            jax.ShapeDtypeStruct((size, groups), F32),
        ],
        [pltpu.VMEM((rows, width), BF16)],
        12 + 12 * grow,
        "slot_grads",
    )(twist, slots, slots, slot_later, near, far, plain_out)

    block = 128
    unroll = 16
    high_count = entries // LOW
    book_grad = pl.pallas_call(
        functools.partial(book_kernel, unroll),
        grid=(inner // block,),
        in_specs=[
            pl.BlockSpec((rows, block), lambda s: (0, s)),
            whole((size, rows, groups)),
            whole((size, groups)),
            pl.BlockSpec((books, block, groups), lambda s: (0, s, 0)),
        ],
        out_specs=whole((books, high_count, LOW * size)),
        out_shape=jax.ShapeDtypeStruct((books, high_count, LOW * size), F32),
        scratch_shapes=[
            pltpu.VMEM((groups // LANES, block * size, LANES), F32),
            pltpu.VMEM((books, block, groups), F32),
            pltpu.VMEM((books, block, groups), F32),
        ],
        compiler_params=params(20 + 6 * grow),
        name="book_grads",
    )(hidden, slot_split, scale_split, codes)

    book_grad = book_grad.reshape(books, entries, size)
    scale_grad = scale_grad.T.reshape(width)
    return (result[None], book_grad[None, None], scale_grad[None, None])


def solution(mesh):
    placed = (
        P("expert", None),
        P("pipe", "expert", None),
        P("pipe", None, None),
        P("pipe", "expert", None),
        P("pipe", "expert", None, None),
        P("pipe", "expert", None, None, None),
        P("pipe", "expert", None, None, None),
        P("pipe", "expert", None),
    )
    return jax.shard_map(
        on_device,
        mesh=mesh,
        in_specs=placed,
        out_specs=(
            P("pipe", "expert", None),
            P("pipe", "expert", None, None, None),
            P("pipe", "expert", None),
        ),
        check_vma=False,
    )
```

time: 255 us -> 231 us (0.906)
  waiting for transfers between devices: 46.8 us -> 21.2 us
  Pallas kernels: 131 us -> 145 us
  between operations: 14.3 us -> 0.89 us
  local copies, waits for them, and re-layouts: 30.8 us -> 23.7 us
  other arithmetic: 1.91 us -> 6.11 us
  starting transfers between devices: 16.4 us -> 20.2 us
    ppermute x3, waiting for transfers between devices: 24.3 us -> 0.01 us  [on_device(): lax.ppermute(own_share, 'pipe', [(p, p - s) for p in range(s, layers)])]
    pallas_call x5 -> x7, Pallas kernels: 81 us -> 94.3 us  [the longest x3 71 us: decode(): pl.pallas_call(functools.partial(decode_kernel, first, last), grid=(count...]
    reshape x6 -> x0, local copies, waits for them, and re-layouts: 8.79 us -> none  [the longest x1 1.69 us: on_device(): exchange(outgoing.reshape(experts, MOST, width + LANES))]
    another operation x0 -> x2, other arithmetic: none -> 5.42 us  [the longest x1 3.48 us: gather_exchange(): return jnp.stack([shares] + [swap(shares, d) for d in range(2, count, 2)])]
    ppermute x0 -> x4, starting transfers between devices: none -> 3.49 us  [swap(): lax.ppermute(value, 'expert', [(i, i ^ distance) for i in range(count)])]
  transfers between devices with their start and end apart: 9 -> 12, of which waited for: 5 -> 3; matrix products, arithmetic and copies ran while one was open for 5% -> 5% of each run, Pallas kernels for 27% -> 34%
where the time goes in v2:
time: 231 us; the launch traced here: 229 us
  Pallas kernels  145 us (63%)
  local copies, waits for them, and re-layouts  23.7 us (10%)
  waiting for transfers between devices  21.2 us (9%)
  starting transfers between devices  20.2 us (9%)
  blocking collectives  10.7 us (5%)
  other arithmetic  6.11 us (3%)
    pallas_call x3, Pallas kernels, decode(): pl.pallas_call(functools.partial(decode_kernel, first, last), grid=(count...  71 us
    pallas_call x1, Pallas kernels, on_device(): pl.pallas_call(functools.partial(book_kernel, unroll), grid=(inner // blo...  45.6 us
    ppermute x3, waiting for transfers between devices, on_device(): later = lax.ppermute(send, 'pipe', [(p, p - 1) for p in range(1, layers)])  21.1 us
    unnamed x47, local copies, waits for them, and re-layouts  18.5 us
    all_to_all x1, blocking collectives, exchange(): lax.all_to_all(value, 'expert', split_axis=0, concat_axis=0, tiled=True)  10.7 us
    all_to_all x2, starting transfers between devices, exchange(): lax.all_to_all(value, 'expert', split_axis=0, concat_axis=0, tiled=True)  8.88 us
    pallas_call x1, Pallas kernels, on_device(): by_columns(slots_kernel, [columns(rows), pl.BlockSpec((rows, LANES), lamb...  8.06 us
    pallas_call x1, Pallas kernels, on_device(): by_columns(score_kernel, [columns(rows), columns(rows), router_spec, rout...  7.24 us
  transfers between devices with their start and end apart: 12, of which 3 were waited for; matrix products, arithmetic and copies ran while one was open for 5% of the time, Pallas kernels for 34%

profile of v2, /device:TPU:0, one launch (start us, length us, event | category | flops | bytes accessed | tf_op | source)
XLA Modules:
  0.0 229.3 jit_solution(12319518963753562584)
XLA Ops:
  0.6 1.7 dynamic-slice_bitcast_fusion
  2.4 1.4 collective-permute-start
  3.8 1.3 collective-permute-start.1
  5.1 1.3 collective-permute-start.2
  6.4 2.1 fusion.logits_ref
  10.4 5.3 %all-to-all-start = ((bf16[8,16,5248]{2,1,0:T(8,128)(2,1)}), bf16[8,16,5248]{2,1,0:T(8,128)(2,1)S(1)}, u32[]{:S(2)}, u32[]{:S(2)}) async-start(bf16[8,16,5248]{2,1,0:T(8,128)(2,1)} %bitcast.59), calls=%async_computation | async-start | bytes 2686976 | tf_op jit(solution)/shard_map/all_to_all | solution.py:351
  17.1 22.6 %decode.3.rest_0_ = f32[8,128,640]{2,1,0:T(8,128)} custom-call(s32[2,768,640]{2,1,0:T(8,128)} %bitcast.55, f32[2,2,8,8,128]{4,3,2,1,0:T(8,128)} %broadcast_in_dim.16.table_ref, bf16[128,768]{1,0:T(8,128)(2,1)} %bitcast.61), custom_call_target="tpu_custom_call" | custom-call | flops 20000000000 | bytes 2000000 | tf_op jit(solution)/shard_map/decode/pallas_call | solution.py:428
  41.9 1.9 pad_maximum_fusion.1
  43.8 2.0 collective-permute-start.3
  45.8 1.5 collective-permute-start.4
  47.3 33.4 %decode.4.rest_0_ = f32[8,128,640]{2,1,0:T(8,128)} custom-call(s32[2,768,640]{2,1,0:T(8,128)} %bitcast.56, f32[2,2,8,8,128]{4,3,2,1,0:T(8,128)} %broadcast_in_dim.16.table_ref, bf16[128,768]{1,0:T(8,128)(2,1)} %bitcast.62, f32[8,128,640]{2,1,0:T(8,128)} %decode.3.rest_0_, f32[8,640]{1,0:T(8,128)} %bitcast.66), custom_call_target="tpu_custom_call", output_to_operand_aliasing={{}: (3, {})} | custom-call | flops 30000001024 | bytes 2000000 | tf_op jit(solution)/shard_map/decode/pallas_call | solution.py:428
  80.7 3.5 %pad_maximum_fusion.near_ref = bf16[4,3,160,640]{3,2,1,0:T(8,128)(2,1)} fusion(bf16[1,3,160,640]{3,2,1,0:T(8,128)(2,1)} %bitcast.20, bf16[1,3,160,640]{3,2,1,0:T(8,128)(2,1)} %bitcast.19, bf16[1,3,160,640]{3,2,1,0:T(8,128)(2,1)} %bitcast.18, bf16[1,3,160,640]{3,2,1,0:T(8,128)(2,1)} %bitcast.17), kind=kLoop, calls=%fused_computation | loop fusion | flops 3686400 | bytes 4915200 | tf_op jit(solution)/shard_map/stack | solution.py:361
  85.4 15.0 %decode.5 = (f32[8,128,640]{2,1,0:T(8,128)}, bf16[128,5120]{1,0:T(8,128)(2,1)}) custom-call(s32[2,768,640]{2,1,0:T(8,128)} %bitcast.57, f32[2,2,8,8,128]{4,3,2,1,0:T(8,128)} %broadcast_in_dim.16.table_ref, bf16[128,768]{1,0:T(8,128)(2,1)} %bitcast.63, f32[8,128,640]{2,1,0:T(8,128)} %decode.4.rest_0_, f32[8,640]{1,0:T(8,128)} %bitcast.67), custom_call_target="tpu_custom_call", output_to_operand_aliasing={{0}: (3, {})} | custom-call | flops 10000000000 | bytes 2000000 | tf_op jit(solution)/shard_map/decode/pallas_call | solution.py:428
  100.4 1.3 copy-done.5
  101.7 1.3 copy-done.15
  103.0 7.2 %scores.1 = bf16[128,896]{1,0:T(8,128)(2,1)S(1)} custom-call(s32[1]{0:T(128)} %bitcast.twist_ref, bf16[128,5120]{1,0:T(8,128)(2,1)S(1)} %copy-done.15, bf16[128,5248]{1,0:T(8,128)(2,1)S(1)} %bitcast.47, bf16[4,3,160,640]{3,2,1,0:T(8,128)(2,1)S(1)} %copy-done.1, bf16[4,3,160,640]{3,2,1,0:T(8,128)(2,1)} %collective-permute-done.6.far_ref), custom_call_target="tpu_custom_call" | custom-call | tf_op jit(solution)/shard_map/scores/pallas_call | solution.py:491
  110.3 10.7 %all_to_all.34 = bf16[8,16,896]{2,1,0:T(8,128)(2,1)S(1)} all-to-all(bf16[8,16,896]{2,1,0:T(8,128)(2,1)S(1)} %bitcast.60), channel_id=1, replica_groups=mesh['pipe'=4,'expert'=8] {'expert'}, dimensions={0} | all-to-all | bytes 458752 | tf_op jit(solution)/shard_map/all_to_all | solution.py:351
  122.1 1.3 collective-permute-start.7
  123.4 7.7 %collective-permute-done.7.later_ref = bf16[128,768]{1,0:T(8,128)(2,1)S(1)} collective-permute-done((bf16[128,768]{1,0:T(8,128)(2,1)S(1)}, bf16[128,768]{1,0:T(8,128)(2,1)S(1)}, u32[]{:S(2)}, u32[]{:S(2)}) %collective-permute-start.7) | collective-permute-done | bytes 196640 | tf_op jit(solution)/shard_map/ppermute | solution.py:516
  133.5 6.6 %collective-permute-done.8.later_ref = bf16[128,768]{1,0:T(8,128)(2,1)S(1)} collective-permute-done((bf16[128,768]{1,0:T(8,128)(2,1)S(1)}, bf16[128,768]{1,0:T(8,128)(2,1)S(1)}, u32[]{:S(2)}, u32[]{:S(2)}) %collective-permute-start.8) | collective-permute-done | bytes 196640 | tf_op jit(solution)/shard_map/ppermute | solution.py:516
  142.6 6.8 %collective-permute-done.9.later_ref = bf16[128,768]{1,0:T(8,128)(2,1)S(1)} collective-permute-done((bf16[128,768]{1,0:T(8,128)(2,1)S(1)}, bf16[128,768]{1,0:T(8,128)(2,1)S(1)}, u32[]{:S(2)}, u32[]{:S(2)}) %collective-permute-start.9) | collective-permute-done | bytes 196640 | tf_op jit(solution)/shard_map/ppermute | solution.py:516
  150.6 3.6 %all-to-all-start.2 = ((bf16[8,16,768]{2,1,0:T(8,128)(2,1)}), bf16[8,16,768]{2,1,0:T(8,128)(2,1)S(1)}, u32[]{:S(2)}, u32[]{:S(2)}) async-start(bf16[8,16,768]{2,1,0:T(8,128)(2,1)} %bitcast.27), calls=%async_computation.2 | async-start | bytes 393216 | tf_op jit(solution)/shard_map/all_to_all | solution.py:351
  154.2 1.7 copy-done.2
  155.9 1.4 copy-done.7
  157.3 1.3 copy-done.9
  158.6 7.2 %finish.1 = bf16[128,5120]{1,0:T(8,128)(2,1)} custom-call(s32[1]{0:T(128)} %bitcast.twist_ref, bf16[128,5120]{1,0:T(8,128)(2,1)S(1)} %copy-done.9, bf16[128,768]{1,0:T(8,128)(2,1)S(1)} %collective-permute-done.9.later_ref, bf16[128,160]{1,0:T(8,128)(2,1)S(1)} %get-tuple-element.34.own_ref, bf16[160,5120]{1,0:T(8,128)(2,1)S(1)} %bitcast.50, ...), custom_call_target="tpu_custom_call" | custom-call | tf_op jit(solution)/shard_map/finish/pallas_call | solution.py:520
  165.9 1.7 copy-done.3
  167.6 1.7 copy-done.11
  169.3 8.1 %slot_grads.1 = (bf16[8,128,640]{2,1,0:T(8,128)(2,1)S(1)}, f32[8,640]{1,0:T(8,128)S(1)}) custom-call(s32[1]{0:T(128)} %bitcast.twist_ref, bf16[128,5248]{1,0:T(8,128)(2,1)S(1)} %bitcast.48, bf16[128,5248]{1,0:T(8,128)(2,1)S(1)} %bitcast.49, bf16[128,768]{1,0:T(8,128)(2,1)S(1)} %bitcast.65, bf16[4,3,160,640]{3,2,1,0:T(8,128)(2,1)S(1)} %copy-done.3, ...), custom_call_target="tpu_custom_call" | custom-call | tf_op jit(solution)/shard_map/slot_grads/pallas_call | solution.py:537
  179.4 2.1 copy-done.10
  181.6 1.3 copy-done.14
  182.9 45.6 %book_grads.1 = f32[2,32,64]{2,1,0:T(8,128)S(1)} custom-call(bf16[128,768]{1,0:T(8,128)(2,1)S(1)} %bitcast.64, bf16[8,128,640]{2,1,0:T(8,128)(2,1)S(1)} %copy-done.14, f32[8,640]{1,0:T(8,128)S(1)} %bitcast.68, s32[2,768,640]{2,1,0:T(8,128)S(1)} %bitcast.58), custom_call_target="tpu_custom_call" | custom-call | tf_op jit(solution)/shard_map/book_grads/pallas_call | solution.py:560
  (67 shorter events, 16.7 us)
Async XLA Ops:
  0.6 5.8 %copy-start = (bf16[1,128,5120]{2,1,0:T(8,128)(2,1)S(1)}, bf16[1,128,5120]{2,1,0:T(8,128)(2,1)}, u32[]{:S(2)}) copy-start(bf16[1,128,5120]{2,1,0:T(8,128)(2,1)} %param.9) | copy-start | bytes 3932164
  2.4 6.1 %copy-start.21 = (s32[1,128,6]{1,0,2:T(1,128)S(1)}, s32[1,128,6]{1,0,2:T(1,128)}, u32[]{:S(2)}) copy-start(s32[1,128,6]{1,0,2:T(1,128)} %param.11) | copy-start | bytes 9220
  2.4 6.1 %copy-start.8 = (bf16[128,5120]{1,0:T(8,128)(2,1)S(1)}, bf16[128,5120]{1,0:T(8,128)(2,1)}, u32[]{:S(2)}) copy-start(bf16[128,5120]{1,0:T(8,128)(2,1)} %grad_ref.3) | copy-start | bytes 3932164
  2.4 39.5 %collective-permute-start = (bf16[160,640]{1,0:T(8,128)(2,1)}, bf16[160,640]{1,0:T(8,128)(2,1)S(1)}, u32[]{:S(2)}, u32[]{:S(2)}) collective-permute-start(bf16[160,640]{1,0:T(8,128)(2,1)} %dynamic-slice_bitcast_fusion), channel_id=1, source_target_pairs={{8,0},{16,8},{24,16},{9,1},{17,9},{25,17},{10,2},{18,10},{26,18},{... | collective-permute-start | bytes 614408 | tf_op jit(solution)/shard_map/ppermute | solution.py:397
  3.8 38.1 %collective-permute-start.1 = (bf16[160,640]{1,0:T(8,128)(2,1)}, bf16[160,640]{1,0:T(8,128)(2,1)}, u32[]{:S(2)}, u32[]{:S(2)}) collective-permute-start(bf16[160,640]{1,0:T(8,128)(2,1)} %dynamic-slice_bitcast_fusion), channel_id=1, source_target_pairs={{16,0},{24,8},{17,1},{25,9},{18,2},{26,10},{19,3},{27,11},{20,4},{... | collective-permute-start | bytes 614408 | tf_op jit(solution)/shard_map/ppermute | solution.py:397
  5.1 36.8 %collective-permute-start.2 = (bf16[160,640]{1,0:T(8,128)(2,1)}, bf16[160,640]{1,0:T(8,128)(2,1)}, u32[]{:S(2)}, u32[]{:S(2)}) collective-permute-start(bf16[160,640]{1,0:T(8,128)(2,1)} %dynamic-slice_bitcast_fusion), channel_id=1, source_target_pairs={{24,0},{25,1},{26,2},{27,3},{28,4},{29,5},{30,6},{31,7}} | collective-permute-start | bytes 614408 | tf_op jit(solution)/shard_map/ppermute | solution.py:397
  10.4 5.3 %copy-start.18 = (bf16[1,1,72,768]{3,2,1,0:T(8,128)(2,1)S(1)}, bf16[1,1,72,768]{3,2,1,0:T(8,128)(2,1)}, u32[]{:S(2)}) copy-start(bf16[1,1,72,768]{3,2,1,0:T(8,128)(2,1)} %param.12) | copy-start | bytes 331780
  10.4 6.1 %copy-start.20 = (bf16[1,1,2,256,8]{3,4,2,1,0:T(8,128)(2,1)S(1)}, bf16[1,1,2,256,8]{3,4,2,1,0:T(8,128)(2,1)}, u32[]{:S(2)}) copy-start(bf16[1,1,2,256,8]{3,4,2,1,0:T(8,128)(2,1)} %param.14) | copy-start | bytes 24580
  10.4 73.9 %all-to-all-start = ((bf16[8,16,5248]{2,1,0:T(8,128)(2,1)}), bf16[8,16,5248]{2,1,0:T(8,128)(2,1)S(1)}, u32[]{:S(2)}, u32[]{:S(2)}) async-start(bf16[8,16,5248]{2,1,0:T(8,128)(2,1)} %bitcast.59), calls=%async_computation | async-start | bytes 2686976 | tf_op jit(solution)/shard_map/all_to_all | solution.py:351
  17.1 23.2 %copy-start.19 = (f32[1,1,5120]{2,1,0:T(1,128)S(1)}, f32[1,1,5120]{2,1,0:T(1,128)}, u32[]{:S(2)}) copy-start(f32[1,1,5120]{2,1,0:T(1,128)} %param.15) | copy-start | bytes 61444
  43.8 36.9 %collective-permute-start.3 = (bf16[3,160,640]{2,1,0:T(8,128)(2,1)}, bf16[3,160,640]{2,1,0:T(8,128)(2,1)}, u32[]{:S(2)}, u32[]{:S(2)}) collective-permute-start(bf16[3,160,640]{2,1,0:T(8,128)(2,1)} %pad_maximum_fusion.1), channel_id=1, source_target_pairs={{0,2},{1,3},{2,0},{3,1},{4,6},{5,7},{6,4},{7,5},{8,10},{9,11},{10,... | collective-permute-start | bytes 1843208 | tf_op jit(solution)/shard_map/ppermute | solution.py:356
  45.8 34.9 %collective-permute-start.4 = (bf16[3,160,640]{2,1,0:T(8,128)(2,1)}, bf16[3,160,640]{2,1,0:T(8,128)(2,1)}, u32[]{:S(2)}, u32[]{:S(2)}) collective-permute-start(bf16[3,160,640]{2,1,0:T(8,128)(2,1)} %pad_maximum_fusion.1), channel_id=1, source_target_pairs={{0,4},{1,5},{2,6},{3,7},{4,0},{5,1},{6,2},{7,3},{8,12},{9,13},{10,... | collective-permute-start | bytes 1843208 | tf_op jit(solution)/shard_map/ppermute | solution.py:356
  47.3 33.4 %collective-permute-start.5 = (bf16[3,160,640]{2,1,0:T(8,128)(2,1)}, bf16[3,160,640]{2,1,0:T(8,128)(2,1)}, u32[]{:S(2)}, u32[]{:S(2)}) collective-permute-start(bf16[3,160,640]{2,1,0:T(8,128)(2,1)} %pad_maximum_fusion.1), channel_id=1, source_target_pairs={{0,6},{1,7},{2,4},{3,5},{4,2},{5,3},{6,0},{7,1},{8,14},{9,15},{10,... | collective-permute-start | bytes 1843208 | tf_op jit(solution)/shard_map/ppermute | solution.py:356
  84.2 1.2 copy-start.4
  85.4 15.0 %collective-permute-start.6 = (bf16[4,3,160,640]{3,2,1,0:T(8,128)(2,1)}, bf16[4,3,160,640]{3,2,1,0:T(8,128)(2,1)}, u32[]{:S(2)}, u32[]{:S(2)}) collective-permute-start(bf16[4,3,160,640]{3,2,1,0:T(8,128)(2,1)} %pad_maximum_fusion.near_ref), channel_id=1, source_target_pairs={{0,1},{1,0},{2,3},{3,2},{4,5},{5,4},{6,7},{7,6},{8,9},{9,8},{10,11... | collective-permute-start | bytes 7372808 | tf_op jit(solution)/shard_map/ppermute | solution.py:356
  85.4 15.0 %copy-start.1 = (bf16[4,3,160,640]{3,2,1,0:T(8,128)(2,1)S(1)}, bf16[4,3,160,640]{3,2,1,0:T(8,128)(2,1)}, u32[]{:S(2)}) copy-start(bf16[4,3,160,640]{3,2,1,0:T(8,128)(2,1)} %pad_maximum_fusion.near_ref) | copy-start | bytes 7372804
  100.4 1.3 copy-start.5
  101.7 1.3 copy-start.15
  122.1 9.0 %collective-permute-start.7 = (bf16[128,768]{1,0:T(8,128)(2,1)S(1)}, bf16[128,768]{1,0:T(8,128)(2,1)S(1)}, u32[]{:S(2)}, u32[]{:S(2)}) collective-permute-start(bf16[128,768]{1,0:T(8,128)(2,1)S(1)} %get-tuple-element.31), channel_id=1, source_target_pairs={{8,0},{16,8},{24,16},{9,1},{17,9},{25,17},{10,2},{18,10},{26,18},{... | collective-permute-start | bytes 589832 | tf_op jit(solution)/shard_map/ppermute | solution.py:516
  132.2 7.9 %collective-permute-start.8 = (bf16[128,768]{1,0:T(8,128)(2,1)S(1)}, bf16[128,768]{1,0:T(8,128)(2,1)S(1)}, u32[]{:S(2)}, u32[]{:S(2)}) collective-permute-start(bf16[128,768]{1,0:T(8,128)(2,1)S(1)} %get-tuple-element.32), channel_id=1, source_target_pairs={{8,0},{16,8},{24,16},{9,1},{17,9},{25,17},{10,2},{18,10},{26,18},{... | collective-permute-start | bytes 589832 | tf_op jit(solution)/shard_map/ppermute | solution.py:516
  141.3 8.1 %collective-permute-start.9 = (bf16[128,768]{1,0:T(8,128)(2,1)S(1)}, bf16[128,768]{1,0:T(8,128)(2,1)S(1)}, u32[]{:S(2)}, u32[]{:S(2)}) collective-permute-start(bf16[128,768]{1,0:T(8,128)(2,1)S(1)} %get-tuple-element.33), channel_id=1, source_target_pairs={{8,0},{16,8},{24,16},{9,1},{17,9},{25,17},{10,2},{18,10},{26,18},{... | collective-permute-start | bytes 589832 | tf_op jit(solution)/shard_map/ppermute | solution.py:516
  150.6 15.2 %all-to-all-start.2 = ((bf16[8,16,768]{2,1,0:T(8,128)(2,1)}), bf16[8,16,768]{2,1,0:T(8,128)(2,1)S(1)}, u32[]{:S(2)}, u32[]{:S(2)}) async-start(bf16[8,16,768]{2,1,0:T(8,128)(2,1)} %bitcast.27), calls=%async_computation.2 | async-start | bytes 393216 | tf_op jit(solution)/shard_map/all_to_all | solution.py:351
  154.2 1.7 copy-start.2
  155.9 1.4 copy-start.7
  157.3 1.3 copy-start.9
  158.6 7.2 %copy-start.6 = (bf16[8,16,5248]{2,1,0:T(8,128)(2,1)S(1)}, bf16[8,16,5248]{2,1,0:T(8,128)(2,1)}, u32[]{:S(2)}) copy-start(bf16[8,16,5248]{2,1,0:T(8,128)(2,1)} %copy-done.4) | copy-start | bytes 4030468
  165.9 1.7 copy-start.3
  167.6 1.7 copy-start.11
  169.3 10.1 %copy-start.16 = (bf16[8,16,768]{2,1,0:T(8,128)(2,1)S(1)}, bf16[8,16,768]{2,1,0:T(8,128)(2,1)}, u32[]{:S(2)}) copy-start(bf16[8,16,768]{2,1,0:T(8,128)(2,1)} %pad.4) | copy-start | bytes 589828
  169.3 10.1 %copy-start.17 = (f32[640,8]{0,1:T(8,128)S(1)}, f32[640,8]{0,1:T(8,128)}, u32[]{:S(2)}) copy-start(f32[640,8]{0,1:T(8,128)} %copy.16) | copy-start | bytes 61444
  179.4 2.1 copy-start.10
  181.6 1.3 copy-start.14
  (2 other events, 2.1 us)

commit v3 on v2

--- a/solution.py
+++ b/solution.py
@@ -13,9 +13,11 @@
 ROUTE_SCALE = 16.0
 LANES = 128
 WIDE = 256
-LOW = 8
+LOW = 6
+HIGH = 48
 F32 = jnp.float32
 BF16 = jnp.bfloat16
+I16 = jnp.int16
 
 
 def params(mib):
@@ -99,6 +101,7 @@
         before_ref, scale_ref, *rest = rest
     plain_out_ref, *rest = rest
     weight_ref = rest[-1]
+    unroll = 8
     step = pl.program_id(0)
     books, block, groups = codes_ref.shape
     entries = table_ref.shape[1]
@@ -112,30 +115,24 @@
         lanes = slice(chunk * LANES, (chunk + 1) * LANES)
 
         def decode_rows(index, carry):
-            values = [[] for _ in range(size)]
-            for half in range(2):
-                at = pl.ds(pl.multiple_of(index * 16 + 8 * half, 8), 8)
-                codes = [codes_ref[b, at, lanes] for b in range(books)]
-                low = [c & (LANES - 1) for c in codes]
-                part = [c >= LANES for c in codes]
+            for member in range(unroll):
+                at = pl.ds(pl.multiple_of((index * unroll + member) * 16, 16), 16)
+                codes = [codes_ref[b, at, lanes].astype(I16) for b in range(books)]
+                low = [c & I16(LANES - 1) for c in codes]
+                part = [c >= I16(LANES) for c in codes]
                 for i in range(size):
-                    total = None
-                    for b in range(books):
-                        value = jnp.where(
+                    values = [
+                        jnp.where(
                             part[b],
                             lane_gather(table_ref[b, 1, i], low[b]),
                             lane_gather(table_ref[b, 0, i], low[b]),
                         )
-                        total = value if total is None else total + value
-                    values[i].append(total)
-            at = pl.ds(pl.multiple_of(index * 16, 16), 16)
-            for i in range(size):
-                weight_ref[at, i * LANES : (i + 1) * LANES] = jnp.concatenate(values[i], 0).astype(
-                    BF16
-                )
+                        for b in range(books)
+                    ]
+                    weight_ref[at, i * LANES : (i + 1) * LANES] = sum(values[1:], values[0])
             return carry
 
-        lax.fori_loop(0, block // 16, decode_rows, 0)
+        lax.fori_loop(0, block // 16 // unroll, decode_rows, 0)
         product = dot(hidden_ref[...], weight_ref[...])
         for i in range(size):
             plain_out_ref[i, :, lanes] += product[:, i * LANES : (i + 1) * LANES]
@@ -158,40 +155,42 @@
             out_ref[:, chunk * span : (chunk + 1) * span] = dot(split, back).astype(BF16)
 
 
-def score_kernel(twist_ref, out_ref, slots_ref, near_ref, far_ref, score_ref, total_ref):
-    i, j = pl.program_id(0), pl.program_id(1)
+def score_kernel(last, twist_ref, out_ref, slots_ref, router_ref, *rest):
+    i = pl.program_id(0)
     rows = out_ref.shape[0]
-    later_count, routed = near_ref.shape[1:3]
-
-    @pl.when((i == 0) & (j == 0))
-    def _():
-        total_ref[...] = jnp.zeros_like(total_ref)
+    later_count, routed, part_width = router_ref.shape[1:]
+    if last:
+        total_before_ref, base_before_ref, score_ref, total_ref, base_ref = rest
+    else:
+        total_ref, base_ref = rest
+
+    @pl.when(i == 0)
+    def _():
+        total_ref[...] = total_before_ref[...] if last else jnp.zeros_like(total_ref)
+        base_ref[...] = base_before_ref[...] if last else jnp.zeros_like(base_ref)
 
     out = out_ref[...]
     base = jnp.sum(slots_ref[...].astype(F32) * out.astype(F32), axis=1, keepdims=True)
-    total_ref[:, later_count * WIDE :] += jnp.broadcast_to(base, (rows, LANES))
-
-    def add(router_ref):
+    base_ref[...] += jnp.broadcast_to(base, (rows, LANES))
+    total_ref[...] += dot_nt(router_ref[0].reshape(later_count * routed, part_width), out)
+
+    if not last:
+        return
+
+    @pl.when(i == pl.num_programs(0) - 1)
+    def _():
+        wide = later_count * WIDE
+        score_ref[:, :wide] = jnp.zeros((rows, wide), BF16)
         for s in range(later_count):
-            total_ref[:, s * WIDE : s * WIDE + routed] += dot_nt(out, router_ref[0, s])
-
-    @pl.when(j == 0)
-    def _():
-        add(near_ref)
-
-    @pl.when(j == 1)
-    def _():
-        add(far_ref)
-
-    @pl.when((i == pl.num_programs(0) - 1) & (j == 1))
-    def _():
-        score_ref[:, : later_count * WIDE] = total_ref[:, : later_count * WIDE].astype(BF16)
-        base = total_ref[:, later_count * WIDE :]
+            score_ref[:, s * WIDE : s * WIDE + routed] = total_ref[
+                s * routed : (s + 1) * routed, :
+            ].T.astype(BF16)
+        base = base_ref[...]
         high = base.astype(BF16).astype(F32)
         middle = (base - high).astype(BF16).astype(F32)
         low = base - high - middle
         column = iota((rows, LANES), 1)
-        score_ref[:, later_count * WIDE :] = jnp.where(
+        score_ref[:, wide:] = jnp.where(
             column == 0,
             high,
             jnp.where(column == 1, middle, jnp.where(column == 2, low, 0.0)),
@@ -286,11 +285,10 @@
 
 
 def book_kernel(
-    unroll, hidden_ref, slots_ref, scale_ref, codes_ref, out_ref, grad_ref, high_ref, low_ref
+    unroll, hidden_ref, slots_ref, scale_ref, codes_ref, out_ref, grad_ref, pair_ref
 ):
     books, block, groups = codes_ref.shape
     size = slots_ref.shape[0]
-    high_count = out_ref.shape[1]
     chunks = groups // LANES
 
     @pl.when(pl.program_id(0) == 0)
@@ -303,14 +301,15 @@
         for c in range(chunks):
             grad_ref[c, pl.ds(i, block, stride=size), :] = grad[:, c * LANES : (c + 1) * LANES]
     for b in range(books):
-        codes = codes_ref[b]
-        high_ref[b] = (codes >> 3).astype(F32)
-        low_ref[b] = (codes & (LOW - 1)).astype(F32)
-    row = iota((16, groups), 0)
-    high_rows = [(row + 16 * k).astype(F32).astype(BF16) for k in range(high_count // 16)]
-    low_rows = [((row >> 3) + 2 * k).astype(F32).astype(BF16) for k in range(LOW // 2)]
-    one = jnp.ones((16, groups), BF16)
-    zero = jnp.zeros((16, groups), BF16)
+        for c in range(chunks):
+            codes = codes_ref[b, :, c * LANES : (c + 1) * LANES]
+            high = (codes * (65536 // LOW + 1)) >> 16
+            pair_ref[b, c] = high * 8 + (codes - high * LOW)
+    row = iota((16, LANES), 0)
+    high_rows = [(row + 16 * k).astype(I16) for k in range(HIGH // 16)]
+    low_rows = [((row >> 3) + 2 * k).astype(I16) for k in range(LOW // 2)]
+    one = jnp.ones((16, LANES), BF16)
+    zero = jnp.zeros((16, LANES), BF16)
 
     def add_rows(index, totals):
         totals = list(totals)
@@ -320,17 +319,20 @@
             for member in range(2):
                 f = index * unroll + pair * 2 + member
                 at = pl.ds(pl.multiple_of(f * size, size), size)
-                values = jnp.concatenate([grad_ref[c, at, :] for c in range(chunks)], 1)
-                values = jnp.concatenate([values, values], 0).astype(BF16)
-                for b in range(books):
-                    high = jnp.broadcast_to(high_ref[b, pl.ds(f, 1), :], (16, groups)).astype(BF16)
-                    low = jnp.broadcast_to(low_ref[b, pl.ds(f, 1), :], (16, groups)).astype(BF16)
-                    left[b].append(
-                        jnp.concatenate([jnp.where(high == r, one, zero) for r in high_rows], 0)
-                    )
-                    right[b].append(
-                        jnp.concatenate([jnp.where(low == r, values, zero) for r in low_rows], 0)
-                    )
+                for c in range(chunks):
+                    values = grad_ref[c, at, :]
+                    values = jnp.concatenate([values, values], 0).astype(BF16)
+                    for b in range(books):
+                        pairs = pair_ref[b, c, pl.ds(f, 8, stride=0), :]
+                        pairs = jnp.concatenate([pairs, pairs], 0).astype(I16)
+                        high = pairs >> I16(3)
+                        low = pairs & I16(7)
+                        left[b].append(
+                            jnp.concatenate([jnp.where(high == r, one, zero) for r in high_rows], 0)
+                        )
+                        right[b].append(
+                            jnp.concatenate([jnp.where(low == r, values, zero) for r in low_rows], 0)
+                        )
             for b in range(books):
                 totals[b] = totals[b] + dot_nt(
                     jnp.concatenate(left[b], 1), jnp.concatenate(right[b], 1)
@@ -415,9 +417,9 @@
     hidden, outgoing = lax.optimization_barrier((hidden, outgoing))
 
     halves = entries // LANES
-    table = codebook.astype(F32).transpose(0, 2, 1).reshape(books, size, halves, LANES)
+    table = codebook.transpose(0, 2, 1).reshape(books, size, halves, LANES)
     table = jnp.broadcast_to(
-        table.transpose(0, 2, 1, 3)[:, :, :, None, :], (books, halves, size, 8, LANES)
+        table.transpose(0, 2, 1, 3)[:, :, :, None, :], (books, halves, size, 16, LANES)
     )
     block = 128
 
@@ -430,7 +432,7 @@
             grid=(count,),
             in_specs=[
                 pl.BlockSpec((books, block, groups), lambda s: (0, s + start, 0)),
-                whole((books, halves, size, 8, LANES)),
+                whole((books, halves, size, 16, LANES)),
                 pl.BlockSpec((rows, block), lambda s: (0, s + start)),
             ]
             + [whole(m.shape) for m in more],
@@ -441,19 +443,20 @@
             input_output_aliases={} if first else {3: 0},
             compiler_params=params(60),
             cost_estimate=pl.CostEstimate(
-                flops=count * 10_000_000_000, bytes_accessed=2_000_000, transcendentals=0
+                flops=count * 5_000_000_000, bytes_accessed=2_000_000, transcendentals=0
             ),
             name="decode",
         )(codes, table, hidden, *more)
 
     blocks = inner // block
-    first_part, second_part = blocks // 3, blocks // 2
-    (plain_out,) = decode(0, first_part, None)
+    (plain_out,) = decode(0, blocks // 3, None)
     plain_out, shares = lax.optimization_barrier((plain_out, shares))
     near = gather_exchange(shares) if direct else None
-    (plain_out,) = decode(first_part, second_part, plain_out)
+    plain_out, expert_out = decode(blocks // 3, blocks - blocks // 3, plain_out)
     if direct:
-        plain_out, near, slots = lax.optimization_barrier((plain_out, near, slots))
+        plain_out, expert_out, near, slots = lax.optimization_barrier(
+            (plain_out, expert_out, near, slots)
+        )
         far = swap(near, 1)
     else:
         routers = lax.all_gather(shares, "expert", axis=0, tiled=False)
@@ -461,8 +464,6 @@
         routers = routers.transpose(0, 2, 1, 3, 4)
         routers = routers.reshape(parts, later_count, routed, part_width)
         near, far = routers[0::2], routers[1::2]
-    done = first_part + second_part
-    plain_out, expert_out = decode(done, blocks - done, plain_out)
 
     grid = (parts // 2, 2)
 
@@ -473,7 +474,7 @@
         (1, later_count, routed, part_width), lambda i, j, t: (i, 0, 0, 0)
     )
 
-    def by_columns(kernel, in_specs, out_specs, out_shape, scratch, mib, name):
+    def by_columns(kernel, in_specs, out_specs, out_shape, scratch, name):
         return pl.pallas_call(
             kernel,
             grid_spec=pltpu.PrefetchScalarGridSpec(
@@ -484,20 +485,41 @@
                 scratch_shapes=scratch,
             ),
             out_shape=out_shape,
-            compiler_params=params(min(56, mib)),
+            compiler_params=params(60),
             name=name,
         )
 
-    scores = by_columns(
-        score_kernel,
-        [columns(rows), columns(rows), router_spec, router_spec],
-        whole((rows, wide + LANES)),
-        jax.ShapeDtypeStruct((rows, wide + LANES), BF16),
-        [pltpu.VMEM((rows, wide + LANES), F32)],
-        8 + 4 * grow,
-        "scores",
-    )(twist, expert_out, slots, near, far)
-    scores = exchange(scores)
+    def score(last, routers, before):
+        def half(height):
+            return pl.BlockSpec((height, part_width), lambda i, t: (0, t[0] ^ (2 * i + last)))
+
+        sums = [((later_count * routed, rows), F32), ((rows, LANES), F32)]
+        return pl.pallas_call(
+            functools.partial(score_kernel, last),
+            grid_spec=pltpu.PrefetchScalarGridSpec(
+                num_scalar_prefetch=1,
+                grid=(parts // 2,),
+                in_specs=[
+                    half(rows),
+                    half(rows),
+                    pl.BlockSpec(
+                        (1, later_count, routed, part_width), lambda i, t: (i, 0, 0, 0)
+                    ),
+                ]
+                + [whole(b.shape) for b in before],
+                out_specs=whole((rows, wide + LANES)) if last else [whole(s) for s, _ in sums],
+                scratch_shapes=[pltpu.VMEM(s, d) for s, d in sums] if last else [],
+            ),
+            out_shape=(
+                jax.ShapeDtypeStruct((rows, wide + LANES), BF16)
+                if last
+                else [jax.ShapeDtypeStruct(s, d) for s, d in sums]
+            ),
+            compiler_params=params(60),
+            name="scores",
+        )(twist, expert_out, slots, routers, *before)
+
+    scores = exchange(score(True, far, score(False, near, [])))
 
     chain = pl.pallas_call(
         chain_kernel,
@@ -530,7 +552,6 @@
         columns(tokens),
         jax.ShapeDtypeStruct((tokens, width), BF16),
         [],
-        12,
         "finish",
     )(twist, out_grad, later, own, router_t, near, far)
 
@@ -550,13 +571,11 @@
             jax.ShapeDtypeStruct((size, groups), F32),
         ],
         [pltpu.VMEM((rows, width), BF16)],
-        12 + 12 * grow,
         "slot_grads",
     )(twist, slots, slots, slot_later, near, far, plain_out)
 
     block = 128
-    unroll = 16
-    high_count = entries // LOW
+    unroll = 32
     book_grad = pl.pallas_call(
         functools.partial(book_kernel, unroll),
         grid=(inner // block,),
@@ -566,18 +585,17 @@
             whole((size, groups)),
             pl.BlockSpec((books, block, groups), lambda s: (0, s, 0)),
         ],
-        out_specs=whole((books, high_count, LOW * size)),
-        out_shape=jax.ShapeDtypeStruct((books, high_count, LOW * size), F32),
+        out_specs=whole((books, HIGH, LOW * size)),
+        out_shape=jax.ShapeDtypeStruct((books, HIGH, LOW * size), F32),
         scratch_shapes=[
             pltpu.VMEM((groups // LANES, block * size, LANES), F32),
-            pltpu.VMEM((books, block, groups), F32),
-            pltpu.VMEM((books, block, groups), F32),
+            pltpu.VMEM((books, groups // LANES, block, LANES), jnp.int32),
         ],
         compiler_params=params(20 + 6 * grow),
         name="book_grads",
     )(hidden, slot_split, scale_split, codes)
 
-    book_grad = book_grad.reshape(books, entries, size)
+    book_grad = book_grad.reshape(books, HIGH * LOW, size)[:, :entries]
     scale_grad = scale_grad.T.reshape(width)
     return (result[None], book_grad[None, None], scale_grad[None, None])
 

time: 231 us -> 180 us (0.78)
  Pallas kernels: 145 us -> 99.4 us
  local copies, waits for them, and re-layouts: 23.7 us -> 12.4 us
  waiting for transfers between devices: 21.2 us -> 28.6 us
    pallas_call x3 -> x2, Pallas kernels: 71 us -> 29.5 us  [decode(): pl.pallas_call(functools.partial(decode_kernel, first, last), grid=(count...]
    unnamed x47 -> x33, local copies, waits for them, and re-layouts: 18.5 us -> 7.13 us
    pallas_call x1, Pallas kernels: 45.6 us -> 34.5 us  [on_device(): pl.pallas_call(functools.partial(book_kernel, unroll), grid=(inner // blo...]
    ppermute x4, waiting for transfers between devices: 0.01 us -> 7.58 us  [swap(): lax.ppermute(value, 'expert', [(i, i ^ distance) for i in range(count)])]
    pallas_call x1, Pallas kernels: 8.06 us -> 11.1 us  [on_device(): by_columns(slots_kernel, [columns(rows), pl.BlockSpec((rows, LANES), lamb...]
    pallas_call x1 -> x2, Pallas kernels: 7.24 us -> 8.8 us  [score(): pl.pallas_call(functools.partial(score_kernel, last), grid_spec=pltpu.Pre...]
  transfers between devices with their start and end apart: 12 -> 12, of which waited for: 3 -> 4; matrix products, arithmetic and copies ran while one was open for 5% -> 6% of each run, Pallas kernels for 34% -> 25%
where the time goes in v3:
time: 180 us; the launch traced here: 179 us
  Pallas kernels  99.4 us (55%)
  waiting for transfers between devices  28.6 us (16%)
  starting transfers between devices  20.3 us (11%)
  local copies, waits for them, and re-layouts  12.4 us (7%)
  blocking collectives  9.89 us (5%)
  other arithmetic  5.13 us (3%)
  matrix products  2.08 us (1%)
    pallas_call x1, Pallas kernels, on_device(): pl.pallas_call(functools.partial(book_kernel, unroll), grid=(inner // blo...  34.5 us
    pallas_call x2, Pallas kernels, decode(): pl.pallas_call(functools.partial(decode_kernel, first, last), grid=(count...  29.5 us
    ppermute x3, waiting for transfers between devices, on_device(): later = lax.ppermute(send, 'pipe', [(p, p - 1) for p in range(1, layers)])  21 us
    pallas_call x1, Pallas kernels, on_device(): by_columns(slots_kernel, [columns(rows), pl.BlockSpec((rows, LANES), lamb...  11.1 us
    all_to_all x1, blocking collectives, exchange(): lax.all_to_all(value, 'expert', split_axis=0, concat_axis=0, tiled=True)  9.89 us
    pallas_call x1, Pallas kernels, on_device(): by_columns(finish_kernel, [columns(tokens), whole((tokens, wide)), whole(...  8.92 us
    pallas_call x2, Pallas kernels, score(): pl.pallas_call(functools.partial(score_kernel, last), grid_spec=pltpu.Pre...  8.8 us
    all_to_all x2, starting transfers between devices, exchange(): lax.all_to_all(value, 'expert', split_axis=0, concat_axis=0, tiled=True)  8.69 us
  transfers between devices with their start and end apart: 12, of which 4 were waited for; matrix products, arithmetic and copies ran while one was open for 6% of the time, Pallas kernels for 25%

profile of v3, /device:TPU:0, one launch (start us, length us, event | category | flops | bytes accessed | tf_op | source)
XLA Modules:
  0.0 178.7 jit_solution(3473063542969319216)
XLA Ops:
  0.6 1.7 dynamic-slice_bitcast_fusion
  2.4 1.4 collective-permute-start
  3.8 1.3 collective-permute-start.1
  5.1 1.3 collective-permute-start.2
  6.4 2.1 %fusion.logits_ref = f32[128,160]{1,0:T(8,128)S(1)} fusion(bf16[1,5120,160]{1,2,0:T(8,128)(2,1)} %param.10, bf16[1,128,5120]{2,1,0:T(8,128)(2,1)S(1)} %copy-done), kind=kOutput, calls=%fused_computation.1 | convolution fusion | flops 209715200 | bytes 3031040 | tf_op jit(solution)/shard_map/dot_general | solution.py:28
  8.5 1.9 %prepare.1 = (f32[128,160]{1,0:T(8,128)S(1)}, bf16[128,128]{1,0:T(8,128)(2,1)S(1)}, bf16[128,5248]{1,0:T(8,128)(2,1)}) custom-call(f32[128,160]{1,0:T(8,128)S(1)} %fusion.logits_ref, s32[6,128]{1,0:T(8,128)S(1)} %bitcast.59, bf16[128,5120]{1,0:T(8,128)(2,1)S(1)} %copy-done.1), custom_call_target="tpu_custom_call" | custom-call | tf_op jit(solution)/shard_map/prepare/pallas_call | solution.py:406
  10.4 5.3 %all-to-all-start = ((bf16[8,16,5248]{2,1,0:T(8,128)(2,1)}), bf16[8,16,5248]{2,1,0:T(8,128)(2,1)S(1)}, u32[]{:S(2)}, u32[]{:S(2)}) async-start(bf16[8,16,5248]{2,1,0:T(8,128)(2,1)} %bitcast.21), calls=%async_computation | async-start | bytes 2686976 | tf_op jit(solution)/shard_map/all_to_all | solution.py:353
  17.2 9.7 %decode.2.rest_0_ = f32[8,128,640]{2,1,0:T(8,128)} custom-call(s32[2,768,640]{2,1,0:T(8,128)} %bitcast.51, bf16[2,2,8,16,128]{4,3,2,1,0:T(8,128)(2,1)} %broadcast_in_dim.19.table_ref, bf16[128,768]{1,0:T(8,128)(2,1)} %bitcast.54), custom_call_target="tpu_custom_call" | custom-call | flops 10000000000 | bytes 2000000 | tf_op jit(solution)/shard_map/decode/pallas_call | solution.py:430
  30.2 2.1 %collective-permute-start.3 = (bf16[3,160,640]{2,1,0:T(8,128)(2,1)S(1)}, bf16[3,160,640]{2,1,0:T(8,128)(2,1)}, u32[]{:S(2)}, u32[]{:S(2)}) collective-permute-start(bf16[3,160,640]{2,1,0:T(8,128)(2,1)S(1)} %pad_maximum_fusion.1), channel_id=1, source_target_pairs={{0,2},{1,3},{2,0},{3,1},{4,6},{5,7},{6,4},{7,5},{8,10},{9,11},{10,... | collective-permute-start | bytes 1843208 | tf_op jit(solution)/shard_map/ppermute | solution.py:358
  32.3 1.5 collective-permute-start.4
  33.8 19.8 %decode.3 = (f32[8,128,640]{2,1,0:T(8,128)}, bf16[128,5120]{1,0:T(8,128)(2,1)}) custom-call(s32[2,768,640]{2,1,0:T(8,128)} %bitcast.52, bf16[2,2,8,16,128]{4,3,2,1,0:T(8,128)(2,1)} %broadcast_in_dim.19.table_ref, bf16[128,768]{1,0:T(8,128)(2,1)} %bitcast.55, f32[8,128,640]{2,1,0:T(8,128)} %decode.2.rest_0_, ...), custom_call_target="tpu_custom_call", output_to_operand_aliasing={{0}: (3, {})} | custom-call | flops 20000000000 | bytes 2000000 | tf_op jit(solution)/shard_map/decode/pallas_call | solution.py:430
  53.6 7.6 %collective-permute-done.4 = bf16[3,160,640]{2,1,0:T(8,128)(2,1)} collective-permute-done((bf16[3,160,640]{2,1,0:T(8,128)(2,1)S(1)}, bf16[3,160,640]{2,1,0:T(8,128)(2,1)}, u32[]{:S(2)}, u32[]{:S(2)}) %collective-permute-start.4) | collective-permute-done | bytes 614432 | tf_op jit(solution)/shard_map/ppermute | solution.py:358
  61.2 3.3 %pad_maximum_fusion.router_ref.near_ref = bf16[4,3,160,640]{3,2,1,0:T(8,128)(2,1)} fusion(bf16[1,3,160,640]{3,2,1,0:T(8,128)(2,1)} %bitcast.20, bf16[1,3,160,640]{3,2,1,0:T(8,128)(2,1)} %bitcast.19, bf16[1,3,160,640]{3,2,1,0:T(8,128)(2,1)} %bitcast.18, bf16[1,3,160,640]{3,2,1,0:T(8,128)(2,1)S(1)} %bitcast.65), kind=kLoop, calls=%fused_computation | loop fusion | flops 3686400 | bytes 4915200 | tf_op jit(solution)/shard_map/stack | solution.py:363
  65.7 4.3 %scores.2 = (f32[480,128]{1,0:T(8,128)}, f32[128,128]{1,0:T(8,128)}) custom-call(s32[1]{0:T(128)} %bitcast.twist_ref, bf16[128,5120]{1,0:T(8,128)(2,1)} %get-tuple-element.30.out_ref, bf16[128,5248]{1,0:T(8,128)(2,1)} %bitcast.60, bf16[4,3,160,640]{3,2,1,0:T(8,128)(2,1)} %pad_maximum_fusion.router_ref.near_ref), custom_call_target="tpu_custom_call" | custom-call | tf_op jit(solution)/shard_map/scores/pallas_call | solution.py:497
  70.0 4.5 %scores.3 = bf16[128,896]{1,0:T(8,128)(2,1)} custom-call(s32[1]{0:T(128)} %bitcast.twist_ref, bf16[128,5120]{1,0:T(8,128)(2,1)} %get-tuple-element.30.out_ref, bf16[128,5248]{1,0:T(8,128)(2,1)} %bitcast.61, bf16[4,3,160,640]{3,2,1,0:T(8,128)(2,1)} %collective-permute-done.6.router_ref.far_ref, f32[480,128]{1,0:T(8,128)} %get-tuple-element.33.rest_0_, ...), custom_call_target="tpu_custom_call" | custom-call | tf_op jit(solution)/shard_map/scores/pallas_call | solution.py:497
  74.5 9.9 %all_to_all.34 = bf16[8,16,896]{2,1,0:T(8,128)(2,1)S(1)} all-to-all(bf16[8,16,896]{2,1,0:T(8,128)(2,1)} %bitcast.67), channel_id=1, replica_groups=mesh['pipe'=4,'expert'=8] {'expert'}, dimensions={0} | all-to-all | bytes 458752 | tf_op jit(solution)/shard_map/all_to_all | solution.py:353
  84.4 1.1 chain.4
  85.5 1.3 collective-permute-start.7
  86.8 7.7 %collective-permute-done.7.later_ref = bf16[128,768]{1,0:T(8,128)(2,1)S(1)} collective-permute-done((bf16[128,768]{1,0:T(8,128)(2,1)S(1)}, bf16[128,768]{1,0:T(8,128)(2,1)S(1)}, u32[]{:S(2)}, u32[]{:S(2)}) %collective-permute-start.7) | collective-permute-done | bytes 196640 | tf_op jit(solution)/shard_map/ppermute | solution.py:538
  94.6 1.1 chain.5
  95.7 1.3 collective-permute-start.8
  97.0 6.7 %collective-permute-done.8.later_ref = bf16[128,768]{1,0:T(8,128)(2,1)S(1)} collective-permute-done((bf16[128,768]{1,0:T(8,128)(2,1)S(1)}, bf16[128,768]{1,0:T(8,128)(2,1)S(1)}, u32[]{:S(2)}, u32[]{:S(2)}) %collective-permute-start.8) | collective-permute-done | bytes 196640 | tf_op jit(solution)/shard_map/ppermute | solution.py:538
  103.6 1.1 chain.6
  104.8 1.5 collective-permute-start.9
  106.3 6.6 %collective-permute-done.9.later_ref = bf16[128,768]{1,0:T(8,128)(2,1)S(1)} collective-permute-done((bf16[128,768]{1,0:T(8,128)(2,1)S(1)}, bf16[128,768]{1,0:T(8,128)(2,1)S(1)}, u32[]{:S(2)}, u32[]{:S(2)}) %collective-permute-start.9) | collective-permute-done | bytes 196640 | tf_op jit(solution)/shard_map/ppermute | solution.py:538
  112.9 1.2 chain.7
  114.7 3.4 %all-to-all-start.2 = ((bf16[8,16,768]{2,1,0:T(8,128)(2,1)}), bf16[8,16,768]{2,1,0:T(8,128)(2,1)S(1)}, u32[]{:S(2)}, u32[]{:S(2)}) async-start(bf16[8,16,768]{2,1,0:T(8,128)(2,1)} %bitcast.27), calls=%async_computation.2 | async-start | bytes 393216 | tf_op jit(solution)/shard_map/all_to_all | solution.py:353
  118.1 8.9 %finish.1 = bf16[128,5120]{1,0:T(8,128)(2,1)} custom-call(s32[1]{0:T(128)} %bitcast.twist_ref, bf16[128,5120]{1,0:T(8,128)(2,1)} %grad_ref.3, bf16[128,768]{1,0:T(8,128)(2,1)} %copy-done.5, bf16[128,160]{1,0:T(8,128)(2,1)} %copy-done.7, bf16[160,5120]{1,0:T(8,128)(2,1)} %bitcast.64, bf16[4,3,160,640]{3,2,1,0:T(8,128)(2,1)} %pad_maximum_fusion.router_ref.near_ref, ...), custom_call_target="tpu_custom_call" | custom-call | tf_op jit(solution)/shard_map/finish/pallas_call | solution.py:542
  127.7 11.1 %slot_grads.1 = (bf16[8,128,640]{2,1,0:T(8,128)(2,1)}, f32[8,640]{1,0:T(8,128)}) custom-call(s32[1]{0:T(128)} %bitcast.twist_ref, bf16[128,5248]{1,0:T(8,128)(2,1)} %bitcast.62, bf16[128,5248]{1,0:T(8,128)(2,1)} %bitcast.63, bf16[128,768]{1,0:T(8,128)(2,1)} %bitcast.68, bf16[4,3,160,640]{3,2,1,0:T(8,128)(2,1)} %pad_maximum_fusion.router_ref.near_ref, ...), custom_call_target="tpu_custom_call" | custom-call | tf_op jit(solution)/shard_map/slot_grads/pallas_call | solution.py:558
  138.8 2.1 %copy-done.2 = s32[1,1,2,768,640]{4,3,2,1,0:T(8,128)S(1)} copy-done((s32[1,1,2,768,640]{4,3,2,1,0:T(8,128)S(1)}, s32[1,1,2,768,640]{4,3,2,1,0:T(8,128)}, u32[]{:S(2)}) %copy-start.2) | copy-done | bytes 3932184
  140.9 1.3 copy-done.3
  142.2 34.5 %book_grads.1 = f32[2,48,48]{2,1,0:T(8,128)S(1)} custom-call(bf16[128,768]{1,0:T(8,128)(2,1)S(1)} %bitcast.56, bf16[8,128,640]{2,1,0:T(8,128)(2,1)S(1)} %copy-done.3, f32[8,640]{1,0:T(8,128)S(1)} %bitcast.58, s32[2,768,640]{2,1,0:T(8,128)S(1)} %bitcast.53), custom_call_target="tpu_custom_call" | custom-call | tf_op jit(solution)/shard_map/book_grads/pallas_call | solution.py:579
  (53 shorter events, 9.2 us)
Async XLA Ops:
  0.6 5.8 %copy-start = (bf16[1,128,5120]{2,1,0:T(8,128)(2,1)S(1)}, bf16[1,128,5120]{2,1,0:T(8,128)(2,1)}, u32[]{:S(2)}) copy-start(bf16[1,128,5120]{2,1,0:T(8,128)(2,1)} %param.9) | copy-start | bytes 3932164
  2.4 6.1 %copy-start.14 = (s32[1,128,6]{1,0,2:T(1,128)S(1)}, s32[1,128,6]{1,0,2:T(1,128)}, u32[]{:S(2)}) copy-start(s32[1,128,6]{1,0,2:T(1,128)} %param.11) | copy-start | bytes 9220
  2.4 6.1 %copy-start.1 = (bf16[128,5120]{1,0:T(8,128)(2,1)S(1)}, bf16[128,5120]{1,0:T(8,128)(2,1)}, u32[]{:S(2)}) copy-start(bf16[128,5120]{1,0:T(8,128)(2,1)} %grad_ref.3) | copy-start | bytes 3932164
  2.4 26.7 %collective-permute-start = (bf16[160,640]{1,0:T(8,128)(2,1)}, bf16[160,640]{1,0:T(8,128)(2,1)S(1)}, u32[]{:S(2)}, u32[]{:S(2)}) collective-permute-start(bf16[160,640]{1,0:T(8,128)(2,1)} %dynamic-slice_bitcast_fusion), channel_id=1, source_target_pairs={{8,0},{16,8},{24,16},{9,1},{17,9},{25,17},{10,2},{18,10},{26,18},{... | collective-permute-start | bytes 614408 | tf_op jit(solution)/shard_map/ppermute | solution.py:399
  3.8 25.3 %collective-permute-start.1 = (bf16[160,640]{1,0:T(8,128)(2,1)}, bf16[160,640]{1,0:T(8,128)(2,1)}, u32[]{:S(2)}, u32[]{:S(2)}) collective-permute-start(bf16[160,640]{1,0:T(8,128)(2,1)} %dynamic-slice_bitcast_fusion), channel_id=1, source_target_pairs={{16,0},{24,8},{17,1},{25,9},{18,2},{26,10},{19,3},{27,11},{20,4},{... | collective-permute-start | bytes 614408 | tf_op jit(solution)/shard_map/ppermute | solution.py:399
  5.1 24.0 %collective-permute-start.2 = (bf16[160,640]{1,0:T(8,128)(2,1)}, bf16[160,640]{1,0:T(8,128)(2,1)}, u32[]{:S(2)}, u32[]{:S(2)}) collective-permute-start(bf16[160,640]{1,0:T(8,128)(2,1)} %dynamic-slice_bitcast_fusion), channel_id=1, source_target_pairs={{24,0},{25,1},{26,2},{27,3},{28,4},{29,5},{30,6},{31,7}} | collective-permute-start | bytes 614408 | tf_op jit(solution)/shard_map/ppermute | solution.py:399
  10.4 5.3 %copy-start.10 = (bf16[1,1,72,768]{3,2,1,0:T(8,128)(2,1)S(1)}, bf16[1,1,72,768]{3,2,1,0:T(8,128)(2,1)}, u32[]{:S(2)}) copy-start(bf16[1,1,72,768]{3,2,1,0:T(8,128)(2,1)} %param.12) | copy-start | bytes 331780
  10.4 6.1 %copy-start.13 = (bf16[1,1,2,256,8]{3,4,2,1,0:T(8,128)(2,1)S(1)}, bf16[1,1,2,256,8]{3,4,2,1,0:T(8,128)(2,1)}, u32[]{:S(2)}) copy-start(bf16[1,1,2,256,8]{3,4,2,1,0:T(8,128)(2,1)} %param.14) | copy-start | bytes 24580
  10.4 54.1 %all-to-all-start = ((bf16[8,16,5248]{2,1,0:T(8,128)(2,1)}), bf16[8,16,5248]{2,1,0:T(8,128)(2,1)S(1)}, u32[]{:S(2)}, u32[]{:S(2)}) async-start(bf16[8,16,5248]{2,1,0:T(8,128)(2,1)} %bitcast.21), calls=%async_computation | async-start | bytes 2686976 | tf_op jit(solution)/shard_map/all_to_all | solution.py:353
  17.2 10.3 %copy-start.11 = (f32[1,1,5120]{2,1,0:T(1,128)S(1)}, f32[1,1,5120]{2,1,0:T(1,128)}, u32[]{:S(2)}) copy-start(f32[1,1,5120]{2,1,0:T(1,128)} %param.15) | copy-start | bytes 61444
  30.2 23.4 %collective-permute-start.3 = (bf16[3,160,640]{2,1,0:T(8,128)(2,1)S(1)}, bf16[3,160,640]{2,1,0:T(8,128)(2,1)}, u32[]{:S(2)}, u32[]{:S(2)}) collective-permute-start(bf16[3,160,640]{2,1,0:T(8,128)(2,1)S(1)} %pad_maximum_fusion.1), channel_id=1, source_target_pairs={{0,2},{1,3},{2,0},{3,1},{4,6},{5,7},{6,4},{7,5},{8,10},{9,11},{10,... | collective-permute-start | bytes 1843208 | tf_op jit(solution)/shard_map/ppermute | solution.py:358
  32.3 28.9 %collective-permute-start.4 = (bf16[3,160,640]{2,1,0:T(8,128)(2,1)S(1)}, bf16[3,160,640]{2,1,0:T(8,128)(2,1)}, u32[]{:S(2)}, u32[]{:S(2)}) collective-permute-start(bf16[3,160,640]{2,1,0:T(8,128)(2,1)S(1)} %pad_maximum_fusion.1), channel_id=1, source_target_pairs={{0,4},{1,5},{2,6},{3,7},{4,0},{5,1},{6,2},{7,3},{8,12},{9,13},{10,... | collective-permute-start | bytes 1843208 | tf_op jit(solution)/shard_map/ppermute | solution.py:358
  33.8 27.4 %collective-permute-start.5 = (bf16[3,160,640]{2,1,0:T(8,128)(2,1)S(1)}, bf16[3,160,640]{2,1,0:T(8,128)(2,1)}, u32[]{:S(2)}, u32[]{:S(2)}) collective-permute-start(bf16[3,160,640]{2,1,0:T(8,128)(2,1)S(1)} %pad_maximum_fusion.1), channel_id=1, source_target_pairs={{0,6},{1,7},{2,4},{3,5},{4,2},{5,3},{6,0},{7,1},{8,14},{9,15},{10,... | collective-permute-start | bytes 1843208 | tf_op jit(solution)/shard_map/ppermute | solution.py:358
  64.5 1.2 copy-start.8
  64.5 5.4 %collective-permute-start.6 = (bf16[4,3,160,640]{3,2,1,0:T(8,128)(2,1)}, bf16[4,3,160,640]{3,2,1,0:T(8,128)(2,1)}, u32[]{:S(2)}, u32[]{:S(2)}) collective-permute-start(bf16[4,3,160,640]{3,2,1,0:T(8,128)(2,1)} %pad_maximum_fusion.router_ref.near_ref), channel_id=1, source_target_pairs={{0,1},{1,0},{2,3},{3,2},{4,5},{5,4},{6,7},{7,6},{8,9},{9,8},{10,11... | collective-permute-start | bytes 7372808 | tf_op jit(solution)/shard_map/ppermute | solution.py:358
  85.5 9.0 %collective-permute-start.7 = (bf16[128,768]{1,0:T(8,128)(2,1)S(1)}, bf16[128,768]{1,0:T(8,128)(2,1)S(1)}, u32[]{:S(2)}, u32[]{:S(2)}) collective-permute-start(bf16[128,768]{1,0:T(8,128)(2,1)S(1)} %get-tuple-element.37), channel_id=1, source_target_pairs={{8,0},{16,8},{24,16},{9,1},{17,9},{25,17},{10,2},{18,10},{26,18},{... | collective-permute-start | bytes 589832 | tf_op jit(solution)/shard_map/ppermute | solution.py:538
  95.7 7.9 %collective-permute-start.8 = (bf16[128,768]{1,0:T(8,128)(2,1)S(1)}, bf16[128,768]{1,0:T(8,128)(2,1)S(1)}, u32[]{:S(2)}, u32[]{:S(2)}) collective-permute-start(bf16[128,768]{1,0:T(8,128)(2,1)S(1)} %get-tuple-element.38), channel_id=1, source_target_pairs={{8,0},{16,8},{24,16},{9,1},{17,9},{25,17},{10,2},{18,10},{26,18},{... | collective-permute-start | bytes 589832 | tf_op jit(solution)/shard_map/ppermute | solution.py:538
  104.8 8.1 %collective-permute-start.9 = (bf16[128,768]{1,0:T(8,128)(2,1)S(1)}, bf16[128,768]{1,0:T(8,128)(2,1)S(1)}, u32[]{:S(2)}, u32[]{:S(2)}) collective-permute-start(bf16[128,768]{1,0:T(8,128)(2,1)S(1)} %get-tuple-element.39), channel_id=1, source_target_pairs={{8,0},{16,8},{24,16},{9,1},{17,9},{25,17},{10,2},{18,10},{26,18},{... | collective-permute-start | bytes 589832 | tf_op jit(solution)/shard_map/ppermute | solution.py:538
  112.9 5.2 %copy-start.5 = (bf16[128,768]{1,0:T(8,128)(2,1)}, bf16[128,768]{1,0:T(8,128)(2,1)S(1)}, u32[]{:S(2)}) copy-start(bf16[128,768]{1,0:T(8,128)(2,1)S(1)} %collective-permute-done.9.later_ref) | copy-start | bytes 589828
  114.1 0.6 copy-start.7
  114.7 12.3 %all-to-all-start.2 = ((bf16[8,16,768]{2,1,0:T(8,128)(2,1)}), bf16[8,16,768]{2,1,0:T(8,128)(2,1)S(1)}, u32[]{:S(2)}, u32[]{:S(2)}) async-start(bf16[8,16,768]{2,1,0:T(8,128)(2,1)} %bitcast.27), calls=%async_computation.2 | async-start | bytes 393216 | tf_op jit(solution)/shard_map/all_to_all | solution.py:353
  127.0 0.7 copy-start.9
  127.7 11.1 %copy-start.4 = (bf16[8,16,768]{2,1,0:T(8,128)(2,1)S(1)}, bf16[8,16,768]{2,1,0:T(8,128)(2,1)}, u32[]{:S(2)}) copy-start(bf16[8,16,768]{2,1,0:T(8,128)(2,1)} %pad.4) | copy-start | bytes 589828
  127.7 11.1 %copy-start.6 = (f32[640,8]{0,1:T(8,128)S(1)}, f32[640,8]{0,1:T(8,128)}, u32[]{:S(2)}) copy-start(f32[640,8]{0,1:T(8,128)} %copy.15) | copy-start | bytes 61444
  138.8 2.1 %copy-start.2 = (s32[1,1,2,768,640]{4,3,2,1,0:T(8,128)S(1)}, s32[1,1,2,768,640]{4,3,2,1,0:T(8,128)}, u32[]{:S(2)}) copy-start(s32[1,1,2,768,640]{4,3,2,1,0:T(8,128)} %param.13) | copy-start | bytes 11796484
  140.9 1.3 copy-start.3
  142.2 35.4 %copy-start.12 = (f32[8,640]{1,0:T(8,128)S(1)}, f32[8,640]{1,0:T(8,128)}, u32[]{:S(2)}) copy-start(f32[8,640]{1,0:T(8,128)} %get-tuple-element.44) | copy-start | bytes 61444

commit v4 on v3

--- a/solution.py
+++ b/solution.py
@@ -64,41 +64,47 @@
     return mask.astype(F32).astype(BF16)
 
 
-def prepare_kernel(logits_ref, routes_ref, grad_ref, probs_ref, select_ref, rows_ref):
+def slot_select(state, rows, routed):
+    tokens, width = state.shape
+    number = jnp.where(iota((tokens, width), 1) >= routed, state, 0.0).astype(BF16)
+    owner = iota((width, rows), 0) - routed == iota((width, rows), 1) // SLOT
+    place = (iota((tokens, rows), 1) % SLOT + 1).astype(F32)
+    return one_hot(jnp.abs(dot(number, one_hot(owner)) - place) < 0.5)
+
+
+def prepare_kernel(logits_ref, routes_ref, grad_ref, state_ref, rows_ref, order_ref):
     tokens, routed = logits_ref.shape
-    top = routes_ref.shape[0]
+    top = routes_ref.shape[1]
     width = grad_ref.shape[1]
     rows = rows_ref.shape[0]
     experts = rows // SLOT
+    state_width = state_ref.shape[1]
     raised = jnp.exp(logits_ref[...])
     probs = raised / jnp.sum(raised, axis=1, keepdims=True)
-    probs_ref[...] = probs
-    expert = iota((experts, tokens), 0)
-    hits = jnp.zeros((experts, tokens), F32)
+    expert = iota((tokens, state_width), 1) - routed
+    named = jnp.zeros((tokens, state_width), F32)
     for k in range(top):
-        hits = hits + (routes_ref[k : k + 1, :] == expert).astype(F32)
-    hits = hits.astype(BF16)
-    earlier = one_hot(iota((tokens, tokens), 0) < iota((tokens, tokens), 1))
-    position = dot(hits, earlier).astype(BF16)
-    owner = one_hot(slot_expert(rows, experts))
-    slot_hit = dot(owner, hits)
-    slot_position = dot(owner, position)
-    place = (iota((rows, tokens), 0) % SLOT).astype(F32)
-    select = one_hot(
-        (slot_hit > 0.5) & (jnp.abs(slot_position - place) < 0.5) & (place < MOST - 0.5)
-    )
-    select_ref[...] = select
+        named = named + (routes_ref[:, k : k + 1] == expert).astype(F32)
+    named = jnp.where(expert < experts, named, 0.0)
+    earlier = one_hot(iota((tokens, tokens), 1) < iota((tokens, tokens), 0))
+    state_ref[...] = named * (dot(earlier, named.astype(BF16)) + 1.0)
+    state_ref[:, :routed] = probs
+    select = slot_select(state_ref[...], rows, routed)
     gate = (ROUTE_SCALE * probs).astype(BF16)
     slot_gate = jnp.sum(
-        jnp.where(slot_expert(rows, routed), dot(select, gate), 0.0), axis=1, keepdims=True
+        jnp.where(slot_expert(rows, routed), dot_tn(select, gate), 0.0), axis=1, keepdims=True
     )
-    rows_ref[:, :width] = dot(select, grad_ref[...]).astype(BF16)
+    rows_ref[:, :width] = dot_tn(select, grad_ref[...]).astype(BF16)
     rows_ref[:, width:] = jnp.broadcast_to(slot_gate, (rows, LANES)).astype(BF16)
+    span = order_ref.shape[0]
+    row = iota((span, span), 0)
+    source = (span // LANES) * (row & (LANES - 1)) + row // LANES
+    order_ref[...] = one_hot(source == iota((span, span), 1))
 
 
 def decode_kernel(first, last, codes_ref, table_ref, hidden_ref, *rest):
     if not first:
-        before_ref, scale_ref, *rest = rest
+        before_ref, scale_ref, order_ref, *rest = rest
     plain_out_ref, *rest = rest
     weight_ref = rest[-1]
     unroll = 8
@@ -144,15 +150,14 @@
     @pl.when(step == pl.num_programs(0) - 1)
     def _():
         span = size * LANES
-        column = iota((span, span), 0)
-        source = size * (column & (LANES - 1)) + column // LANES
-        back = (source == iota((span, span), 1)).astype(F32).astype(BF16)
         for chunk in range(groups // LANES):
             lanes = slice(chunk * LANES, (chunk + 1) * LANES)
             split = jnp.concatenate(
                 [plain_out_ref[i, :, lanes] * scale_ref[i : i + 1, lanes] for i in range(size)], 1
             ).astype(BF16)
-            out_ref[:, chunk * span : (chunk + 1) * span] = dot(split, back).astype(BF16)
+            out_ref[:, chunk * span : (chunk + 1) * span] = dot(
+                split, order_ref[...]
+            ).astype(BF16)
 
 
 def score_kernel(last, twist_ref, out_ref, slots_ref, router_ref, *rest):
@@ -197,27 +202,68 @@
         ).astype(BF16)
 
 
-def chain_kernel(scores_ref, later_ref, probs_ref, select_ref, own_ref, send_ref, picked_ref):
-    rows = scores_ref.shape[0]
-    tokens, wide = later_ref.shape
-    routed = probs_ref.shape[1]
-    later = later_ref[...]
-    select = select_ref[...]
-    picked = dot(select, later)
-    picked_ref[...] = picked.astype(BF16)
-    score = jnp.sum(picked * scores_ref[:, :wide].astype(F32), axis=1, keepdims=True) + jnp.sum(
-        scores_ref[:, wide:].astype(F32), axis=1, keepdims=True
+def response_kernel(routed, scores_ref, state_ref, *rest):
+    *later_refs, response_ref = rest
+    later_count = len(later_refs)
+    rows, width = response_ref.shape
+    experts = rows // SLOT
+    select = slot_select(state_ref[...], rows, routed)
+    column = iota((routed, width), 1)
+    entry = iota((routed, width), 0)
+    base_row, base_column = iota((LANES, width), 0), iota((LANES, width), 1)
+    total = dot(
+        scores_ref[:, later_count * WIDE :],
+        one_hot((base_column - later_count * experts == base_row) & (base_row < 3)),
     )
-    score = score.astype(BF16).astype(F32)
-    placed = jnp.where(slot_expert(rows, routed), score, 0.0).astype(BF16)
-    spread = dot_tn(select, placed)
-    probs = probs_ref[...]
-    weighted = jnp.sum(probs * spread, axis=1, keepdims=True)
-    own = (ROUTE_SCALE * probs * (spread - weighted)).astype(BF16)
-    own_ref[...] = own
-    send_ref[:, :WIDE] = jnp.zeros((tokens, WIDE), BF16)
-    send_ref[:, :routed] = own
-    send_ref[:, WIDE:] = later[:, : wide - WIDE]
+    for s in range(later_count):
+        probs = later_refs[s][:, :routed]
+        high = probs.astype(BF16)
+        low = (probs - high.astype(F32)).astype(BF16)
+        picked = dot_tn(select, high) + dot_tn(select, low)
+        product = scores_ref[:, s * WIDE : s * WIDE + routed].astype(F32)
+        mean = jnp.sum(picked * product, axis=1, keepdims=True)
+        response = (ROUTE_SCALE * picked * (product - mean)).astype(BF16)
+        total = total + dot(
+            response, one_hot((column - s * experts == entry) & (entry < experts))
+        )
+    response_ref[...] = total.astype(BF16)
+
+
+def chain_kernel(routed, *refs):
+    own_ref, later_ref, picked_ref = refs[-3:]
+    count = (len(refs) - 3) // 2
+    response_refs, state_refs = refs[:count], refs[count : 2 * count]
+    rows, width = response_refs[0].shape
+    tokens = state_refs[0].shape[0]
+    experts = rows // SLOT
+    column = iota((rows, width), 1)
+    slot = iota((rows, width), 0)
+    base = column >= (count - 1) * experts
+    stacks = [jnp.zeros((tokens, width), F32) for _ in range(count)]
+    own_select = None
+    for s in range(count - 1, -1, -1):
+        select = slot_select(state_refs[s][...], rows, routed)
+        response = response_refs[s][...].astype(F32)
+        terms = jnp.where(base, response, 0.0)
+        if s < count - 1:
+            terms = terms + dot_tn(select, stacks[s].astype(BF16)) * response
+        score = jnp.sum(terms, axis=1, keepdims=True).astype(BF16).astype(F32)
+        for u in range(s):
+            first = (s - u - 1) * experts
+            placed = jnp.where(column - first == slot // SLOT, score, 0.0).astype(BF16)
+            stacks[u] = stacks[u] + dot(select, placed)
+        placed = jnp.where(slot_expert(rows, routed), score, 0.0).astype(BF16)
+        spread = dot(select, placed)
+        probs = state_refs[s][:, :routed]
+        weighted = jnp.sum(probs * spread, axis=1, keepdims=True)
+        dlogit = (ROUTE_SCALE * probs * (spread - weighted)).astype(BF16)
+        if s == 0:
+            own_ref[...] = dlogit
+            own_select = select
+        else:
+            later_ref[:, (s - 1) * WIDE : s * WIDE] = jnp.zeros((tokens, WIDE), BF16)
+            later_ref[:, (s - 1) * WIDE : (s - 1) * WIDE + routed] = dlogit
+    picked_ref[...] = dot_tn(own_select, later_ref[...]).astype(BF16)
 
 
 def add_layers(current, later_ref, router_ref):
@@ -228,54 +274,53 @@
     return current
 
 
+def halves_of(twist, part_width):
+    return [
+        pl.ds(pl.multiple_of(((twist & 1) ^ far) * part_width, LANES), part_width)
+        for far in range(2)
+    ]
+
+
 def finish_kernel(
     twist_ref, grad_ref, later_ref, own_ref, router_ref, near_ref, far_ref, result_ref
 ):
-    def finish(routers_ref):
-        current = add_layers(grad_ref[...], later_ref, routers_ref)
-        result_ref[...] = (current.astype(F32) + dot(own_ref[...], router_ref[...])).astype(BF16)
-
-    @pl.when(pl.program_id(1) == 0)
+    places = halves_of(twist_ref[0], near_ref.shape[3])
+    grads = [grad_ref[:, at] for at in places]
+    routers = [router_ref[:, at] for at in places]
+    results = []
+    for grad, router, routers_ref in zip(grads, routers, (near_ref, far_ref)):
+        current = add_layers(grad, later_ref, routers_ref)
+        results.append((current.astype(F32) + dot(own_ref[...], router)).astype(BF16))
+    for at, result in zip(places, results):
+        result_ref[:, at] = result
+
+
+def slots_kernel(
+    twist_ref, slots_ref, gates_ref, later_ref, near_ref, far_ref, plain_out_ref, order_ref,
+    split_ref, scale_grad_ref, grad_ref
+):
+    i = pl.program_id(0)
+    part_width = near_ref.shape[3]
+    size, _, groups = plain_out_ref.shape
+    span = size * LANES
+    twist = twist_ref[0]
+    pair = ((twist >> 1) ^ i) * 2
+    gate = gates_ref[:, :1].astype(F32)
+    places = halves_of(twist, part_width)
+    slots = [slots_ref[:, at] for at in places]
+    grads = [
+        (gate * add_layers(part, later_ref, routers_ref).astype(F32)).astype(BF16)
+        for part, routers_ref in zip(slots, (near_ref, far_ref))
+    ]
+    for far in range(2):
+        first = (pair + ((twist & 1) ^ far)) * part_width
+        grad_ref[:, pl.ds(pl.multiple_of(first, LANES), part_width)] = grads[far]
+
+    @pl.when(i == pl.num_programs(0) - 1)
     def _():
-        finish(near_ref)
-
-    @pl.when(pl.program_id(1) == 1)
-    def _():
-        finish(far_ref)
-
-
-def slots_kernel(
-    twist_ref, slots_ref, gates_ref, later_ref, near_ref, far_ref, plain_out_ref, split_ref,
-    scale_grad_ref, grad_ref
-):
-    i, j = pl.program_id(0), pl.program_id(1)
-    part_width = slots_ref.shape[1]
-    size = plain_out_ref.shape[0]
-    groups = plain_out_ref.shape[2]
-    span = size * LANES
-    at = pl.ds(pl.multiple_of((twist_ref[0] ^ (2 * i + j)) * part_width, LANES), part_width)
-    gate = gates_ref[:, :1].astype(F32)
-
-    def put(routers_ref):
-        current = add_layers(slots_ref[...], later_ref, routers_ref)
-        grad_ref[:, at] = (gate * current.astype(F32)).astype(BF16)
-
-    @pl.when(j == 0)
-    def _():
-        put(near_ref)
-
-    @pl.when(j == 1)
-    def _():
-        put(far_ref)
-
-    @pl.when((i == pl.num_programs(0) - 1) & (j == 1))
-    def _():
-        column = iota((span, span), 1)
-        source = size * (column & (LANES - 1)) + column // LANES
-        order = one_hot(source == iota((span, span), 0))
         for chunk in range(groups // LANES):
             lanes = slice(chunk * LANES, (chunk + 1) * LANES)
-            split = dot(grad_ref[:, chunk * span : (chunk + 1) * span], order)
+            split = dot_nt(grad_ref[:, chunk * span : (chunk + 1) * span], order_ref[...])
             for i in range(size):
                 part = split[:, i * LANES : (i + 1) * LANES]
                 split_ref[i, :, lanes] = part.astype(BF16)
@@ -358,6 +403,13 @@
     return lax.ppermute(value, "expert", [(i, i ^ distance) for i in range(count)])
 
 
+def pass_down(value, layers):
+    return [
+        lax.ppermute(value, "pipe", [(p, p - s) for p in range(s, layers)])
+        for s in range(1, layers)
+    ]
+
+
 def gather_exchange(shares):
     count = lax.axis_size("expert")
     return jnp.stack([shares] + [swap(shares, d) for d in range(2, count, 2)])
@@ -394,27 +446,24 @@
         ((place % sharers) * share_rows, (place // sharers) * part_width),
         (share_rows, part_width),
     )
-    shares = jnp.stack(
-        [
-            lax.ppermute(own_share, "pipe", [(p, p - s) for p in range(s, layers)])
-            for s in range(1, layers)
-        ]
-    )
+    shares = jnp.stack(pass_down(own_share, layers))
     twist = jnp.full((1,), place if direct else 0, jnp.int32)
 
     logits = dot(saved_inputs[0], router[0])
-    probs, select, outgoing = pl.pallas_call(
+    state_width = -(-(routed + experts) // LANES) * LANES
+    span = size * LANES
+    state, outgoing, order = pl.pallas_call(
         prepare_kernel,
         out_shape=(
-            jax.ShapeDtypeStruct((tokens, routed), F32),
-            jax.ShapeDtypeStruct((rows, tokens), BF16),
+            jax.ShapeDtypeStruct((tokens, state_width), F32),
             jax.ShapeDtypeStruct((rows, width + LANES), BF16),
+            jax.ShapeDtypeStruct((span, span), BF16),
         ),
-        compiler_params=params(12 + 6 * grow),
+        compiler_params=params(20 + 6 * grow),
         name="prepare",
-    )(logits, routes[0].T, out_grad)
+    )(logits, routes[0], out_grad)
     slots = exchange(outgoing)
-    hidden, outgoing = lax.optimization_barrier((hidden, outgoing))
+    hidden, outgoing, scale_split = lax.optimization_barrier((hidden, outgoing, scale_split))
 
     halves = entries // LANES
     table = codebook.transpose(0, 2, 1).reshape(books, size, halves, LANES)
@@ -426,7 +475,7 @@
     def decode(start, count, before):
         first = before is None
         last = start + count == inner // block
-        more = [] if first else [before, scale_split]
+        more = [] if first else [before, scale_split, order]
         return pl.pallas_call(
             functools.partial(decode_kernel, first, last),
             grid=(count,),
@@ -449,10 +498,12 @@
         )(codes, table, hidden, *more)
 
     blocks = inner // block
-    (plain_out,) = decode(0, blocks // 3, None)
-    plain_out, shares = lax.optimization_barrier((plain_out, shares))
+    early = max(1, blocks // 6)
+    (plain_out,) = decode(0, early, None)
+    plain_out, shares, later_state = lax.optimization_barrier((plain_out, shares, state))
     near = gather_exchange(shares) if direct else None
-    plain_out, expert_out = decode(blocks // 3, blocks - blocks // 3, plain_out)
+    states = [state] + pass_down(later_state, layers)
+    plain_out, expert_out = decode(early, blocks - early, plain_out)
     if direct:
         plain_out, expert_out, near, slots = lax.optimization_barrier(
             (plain_out, expert_out, near, slots)
@@ -465,14 +516,12 @@
         routers = routers.reshape(parts, later_count, routed, part_width)
         near, far = routers[0::2], routers[1::2]
 
-    grid = (parts // 2, 2)
+    grid = (parts // 2,)
 
     def columns(height):
-        return pl.BlockSpec((height, part_width), lambda i, j, t: (0, t[0] ^ (2 * i + j)))
-
-    router_spec = pl.BlockSpec(
-        (1, later_count, routed, part_width), lambda i, j, t: (i, 0, 0, 0)
-    )
+        return pl.BlockSpec((height, 2 * part_width), lambda i, t: (0, (t[0] >> 1) ^ i))
+
+    router_spec = pl.BlockSpec((1, later_count, routed, part_width), lambda i, t: (i, 0, 0, 0))
 
     def by_columns(kernel, in_specs, out_specs, out_shape, scratch, name):
         return pl.pallas_call(
@@ -521,21 +570,23 @@
 
     scores = exchange(score(True, far, score(False, near, [])))
 
-    chain = pl.pallas_call(
-        chain_kernel,
+    response_width = -(-(later_count * experts + 3) // LANES) * LANES
+    response = pl.pallas_call(
+        functools.partial(response_kernel, routed),
+        out_shape=jax.ShapeDtypeStruct((rows, response_width), BF16),
+        compiler_params=params(12 + 4 * grow),
+        name="responses",
+    )(scores, *states)
+    own, later, picked = pl.pallas_call(
+        functools.partial(chain_kernel, routed),
         out_shape=(
             jax.ShapeDtypeStruct((tokens, routed), BF16),
             jax.ShapeDtypeStruct((tokens, wide), BF16),
             jax.ShapeDtypeStruct((rows, wide), BF16),
         ),
-        compiler_params=params(8 + 4 * grow),
+        compiler_params=params(12 + 4 * grow),
         name="chain",
-    )
-    later = jnp.zeros((tokens, wide), BF16)
-    for step in range(layers):
-        own, send, picked = chain(scores, later, probs, select)
-        if step + 1 < layers:
-            later = lax.ppermute(send, "pipe", [(p, p - 1) for p in range(1, layers)])
+    )(response, *pass_down(response, layers), *states)
 
     slot_later = exchange(picked)
 
@@ -564,6 +615,7 @@
             router_spec,
             router_spec,
             whole((size, rows, groups)),
+            whole((span, span)),
         ],
         [whole((size, rows, groups)), whole((size, groups))],
         [
@@ -572,10 +624,10 @@
         ],
         [pltpu.VMEM((rows, width), BF16)],
         "slot_grads",
-    )(twist, slots, slots, slot_later, near, far, plain_out)
+    )(twist, slots, slots, slot_later, near, far, plain_out, order)
 
     block = 128
-    unroll = 32
+    unroll = 64
     book_grad = pl.pallas_call(
         functools.partial(book_kernel, unroll),
         grid=(inner // block,),
@@ -591,7 +643,7 @@
             pltpu.VMEM((groups // LANES, block * size, LANES), F32),
             pltpu.VMEM((books, groups // LANES, block, LANES), jnp.int32),
         ],
-        compiler_params=params(20 + 6 * grow),
+        compiler_params=params(60),
         name="book_grads",
     )(hidden, slot_split, scale_split, codes)
 

time: 180 us -> 174 us (0.967)
  blocking collectives: 9.89 us -> 0 us
  starting transfers between devices: 20.3 us -> 28.1 us
  Pallas kernels: 99.4 us -> 94.7 us
    all_to_all x1 -> x0, blocking collectives: 9.89 us -> none  [exchange(): lax.all_to_all(value, 'expert', split_axis=0, concat_axis=0, tiled=True)]
    ppermute x6 -> x9, starting transfers between devices: 8.02 us -> 11.9 us  [pass_down(): lax.ppermute(value, 'pipe', [(p, p - s) for p in range(s, layers)])]
    all_to_all x2 -> x3, starting transfers between devices: 8.69 us -> 12.6 us  [exchange(): lax.all_to_all(value, 'expert', split_axis=0, concat_axis=0, tiled=True)]
    pallas_call x1, Pallas kernels: 8.92 us -> 5.97 us  [on_device(): by_columns(finish_kernel, [columns(tokens), whole((tokens, wide)), whole(...]
    pallas_call x5 -> x3, Pallas kernels: 6.51 us -> 5.04 us  [the longest x1 2.32 us: on_device(): pl.pallas_call(functools.partial(chain_kernel, routed), out_shape=(jax.Sh...]
    ppermute x6 -> x9, waiting for transfers between devices: 21 us -> 22.2 us  [pass_down(): lax.ppermute(value, 'pipe', [(p, p - s) for p in range(s, layers)])]
    unnamed x33 -> x31, local copies, waits for them, and re-layouts: 7.13 us -> 7.55 us
  transfers between devices with their start and end apart: 12 -> 16, of which waited for: 4 -> 7; matrix products, arithmetic and copies ran while one was open for 6% -> 6% of each run, Pallas kernels for 25% -> 24%
where the time goes in v4:
time: 174 us; the launch traced here: 173 us
  Pallas kernels  94.7 us (54%)
  waiting for transfers between devices  28.5 us (16%)
  starting transfers between devices  28.1 us (16%)
  local copies, waits for them, and re-layouts  13.6 us (8%)
  other arithmetic  5.22 us (3%)
  matrix products  2.08 us (1%)
    pallas_call x1, Pallas kernels, on_device(): pl.pallas_call(functools.partial(book_kernel, unroll), grid=(inner // blo...  34.5 us
    pallas_call x2, Pallas kernels, decode(): pl.pallas_call(functools.partial(decode_kernel, first, last), grid=(count...  29.8 us
    ppermute x9, waiting for transfers between devices, pass_down(): lax.ppermute(value, 'pipe', [(p, p - s) for p in range(s, layers)])  22.2 us
    all_to_all x3, starting transfers between devices, exchange(): lax.all_to_all(value, 'expert', split_axis=0, concat_axis=0, tiled=True)  12.6 us
    ppermute x9, starting transfers between devices, pass_down(): lax.ppermute(value, 'pipe', [(p, p - s) for p in range(s, layers)])  11.9 us
    pallas_call x1, Pallas kernels, on_device(): by_columns(slots_kernel, [columns(rows), pl.BlockSpec((rows, LANES), lamb...  10.5 us
    pallas_call x2, Pallas kernels, score(): pl.pallas_call(functools.partial(score_kernel, last), grid_spec=pltpu.Pre...  8.77 us
    unnamed x31, local copies, waits for them, and re-layouts  7.55 us
  transfers between devices with their start and end apart: 16, of which 7 were waited for; matrix products, arithmetic and copies ran while one was open for 6% of the time, Pallas kernels for 24%

profile of v4, /device:TPU:0, one launch (start us, length us, event | category | flops | bytes accessed | tf_op | source)
XLA Modules:
  0.0 173.1 jit_solution(8368889375710880832)
XLA Ops:
  0.6 1.7 %dynamic-slice_bitcast_fusion = bf16[160,640]{1,0:T(8,128)(2,1)} fusion(bf16[1,5120,160]{1,2,0:T(8,128)(2,1)} %param.10, s32[]{:T(128)S(6)} %select_n.11), kind=kLoop, calls=%fused_computation.6 | loop fusion | bytes 409604 | tf_op jit(solution)/shard_map/dynamic_slice | solution.py:444
  2.4 1.4 collective-permute-start
  3.8 1.3 collective-permute-start.1
  5.1 1.3 collective-permute-start.2
  6.4 2.1 %fusion.logits_ref = f32[128,160]{1,0:T(8,128)S(1)} fusion(bf16[1,5120,160]{1,2,0:T(8,128)(2,1)} %param.10, bf16[1,128,5120]{2,1,0:T(8,128)(2,1)S(1)} %copy-done), kind=kOutput, calls=%fused_computation.1 | convolution fusion | flops 209715200 | bytes 3031040 | tf_op jit(solution)/shard_map/dot_general | solution.py:28
  8.6 1.8 %prepare.1 = (f32[128,256]{1,0:T(8,128)S(1)}, bf16[128,5248]{1,0:T(8,128)(2,1)S(1)}, bf16[1024,1024]{1,0:T(8,128)(2,1)S(1)}) custom-call(f32[128,160]{1,0:T(8,128)S(1)} %fusion.logits_ref, s32[128,6]{1,0:T(8,128)S(1)} %bitcast.45, bf16[128,5120]{1,0:T(8,128)(2,1)S(1)} %copy-done.1), custom_call_target="tpu_custom_call" | custom-call | tf_op jit(solution)/shard_map/prepare/pallas_call | solution.py:455
  10.4 1.4 copy-done.2
  12.9 5.3 %all-to-all-start = ((bf16[8,16,5248]{2,1,0:T(8,128)(2,1)}), bf16[8,16,5248]{2,1,0:T(8,128)(2,1)S(1)}, u32[]{:S(2)}, u32[]{:S(2)}) async-start(bf16[8,16,5248]{2,1,0:T(8,128)(2,1)} %bitcast.43), calls=%async_computation | async-start | bytes 2686976 | tf_op jit(solution)/shard_map/all_to_all | solution.py:398
  21.9 6.0 %decode.2.rest_0_ = f32[8,128,640]{2,1,0:T(8,128)} custom-call(s32[2,768,640]{2,1,0:T(8,128)} %bitcast.51, bf16[2,2,8,16,128]{4,3,2,1,0:T(8,128)(2,1)} %broadcast_in_dim.16.table_ref, bf16[128,768]{1,0:T(8,128)(2,1)} %bitcast.57), custom_call_target="tpu_custom_call" | custom-call | flops 5000000000 | bytes 2000000 | tf_op jit(solution)/shard_map/decode/pallas_call | solution.py:479
  29.8 2.1 %collective-permute-start.3 = (bf16[3,160,640]{2,1,0:T(8,128)(2,1)S(1)}, bf16[3,160,640]{2,1,0:T(8,128)(2,1)}, u32[]{:S(2)}, u32[]{:S(2)}) collective-permute-start(bf16[3,160,640]{2,1,0:T(8,128)(2,1)S(1)} %pad_maximum_fusion.1), channel_id=1, source_target_pairs={{0,2},{1,3},{2,0},{3,1},{4,6},{5,7},{6,4},{7,5},{8,10},{9,11},{10,... | collective-permute-start | bytes 1843208 | tf_op jit(solution)/shard_map/ppermute | solution.py:403
  31.9 1.5 collective-permute-start.4
  33.4 23.8 %decode.3 = (f32[8,128,640]{2,1,0:T(8,128)}, bf16[128,5120]{1,0:T(8,128)(2,1)}) custom-call(s32[2,768,640]{2,1,0:T(8,128)} %bitcast.52, bf16[2,2,8,16,128]{4,3,2,1,0:T(8,128)(2,1)} %broadcast_in_dim.16.table_ref, bf16[128,768]{1,0:T(8,128)(2,1)} %bitcast.58, f32[8,128,640]{2,1,0:T(8,128)} %decode.2.rest_0_, ...), custom_call_target="tpu_custom_call", output_to_operand_aliasing={{0}: (3, {})} | custom-call | flops 24999999488 | bytes 2000000 | tf_op jit(solution)/shard_map/decode/pallas_call | solution.py:479
  57.2 6.1 %collective-permute-done.5 = bf16[3,160,640]{2,1,0:T(8,128)(2,1)} collective-permute-done((bf16[3,160,640]{2,1,0:T(8,128)(2,1)S(1)}, bf16[3,160,640]{2,1,0:T(8,128)(2,1)}, u32[]{:S(2)}, u32[]{:S(2)}) %collective-permute-start.5) | collective-permute-done | bytes 614432 | tf_op jit(solution)/shard_map/ppermute | solution.py:403
  63.3 3.3 %pad_maximum_fusion.router_ref.near_ref = bf16[4,3,160,640]{3,2,1,0:T(8,128)(2,1)} fusion(bf16[1,3,160,640]{3,2,1,0:T(8,128)(2,1)} %bitcast.20, bf16[1,3,160,640]{3,2,1,0:T(8,128)(2,1)} %bitcast.19, bf16[1,3,160,640]{3,2,1,0:T(8,128)(2,1)} %bitcast.18, bf16[1,3,160,640]{3,2,1,0:T(8,128)(2,1)S(1)} %bitcast.54), kind=kLoop, calls=%fused_computation | loop fusion | flops 3686400 | bytes 4915200 | tf_op jit(solution)/shard_map/stack | solution.py:415
  67.7 4.3 %scores.2 = (f32[480,128]{1,0:T(8,128)}, f32[128,128]{1,0:T(8,128)}) custom-call(s32[1]{0:T(128)} %bitcast.twist_ref, bf16[128,5120]{1,0:T(8,128)(2,1)} %get-tuple-element.33.out_ref, bf16[128,5248]{1,0:T(8,128)(2,1)} %bitcast.46, bf16[4,3,160,640]{3,2,1,0:T(8,128)(2,1)} %pad_maximum_fusion.router_ref.near_ref), custom_call_target="tpu_custom_call" | custom-call | tf_op jit(solution)/shard_map/scores/pallas_call | solution.py:546
  72.0 4.5 %scores.3 = bf16[128,896]{1,0:T(8,128)(2,1)} custom-call(s32[1]{0:T(128)} %bitcast.twist_ref, bf16[128,5120]{1,0:T(8,128)(2,1)} %get-tuple-element.33.out_ref, bf16[128,5248]{1,0:T(8,128)(2,1)} %bitcast.47, bf16[4,3,160,640]{3,2,1,0:T(8,128)(2,1)} %collective-permute-done.6.router_ref.far_ref, f32[480,128]{1,0:T(8,128)} %get-tuple-element.36.rest_0_, ...), custom_call_target="tpu_custom_call" | custom-call | tf_op jit(solution)/shard_map/scores/pallas_call | solution.py:546
  76.5 3.4 %all-to-all-start.1 = ((bf16[8,16,896]{2,1,0:T(8,128)(2,1)}), bf16[8,16,896]{2,1,0:T(8,128)(2,1)S(1)}, u32[]{:S(2)}, u32[]{:S(2)}) async-start(bf16[8,16,896]{2,1,0:T(8,128)(2,1)} %bitcast.56), calls=%async_computation.1 | async-start | bytes 458752 | tf_op jit(solution)/shard_map/all_to_all | solution.py:398
  79.9 1.3 collective-permute-start.7
  81.2 1.3 collective-permute-start.8
  82.5 1.5 collective-permute-start.9
  84.0 4.5 %collective-permute-done.7.rest_0_.refs_5_ = f32[128,256]{1,0:T(8,128)S(1)} collective-permute-done((f32[128,256]{1,0:T(8,128)S(1)}, f32[128,256]{1,0:T(8,128)S(1)}, u32[]{:S(2)}, u32[]{:S(2)}) %collective-permute-start.7) | collective-permute-done | bytes 131104 | tf_op jit(solution)/shard_map/ppermute | solution.py:408
  88.5 10.1 %collective-permute-done.8.rest_1_.refs_6_ = f32[128,256]{1,0:T(8,128)S(1)} collective-permute-done((f32[128,256]{1,0:T(8,128)S(1)}, f32[128,256]{1,0:T(8,128)S(1)}, u32[]{:S(2)}, u32[]{:S(2)}) %collective-permute-start.8) | collective-permute-done | bytes 131104 | tf_op jit(solution)/shard_map/ppermute | solution.py:408
  99.6 1.3 collective-permute-start.10
  100.9 1.3 collective-permute-start.11
  103.5 1.9 %collective-permute-done.10.refs_1_ = bf16[128,128]{1,0:T(8,128)(2,1)S(1)} collective-permute-done((bf16[128,128]{1,0:T(8,128)(2,1)S(1)}, bf16[128,128]{1,0:T(8,128)(2,1)S(1)}, u32[]{:S(2)}, u32[]{:S(2)}) %collective-permute-start.10) | collective-permute-done | bytes 32800 | tf_op jit(solution)/shard_map/ppermute | solution.py:408
  105.4 2.2 %collective-permute-done.11.refs_2_ = bf16[128,128]{1,0:T(8,128)(2,1)S(1)} collective-permute-done((bf16[128,128]{1,0:T(8,128)(2,1)S(1)}, bf16[128,128]{1,0:T(8,128)(2,1)S(1)}, u32[]{:S(2)}, u32[]{:S(2)}) %collective-permute-start.11) | collective-permute-done | bytes 32800 | tf_op jit(solution)/shard_map/ppermute | solution.py:408
  107.6 3.4 %collective-permute-done.12.refs_3_ = bf16[128,128]{1,0:T(8,128)(2,1)S(1)} collective-permute-done((bf16[128,128]{1,0:T(8,128)(2,1)S(1)}, bf16[128,128]{1,0:T(8,128)(2,1)S(1)}, u32[]{:S(2)}, u32[]{:S(2)}) %collective-permute-start.12) | collective-permute-done | bytes 32800 | tf_op jit(solution)/shard_map/ppermute | solution.py:408
  110.9 2.3 %chain.1 = (bf16[128,160]{1,0:T(8,128)(2,1)S(1)}, bf16[128,768]{1,0:T(8,128)(2,1)S(1)}, bf16[128,768]{1,0:T(8,128)(2,1)}) custom-call(bf16[128,128]{1,0:T(8,128)(2,1)S(1)} %responses.1.refs_0_, bf16[128,128]{1,0:T(8,128)(2,1)S(1)} %collective-permute-done.10.refs_1_, bf16[128,128]{1,0:T(8,128)(2,1)S(1)} %collective-permute-done.11.refs_2_, ...), custom_call_target="tpu_custom_call" | custom-call | tf_op jit(solution)/shard_map/chain/pallas_call | solution.py:580
  114.6 3.9 %all-to-all-start.2 = ((bf16[8,16,768]{2,1,0:T(8,128)(2,1)}), bf16[8,16,768]{2,1,0:T(8,128)(2,1)S(1)}, u32[]{:S(2)}, u32[]{:S(2)}) async-start(bf16[8,16,768]{2,1,0:T(8,128)(2,1)} %bitcast.27), calls=%async_computation.2 | async-start | bytes 393216 | tf_op jit(solution)/shard_map/all_to_all | solution.py:398
  118.4 6.0 %finish.1 = bf16[128,5120]{1,0:T(8,128)(2,1)} custom-call(s32[1]{0:T(128)} %bitcast.twist_ref, bf16[128,5120]{1,0:T(8,128)(2,1)} %grad_ref.3, bf16[128,768]{1,0:T(8,128)(2,1)} %copy-done.4, bf16[128,160]{1,0:T(8,128)(2,1)} %copy-done.5, bf16[160,5120]{1,0:T(8,128)(2,1)} %bitcast.50, bf16[4,3,160,640]{3,2,1,0:T(8,128)(2,1)} %pad_maximum_fusion.router_ref.near_ref, ...), custom_call_target="tpu_custom_call" | custom-call | tf_op jit(solution)/shard_map/finish/pallas_call | solution.py:593
  125.4 10.5 %slot_grads.1 = (bf16[8,128,640]{2,1,0:T(8,128)(2,1)}, f32[8,640]{1,0:T(8,128)}) custom-call(s32[1]{0:T(128)} %bitcast.twist_ref, bf16[128,5248]{1,0:T(8,128)(2,1)} %bitcast.48, bf16[128,5248]{1,0:T(8,128)(2,1)} %bitcast.49, bf16[128,768]{1,0:T(8,128)(2,1)} %bitcast.60, bf16[4,3,160,640]{3,2,1,0:T(8,128)(2,1)} %pad_maximum_fusion.router_ref.near_ref, ...), custom_call_target="tpu_custom_call" | custom-call | tf_op jit(solution)/shard_map/slot_grads/pallas_call | solution.py:609
  135.9 34.5 %book_grads.1 = f32[2,48,48]{2,1,0:T(8,128)} custom-call(bf16[128,768]{1,0:T(8,128)(2,1)} %bitcast.59, bf16[8,128,640]{2,1,0:T(8,128)(2,1)} %get-tuple-element.43.slots_ref, f32[8,640]{1,0:T(8,128)} %bitcast.63, s32[2,768,640]{2,1,0:T(8,128)} %bitcast.53), custom_call_target="tpu_custom_call" | custom-call | tf_op jit(solution)/shard_map/book_grads/pallas_call | solution.py:631
  (55 shorter events, 14.9 us)
Async XLA Ops:
  0.6 5.8 %copy-start = (bf16[1,128,5120]{2,1,0:T(8,128)(2,1)S(1)}, bf16[1,128,5120]{2,1,0:T(8,128)(2,1)}, u32[]{:S(2)}) copy-start(bf16[1,128,5120]{2,1,0:T(8,128)(2,1)} %param.9) | copy-start | bytes 3932164
  2.4 6.1 %copy-start.13 = (s32[1,128,6]{1,0,2:T(1,128)S(1)}, s32[1,128,6]{1,0,2:T(1,128)}, u32[]{:S(2)}) copy-start(s32[1,128,6]{1,0,2:T(1,128)} %param.11) | copy-start | bytes 9220
  2.4 6.2 %copy-start.1 = (bf16[128,5120]{1,0:T(8,128)(2,1)S(1)}, bf16[128,5120]{1,0:T(8,128)(2,1)}, u32[]{:S(2)}) copy-start(bf16[128,5120]{1,0:T(8,128)(2,1)} %grad_ref.3) | copy-start | bytes 3932164
  2.4 25.5 %collective-permute-start = (bf16[160,640]{1,0:T(8,128)(2,1)}, bf16[160,640]{1,0:T(8,128)(2,1)S(1)}, u32[]{:S(2)}, u32[]{:S(2)}) collective-permute-start(bf16[160,640]{1,0:T(8,128)(2,1)} %dynamic-slice_bitcast_fusion), channel_id=1, source_target_pairs={{8,0},{16,8},{24,16},{9,1},{17,9},{25,17},{10,2},{18,10},{26,18},{... | collective-permute-start | bytes 614408 | tf_op jit(solution)/shard_map/ppermute | solution.py:408
  3.8 24.1 %collective-permute-start.1 = (bf16[160,640]{1,0:T(8,128)(2,1)}, bf16[160,640]{1,0:T(8,128)(2,1)}, u32[]{:S(2)}, u32[]{:S(2)}) collective-permute-start(bf16[160,640]{1,0:T(8,128)(2,1)} %dynamic-slice_bitcast_fusion), channel_id=1, source_target_pairs={{16,0},{24,8},{17,1},{25,9},{18,2},{26,10},{19,3},{27,11},{20,4},{... | collective-permute-start | bytes 614408 | tf_op jit(solution)/shard_map/ppermute | solution.py:408
  5.1 22.8 %collective-permute-start.2 = (bf16[160,640]{1,0:T(8,128)(2,1)}, bf16[160,640]{1,0:T(8,128)(2,1)}, u32[]{:S(2)}, u32[]{:S(2)}) collective-permute-start(bf16[160,640]{1,0:T(8,128)(2,1)} %dynamic-slice_bitcast_fusion), channel_id=1, source_target_pairs={{24,0},{25,1},{26,2},{27,3},{28,4},{29,5},{30,6},{31,7}} | collective-permute-start | bytes 614408 | tf_op jit(solution)/shard_map/ppermute | solution.py:408
  10.4 1.4 copy-start.2
  11.8 1.1 copy-start.3
  12.9 5.3 %copy-start.9 = (bf16[1,1,72,768]{3,2,1,0:T(8,128)(2,1)S(1)}, bf16[1,1,72,768]{3,2,1,0:T(8,128)(2,1)}, u32[]{:S(2)}) copy-start(bf16[1,1,72,768]{3,2,1,0:T(8,128)(2,1)} %param.12) | copy-start | bytes 331780
  12.9 5.9 %copy-start.10 = (f32[1,1,5120]{2,1,0:T(1,128)S(1)}, f32[1,1,5120]{2,1,0:T(1,128)}, u32[]{:S(2)}) copy-start(f32[1,1,5120]{2,1,0:T(1,128)} %param.15) | copy-start | bytes 61444
  12.9 8.2 %copy-start.12 = (bf16[1,1,2,256,8]{3,4,2,1,0:T(8,128)(2,1)S(1)}, bf16[1,1,2,256,8]{3,4,2,1,0:T(8,128)(2,1)}, u32[]{:S(2)}) copy-start(bf16[1,1,2,256,8]{3,4,2,1,0:T(8,128)(2,1)} %param.14) | copy-start | bytes 24580
  12.9 53.7 %all-to-all-start = ((bf16[8,16,5248]{2,1,0:T(8,128)(2,1)}), bf16[8,16,5248]{2,1,0:T(8,128)(2,1)S(1)}, u32[]{:S(2)}, u32[]{:S(2)}) async-start(bf16[8,16,5248]{2,1,0:T(8,128)(2,1)} %bitcast.43), calls=%async_computation | async-start | bytes 2686976 | tf_op jit(solution)/shard_map/all_to_all | solution.py:398
  27.9 0.7 copy-start.8
  29.8 27.4 %collective-permute-start.3 = (bf16[3,160,640]{2,1,0:T(8,128)(2,1)S(1)}, bf16[3,160,640]{2,1,0:T(8,128)(2,1)}, u32[]{:S(2)}, u32[]{:S(2)}) collective-permute-start(bf16[3,160,640]{2,1,0:T(8,128)(2,1)S(1)} %pad_maximum_fusion.1), channel_id=1, source_target_pairs={{0,2},{1,3},{2,0},{3,1},{4,6},{5,7},{6,4},{7,5},{8,10},{9,11},{10,... | collective-permute-start | bytes 1843208 | tf_op jit(solution)/shard_map/ppermute | solution.py:403
  31.9 25.3 %collective-permute-start.4 = (bf16[3,160,640]{2,1,0:T(8,128)(2,1)S(1)}, bf16[3,160,640]{2,1,0:T(8,128)(2,1)}, u32[]{:S(2)}, u32[]{:S(2)}) collective-permute-start(bf16[3,160,640]{2,1,0:T(8,128)(2,1)S(1)} %pad_maximum_fusion.1), channel_id=1, source_target_pairs={{0,4},{1,5},{2,6},{3,7},{4,0},{5,1},{6,2},{7,3},{8,12},{9,13},{10,... | collective-permute-start | bytes 1843208 | tf_op jit(solution)/shard_map/ppermute | solution.py:403
  33.3 30.0 %collective-permute-start.5 = (bf16[3,160,640]{2,1,0:T(8,128)(2,1)S(1)}, bf16[3,160,640]{2,1,0:T(8,128)(2,1)}, u32[]{:S(2)}, u32[]{:S(2)}) collective-permute-start(bf16[3,160,640]{2,1,0:T(8,128)(2,1)S(1)} %pad_maximum_fusion.1), channel_id=1, source_target_pairs={{0,6},{1,7},{2,4},{3,5},{4,2},{5,3},{6,0},{7,1},{8,14},{9,15},{10,... | collective-permute-start | bytes 1843208 | tf_op jit(solution)/shard_map/ppermute | solution.py:403
  66.6 1.1 copy-start.6
  66.6 5.3 %collective-permute-start.6 = (bf16[4,3,160,640]{3,2,1,0:T(8,128)(2,1)}, bf16[4,3,160,640]{3,2,1,0:T(8,128)(2,1)}, u32[]{:S(2)}, u32[]{:S(2)}) collective-permute-start(bf16[4,3,160,640]{3,2,1,0:T(8,128)(2,1)} %pad_maximum_fusion.router_ref.near_ref), channel_id=1, source_target_pairs={{0,1},{1,0},{2,3},{3,2},{4,5},{5,4},{6,7},{7,6},{8,9},{9,8},{10,11... | collective-permute-start | bytes 7372808 | tf_op jit(solution)/shard_map/ppermute | solution.py:403
  76.5 22.2 %all-to-all-start.1 = ((bf16[8,16,896]{2,1,0:T(8,128)(2,1)}), bf16[8,16,896]{2,1,0:T(8,128)(2,1)S(1)}, u32[]{:S(2)}, u32[]{:S(2)}) async-start(bf16[8,16,896]{2,1,0:T(8,128)(2,1)} %bitcast.56), calls=%async_computation.1 | async-start | bytes 458752 | tf_op jit(solution)/shard_map/all_to_all | solution.py:398
  79.9 8.6 %collective-permute-start.7 = (f32[128,256]{1,0:T(8,128)S(1)}, f32[128,256]{1,0:T(8,128)S(1)}, u32[]{:S(2)}, u32[]{:S(2)}) collective-permute-start(f32[128,256]{1,0:T(8,128)S(1)} %get-tuple-element.38.state_ref.refs_4_), channel_id=1, source_target_pairs={{8,0},{16,8},{24,16},{9,1},{17,9},{25,17},{10,2},{18,10},{26,18},{... | collective-permute-start | bytes 393224 | tf_op jit(solution)/shard_map/ppermute | solution.py:408
  81.2 17.4 %collective-permute-start.8 = (f32[128,256]{1,0:T(8,128)S(1)}, f32[128,256]{1,0:T(8,128)S(1)}, u32[]{:S(2)}, u32[]{:S(2)}) collective-permute-start(f32[128,256]{1,0:T(8,128)S(1)} %get-tuple-element.38.state_ref.refs_4_), channel_id=1, source_target_pairs={{16,0},{24,8},{17,1},{25,9},{18,2},{26,10},{19,3},{27,11},{20,4},{... | collective-permute-start | bytes 393224 | tf_op jit(solution)/shard_map/ppermute | solution.py:408
  82.5 16.2 %collective-permute-start.9 = (f32[128,256]{1,0:T(8,128)S(1)}, f32[128,256]{1,0:T(8,128)S(1)}, u32[]{:S(2)}, u32[]{:S(2)}) collective-permute-start(f32[128,256]{1,0:T(8,128)S(1)} %get-tuple-element.38.state_ref.refs_4_), channel_id=1, source_target_pairs={{24,0},{25,1},{26,2},{27,3},{28,4},{29,5},{30,6},{31,7}} | collective-permute-start | bytes 393224 | tf_op jit(solution)/shard_map/ppermute | solution.py:408
  99.6 5.8 %collective-permute-start.10 = (bf16[128,128]{1,0:T(8,128)(2,1)S(1)}, bf16[128,128]{1,0:T(8,128)(2,1)S(1)}, u32[]{:S(2)}, u32[]{:S(2)}) collective-permute-start(bf16[128,128]{1,0:T(8,128)(2,1)S(1)} %responses.1.refs_0_), channel_id=1, source_target_pairs={{8,0},{16,8},{24,16},{9,1},{17,9},{25,17},{10,2},{18,10},{26,18},{... | collective-permute-start | bytes 98312 | tf_op jit(solution)/shard_map/ppermute | solution.py:408
  100.9 6.7 %collective-permute-start.11 = (bf16[128,128]{1,0:T(8,128)(2,1)S(1)}, bf16[128,128]{1,0:T(8,128)(2,1)S(1)}, u32[]{:S(2)}, u32[]{:S(2)}) collective-permute-start(bf16[128,128]{1,0:T(8,128)(2,1)S(1)} %responses.1.refs_0_), channel_id=1, source_target_pairs={{16,0},{24,8},{17,1},{25,9},{18,2},{26,10},{19,3},{27,11},{20,4},{... | collective-permute-start | bytes 98312 | tf_op jit(solution)/shard_map/ppermute | solution.py:408
  102.2 8.8 %collective-permute-start.12 = (bf16[128,128]{1,0:T(8,128)(2,1)S(1)}, bf16[128,128]{1,0:T(8,128)(2,1)S(1)}, u32[]{:S(2)}, u32[]{:S(2)}) collective-permute-start(bf16[128,128]{1,0:T(8,128)(2,1)S(1)} %responses.1.refs_0_), channel_id=1, source_target_pairs={{24,0},{25,1},{26,2},{27,3},{28,4},{29,5},{30,6},{31,7}} | collective-permute-start | bytes 98312 | tf_op jit(solution)/shard_map/ppermute | solution.py:408
  113.3 0.7 copy-start.4
  113.9 0.6 copy-start.5
  114.6 10.1 %all-to-all-start.2 = ((bf16[8,16,768]{2,1,0:T(8,128)(2,1)}), bf16[8,16,768]{2,1,0:T(8,128)(2,1)S(1)}, u32[]{:S(2)}, u32[]{:S(2)}) async-start(bf16[8,16,768]{2,1,0:T(8,128)(2,1)} %bitcast.27), calls=%async_computation.2 | async-start | bytes 393216 | tf_op jit(solution)/shard_map/all_to_all | solution.py:398
  124.7 0.7 copy-start.7
  135.9 36.2 %copy-start.11 = (f32[8,640]{1,0:T(8,128)S(1)}, f32[8,640]{1,0:T(8,128)}, u32[]{:S(2)}) copy-start(f32[8,640]{1,0:T(8,128)} %get-tuple-element.44) | copy-start | bytes 61444

commit v5 on v4

--- a/solution.py
+++ b/solution.py
@@ -149,15 +149,15 @@
 
     @pl.when(step == pl.num_programs(0) - 1)
     def _():
+        rows = plain_out_ref.shape[1]
+        split = [
+            jnp.concatenate([plain_out_ref[i, :, at] * scale_ref[i : i + 1, at] for i in range(size)], 1)
+            for at in (slice(c * LANES, (c + 1) * LANES) for c in range(groups // LANES))
+        ]
+        back = dot(jnp.concatenate(split, 0).astype(BF16), order_ref[...]).astype(BF16)
         span = size * LANES
         for chunk in range(groups // LANES):
-            lanes = slice(chunk * LANES, (chunk + 1) * LANES)
-            split = jnp.concatenate(
-                [plain_out_ref[i, :, lanes] * scale_ref[i : i + 1, lanes] for i in range(size)], 1
-            ).astype(BF16)
-            out_ref[:, chunk * span : (chunk + 1) * span] = dot(
-                split, order_ref[...]
-            ).astype(BF16)
+            out_ref[:, chunk * span : (chunk + 1) * span] = back[chunk * rows : (chunk + 1) * rows]
 
 
 def score_kernel(last, twist_ref, out_ref, slots_ref, router_ref, *rest):
@@ -318,11 +318,14 @@
 
     @pl.when(i == pl.num_programs(0) - 1)
     def _():
-        for chunk in range(groups // LANES):
-            lanes = slice(chunk * LANES, (chunk + 1) * LANES)
-            split = dot_nt(grad_ref[:, chunk * span : (chunk + 1) * span], order_ref[...])
+        rows = grad_ref.shape[0]
+        chunks = groups // LANES
+        grad = [grad_ref[:, c * span : (c + 1) * span] for c in range(chunks)]
+        split = dot_nt(jnp.concatenate(grad, 0), order_ref[...])
+        for c in range(chunks):
+            lanes = slice(c * LANES, (c + 1) * LANES)
             for i in range(size):
-                part = split[:, i * LANES : (i + 1) * LANES]
+                part = split[c * rows : (c + 1) * rows, i * LANES : (i + 1) * LANES]
                 split_ref[i, :, lanes] = part.astype(BF16)
                 scale_grad_ref[i : i + 1, lanes] = jnp.sum(
                     part * plain_out_ref[i, :, lanes], axis=0, keepdims=True
@@ -410,6 +413,39 @@
     ]
 
 
+def join_kernel(count, *refs):
+    *part_refs, out_ref, sems = refs
+    copies = [
+        pltpu.make_async_copy(ref, out_ref.at[k], sems.at[k])
+        for k, ref in enumerate(part_refs[:count])
+    ]
+    first = 0
+    for k in range(count, len(part_refs)):
+        last = first + part_refs[k].shape[1]
+        copies.append(
+            pltpu.make_async_copy(part_refs[k], out_ref.at[count, :, first:last], sems.at[k])
+        )
+        first = last
+    for copy in copies:
+        copy.start()
+    for copy in copies:
+        copy.wait()
+
+
+def join(wholes, pieces):
+    parts = wholes + pieces
+    anywhere = pl.BlockSpec(memory_space=pl.ANY)
+    return pl.pallas_call(
+        functools.partial(join_kernel, len(wholes)),
+        in_specs=[anywhere] * len(parts),
+        out_specs=anywhere,
+        out_shape=jax.ShapeDtypeStruct((len(wholes) + 1,) + wholes[0].shape, wholes[0].dtype),
+        scratch_shapes=[pltpu.SemaphoreType.DMA((len(parts),))],
+        compiler_params=params(60),
+        name="join",
+    )(*parts)
+
+
 def gather_exchange(shares):
     count = lax.axis_size("expert")
     return jnp.stack([shares] + [swap(shares, d) for d in range(2, count, 2)])
@@ -459,7 +495,7 @@
             jax.ShapeDtypeStruct((rows, width + LANES), BF16),
             jax.ShapeDtypeStruct((span, span), BF16),
         ),
-        compiler_params=params(20 + 6 * grow),
+        compiler_params=params(60),
         name="prepare",
     )(logits, routes[0], out_grad)
     slots = exchange(outgoing)
@@ -501,12 +537,26 @@
     early = max(1, blocks // 6)
     (plain_out,) = decode(0, early, None)
     plain_out, shares, later_state = lax.optimization_barrier((plain_out, shares, state))
-    near = gather_exchange(shares) if direct else None
+    middle = early
+    near = None
+    if direct and experts == 8:
+        half = routed // 2
+        beside, above = swap(shares, 2), swap(shares, 4)
+        middle = blocks // 2
+        (plain_out,) = decode(early, middle - early, plain_out)
+        plain_out, beside, above, later_state = lax.optimization_barrier(
+            (plain_out, beside, above, later_state)
+        )
+        upper, lower = swap(beside[:, :half], 4), swap(above[:, half:], 2)
+    elif direct:
+        near = gather_exchange(shares)
     states = [state] + pass_down(later_state, layers)
-    plain_out, expert_out = decode(early, blocks - early, plain_out)
+    plain_out, expert_out = decode(middle, blocks - middle, plain_out)
     if direct:
-        plain_out, expert_out, near, slots = lax.optimization_barrier(
-            (plain_out, expert_out, near, slots)
+        if near is None:
+            near = join([shares, beside, above], [upper, lower])
+        plain_out, expert_out, near, slots, states = lax.optimization_barrier(
+            (plain_out, expert_out, near, slots, states)
         )
         far = swap(near, 1)
     else:

time: 174 us -> 247 us (1.42)
  Pallas kernels: 94.7 us -> 175 us
  waiting for transfers between devices: 28.5 us -> 11.8 us
  blocking collectives: 0 us -> 9.92 us
  local copies, waits for them, and re-layouts: 13.6 us -> 16.5 us
  other arithmetic: 5.22 us -> 2.62 us
    pallas_call x0 -> x1, Pallas kernels: none -> 75.6 us  [join(): pl.pallas_call(functools.partial(join_kernel, len(wholes)), in_specs=[any...]
    ppermute x9, waiting for transfers between devices: 22.2 us -> 6.59 us  [pass_down(): lax.ppermute(value, 'pipe', [(p, p - s) for p in range(s, layers)])]
    all_to_all x0 -> x1, blocking collectives: none -> 9.92 us  [exchange(): lax.all_to_all(value, 'expert', split_axis=0, concat_axis=0, tiled=True)]
    pallas_call x2 -> x3, Pallas kernels: 29.8 us -> 34.1 us  [decode(): pl.pallas_call(functools.partial(decode_kernel, first, last), grid=(count...]
    all_to_all x3 -> x2, starting transfers between devices: 12.6 us -> 8.92 us  [exchange(): lax.all_to_all(value, 'expert', split_axis=0, concat_axis=0, tiled=True)]
    slice x0 -> x2, local copies, waits for them, and re-layouts: none -> 3.42 us  [on_device(): upper, lower = (swap(beside[:, :half], 4), swap(above[:, half:], 2))]
    another operation x1 -> x0, other arithmetic: 3.32 us -> none  [gather_exchange(): return jnp.stack([shares] + [swap(shares, d) for d in range(2, count, 2)])]
    pallas_call x1, Pallas kernels: 1.79 us -> 4.59 us  [on_device(): pl.pallas_call(prepare_kernel, out_shape=(jax.ShapeDtypeStruct((tokens, s...]
  transfers between devices with their start and end apart: 16 -> 16, of which waited for: 7 -> 2; matrix products, arithmetic and copies ran while one was open for 6% -> 5% of each run, Pallas kernels for 24% -> 51%
where the time goes in v5:
time: 247 us; the launch traced here: 246 us
  Pallas kernels  175 us (71%)
  starting transfers between devices  25.7 us (10%)
  local copies, waits for them, and re-layouts  16.5 us (7%)
  waiting for transfers between devices  11.8 us (5%)
  blocking collectives  9.92 us (4%)
  matrix products  2.73 us (1%)
  other arithmetic  2.62 us (1%)
    pallas_call x1, Pallas kernels, join(): pl.pallas_call(functools.partial(join_kernel, len(wholes)), in_specs=[any...  75.6 us
    pallas_call x1, Pallas kernels, on_device(): pl.pallas_call(functools.partial(book_kernel, unroll), grid=(inner // blo...  34.6 us
    pallas_call x3, Pallas kernels, decode(): pl.pallas_call(functools.partial(decode_kernel, first, last), grid=(count...  34.1 us
    ppermute x9, starting transfers between devices, pass_down(): lax.ppermute(value, 'pipe', [(p, p - s) for p in range(s, layers)])  11.8 us
    all_to_all x1, blocking collectives, exchange(): lax.all_to_all(value, 'expert', split_axis=0, concat_axis=0, tiled=True)  9.92 us
    all_to_all x2, starting transfers between devices, exchange(): lax.all_to_all(value, 'expert', split_axis=0, concat_axis=0, tiled=True)  8.92 us
    pallas_call x2, Pallas kernels, score(): pl.pallas_call(functools.partial(score_kernel, last), grid_spec=pltpu.Pre...  8.76 us
    pallas_call x1, Pallas kernels, on_device(): by_columns(slots_kernel, [columns(rows), pl.BlockSpec((rows, LANES), lamb...  8.64 us
  transfers between devices with their start and end apart: 16, of which 2 were waited for; matrix products, arithmetic and copies ran while one was open for 5% of the time, Pallas kernels for 51%

profile of v5, /device:TPU:0, one launch (start us, length us, event | category | flops | bytes accessed | tf_op | source)
XLA Modules:
  0.0 245.6 jit_solution(12831988491008444390)
XLA Ops:
  0.6 1.7 dynamic-slice_bitcast_fusion
  3.7 1.3 collective-permute-start.1
  5.0 1.3 collective-permute-start
  6.3 1.4 copy.16
  7.7 2.7 %fusion.logits_ref = f32[128,160]{1,0:T(8,128)} fusion(bf16[1,5120,160]{1,2,0:T(8,128)(2,1)} %param.10, bf16[1,128,5120]{2,1,0:T(8,128)(2,1)S(1)} %copy-done), kind=kOutput, calls=%fused_computation | convolution fusion | flops 209715200 | bytes 3031040 | tf_op jit(solution)/shard_map/dot_general | solution.py:28
  10.4 4.6 %prepare.1 = (f32[128,256]{1,0:T(8,128)}, bf16[128,5248]{1,0:T(8,128)(2,1)}, bf16[1024,1024]{1,0:T(8,128)(2,1)}) custom-call(f32[128,160]{1,0:T(8,128)} %fusion.logits_ref, s32[128,6]{1,0:T(8,128)} %bitcast.57, bf16[128,5120]{1,0:T(8,128)(2,1)} %grad_ref.3), custom_call_target="tpu_custom_call" | custom-call | tf_op jit(solution)/shard_map/prepare/pallas_call | solution.py:491
  15.0 5.3 %all-to-all-start = ((bf16[8,16,5248]{2,1,0:T(8,128)(2,1)}), bf16[8,16,5248]{2,1,0:T(8,128)(2,1)S(1)}, u32[]{:S(2)}, u32[]{:S(2)}) async-start(bf16[8,16,5248]{2,1,0:T(8,128)(2,1)} %bitcast.49), calls=%async_computation | async-start | bytes 2686976 | tf_op jit(solution)/shard_map/all_to_all | solution.py:401
  23.9 6.0 %decode.3.rest_0_ = f32[8,128,640]{2,1,0:T(8,128)} custom-call(s32[2,768,640]{2,1,0:T(8,128)} %bitcast.45, bf16[2,2,8,16,128]{4,3,2,1,0:T(8,128)(2,1)} %broadcast_in_dim.16.table_ref, bf16[128,768]{1,0:T(8,128)(2,1)} %bitcast.52), custom_call_target="tpu_custom_call" | custom-call | flops 5000000000 | bytes 2000000 | tf_op jit(solution)/shard_map/decode/pallas_call | solution.py:515
  30.0 1.9 pad_maximum_fusion.refs_0_
  31.9 2.0 collective-permute-start.4
  33.9 1.5 collective-permute-start.3
  35.4 11.3 %decode.4.rest_0_ = f32[8,128,640]{2,1,0:T(8,128)} custom-call(s32[2,768,640]{2,1,0:T(8,128)} %bitcast.46, bf16[2,2,8,16,128]{4,3,2,1,0:T(8,128)(2,1)} %broadcast_in_dim.16.table_ref, bf16[128,768]{1,0:T(8,128)(2,1)} %bitcast.53, f32[8,128,640]{2,1,0:T(8,128)} %decode.3.rest_0_, f32[8,640]{1,0:T(8,128)} %bitcast.59, ...), custom_call_target="tpu_custom_call", output_to_operand_aliasing={{}: (3, {})} | custom-call | flops 10000000000 | bytes 2000000 | tf_op jit(solution)/shard_map/decode/pallas_call | solution.py:515
  46.7 5.2 %collective-permute-done.4.refs_2_ = bf16[3,160,640]{2,1,0:T(8,128)(2,1)} collective-permute-done((bf16[3,160,640]{2,1,0:T(8,128)(2,1)}, bf16[3,160,640]{2,1,0:T(8,128)(2,1)}, u32[]{:S(2)}, u32[]{:S(2)}) %collective-permute-start.4) | collective-permute-done | bytes 614432 | tf_op jit(solution)/shard_map/ppermute | solution.py:406
  51.9 1.3 collective-permute-start.9
  53.2 1.3 collective-permute-start.8
  54.5 1.5 collective-permute-start.7
  56.0 1.7 slice.9
  57.7 1.7 slice.10
  60.8 16.7 %decode.5 = (f32[8,128,640]{2,1,0:T(8,128)}, bf16[128,5120]{1,0:T(8,128)(2,1)}) custom-call(s32[2,768,640]{2,1,0:T(8,128)} %bitcast.47, bf16[2,2,8,16,128]{4,3,2,1,0:T(8,128)(2,1)} %broadcast_in_dim.16.table_ref, bf16[128,768]{1,0:T(8,128)(2,1)} %bitcast.54, f32[8,128,640]{2,1,0:T(8,128)} %decode.4.rest_0_, ...), custom_call_target="tpu_custom_call", output_to_operand_aliasing={{0}: (3, {})} | custom-call | flops 15000000512 | bytes 2000000 | tf_op jit(solution)/shard_map/decode/pallas_call | solution.py:515
  79.0 75.6 %join.1.router_ref.near_ref = bf16[4,3,160,640]{3,2,1,0:T(8,128)(2,1)} custom-call(bf16[3,160,640]{2,1,0:T(8,128)(2,1)} %pad_maximum_fusion.refs_0_, bf16[3,160,640]{2,1,0:T(8,128)(2,1)} %collective-permute-done.3.refs_1_, bf16[3,160,640]{2,1,0:T(8,128)(2,1)} %collective-permute-done.4.refs_2_, bf16[3,80,640]{2,1,0:T(8,128)(2,1)} %copy-done.7, ...), custom_call_target="tpu_custom_call" | custom-call | tf_op jit(solution)/shard_map/join/pallas_call | solution.py:438
  155.7 4.3 %scores.2 = (f32[480,128]{1,0:T(8,128)}, f32[128,128]{1,0:T(8,128)}) custom-call(s32[1]{0:T(128)} %bitcast.twist_ref, bf16[128,5120]{1,0:T(8,128)(2,1)} %get-tuple-element.46.out_ref, bf16[128,5248]{1,0:T(8,128)(2,1)} %bitcast.40, bf16[4,3,160,640]{3,2,1,0:T(8,128)(2,1)} %join.1.router_ref.near_ref), custom_call_target="tpu_custom_call" | custom-call | tf_op jit(solution)/shard_map/scores/pallas_call | solution.py:596
  160.0 4.5 %scores.3 = bf16[128,896]{1,0:T(8,128)(2,1)} custom-call(s32[1]{0:T(128)} %bitcast.twist_ref, bf16[128,5120]{1,0:T(8,128)(2,1)} %get-tuple-element.46.out_ref, bf16[128,5248]{1,0:T(8,128)(2,1)} %bitcast.41, bf16[4,3,160,640]{3,2,1,0:T(8,128)(2,1)} %collective-permute-done.10.router_ref.far_ref, f32[480,128]{1,0:T(8,128)} %get-tuple-element.49.rest_0_, ...), custom_call_target="tpu_custom_call" | custom-call | tf_op jit(solution)/shard_map/scores/pallas_call | solution.py:596
  164.5 9.9 %all_to_all.34 = bf16[8,16,896]{2,1,0:T(8,128)(2,1)S(1)} all-to-all(bf16[8,16,896]{2,1,0:T(8,128)(2,1)} %bitcast.51), channel_id=1, replica_groups=mesh['pipe'=4,'expert'=8] {'expert'}, dimensions={0} | all-to-all | bytes 458752 | tf_op jit(solution)/shard_map/all_to_all | solution.py:401
  175.3 1.3 collective-permute-start.13
  176.6 1.3 collective-permute-start.12
  177.9 1.3 collective-permute-start.11
  179.2 6.6 %collective-permute-done.13.refs_3_ = bf16[128,128]{1,0:T(8,128)(2,1)S(1)} collective-permute-done((bf16[128,128]{1,0:T(8,128)(2,1)S(1)}, bf16[128,128]{1,0:T(8,128)(2,1)S(1)}, u32[]{:S(2)}, u32[]{:S(2)}) %collective-permute-start.13) | collective-permute-done | bytes 32800 | tf_op jit(solution)/shard_map/ppermute | solution.py:411
  185.8 2.3 chain.1
  189.4 3.6 %all-to-all-start.2 = ((bf16[8,16,768]{2,1,0:T(8,128)(2,1)}), bf16[8,16,768]{2,1,0:T(8,128)(2,1)S(1)}, u32[]{:S(2)}, u32[]{:S(2)}) async-start(bf16[8,16,768]{2,1,0:T(8,128)(2,1)} %bitcast.23), calls=%async_computation.2 | async-start | bytes 393216 | tf_op jit(solution)/shard_map/all_to_all | solution.py:401
  193.1 6.0 %finish.1 = bf16[128,5120]{1,0:T(8,128)(2,1)} custom-call(s32[1]{0:T(128)} %bitcast.twist_ref, bf16[128,5120]{1,0:T(8,128)(2,1)} %grad_ref.3, bf16[128,768]{1,0:T(8,128)(2,1)} %copy-done.2, bf16[128,160]{1,0:T(8,128)(2,1)} %copy-done.3, bf16[160,5120]{1,0:T(8,128)(2,1)} %bitcast.44, bf16[4,3,160,640]{3,2,1,0:T(8,128)(2,1)} %join.1.router_ref.near_ref, ...), custom_call_target="tpu_custom_call" | custom-call | tf_op jit(solution)/shard_map/finish/pallas_call | solution.py:643
  199.8 8.6 %slot_grads.1 = (bf16[8,128,640]{2,1,0:T(8,128)(2,1)}, f32[8,640]{1,0:T(8,128)}) custom-call(s32[1]{0:T(128)} %bitcast.twist_ref, bf16[128,5248]{1,0:T(8,128)(2,1)} %bitcast.42, bf16[128,5248]{1,0:T(8,128)(2,1)} %bitcast.43, bf16[128,768]{1,0:T(8,128)(2,1)} %bitcast.56, bf16[4,3,160,640]{3,2,1,0:T(8,128)(2,1)} %join.1.router_ref.near_ref, ...), custom_call_target="tpu_custom_call" | custom-call | tf_op jit(solution)/shard_map/slot_grads/pallas_call | solution.py:659
  208.4 34.6 %book_grads.1 = f32[2,48,48]{2,1,0:T(8,128)} custom-call(bf16[128,768]{1,0:T(8,128)(2,1)} %bitcast.55, bf16[8,128,640]{2,1,0:T(8,128)(2,1)} %get-tuple-element.59.slots_ref, f32[8,640]{1,0:T(8,128)} %bitcast.61, s32[2,768,640]{2,1,0:T(8,128)} %bitcast.48), custom_call_target="tpu_custom_call" | custom-call | tf_op jit(solution)/shard_map/book_grads/pallas_call | solution.py:681
  (55 shorter events, 14.4 us)
Async XLA Ops:
  0.6 7.1 %copy-start = (bf16[1,128,5120]{2,1,0:T(8,128)(2,1)S(1)}, bf16[1,128,5120]{2,1,0:T(8,128)(2,1)}, u32[]{:S(2)}) copy-start(bf16[1,128,5120]{2,1,0:T(8,128)(2,1)} %param.9) | copy-start | bytes 3932164
  2.4 27.6 %collective-permute-start.2 = (bf16[160,640]{1,0:T(8,128)(2,1)}, bf16[160,640]{1,0:T(8,128)(2,1)S(1)}, u32[]{:S(2)}, u32[]{:S(2)}) collective-permute-start(bf16[160,640]{1,0:T(8,128)(2,1)} %dynamic-slice_bitcast_fusion), channel_id=1, source_target_pairs={{24,0},{25,1},{26,2},{27,3},{28,4},{29,5},{30,6},{31,7}} | collective-permute-start | bytes 614408 | tf_op jit(solution)/shard_map/ppermute | solution.py:411
  3.7 26.3 %collective-permute-start.1 = (bf16[160,640]{1,0:T(8,128)(2,1)}, bf16[160,640]{1,0:T(8,128)(2,1)}, u32[]{:S(2)}, u32[]{:S(2)}) collective-permute-start(bf16[160,640]{1,0:T(8,128)(2,1)} %dynamic-slice_bitcast_fusion), channel_id=1, source_target_pairs={{16,0},{24,8},{17,1},{25,9},{18,2},{26,10},{19,3},{27,11},{20,4},{... | collective-permute-start | bytes 614408 | tf_op jit(solution)/shard_map/ppermute | solution.py:411
  5.0 25.0 %collective-permute-start = (bf16[160,640]{1,0:T(8,128)(2,1)}, bf16[160,640]{1,0:T(8,128)(2,1)}, u32[]{:S(2)}, u32[]{:S(2)}) collective-permute-start(bf16[160,640]{1,0:T(8,128)(2,1)} %dynamic-slice_bitcast_fusion), channel_id=1, source_target_pairs={{8,0},{16,8},{24,16},{9,1},{17,9},{25,17},{10,2},{18,10},{26,18},{... | collective-permute-start | bytes 614408 | tf_op jit(solution)/shard_map/ppermute | solution.py:411
  15.0 5.3 %copy-start.8 = (bf16[1,1,72,768]{3,2,1,0:T(8,128)(2,1)S(1)}, bf16[1,1,72,768]{3,2,1,0:T(8,128)(2,1)}, u32[]{:S(2)}) copy-start(bf16[1,1,72,768]{3,2,1,0:T(8,128)(2,1)} %param.12) | copy-start | bytes 331780
  15.0 5.9 %copy-start.9 = (f32[1,1,5120]{2,1,0:T(1,128)S(1)}, f32[1,1,5120]{2,1,0:T(1,128)}, u32[]{:S(2)}) copy-start(f32[1,1,5120]{2,1,0:T(1,128)} %param.15) | copy-start | bytes 61444
  15.0 8.2 %copy-start.11 = (bf16[1,1,2,256,8]{3,4,2,1,0:T(8,128)(2,1)S(1)}, bf16[1,1,2,256,8]{3,4,2,1,0:T(8,128)(2,1)}, u32[]{:S(2)}) copy-start(bf16[1,1,2,256,8]{3,4,2,1,0:T(8,128)(2,1)} %param.14) | copy-start | bytes 24580
  15.0 139.6 %all-to-all-start = ((bf16[8,16,5248]{2,1,0:T(8,128)(2,1)}), bf16[8,16,5248]{2,1,0:T(8,128)(2,1)S(1)}, u32[]{:S(2)}, u32[]{:S(2)}) async-start(bf16[8,16,5248]{2,1,0:T(8,128)(2,1)} %bitcast.49), calls=%async_computation | async-start | bytes 2686976 | tf_op jit(solution)/shard_map/all_to_all | solution.py:401
  31.9 20.0 %collective-permute-start.4 = (bf16[3,160,640]{2,1,0:T(8,128)(2,1)}, bf16[3,160,640]{2,1,0:T(8,128)(2,1)}, u32[]{:S(2)}, u32[]{:S(2)}) collective-permute-start(bf16[3,160,640]{2,1,0:T(8,128)(2,1)} %pad_maximum_fusion.refs_0_), channel_id=1, source_target_pairs={{0,4},{1,5},{2,6},{3,7},{4,0},{5,1},{6,2},{7,3},{8,12},{9,13},{10,... | collective-permute-start | bytes 1843208 | tf_op jit(solution)/shard_map/ppermute | solution.py:406
  33.9 18.0 %collective-permute-start.3 = (bf16[3,160,640]{2,1,0:T(8,128)(2,1)}, bf16[3,160,640]{2,1,0:T(8,128)(2,1)}, u32[]{:S(2)}, u32[]{:S(2)}) collective-permute-start(bf16[3,160,640]{2,1,0:T(8,128)(2,1)} %pad_maximum_fusion.refs_0_), channel_id=1, source_target_pairs={{0,2},{1,3},{2,0},{3,1},{4,6},{5,7},{6,4},{7,5},{8,10},{9,11},{10,... | collective-permute-start | bytes 1843208 | tf_op jit(solution)/shard_map/ppermute | solution.py:406
  35.4 16.5 %copy-start.1 = (f32[128,256]{1,0:T(8,128)S(1)}, f32[128,256]{1,0:T(8,128)}, u32[]{:S(2)}) copy-start(f32[128,256]{1,0:T(8,128)} %get-tuple-element.51.state_ref.refs_4_) | copy-start | bytes 393220
  51.9 102.7 %collective-permute-start.9 = (f32[128,256]{1,0:T(8,128)S(1)}, f32[128,256]{1,0:T(8,128)S(1)}, u32[]{:S(2)}, u32[]{:S(2)}) collective-permute-start(f32[128,256]{1,0:T(8,128)S(1)} %copy-done.1), channel_id=1, source_target_pairs={{24,0},{25,1},{26,2},{27,3},{28,4},{29,5},{30,6},{31,7}} | collective-permute-start | bytes 393224 | tf_op jit(solution)/shard_map/ppermute | solution.py:411
  53.2 101.4 %collective-permute-start.8 = (f32[128,256]{1,0:T(8,128)S(1)}, f32[128,256]{1,0:T(8,128)S(1)}, u32[]{:S(2)}, u32[]{:S(2)}) collective-permute-start(f32[128,256]{1,0:T(8,128)S(1)} %copy-done.1), channel_id=1, source_target_pairs={{16,0},{24,8},{17,1},{25,9},{18,2},{26,10},{19,3},{27,11},{20,4},{... | collective-permute-start | bytes 393224 | tf_op jit(solution)/shard_map/ppermute | solution.py:411
  54.5 100.1 %collective-permute-start.7 = (f32[128,256]{1,0:T(8,128)S(1)}, f32[128,256]{1,0:T(8,128)S(1)}, u32[]{:S(2)}, u32[]{:S(2)}) collective-permute-start(f32[128,256]{1,0:T(8,128)S(1)} %copy-done.1), channel_id=1, source_target_pairs={{8,0},{16,8},{24,16},{9,1},{17,9},{25,17},{10,2},{18,10},{26,18},{... | collective-permute-start | bytes 393224 | tf_op jit(solution)/shard_map/ppermute | solution.py:411
  59.4 18.2 %collective-permute-start.6 = (bf16[3,80,640]{2,1,0:T(8,128)(2,1)}, bf16[3,80,640]{2,1,0:T(8,128)(2,1)S(1)}, u32[]{:S(2)}, u32[]{:S(2)}) collective-permute-start(bf16[3,80,640]{2,1,0:T(8,128)(2,1)} %slice.10), channel_id=1, source_target_pairs={{0,2},{1,3},{2,0},{3,1},{4,6},{5,7},{6,4},{7,5},{8,10},{9,11},{10,... | collective-permute-start | bytes 921608 | tf_op jit(solution)/shard_map/ppermute | solution.py:406
  60.2 17.4 %collective-permute-start.5 = (bf16[3,80,640]{2,1,0:T(8,128)(2,1)}, bf16[3,80,640]{2,1,0:T(8,128)(2,1)S(1)}, u32[]{:S(2)}, u32[]{:S(2)}) collective-permute-start(bf16[3,80,640]{2,1,0:T(8,128)(2,1)} %slice.9), channel_id=1, source_target_pairs={{0,4},{1,5},{2,6},{3,7},{4,0},{5,1},{6,2},{7,3},{8,12},{9,13},{10,... | collective-permute-start | bytes 921608 | tf_op jit(solution)/shard_map/ppermute | solution.py:406
  77.6 0.7 copy-start.6
  78.3 0.7 copy-start.7
  154.6 1.1 copy-start.4
  154.6 5.3 %collective-permute-start.10 = (bf16[4,3,160,640]{3,2,1,0:T(8,128)(2,1)}, bf16[4,3,160,640]{3,2,1,0:T(8,128)(2,1)}, u32[]{:S(2)}, u32[]{:S(2)}) collective-permute-start(bf16[4,3,160,640]{3,2,1,0:T(8,128)(2,1)} %join.1.router_ref.near_ref), channel_id=1, source_target_pairs={{0,1},{1,0},{2,3},{3,2},{4,5},{5,4},{6,7},{7,6},{8,9},{9,8},{10,11... | collective-permute-start | bytes 7372808 | tf_op jit(solution)/shard_map/ppermute | solution.py:406
  175.3 10.5 %collective-permute-start.13 = (bf16[128,128]{1,0:T(8,128)(2,1)S(1)}, bf16[128,128]{1,0:T(8,128)(2,1)S(1)}, u32[]{:S(2)}, u32[]{:S(2)}) collective-permute-start(bf16[128,128]{1,0:T(8,128)(2,1)S(1)} %responses.1.refs_0_), channel_id=1, source_target_pairs={{24,0},{25,1},{26,2},{27,3},{28,4},{29,5},{30,6},{31,7}} | collective-permute-start | bytes 98312 | tf_op jit(solution)/shard_map/ppermute | solution.py:411
  176.6 9.2 %collective-permute-start.12 = (bf16[128,128]{1,0:T(8,128)(2,1)S(1)}, bf16[128,128]{1,0:T(8,128)(2,1)S(1)}, u32[]{:S(2)}, u32[]{:S(2)}) collective-permute-start(bf16[128,128]{1,0:T(8,128)(2,1)S(1)} %responses.1.refs_0_), channel_id=1, source_target_pairs={{16,0},{24,8},{17,1},{25,9},{18,2},{26,10},{19,3},{27,11},{20,4},{... | collective-permute-start | bytes 98312 | tf_op jit(solution)/shard_map/ppermute | solution.py:411
  177.9 7.9 %collective-permute-start.11 = (bf16[128,128]{1,0:T(8,128)(2,1)S(1)}, bf16[128,128]{1,0:T(8,128)(2,1)S(1)}, u32[]{:S(2)}, u32[]{:S(2)}) collective-permute-start(bf16[128,128]{1,0:T(8,128)(2,1)S(1)} %responses.1.refs_0_), channel_id=1, source_target_pairs={{8,0},{16,8},{24,16},{9,1},{17,9},{25,17},{10,2},{18,10},{26,18},{... | collective-permute-start | bytes 98312 | tf_op jit(solution)/shard_map/ppermute | solution.py:411
  188.1 0.7 copy-start.2
  188.8 0.6 copy-start.3
  189.4 9.6 %all-to-all-start.2 = ((bf16[8,16,768]{2,1,0:T(8,128)(2,1)}), bf16[8,16,768]{2,1,0:T(8,128)(2,1)S(1)}, u32[]{:S(2)}, u32[]{:S(2)}) async-start(bf16[8,16,768]{2,1,0:T(8,128)(2,1)} %bitcast.23), calls=%async_computation.2 | async-start | bytes 393216 | tf_op jit(solution)/shard_map/all_to_all | solution.py:401
  199.1 0.7 copy-start.5
  208.4 36.2 %copy-start.10 = (f32[8,640]{1,0:T(8,128)S(1)}, f32[8,640]{1,0:T(8,128)}, u32[]{:S(2)}) copy-start(f32[8,640]{1,0:T(8,128)} %get-tuple-element.60) | copy-start | bytes 61444

commit v6 on v4

--- a/solution.py
+++ b/solution.py
@@ -149,15 +149,15 @@
 
     @pl.when(step == pl.num_programs(0) - 1)
     def _():
+        rows = plain_out_ref.shape[1]
+        split = [
+            jnp.concatenate([plain_out_ref[i, :, at] * scale_ref[i : i + 1, at] for i in range(size)], 1)
+            for at in (slice(c * LANES, (c + 1) * LANES) for c in range(groups // LANES))
+        ]
+        back = dot(jnp.concatenate(split, 0).astype(BF16), order_ref[...]).astype(BF16)
         span = size * LANES
         for chunk in range(groups // LANES):
-            lanes = slice(chunk * LANES, (chunk + 1) * LANES)
-            split = jnp.concatenate(
-                [plain_out_ref[i, :, lanes] * scale_ref[i : i + 1, lanes] for i in range(size)], 1
-            ).astype(BF16)
-            out_ref[:, chunk * span : (chunk + 1) * span] = dot(
-                split, order_ref[...]
-            ).astype(BF16)
+            out_ref[:, chunk * span : (chunk + 1) * span] = back[chunk * rows : (chunk + 1) * rows]
 
 
 def score_kernel(last, twist_ref, out_ref, slots_ref, router_ref, *rest):
@@ -318,11 +318,14 @@
 
     @pl.when(i == pl.num_programs(0) - 1)
     def _():
-        for chunk in range(groups // LANES):
-            lanes = slice(chunk * LANES, (chunk + 1) * LANES)
-            split = dot_nt(grad_ref[:, chunk * span : (chunk + 1) * span], order_ref[...])
+        rows = grad_ref.shape[0]
+        chunks = groups // LANES
+        grad = [grad_ref[:, c * span : (c + 1) * span] for c in range(chunks)]
+        split = dot_nt(jnp.concatenate(grad, 0), order_ref[...])
+        for c in range(chunks):
+            lanes = slice(c * LANES, (c + 1) * LANES)
             for i in range(size):
-                part = split[:, i * LANES : (i + 1) * LANES]
+                part = split[c * rows : (c + 1) * rows, i * LANES : (i + 1) * LANES]
                 split_ref[i, :, lanes] = part.astype(BF16)
                 scale_grad_ref[i : i + 1, lanes] = jnp.sum(
                     part * plain_out_ref[i, :, lanes], axis=0, keepdims=True
@@ -410,9 +413,24 @@
     ]
 
 
-def gather_exchange(shares):
+def join_kernel(*refs):
+    *part_refs, out_ref = refs
+    for k, ref in enumerate(part_refs):
+        out_ref[k] = ref[...]
+
+
+def join(parts):
+    return pl.pallas_call(
+        join_kernel,
+        out_shape=jax.ShapeDtypeStruct((len(parts),) + parts[0].shape, parts[0].dtype),
+        compiler_params=params(60),
+        name="join",
+    )(*parts)
+
+
+def exchange_near(shares):
     count = lax.axis_size("expert")
-    return jnp.stack([shares] + [swap(shares, d) for d in range(2, count, 2)])
+    return [shares] + [swap(shares, d) for d in range(2, count, 2)]
 
 
 def on_device(out_grad, saved_inputs, router, routes, hidden_saved, codes, codebook, scale):
@@ -500,13 +518,15 @@
     blocks = inner // block
     early = max(1, blocks // 6)
     (plain_out,) = decode(0, early, None)
-    plain_out, shares, later_state = lax.optimization_barrier((plain_out, shares, state))
-    near = gather_exchange(shares) if direct else None
-    states = [state] + pass_down(later_state, layers)
+    later_states = pass_down(state, layers)
+    plain_out, shares, farthest = lax.optimization_barrier((plain_out, shares, later_states[-1]))
+    near = exchange_near(shares) if direct else None
+    states = [state] + later_states[:-1] + [farthest]
     plain_out, expert_out = decode(early, blocks - early, plain_out)
     if direct:
-        plain_out, expert_out, near, slots = lax.optimization_barrier(
-            (plain_out, expert_out, near, slots)
+        near = join(near)
+        plain_out, expert_out, near, slots, states = lax.optimization_barrier(
+            (plain_out, expert_out, near, slots, states)
         )
         far = swap(near, 1)
     else:

time: 174 us -> 162 us (0.931)
  waiting for transfers between devices: 28.5 us -> 10.2 us
  blocking collectives: 0 us -> 9.89 us
  starting transfers between devices: 28.1 us -> 24.2 us
  other arithmetic: 5.22 us -> 2.73 us
    ppermute x9, waiting for transfers between devices: 22.2 us -> 6.42 us  [pass_down(): lax.ppermute(value, 'pipe', [(p, p - s) for p in range(s, layers)])]
    all_to_all x0 -> x1, blocking collectives: none -> 9.89 us  [exchange(): lax.all_to_all(value, 'expert', split_axis=0, concat_axis=0, tiled=True)]
    all_to_all x3 -> x2, starting transfers between devices: 12.6 us -> 8.58 us  [exchange(): lax.all_to_all(value, 'expert', split_axis=0, concat_axis=0, tiled=True)]
    another operation x1 -> x0, other arithmetic: 3.32 us -> none  [gather_exchange(): return jnp.stack([shares] + [swap(shares, d) for d in range(2, count, 2)])]
    pallas_call x0 -> x1, Pallas kernels: none -> 3.3 us  [join(): pl.pallas_call(join_kernel, out_shape=jax.ShapeDtypeStruct((len(parts),)...]
    ppermute x4, waiting for transfers between devices: 6.11 us -> 3.64 us  [swap(): lax.ppermute(value, 'expert', [(i, i ^ distance) for i in range(count)])]
    pallas_call x1, Pallas kernels: 10.5 us -> 8.6 us  [on_device(): by_columns(slots_kernel, [columns(rows), pl.BlockSpec((rows, LANES), lamb...]
    unnamed x31 -> x27, local copies, waits for them, and re-layouts: 7.55 us -> 7.49 us
  transfers between devices with their start and end apart: 16 -> 15, of which waited for: 7 -> 4; matrix products, arithmetic and copies ran while one was open for 6% -> 6% of each run, Pallas kernels for 24% -> 28%
where the time goes in v6:
time: 162 us; the launch traced here: 161 us
  Pallas kernels  96.1 us (59%)
  starting transfers between devices  24.2 us (15%)
  local copies, waits for them, and re-layouts  15.1 us (9%)
  waiting for transfers between devices  10.2 us (6%)
  blocking collectives  9.89 us (6%)
  other arithmetic  2.73 us (2%)
  matrix products  2.08 us (1%)
    pallas_call x1, Pallas kernels, on_device(): pl.pallas_call(functools.partial(book_kernel, unroll), grid=(inner // blo...  34.6 us
    pallas_call x2, Pallas kernels, decode(): pl.pallas_call(functools.partial(decode_kernel, first, last), grid=(count...  29.8 us
    ppermute x9, starting transfers between devices, pass_down(): lax.ppermute(value, 'pipe', [(p, p - s) for p in range(s, layers)])  12 us
    all_to_all x1, blocking collectives, exchange(): lax.all_to_all(value, 'expert', split_axis=0, concat_axis=0, tiled=True)  9.89 us
    pallas_call x2, Pallas kernels, score(): pl.pallas_call(functools.partial(score_kernel, last), grid_spec=pltpu.Pre...  8.78 us
    pallas_call x1, Pallas kernels, on_device(): by_columns(slots_kernel, [columns(rows), pl.BlockSpec((rows, LANES), lamb...  8.6 us
    all_to_all x2, starting transfers between devices, exchange(): lax.all_to_all(value, 'expert', split_axis=0, concat_axis=0, tiled=True)  8.58 us
    unnamed x27, local copies, waits for them, and re-layouts  7.49 us
  transfers between devices with their start and end apart: 15, of which 4 were waited for; matrix products, arithmetic and copies ran while one was open for 6% of the time, Pallas kernels for 28%

profile of v6, /device:TPU:0, one launch (start us, length us, event | category | flops | bytes accessed | tf_op | source)
XLA Modules:
  0.0 161.2 jit_solution(8130600898523311392)
XLA Ops:
  0.6 1.7 %dynamic-slice_bitcast_fusion = bf16[160,640]{1,0:T(8,128)(2,1)} fusion(bf16[1,5120,160]{1,2,0:T(8,128)(2,1)} %param.10, s32[]{:T(128)S(6)} %select_n.11), kind=kLoop, calls=%fused_computation.5 | loop fusion | bytes 409604 | tf_op jit(solution)/shard_map/dynamic_slice | solution.py:462
  2.4 1.4 collective-permute-start.2
  3.8 1.3 collective-permute-start.1
  5.1 1.3 collective-permute-start
  7.2 2.1 %fusion.logits_ref = f32[128,160]{1,0:T(8,128)S(1)} fusion(bf16[1,5120,160]{1,2,0:T(8,128)(2,1)} %param.10, bf16[1,128,5120]{2,1,0:T(8,128)(2,1)S(1)} %copy-done), kind=kOutput, calls=%fused_computation | convolution fusion | flops 209715200 | bytes 3031040 | tf_op jit(solution)/shard_map/dot_general | solution.py:28
  9.3 1.8 %prepare.1 = (f32[128,256]{1,0:T(8,128)S(1)}, bf16[128,5248]{1,0:T(8,128)(2,1)S(1)}, bf16[1024,1024]{1,0:T(8,128)(2,1)S(1)}) custom-call(f32[128,160]{1,0:T(8,128)S(1)} %fusion.logits_ref, s32[128,6]{1,0:T(8,128)S(1)} %bitcast.41, bf16[128,5120]{1,0:T(8,128)(2,1)S(1)} %copy-done.1), custom_call_target="tpu_custom_call" | custom-call | tf_op jit(solution)/shard_map/prepare/pallas_call | solution.py:473
  11.1 1.4 copy-done.2
  12.5 1.1 copy-done.3
  13.6 1.4 collective-permute-start.8
  15.0 1.3 collective-permute-start.3
  16.3 5.2 %all-to-all-start = ((bf16[8,16,5248]{2,1,0:T(8,128)(2,1)}), bf16[8,16,5248]{2,1,0:T(8,128)(2,1)S(1)}, u32[]{:S(2)}, u32[]{:S(2)}) async-start(bf16[8,16,5248]{2,1,0:T(8,128)(2,1)} %bitcast.39), calls=%async_computation | async-start | bytes 2686976 | tf_op jit(solution)/shard_map/all_to_all | solution.py:401
  24.4 1.6 %pad.4 = bf16[8,16,768]{2,1,0:T(8,128)(2,1)} pad(bf16[8,9,768]{2,1,0:T(8,128)(2,1)} %reshape_squeeze.6, bf16[]{:T(256)} %constant.29.clone.1), padding=0_0x0_7x0_0 | pad | bytes 307202 | tf_op jit(solution)/shard_map/jit(_pad)/pad | solution.py:454
  26.7 6.1 %decode.2.rest_0_ = f32[8,128,640]{2,1,0:T(8,128)} custom-call(s32[2,768,640]{2,1,0:T(8,128)} %bitcast.47, bf16[2,2,8,16,128]{4,3,2,1,0:T(8,128)(2,1)} %broadcast_in_dim.16.table_ref, bf16[128,768]{1,0:T(8,128)(2,1)} %bitcast.52), custom_call_target="tpu_custom_call" | custom-call | flops 5000000000 | bytes 2000000 | tf_op jit(solution)/shard_map/decode/pallas_call | solution.py:497
  32.8 1.3 collective-permute-start.7
  34.1 2.0 %pad_maximum_fusion.refs_0_ = bf16[3,160,640]{2,1,0:T(8,128)(2,1)} fusion(bf16[1,160,640]{2,1,0:T(8,128)(2,1)} %bitcast.16, bf16[1,160,640]{2,1,0:T(8,128)(2,1)} %bitcast.15, bf16[1,160,640]{2,1,0:T(8,128)(2,1)} %bitcast.13), kind=kLoop, calls=%fused_computation.3 | loop fusion | flops 614400 | bytes 1228800 | tf_op jit(solution)/shard_map/stack | solution.py:467
  36.1 2.9 %collective-permute-start.6 = (bf16[3,160,640]{2,1,0:T(8,128)(2,1)}, bf16[3,160,640]{2,1,0:T(8,128)(2,1)}, u32[]{:S(2)}, u32[]{:S(2)}) collective-permute-start(bf16[3,160,640]{2,1,0:T(8,128)(2,1)} %pad_maximum_fusion.refs_0_), channel_id=1, source_target_pairs={{0,6},{1,7},{2,4},{3,5},{4,2},{5,3},{6,0},{7,1},{8,14},{9,15},{10,... | collective-permute-start | bytes 1843208 | tf_op jit(solution)/shard_map/ppermute | solution.py:406
  39.6 23.8 %decode.3 = (f32[8,128,640]{2,1,0:T(8,128)}, bf16[128,5120]{1,0:T(8,128)(2,1)}) custom-call(s32[2,768,640]{2,1,0:T(8,128)} %bitcast.48, bf16[2,2,8,16,128]{4,3,2,1,0:T(8,128)(2,1)} %broadcast_in_dim.16.table_ref, bf16[128,768]{1,0:T(8,128)(2,1)} %bitcast.53, f32[8,128,640]{2,1,0:T(8,128)} %decode.2.rest_0_, ...), custom_call_target="tpu_custom_call", output_to_operand_aliasing={{0}: (3, {})} | custom-call | flops 24999999488 | bytes 2000000 | tf_op jit(solution)/shard_map/decode/pallas_call | solution.py:497
  63.4 3.4 %collective-permute-done.5.refs_2_ = bf16[3,160,640]{2,1,0:T(8,128)(2,1)} collective-permute-done((bf16[3,160,640]{2,1,0:T(8,128)(2,1)}, bf16[3,160,640]{2,1,0:T(8,128)(2,1)}, u32[]{:S(2)}, u32[]{:S(2)}) %collective-permute-start.5) | collective-permute-done | bytes 614432 | tf_op jit(solution)/shard_map/ppermute | solution.py:406
  67.0 3.3 %join.1.router_ref.near_ref = bf16[4,3,160,640]{3,2,1,0:T(8,128)(2,1)} custom-call(bf16[3,160,640]{2,1,0:T(8,128)(2,1)} %pad_maximum_fusion.refs_0_, bf16[3,160,640]{2,1,0:T(8,128)(2,1)} %collective-permute-done.4.refs_1_, bf16[3,160,640]{2,1,0:T(8,128)(2,1)} %collective-permute-done.5.refs_2_, bf16[3,160,640]{2,1,0:T(8,128)(2,1)} %collective-permute-done.6.refs_3_), custom_call_target="tpu_custom_call" | custom-call | tf_op jit(solution)/shard_map/join/pallas_call | solution.py:423
  70.4 1.0 copy-done.6
  71.4 4.3 %scores.2 = (f32[480,128]{1,0:T(8,128)}, f32[128,128]{1,0:T(8,128)}) custom-call(s32[1]{0:T(128)} %bitcast.twist_ref, bf16[128,5120]{1,0:T(8,128)(2,1)} %get-tuple-element.38.out_ref, bf16[128,5248]{1,0:T(8,128)(2,1)} %bitcast.42, bf16[4,3,160,640]{3,2,1,0:T(8,128)(2,1)} %join.1.router_ref.near_ref), custom_call_target="tpu_custom_call" | custom-call | tf_op jit(solution)/shard_map/scores/pallas_call | solution.py:566
  75.7 4.5 %scores.3 = bf16[128,896]{1,0:T(8,128)(2,1)} custom-call(s32[1]{0:T(128)} %bitcast.twist_ref, bf16[128,5120]{1,0:T(8,128)(2,1)} %get-tuple-element.38.out_ref, bf16[128,5248]{1,0:T(8,128)(2,1)} %bitcast.43, bf16[4,3,160,640]{3,2,1,0:T(8,128)(2,1)} %collective-permute-done.9.router_ref.far_ref, f32[480,128]{1,0:T(8,128)} %get-tuple-element.41.rest_0_, ...), custom_call_target="tpu_custom_call" | custom-call | tf_op jit(solution)/shard_map/scores/pallas_call | solution.py:566
  80.2 9.9 %all_to_all.34 = bf16[8,16,896]{2,1,0:T(8,128)(2,1)S(1)} all-to-all(bf16[8,16,896]{2,1,0:T(8,128)(2,1)} %bitcast.51), channel_id=1, replica_groups=mesh['pipe'=4,'expert'=8] {'expert'}, dimensions={0} | all-to-all | bytes 458752 | tf_op jit(solution)/shard_map/all_to_all | solution.py:401
  91.0 1.3 collective-permute-start.12
  92.3 1.3 collective-permute-start.11
  93.6 1.5 collective-permute-start.10
  95.1 6.4 %collective-permute-done.12.refs_3_ = bf16[128,128]{1,0:T(8,128)(2,1)S(1)} collective-permute-done((bf16[128,128]{1,0:T(8,128)(2,1)S(1)}, bf16[128,128]{1,0:T(8,128)(2,1)S(1)}, u32[]{:S(2)}, u32[]{:S(2)}) %collective-permute-start.12) | collective-permute-done | bytes 32800 | tf_op jit(solution)/shard_map/ppermute | solution.py:411
  101.5 2.3 %chain.1 = (bf16[128,160]{1,0:T(8,128)(2,1)S(1)}, bf16[128,768]{1,0:T(8,128)(2,1)S(1)}, bf16[128,768]{1,0:T(8,128)(2,1)}) custom-call(bf16[128,128]{1,0:T(8,128)(2,1)S(1)} %responses.1.refs_0_, bf16[128,128]{1,0:T(8,128)(2,1)S(1)} %collective-permute-done.10.refs_1_, bf16[128,128]{1,0:T(8,128)(2,1)S(1)} %collective-permute-done.11.refs_2_, ...), custom_call_target="tpu_custom_call" | custom-call | tf_op jit(solution)/shard_map/chain/pallas_call | solution.py:600
  105.1 3.4 %all-to-all-start.2 = ((bf16[8,16,768]{2,1,0:T(8,128)(2,1)}), bf16[8,16,768]{2,1,0:T(8,128)(2,1)S(1)}, u32[]{:S(2)}, u32[]{:S(2)}) async-start(bf16[8,16,768]{2,1,0:T(8,128)(2,1)} %bitcast.23), calls=%async_computation.2 | async-start | bytes 393216 | tf_op jit(solution)/shard_map/all_to_all | solution.py:401
  108.5 6.0 %finish.1 = bf16[128,5120]{1,0:T(8,128)(2,1)} custom-call(s32[1]{0:T(128)} %bitcast.twist_ref, bf16[128,5120]{1,0:T(8,128)(2,1)} %grad_ref.3, bf16[128,768]{1,0:T(8,128)(2,1)} %copy-done.4, bf16[128,160]{1,0:T(8,128)(2,1)} %copy-done.5, bf16[160,5120]{1,0:T(8,128)(2,1)} %bitcast.46, bf16[4,3,160,640]{3,2,1,0:T(8,128)(2,1)} %join.1.router_ref.near_ref, ...), custom_call_target="tpu_custom_call" | custom-call | tf_op jit(solution)/shard_map/finish/pallas_call | solution.py:613
  115.3 8.6 %slot_grads.1 = (bf16[8,128,640]{2,1,0:T(8,128)(2,1)}, f32[8,640]{1,0:T(8,128)}) custom-call(s32[1]{0:T(128)} %bitcast.twist_ref, bf16[128,5248]{1,0:T(8,128)(2,1)} %bitcast.44, bf16[128,5248]{1,0:T(8,128)(2,1)} %bitcast.45, bf16[128,768]{1,0:T(8,128)(2,1)} %bitcast.55, bf16[4,3,160,640]{3,2,1,0:T(8,128)(2,1)} %join.1.router_ref.near_ref, ...), custom_call_target="tpu_custom_call" | custom-call | tf_op jit(solution)/shard_map/slot_grads/pallas_call | solution.py:629
  123.9 34.6 %book_grads.1 = f32[2,48,48]{2,1,0:T(8,128)} custom-call(bf16[128,768]{1,0:T(8,128)(2,1)} %bitcast.54, bf16[8,128,640]{2,1,0:T(8,128)(2,1)} %get-tuple-element.51.slots_ref, f32[8,640]{1,0:T(8,128)} %bitcast.57, s32[2,768,640]{2,1,0:T(8,128)} %bitcast.49), custom_call_target="tpu_custom_call" | custom-call | tf_op jit(solution)/shard_map/book_grads/pallas_call | solution.py:651
  (50 shorter events, 11.0 us)
Async XLA Ops:
  0.6 6.6 %copy-start = (bf16[1,128,5120]{2,1,0:T(8,128)(2,1)S(1)}, bf16[1,128,5120]{2,1,0:T(8,128)(2,1)}, u32[]{:S(2)}) copy-start(bf16[1,128,5120]{2,1,0:T(8,128)(2,1)} %param.9) | copy-start | bytes 3932164
  2.4 6.9 %copy-start.1 = (bf16[128,5120]{1,0:T(8,128)(2,1)S(1)}, bf16[128,5120]{1,0:T(8,128)(2,1)}, u32[]{:S(2)}) copy-start(bf16[128,5120]{1,0:T(8,128)(2,1)} %grad_ref.3) | copy-start | bytes 3932164
  2.4 30.4 %collective-permute-start.2 = (bf16[160,640]{1,0:T(8,128)(2,1)}, bf16[160,640]{1,0:T(8,128)(2,1)}, u32[]{:S(2)}, u32[]{:S(2)}) collective-permute-start(bf16[160,640]{1,0:T(8,128)(2,1)} %dynamic-slice_bitcast_fusion), channel_id=1, source_target_pairs={{24,0},{25,1},{26,2},{27,3},{28,4},{29,5},{30,6},{31,7}} | collective-permute-start | bytes 614408 | tf_op jit(solution)/shard_map/ppermute | solution.py:411
  3.8 30.2 %collective-permute-start.1 = (bf16[160,640]{1,0:T(8,128)(2,1)}, bf16[160,640]{1,0:T(8,128)(2,1)}, u32[]{:S(2)}, u32[]{:S(2)}) collective-permute-start(bf16[160,640]{1,0:T(8,128)(2,1)} %dynamic-slice_bitcast_fusion), channel_id=1, source_target_pairs={{16,0},{24,8},{17,1},{25,9},{18,2},{26,10},{19,3},{27,11},{20,4},{... | collective-permute-start | bytes 614408 | tf_op jit(solution)/shard_map/ppermute | solution.py:411
  5.1 29.0 %collective-permute-start = (bf16[160,640]{1,0:T(8,128)(2,1)}, bf16[160,640]{1,0:T(8,128)(2,1)}, u32[]{:S(2)}, u32[]{:S(2)}) collective-permute-start(bf16[160,640]{1,0:T(8,128)(2,1)} %dynamic-slice_bitcast_fusion), channel_id=1, source_target_pairs={{8,0},{16,8},{24,16},{9,1},{17,9},{25,17},{10,2},{18,10},{26,18},{... | collective-permute-start | bytes 614408 | tf_op jit(solution)/shard_map/ppermute | solution.py:411
  11.1 1.4 copy-start.2
  12.5 1.1 copy-start.3
  13.6 7.9 %copy-start.8 = (bf16[1,1,72,768]{3,2,1,0:T(8,128)(2,1)S(1)}, bf16[1,1,72,768]{3,2,1,0:T(8,128)(2,1)}, u32[]{:S(2)}) copy-start(bf16[1,1,72,768]{3,2,1,0:T(8,128)(2,1)} %param.12) | copy-start | bytes 331780
  13.6 9.2 %copy-start.9 = (f32[1,1,5120]{2,1,0:T(1,128)S(1)}, f32[1,1,5120]{2,1,0:T(1,128)}, u32[]{:S(2)}) copy-start(f32[1,1,5120]{2,1,0:T(1,128)} %param.15) | copy-start | bytes 61444
  13.6 56.7 %collective-permute-start.8 = (f32[128,256]{1,0:T(8,128)S(1)}, f32[128,256]{1,0:T(8,128)S(1)}, u32[]{:S(2)}, u32[]{:S(2)}) collective-permute-start(f32[128,256]{1,0:T(8,128)S(1)} %get-tuple-element.43.state_ref.refs_4_), channel_id=1, source_target_pairs={{16,0},{24,8},{17,1},{25,9},{18,2},{26,10},{19,3},{27,11},{20,4},{... | collective-permute-start | bytes 393224 | tf_op jit(solution)/shard_map/ppermute | solution.py:411
  15.0 21.1 %collective-permute-start.3 = (f32[128,256]{1,0:T(8,128)S(1)}, f32[128,256]{1,0:T(8,128)S(1)}, u32[]{:S(2)}, u32[]{:S(2)}) collective-permute-start(f32[128,256]{1,0:T(8,128)S(1)} %get-tuple-element.43.state_ref.refs_4_), channel_id=1, source_target_pairs={{24,0},{25,1},{26,2},{27,3},{28,4},{29,5},{30,6},{31,7}} | collective-permute-start | bytes 393224 | tf_op jit(solution)/shard_map/ppermute | solution.py:411
  16.3 9.7 %copy-start.11 = (bf16[1,1,2,256,8]{3,4,2,1,0:T(8,128)(2,1)S(1)}, bf16[1,1,2,256,8]{3,4,2,1,0:T(8,128)(2,1)}, u32[]{:S(2)}) copy-start(bf16[1,1,2,256,8]{3,4,2,1,0:T(8,128)(2,1)} %param.14) | copy-start | bytes 24580
  16.3 54.0 %all-to-all-start = ((bf16[8,16,5248]{2,1,0:T(8,128)(2,1)}), bf16[8,16,5248]{2,1,0:T(8,128)(2,1)S(1)}, u32[]{:S(2)}, u32[]{:S(2)}) async-start(bf16[8,16,5248]{2,1,0:T(8,128)(2,1)} %bitcast.39), calls=%async_computation | async-start | bytes 2686976 | tf_op jit(solution)/shard_map/all_to_all | solution.py:401
  32.8 37.6 %collective-permute-start.7 = (f32[128,256]{1,0:T(8,128)S(1)}, f32[128,256]{1,0:T(8,128)S(1)}, u32[]{:S(2)}, u32[]{:S(2)}) collective-permute-start(f32[128,256]{1,0:T(8,128)S(1)} %get-tuple-element.43.state_ref.refs_4_), channel_id=1, source_target_pairs={{8,0},{16,8},{24,16},{9,1},{17,9},{25,17},{10,2},{18,10},{26,18},{... | collective-permute-start | bytes 393224 | tf_op jit(solution)/shard_map/ppermute | solution.py:411
  36.1 27.3 %collective-permute-start.6 = (bf16[3,160,640]{2,1,0:T(8,128)(2,1)}, bf16[3,160,640]{2,1,0:T(8,128)(2,1)}, u32[]{:S(2)}, u32[]{:S(2)}) collective-permute-start(bf16[3,160,640]{2,1,0:T(8,128)(2,1)} %pad_maximum_fusion.refs_0_), channel_id=1, source_target_pairs={{0,6},{1,7},{2,4},{3,5},{4,2},{5,3},{6,0},{7,1},{8,14},{9,15},{10,... | collective-permute-start | bytes 1843208 | tf_op jit(solution)/shard_map/ppermute | solution.py:406
  39.0 27.7 %collective-permute-start.5 = (bf16[3,160,640]{2,1,0:T(8,128)(2,1)}, bf16[3,160,640]{2,1,0:T(8,128)(2,1)}, u32[]{:S(2)}, u32[]{:S(2)}) collective-permute-start(bf16[3,160,640]{2,1,0:T(8,128)(2,1)} %pad_maximum_fusion.refs_0_), channel_id=1, source_target_pairs={{0,4},{1,5},{2,6},{3,7},{4,0},{5,1},{6,2},{7,3},{8,12},{9,13},{10,... | collective-permute-start | bytes 1843208 | tf_op jit(solution)/shard_map/ppermute | solution.py:406
  39.6 27.4 %collective-permute-start.4 = (bf16[3,160,640]{2,1,0:T(8,128)(2,1)}, bf16[3,160,640]{2,1,0:T(8,128)(2,1)}, u32[]{:S(2)}, u32[]{:S(2)}) collective-permute-start(bf16[3,160,640]{2,1,0:T(8,128)(2,1)} %pad_maximum_fusion.refs_0_), channel_id=1, source_target_pairs={{0,2},{1,3},{2,0},{3,1},{4,6},{5,7},{6,4},{7,5},{8,10},{9,11},{10,... | collective-permute-start | bytes 1843208 | tf_op jit(solution)/shard_map/ppermute | solution.py:406
  70.3 1.1 copy-start.6
  70.3 5.3 %collective-permute-start.9 = (bf16[4,3,160,640]{3,2,1,0:T(8,128)(2,1)}, bf16[4,3,160,640]{3,2,1,0:T(8,128)(2,1)}, u32[]{:S(2)}, u32[]{:S(2)}) collective-permute-start(bf16[4,3,160,640]{3,2,1,0:T(8,128)(2,1)} %join.1.router_ref.near_ref), channel_id=1, source_target_pairs={{0,1},{1,0},{2,3},{3,2},{4,5},{5,4},{6,7},{7,6},{8,9},{9,8},{10,11... | collective-permute-start | bytes 7372808 | tf_op jit(solution)/shard_map/ppermute | solution.py:406
  91.0 10.5 %collective-permute-start.12 = (bf16[128,128]{1,0:T(8,128)(2,1)S(1)}, bf16[128,128]{1,0:T(8,128)(2,1)S(1)}, u32[]{:S(2)}, u32[]{:S(2)}) collective-permute-start(bf16[128,128]{1,0:T(8,128)(2,1)S(1)} %responses.1.refs_0_), channel_id=1, source_target_pairs={{24,0},{25,1},{26,2},{27,3},{28,4},{29,5},{30,6},{31,7}} | collective-permute-start | bytes 98312 | tf_op jit(solution)/shard_map/ppermute | solution.py:411
  92.3 9.2 %collective-permute-start.11 = (bf16[128,128]{1,0:T(8,128)(2,1)S(1)}, bf16[128,128]{1,0:T(8,128)(2,1)S(1)}, u32[]{:S(2)}, u32[]{:S(2)}) collective-permute-start(bf16[128,128]{1,0:T(8,128)(2,1)S(1)} %responses.1.refs_0_), channel_id=1, source_target_pairs={{16,0},{24,8},{17,1},{25,9},{18,2},{26,10},{19,3},{27,11},{20,4},{... | collective-permute-start | bytes 98312 | tf_op jit(solution)/shard_map/ppermute | solution.py:411
  93.6 7.9 %collective-permute-start.10 = (bf16[128,128]{1,0:T(8,128)(2,1)S(1)}, bf16[128,128]{1,0:T(8,128)(2,1)S(1)}, u32[]{:S(2)}, u32[]{:S(2)}) collective-permute-start(bf16[128,128]{1,0:T(8,128)(2,1)S(1)} %responses.1.refs_0_), channel_id=1, source_target_pairs={{8,0},{16,8},{24,16},{9,1},{17,9},{25,17},{10,2},{18,10},{26,18},{... | collective-permute-start | bytes 98312 | tf_op jit(solution)/shard_map/ppermute | solution.py:411
  103.8 0.7 copy-start.4
  104.5 0.6 copy-start.5
  105.1 9.6 %all-to-all-start.2 = ((bf16[8,16,768]{2,1,0:T(8,128)(2,1)}), bf16[8,16,768]{2,1,0:T(8,128)(2,1)S(1)}, u32[]{:S(2)}, u32[]{:S(2)}) async-start(bf16[8,16,768]{2,1,0:T(8,128)(2,1)} %bitcast.23), calls=%async_computation.2 | async-start | bytes 393216 | tf_op jit(solution)/shard_map/all_to_all | solution.py:401
  114.6 0.7 copy-start.7
  123.9 36.2 %copy-start.10 = (f32[8,640]{1,0:T(8,128)S(1)}, f32[8,640]{1,0:T(8,128)}, u32[]{:S(2)}) copy-start(f32[8,640]{1,0:T(8,128)} %get-tuple-element.52) | copy-start | bytes 61444

commit v7 on v6

--- a/solution.py
+++ b/solution.py
@@ -62,6 +62,14 @@
 
 def one_hot(mask):
     return mask.astype(F32).astype(BF16)
+
+
+def spread_slots(hidden, rows):
+    row = iota((rows, hidden.shape[0]), 0)
+    place = row % SLOT
+    source = iota((rows, hidden.shape[0]), 1)
+    spread = one_hot((row // SLOT * MOST + place == source) & (place < MOST))
+    return dot(spread, hidden).astype(BF16)
 
 
 def slot_select(state, rows, routed):
@@ -102,11 +110,9 @@
     order_ref[...] = one_hot(source == iota((span, span), 1))
 
 
-def decode_kernel(first, last, codes_ref, table_ref, hidden_ref, *rest):
-    if not first:
-        before_ref, scale_ref, order_ref, *rest = rest
-    plain_out_ref, *rest = rest
-    weight_ref = rest[-1]
+def decode_kernel(
+    codes_ref, table_ref, hidden_ref, scale_ref, order_ref, plain_out_ref, out_ref, weight_ref
+):
     unroll = 8
     step = pl.program_id(0)
     books, block, groups = codes_ref.shape
@@ -115,8 +121,9 @@
 
     @pl.when(step == 0)
     def _():
-        plain_out_ref[...] = jnp.zeros_like(plain_out_ref) if first else before_ref[...]
-
+        plain_out_ref[...] = jnp.zeros_like(plain_out_ref)
+
+    hidden = spread_slots(hidden_ref[...], out_ref.shape[0])
     for chunk in range(groups // LANES):
         lanes = slice(chunk * LANES, (chunk + 1) * LANES)
 
@@ -139,13 +146,9 @@
             return carry
 
         lax.fori_loop(0, block // 16 // unroll, decode_rows, 0)
-        product = dot(hidden_ref[...], weight_ref[...])
+        product = dot(hidden, weight_ref[...])
         for i in range(size):
             plain_out_ref[i, :, lanes] += product[:, i * LANES : (i + 1) * LANES]
-
-    if not last:
-        return
-    out_ref = rest[0]
 
     @pl.when(step == pl.num_programs(0) - 1)
     def _():
@@ -160,46 +163,45 @@
             out_ref[:, chunk * span : (chunk + 1) * span] = back[chunk * rows : (chunk + 1) * rows]
 
 
-def score_kernel(last, twist_ref, out_ref, slots_ref, router_ref, *rest):
-    i = pl.program_id(0)
+def score_near_kernel(twist_ref, out_ref, slots_ref, router_ref, total_ref, base_ref):
+    rows, width = out_ref.shape
+    total_ref[...] = add_products(0, twist_ref[0], out_ref, router_ref, None)
+    base = jnp.zeros((rows, LANES), F32)
+    for c in range(width // LANES):
+        at = slice(c * LANES, (c + 1) * LANES)
+        base = base + slots_ref[:, at].astype(F32) * out_ref[:, at].astype(F32)
+    base_ref[...] = jnp.broadcast_to(jnp.sum(base, axis=1, keepdims=True), (rows, LANES))
+
+
+def add_products(far, twist, out_ref, router_ref, total):
+    parts, later_count, routed, part_width = router_ref.shape
+    for i in range(parts):
+        first = (twist ^ (2 * i + far)) * part_width
+        out = out_ref[:, pl.ds(pl.multiple_of(first, LANES), part_width)]
+        product = dot_nt(router_ref[i].reshape(later_count * routed, part_width), out)
+        total = product if total is None else total + product
+    return total
+
+
+def score_far_kernel(twist_ref, out_ref, router_ref, total_ref, base_ref, score_ref):
     rows = out_ref.shape[0]
-    later_count, routed, part_width = router_ref.shape[1:]
-    if last:
-        total_before_ref, base_before_ref, score_ref, total_ref, base_ref = rest
-    else:
-        total_ref, base_ref = rest
-
-    @pl.when(i == 0)
-    def _():
-        total_ref[...] = total_before_ref[...] if last else jnp.zeros_like(total_ref)
-        base_ref[...] = base_before_ref[...] if last else jnp.zeros_like(base_ref)
-
-    out = out_ref[...]
-    base = jnp.sum(slots_ref[...].astype(F32) * out.astype(F32), axis=1, keepdims=True)
-    base_ref[...] += jnp.broadcast_to(base, (rows, LANES))
-    total_ref[...] += dot_nt(router_ref[0].reshape(later_count * routed, part_width), out)
-
-    if not last:
-        return
-
-    @pl.when(i == pl.num_programs(0) - 1)
-    def _():
-        wide = later_count * WIDE
-        score_ref[:, :wide] = jnp.zeros((rows, wide), BF16)
-        for s in range(later_count):
-            score_ref[:, s * WIDE : s * WIDE + routed] = total_ref[
-                s * routed : (s + 1) * routed, :
-            ].T.astype(BF16)
-        base = base_ref[...]
-        high = base.astype(BF16).astype(F32)
-        middle = (base - high).astype(BF16).astype(F32)
-        low = base - high - middle
-        column = iota((rows, LANES), 1)
-        score_ref[:, wide:] = jnp.where(
-            column == 0,
-            high,
-            jnp.where(column == 1, middle, jnp.where(column == 2, low, 0.0)),
-        ).astype(BF16)
+    later_count, routed = router_ref.shape[1:3]
+    wide = later_count * WIDE
+    total = add_products(1, twist_ref[0], out_ref, router_ref, total_ref[...])
+    score_ref[:, :wide] = jnp.zeros((rows, wide), BF16)
+    for s in range(later_count):
+        part = total[s * routed : (s + 1) * routed, :].T
+        score_ref[:, s * WIDE : s * WIDE + routed] = part.astype(BF16)
+    base = base_ref[...]
+    high = base.astype(BF16).astype(F32)
+    middle = (base - high).astype(BF16).astype(F32)
+    low = base - high - middle
+    column = iota((rows, LANES), 1)
+    score_ref[:, wide:] = jnp.where(
+        column == 0,
+        high,
+        jnp.where(column == 1, middle, jnp.where(column == 2, low, 0.0)),
+    ).astype(BF16)
 
 
 def response_kernel(routed, scores_ref, state_ref, *rest):
@@ -343,7 +345,7 @@
     def _():
         out_ref[...] = jnp.zeros_like(out_ref)
 
-    hidden = hidden_ref[...]
+    hidden = spread_slots(hidden_ref[...], slots_ref.shape[1])
     for i in range(size):
         grad = dot_tn(hidden, slots_ref[i]) * scale_ref[i : i + 1, :]
         for c in range(chunks):
@@ -451,8 +453,6 @@
     grow = max(1, rows // 128)
     router_t = router[0].T
     scale_split = scale[0, 0].reshape(groups, size).T
-    hidden = jnp.pad(hidden.reshape(experts, MOST, inner), ((0, 0), (0, SLOT - MOST), (0, 0)))
-    hidden = hidden.reshape(rows, inner)
 
     parts = math.gcd(width // LANES, experts)
     direct = parts == experts
@@ -464,7 +464,7 @@
         ((place % sharers) * share_rows, (place // sharers) * part_width),
         (share_rows, part_width),
     )
-    shares = jnp.stack(pass_down(own_share, layers))
+    shares = join(pass_down(own_share, layers))
     twist = jnp.full((1,), place if direct else 0, jnp.int32)
 
     logits = dot(saved_inputs[0], router[0])
@@ -490,39 +490,37 @@
     )
     block = 128
 
-    def decode(start, count, before):
-        first = before is None
-        last = start + count == inner // block
-        more = [] if first else [before, scale_split, order]
+    blocks = inner // block
+
+    def decode():
         return pl.pallas_call(
-            functools.partial(decode_kernel, first, last),
-            grid=(count,),
+            decode_kernel,
+            grid=(blocks,),
             in_specs=[
-                pl.BlockSpec((books, block, groups), lambda s: (0, s + start, 0)),
+                pl.BlockSpec((books, block, groups), lambda s: (0, s, 0)),
                 whole((books, halves, size, 16, LANES)),
-                pl.BlockSpec((rows, block), lambda s: (0, s + start)),
-            ]
-            + [whole(m.shape) for m in more],
-            out_specs=[whole((size, rows, groups))] + [whole((rows, width))] * last,
-            out_shape=[jax.ShapeDtypeStruct((size, rows, groups), F32)]
-            + [jax.ShapeDtypeStruct((rows, width), BF16)] * last,
+                pl.BlockSpec((experts * MOST, block), lambda s: (0, s)),
+                whole((size, groups)),
+                whole((span, span)),
+            ],
+            out_specs=[whole((size, rows, groups)), whole((rows, width))],
+            out_shape=[
+                jax.ShapeDtypeStruct((size, rows, groups), F32),
+                jax.ShapeDtypeStruct((rows, width), BF16),
+            ],
             scratch_shapes=[pltpu.VMEM((block, size * LANES), BF16)],
-            input_output_aliases={} if first else {3: 0},
             compiler_params=params(60),
             cost_estimate=pl.CostEstimate(
-                flops=count * 5_000_000_000, bytes_accessed=2_000_000, transcendentals=0
+                flops=blocks * 5_000_000_000, bytes_accessed=10_000_000, transcendentals=0
             ),
             name="decode",
-        )(codes, table, hidden, *more)
-
-    blocks = inner // block
-    early = max(1, blocks // 6)
-    (plain_out,) = decode(0, early, None)
+        )(codes, table, hidden, scale_split, order)
+
     later_states = pass_down(state, layers)
-    plain_out, shares, farthest = lax.optimization_barrier((plain_out, shares, later_states[-1]))
+    hidden, shares, farthest = lax.optimization_barrier((hidden, shares, later_states[-1]))
     near = exchange_near(shares) if direct else None
     states = [state] + later_states[:-1] + [farthest]
-    plain_out, expert_out = decode(early, blocks - early, plain_out)
+    plain_out, expert_out = decode()
     if direct:
         near = join(near)
         plain_out, expert_out, near, slots, states = lax.optimization_barrier(
@@ -558,37 +556,32 @@
             name=name,
         )
 
-    def score(last, routers, before):
-        def half(height):
-            return pl.BlockSpec((height, part_width), lambda i, t: (0, t[0] ^ (2 * i + last)))
-
-        sums = [((later_count * routed, rows), F32), ((rows, LANES), F32)]
+    def score(kernel, operands, out_shape):
         return pl.pallas_call(
-            functools.partial(score_kernel, last),
+            kernel,
             grid_spec=pltpu.PrefetchScalarGridSpec(
                 num_scalar_prefetch=1,
-                grid=(parts // 2,),
-                in_specs=[
-                    half(rows),
-                    half(rows),
-                    pl.BlockSpec(
-                        (1, later_count, routed, part_width), lambda i, t: (i, 0, 0, 0)
-                    ),
-                ]
-                + [whole(b.shape) for b in before],
-                out_specs=whole((rows, wide + LANES)) if last else [whole(s) for s, _ in sums],
-                scratch_shapes=[pltpu.VMEM(s, d) for s, d in sums] if last else [],
+                grid=(1,),
+                in_specs=[whole(a.shape) for a in operands],
+                out_specs=jax.tree.map(lambda a: whole(a.shape), out_shape),
             ),
-            out_shape=(
-                jax.ShapeDtypeStruct((rows, wide + LANES), BF16)
-                if last
-                else [jax.ShapeDtypeStruct(s, d) for s, d in sums]
-            ),
+            out_shape=out_shape,
             compiler_params=params(60),
             name="scores",
-        )(twist, expert_out, slots, routers, *before)
-
-    scores = exchange(score(True, far, score(False, near, [])))
+        )(twist, *operands)
+
+    sums = [
+        jax.ShapeDtypeStruct((later_count * routed, rows), F32),
+        jax.ShapeDtypeStruct((rows, LANES), F32),
+    ]
+    sums = score(score_near_kernel, [expert_out, slots, near], sums)
+    scores = exchange(
+        score(
+            score_far_kernel,
+            [expert_out, far, *sums],
+            jax.ShapeDtypeStruct((rows, wide + LANES), BF16),
+        )
+    )
 
     response_width = -(-(later_count * experts + 3) // LANES) * LANES
     response = pl.pallas_call(
@@ -652,7 +645,7 @@
         functools.partial(book_kernel, unroll),
         grid=(inner // block,),
         in_specs=[
-            pl.BlockSpec((rows, block), lambda s: (0, s)),
+            pl.BlockSpec((experts * MOST, block), lambda s: (0, s)),
             whole((size, rows, groups)),
             whole((size, groups)),
             pl.BlockSpec((books, block, groups), lambda s: (0, s, 0)),

time: 162 us -> 160 us (0.988)
  waiting for transfers between devices: 10.2 us -> 14.6 us
  local copies, waits for them, and re-layouts: 15.1 us -> 12 us
  other arithmetic: 2.73 us -> 0.69 us
    pallas_call x4 -> x3, Pallas kernels: 38.6 us -> 34.3 us  [the longest x1 26.3 us: decode(): pl.pallas_call(decode_kernel, grid=(blocks,), in_specs=[pl.BlockSpec((boo...]
    ppermute x4, waiting for transfers between devices: 3.64 us -> 7.76 us  [swap(): lax.ppermute(value, 'expert', [(i, i ^ distance) for i in range(count)])]
    another operation x1 -> x0, other arithmetic: 2.04 us -> none  [on_device(): shares = jnp.stack(pass_down(own_share, layers))]
    pallas_call x1 -> x2, Pallas kernels: 3.3 us -> 5.31 us  [join(): pl.pallas_call(join_kernel, out_shape=jax.ShapeDtypeStruct((len(parts),)...]
  transfers between devices with their start and end apart: 15 -> 15, of which waited for: 4 -> 4; matrix products, arithmetic and copies ran while one was open for 6% -> 3% of each run, Pallas kernels for 28% -> 27%
where the time goes in v7:
time: 160 us; the launch traced here: 159 us
  Pallas kernels  94.5 us (59%)
  starting transfers between devices  24.3 us (15%)
  waiting for transfers between devices  14.6 us (9%)
  local copies, waits for them, and re-layouts  12 us (8%)
  blocking collectives  9.89 us (6%)
  matrix products  2.08 us (1%)
    pallas_call x1, Pallas kernels, on_device(): pl.pallas_call(functools.partial(book_kernel, unroll), grid=(inner // blo...  35.3 us
    pallas_call x1, Pallas kernels, decode(): pl.pallas_call(decode_kernel, grid=(blocks,), in_specs=[pl.BlockSpec((boo...  26.3 us
    ppermute x9, starting transfers between devices, pass_down(): lax.ppermute(value, 'pipe', [(p, p - s) for p in range(s, layers)])  11.9 us
    all_to_all x1, blocking collectives, exchange(): lax.all_to_all(value, 'expert', split_axis=0, concat_axis=0, tiled=True)  9.89 us
    all_to_all x2, starting transfers between devices, exchange(): lax.all_to_all(value, 'expert', split_axis=0, concat_axis=0, tiled=True)  8.76 us
    pallas_call x1, Pallas kernels, on_device(): by_columns(slots_kernel, [columns(rows), pl.BlockSpec((rows, LANES), lamb...  8.6 us
    pallas_call x2, Pallas kernels, score(): pl.pallas_call(kernel, grid_spec=pltpu.PrefetchScalarGridSpec(num_scalar_...  7.93 us
    ppermute x4, waiting for transfers between devices, swap(): lax.ppermute(value, 'expert', [(i, i ^ distance) for i in range(count)])  7.76 us
  transfers between devices with their start and end apart: 15, of which 4 were waited for; matrix products, arithmetic and copies ran while one was open for 3% of the time, Pallas kernels for 27%

profile of v7, /device:TPU:0, one launch (start us, length us, event | category | flops | bytes accessed | tf_op | source)
XLA Modules:
  0.0 159.0 jit_solution(11504711296991571091)
XLA Ops:
  0.6 1.7 %dynamic-slice_bitcast_fusion = bf16[160,640]{1,0:T(8,128)(2,1)} fusion(bf16[1,5120,160]{1,2,0:T(8,128)(2,1)} %param.10, s32[]{:T(128)S(6)} %select_n.11), kind=kLoop, calls=%fused_computation.4 | loop fusion | bytes 409604 | tf_op jit(solution)/shard_map/dynamic_slice | solution.py:462
  2.4 1.4 collective-permute-start.2
  3.8 1.3 collective-permute-start.1
  5.1 1.3 collective-permute-start
  6.4 2.1 %fusion.logits_ref = f32[128,160]{1,0:T(8,128)S(1)} fusion(bf16[1,5120,160]{1,2,0:T(8,128)(2,1)} %param.10, bf16[1,128,5120]{2,1,0:T(8,128)(2,1)S(1)} %copy-done), kind=kOutput, calls=%fused_computation | convolution fusion | flops 209715200 | bytes 3031040 | tf_op jit(solution)/shard_map/dot_general | solution.py:28
  8.6 1.8 %prepare.1 = (f32[128,256]{1,0:T(8,128)S(1)}, bf16[128,5248]{1,0:T(8,128)(2,1)S(1)}, bf16[1024,1024]{1,0:T(8,128)(2,1)S(1)}) custom-call(f32[128,160]{1,0:T(8,128)S(1)} %fusion.logits_ref, s32[128,6]{1,0:T(8,128)S(1)} %bitcast.36, bf16[128,5120]{1,0:T(8,128)(2,1)S(1)} %copy-done.1), custom_call_target="tpu_custom_call" | custom-call | tf_op jit(solution)/shard_map/prepare/pallas_call | solution.py:473
  10.4 1.4 copy-done.2
  11.8 1.1 copy-done.3
  12.9 1.4 collective-permute-start.3
  14.3 1.3 collective-permute-start.8
  15.6 5.2 %all-to-all-start = ((bf16[8,16,5248]{2,1,0:T(8,128)(2,1)}), bf16[8,16,5248]{2,1,0:T(8,128)(2,1)S(1)}, u32[]{:S(2)}, u32[]{:S(2)}) async-start(bf16[8,16,5248]{2,1,0:T(8,128)(2,1)} %bitcast.34), calls=%async_computation | async-start | bytes 2686976 | tf_op jit(solution)/shard_map/all_to_all | solution.py:403
  23.0 1.3 collective-permute-start.7
  24.3 2.0 %join.2.refs_0_ = bf16[3,160,640]{2,1,0:T(8,128)(2,1)} custom-call(bf16[160,640]{1,0:T(8,128)(2,1)} %collective-permute-done.refs_0_, bf16[160,640]{1,0:T(8,128)(2,1)} %collective-permute-done.1.refs_1_, bf16[160,640]{1,0:T(8,128)(2,1)} %collective-permute-done.2.refs_2_), custom_call_target="tpu_custom_call" | custom-call | tf_op jit(solution)/shard_map/join/pallas_call | solution.py:425
  26.6 3.0 %collective-permute-start.6 = (bf16[3,160,640]{2,1,0:T(8,128)(2,1)}, bf16[3,160,640]{2,1,0:T(8,128)(2,1)}, u32[]{:S(2)}, u32[]{:S(2)}) collective-permute-start(bf16[3,160,640]{2,1,0:T(8,128)(2,1)} %join.2.refs_0_), channel_id=1, source_target_pairs={{0,6},{1,7},{2,4},{3,5},{4,2},{5,3},{6,0},{7,1},{8,14},{9,15},{10,... | collective-permute-start | bytes 1843208 | tf_op jit(solution)/shard_map/ppermute | solution.py:408
  30.9 26.3 %decode.1 = (f32[8,128,640]{2,1,0:T(8,128)}, bf16[128,5120]{1,0:T(8,128)(2,1)}) custom-call(s32[2,768,640]{2,1,0:T(8,128)} %bitcast.41, bf16[2,2,8,16,128]{4,3,2,1,0:T(8,128)(2,1)} %broadcast_in_dim.16.table_ref, bf16[72,768]{1,0:T(8,128)(2,1)} %bitcast.46, f32[8,640]{1,0:T(8,128)} %bitcast.48, bf16[1024,1024]{1,0:T(8,128)(2,1)} %copy-done.2), custom_call_target="tpu_custom_call" | custom-call | flops 30000001024 | bytes 10000000 | tf_op jit(solution)/shard_map/decode/pallas_call | solution.py:496
  57.2 7.7 %collective-permute-done.5.refs_2_ = bf16[3,160,640]{2,1,0:T(8,128)(2,1)} collective-permute-done((bf16[3,160,640]{2,1,0:T(8,128)(2,1)}, bf16[3,160,640]{2,1,0:T(8,128)(2,1)}, u32[]{:S(2)}, u32[]{:S(2)}) %collective-permute-start.5) | collective-permute-done | bytes 614432 | tf_op jit(solution)/shard_map/ppermute | solution.py:408
  65.0 3.3 %join.3.router_ref.near_ref = bf16[4,3,160,640]{3,2,1,0:T(8,128)(2,1)} custom-call(bf16[3,160,640]{2,1,0:T(8,128)(2,1)} %join.2.refs_0_, bf16[3,160,640]{2,1,0:T(8,128)(2,1)} %collective-permute-done.4.refs_1_, bf16[3,160,640]{2,1,0:T(8,128)(2,1)} %collective-permute-done.5.refs_2_, bf16[3,160,640]{2,1,0:T(8,128)(2,1)} %collective-permute-done.6.refs_3_), custom_call_target="tpu_custom_call" | custom-call | tf_op jit(solution)/shard_map/join/pallas_call | solution.py:425
  68.4 1.0 copy-done.6
  69.4 4.2 %scores.2 = (f32[480,128]{1,0:T(8,128)}, f32[128,128]{1,0:T(8,128)}) custom-call(s32[1]{0:T(128)} %bitcast.twist_ref, bf16[128,5120]{1,0:T(8,128)(2,1)} %get-tuple-element.38.out_ref, bf16[128,5248]{1,0:T(8,128)(2,1)} %bitcast.37, bf16[4,3,160,640]{3,2,1,0:T(8,128)(2,1)} %join.3.router_ref.near_ref), custom_call_target="tpu_custom_call" | custom-call | tf_op jit(solution)/shard_map/scores/pallas_call | solution.py:560
  73.6 3.7 %scores.3 = bf16[128,896]{1,0:T(8,128)(2,1)} custom-call(s32[1]{0:T(128)} %bitcast.twist_ref, bf16[128,5120]{1,0:T(8,128)(2,1)} %get-tuple-element.38.out_ref, bf16[4,3,160,640]{3,2,1,0:T(8,128)(2,1)} %collective-permute-done.9.router_ref.far_ref, f32[480,128]{1,0:T(8,128)} %get-tuple-element.41.total_ref, f32[128,128]{1,0:T(8,128)} %get-tuple-element.42.base_ref), custom_call_target="tpu_custom_call" | custom-call | tf_op jit(solution)/shard_map/scores/pallas_call | solution.py:560
  77.3 9.9 %all_to_all.34 = bf16[8,16,896]{2,1,0:T(8,128)(2,1)S(1)} all-to-all(bf16[8,16,896]{2,1,0:T(8,128)(2,1)} %bitcast.44), channel_id=1, replica_groups=mesh['pipe'=4,'expert'=8] {'expert'}, dimensions={0} | all-to-all | bytes 458752 | tf_op jit(solution)/shard_map/all_to_all | solution.py:403
  87.2 0.9 responses.1.refs_0_
  88.1 1.3 collective-permute-start.12
  89.4 1.3 collective-permute-start.11
  90.7 1.3 collective-permute-start.10
  92.0 6.5 %collective-permute-done.12.refs_3_ = bf16[128,128]{1,0:T(8,128)(2,1)S(1)} collective-permute-done((bf16[128,128]{1,0:T(8,128)(2,1)S(1)}, bf16[128,128]{1,0:T(8,128)(2,1)S(1)}, u32[]{:S(2)}, u32[]{:S(2)}) %collective-permute-start.12) | collective-permute-done | bytes 32800 | tf_op jit(solution)/shard_map/ppermute | solution.py:413
  98.6 2.3 %chain.1 = (bf16[128,160]{1,0:T(8,128)(2,1)S(1)}, bf16[128,768]{1,0:T(8,128)(2,1)S(1)}, bf16[128,768]{1,0:T(8,128)(2,1)}) custom-call(bf16[128,128]{1,0:T(8,128)(2,1)S(1)} %responses.1.refs_0_, bf16[128,128]{1,0:T(8,128)(2,1)S(1)} %collective-permute-done.10.refs_1_, bf16[128,128]{1,0:T(8,128)(2,1)S(1)} %collective-permute-done.11.refs_2_, ...), custom_call_target="tpu_custom_call" | custom-call | tf_op jit(solution)/shard_map/chain/pallas_call | solution.py:593
  102.2 3.6 %all-to-all-start.2 = ((bf16[8,16,768]{2,1,0:T(8,128)(2,1)}), bf16[8,16,768]{2,1,0:T(8,128)(2,1)S(1)}, u32[]{:S(2)}, u32[]{:S(2)}) async-start(bf16[8,16,768]{2,1,0:T(8,128)(2,1)} %bitcast.20), calls=%async_computation.2 | async-start | bytes 393216 | tf_op jit(solution)/shard_map/all_to_all | solution.py:403
  105.7 6.0 %finish.1 = bf16[128,5120]{1,0:T(8,128)(2,1)} custom-call(s32[1]{0:T(128)} %bitcast.twist_ref, bf16[128,5120]{1,0:T(8,128)(2,1)} %grad_ref.3, bf16[128,768]{1,0:T(8,128)(2,1)} %copy-done.4, bf16[128,160]{1,0:T(8,128)(2,1)} %copy-done.5, bf16[160,5120]{1,0:T(8,128)(2,1)} %bitcast.40, bf16[4,3,160,640]{3,2,1,0:T(8,128)(2,1)} %join.3.router_ref.near_ref, ...), custom_call_target="tpu_custom_call" | custom-call | tf_op jit(solution)/shard_map/finish/pallas_call | solution.py:606
  112.4 8.6 %slot_grads.1 = (bf16[8,128,640]{2,1,0:T(8,128)(2,1)}, f32[8,640]{1,0:T(8,128)}) custom-call(s32[1]{0:T(128)} %bitcast.twist_ref, bf16[128,5248]{1,0:T(8,128)(2,1)} %bitcast.38, bf16[128,5248]{1,0:T(8,128)(2,1)} %bitcast.39, bf16[128,768]{1,0:T(8,128)(2,1)} %bitcast.45, bf16[4,3,160,640]{3,2,1,0:T(8,128)(2,1)} %join.3.router_ref.near_ref, ...), custom_call_target="tpu_custom_call" | custom-call | tf_op jit(solution)/shard_map/slot_grads/pallas_call | solution.py:622
  121.0 35.3 %book_grads.1 = f32[2,48,48]{2,1,0:T(8,128)} custom-call(bf16[72,768]{1,0:T(8,128)(2,1)} %bitcast.47, bf16[8,128,640]{2,1,0:T(8,128)(2,1)} %get-tuple-element.51.slots_ref, f32[8,640]{1,0:T(8,128)} %bitcast.49, s32[2,768,640]{2,1,0:T(8,128)} %bitcast.42), custom_call_target="tpu_custom_call" | custom-call | tf_op jit(solution)/shard_map/book_grads/pallas_call | solution.py:644
  156.3 0.9 reshape.24
  (47 shorter events, 7.7 us)
Async XLA Ops:
  0.6 5.8 %copy-start = (bf16[1,128,5120]{2,1,0:T(8,128)(2,1)S(1)}, bf16[1,128,5120]{2,1,0:T(8,128)(2,1)}, u32[]{:S(2)}) copy-start(bf16[1,128,5120]{2,1,0:T(8,128)(2,1)} %param.9) | copy-start | bytes 3932164
  2.4 6.1 %copy-start.11 = (s32[1,128,6]{1,0,2:T(1,128)S(1)}, s32[1,128,6]{1,0,2:T(1,128)}, u32[]{:S(2)}) copy-start(s32[1,128,6]{1,0,2:T(1,128)} %param.11) | copy-start | bytes 9220
  2.4 6.2 %copy-start.1 = (bf16[128,5120]{1,0:T(8,128)(2,1)S(1)}, bf16[128,5120]{1,0:T(8,128)(2,1)}, u32[]{:S(2)}) copy-start(bf16[128,5120]{1,0:T(8,128)(2,1)} %grad_ref.3) | copy-start | bytes 3932164
  2.4 20.6 %collective-permute-start.2 = (bf16[160,640]{1,0:T(8,128)(2,1)}, bf16[160,640]{1,0:T(8,128)(2,1)}, u32[]{:S(2)}, u32[]{:S(2)}) collective-permute-start(bf16[160,640]{1,0:T(8,128)(2,1)} %dynamic-slice_bitcast_fusion), channel_id=1, source_target_pairs={{24,0},{25,1},{26,2},{27,3},{28,4},{29,5},{30,6},{31,7}} | collective-permute-start | bytes 614408 | tf_op jit(solution)/shard_map/ppermute | solution.py:413
  3.8 20.5 %collective-permute-start.1 = (bf16[160,640]{1,0:T(8,128)(2,1)}, bf16[160,640]{1,0:T(8,128)(2,1)}, u32[]{:S(2)}, u32[]{:S(2)}) collective-permute-start(bf16[160,640]{1,0:T(8,128)(2,1)} %dynamic-slice_bitcast_fusion), channel_id=1, source_target_pairs={{16,0},{24,8},{17,1},{25,9},{18,2},{26,10},{19,3},{27,11},{20,4},{... | collective-permute-start | bytes 614408 | tf_op jit(solution)/shard_map/ppermute | solution.py:413
  5.1 19.2 %collective-permute-start = (bf16[160,640]{1,0:T(8,128)(2,1)}, bf16[160,640]{1,0:T(8,128)(2,1)}, u32[]{:S(2)}, u32[]{:S(2)}) collective-permute-start(bf16[160,640]{1,0:T(8,128)(2,1)} %dynamic-slice_bitcast_fusion), channel_id=1, source_target_pairs={{8,0},{16,8},{24,16},{9,1},{17,9},{25,17},{10,2},{18,10},{26,18},{... | collective-permute-start | bytes 614408 | tf_op jit(solution)/shard_map/ppermute | solution.py:413
  10.4 1.4 copy-start.2
  11.8 1.1 copy-start.3
  12.9 8.4 %copy-start.8 = (f32[1,1,5120]{2,1,0:T(1,128)S(1)}, f32[1,1,5120]{2,1,0:T(1,128)}, u32[]{:S(2)}) copy-start(f32[1,1,5120]{2,1,0:T(1,128)} %param.15) | copy-start | bytes 61444
  12.9 13.7 %collective-permute-start.3 = (f32[128,256]{1,0:T(8,128)S(1)}, f32[128,256]{1,0:T(8,128)S(1)}, u32[]{:S(2)}, u32[]{:S(2)}) collective-permute-start(f32[128,256]{1,0:T(8,128)S(1)} %get-tuple-element.43.state_ref.refs_4_), channel_id=1, source_target_pairs={{24,0},{25,1},{26,2},{27,3},{28,4},{29,5},{30,6},{31,7}} | collective-permute-start | bytes 393224 | tf_op jit(solution)/shard_map/ppermute | solution.py:413
  14.3 53.9 %collective-permute-start.8 = (f32[128,256]{1,0:T(8,128)S(1)}, f32[128,256]{1,0:T(8,128)S(1)}, u32[]{:S(2)}, u32[]{:S(2)}) collective-permute-start(f32[128,256]{1,0:T(8,128)S(1)} %get-tuple-element.43.state_ref.refs_4_), channel_id=1, source_target_pairs={{16,0},{24,8},{17,1},{25,9},{18,2},{26,10},{19,3},{27,11},{20,4},{... | collective-permute-start | bytes 393224 | tf_op jit(solution)/shard_map/ppermute | solution.py:413
  15.6 52.6 %all-to-all-start = ((bf16[8,16,5248]{2,1,0:T(8,128)(2,1)}), bf16[8,16,5248]{2,1,0:T(8,128)(2,1)S(1)}, u32[]{:S(2)}, u32[]{:S(2)}) async-start(bf16[8,16,5248]{2,1,0:T(8,128)(2,1)} %bitcast.34), calls=%async_computation | async-start | bytes 2686976 | tf_op jit(solution)/shard_map/all_to_all | solution.py:403
  20.8 9.4 %copy-start.10 = (bf16[1,1,2,256,8]{3,4,2,1,0:T(8,128)(2,1)S(1)}, bf16[1,1,2,256,8]{3,4,2,1,0:T(8,128)(2,1)}, u32[]{:S(2)}) copy-start(bf16[1,1,2,256,8]{3,4,2,1,0:T(8,128)(2,1)} %param.14) | copy-start | bytes 24580
  23.0 45.3 %collective-permute-start.7 = (f32[128,256]{1,0:T(8,128)S(1)}, f32[128,256]{1,0:T(8,128)S(1)}, u32[]{:S(2)}, u32[]{:S(2)}) collective-permute-start(f32[128,256]{1,0:T(8,128)S(1)} %get-tuple-element.43.state_ref.refs_4_), channel_id=1, source_target_pairs={{8,0},{16,8},{24,16},{9,1},{17,9},{25,17},{10,2},{18,10},{26,18},{... | collective-permute-start | bytes 393224 | tf_op jit(solution)/shard_map/ppermute | solution.py:413
  26.6 30.6 %collective-permute-start.6 = (bf16[3,160,640]{2,1,0:T(8,128)(2,1)}, bf16[3,160,640]{2,1,0:T(8,128)(2,1)}, u32[]{:S(2)}, u32[]{:S(2)}) collective-permute-start(bf16[3,160,640]{2,1,0:T(8,128)(2,1)} %join.2.refs_0_), channel_id=1, source_target_pairs={{0,6},{1,7},{2,4},{3,5},{4,2},{5,3},{6,0},{7,1},{8,14},{9,15},{10,... | collective-permute-start | bytes 1843208 | tf_op jit(solution)/shard_map/ppermute | solution.py:408
  29.7 35.2 %collective-permute-start.5 = (bf16[3,160,640]{2,1,0:T(8,128)(2,1)}, bf16[3,160,640]{2,1,0:T(8,128)(2,1)}, u32[]{:S(2)}, u32[]{:S(2)}) collective-permute-start(bf16[3,160,640]{2,1,0:T(8,128)(2,1)} %join.2.refs_0_), channel_id=1, source_target_pairs={{0,4},{1,5},{2,6},{3,7},{4,0},{5,1},{6,2},{7,3},{8,12},{9,13},{10,... | collective-permute-start | bytes 1843208 | tf_op jit(solution)/shard_map/ppermute | solution.py:408
  30.2 34.8 %collective-permute-start.4 = (bf16[3,160,640]{2,1,0:T(8,128)(2,1)}, bf16[3,160,640]{2,1,0:T(8,128)(2,1)}, u32[]{:S(2)}, u32[]{:S(2)}) collective-permute-start(bf16[3,160,640]{2,1,0:T(8,128)(2,1)} %join.2.refs_0_), channel_id=1, source_target_pairs={{0,2},{1,3},{2,0},{3,1},{4,6},{5,7},{6,4},{7,5},{8,10},{9,11},{10,... | collective-permute-start | bytes 1843208 | tf_op jit(solution)/shard_map/ppermute | solution.py:408
  68.3 1.1 copy-start.6
  68.3 5.3 %collective-permute-start.9 = (bf16[4,3,160,640]{3,2,1,0:T(8,128)(2,1)}, bf16[4,3,160,640]{3,2,1,0:T(8,128)(2,1)}, u32[]{:S(2)}, u32[]{:S(2)}) collective-permute-start(bf16[4,3,160,640]{3,2,1,0:T(8,128)(2,1)} %join.3.router_ref.near_ref), channel_id=1, source_target_pairs={{0,1},{1,0},{2,3},{3,2},{4,5},{5,4},{6,7},{7,6},{8,9},{9,8},{10,11... | collective-permute-start | bytes 7372808 | tf_op jit(solution)/shard_map/ppermute | solution.py:408
  88.1 10.4 %collective-permute-start.12 = (bf16[128,128]{1,0:T(8,128)(2,1)S(1)}, bf16[128,128]{1,0:T(8,128)(2,1)S(1)}, u32[]{:S(2)}, u32[]{:S(2)}) collective-permute-start(bf16[128,128]{1,0:T(8,128)(2,1)S(1)} %responses.1.refs_0_), channel_id=1, source_target_pairs={{24,0},{25,1},{26,2},{27,3},{28,4},{29,5},{30,6},{31,7}} | collective-permute-start | bytes 98312 | tf_op jit(solution)/shard_map/ppermute | solution.py:413
  89.4 9.1 %collective-permute-start.11 = (bf16[128,128]{1,0:T(8,128)(2,1)S(1)}, bf16[128,128]{1,0:T(8,128)(2,1)S(1)}, u32[]{:S(2)}, u32[]{:S(2)}) collective-permute-start(bf16[128,128]{1,0:T(8,128)(2,1)S(1)} %responses.1.refs_0_), channel_id=1, source_target_pairs={{16,0},{24,8},{17,1},{25,9},{18,2},{26,10},{19,3},{27,11},{20,4},{... | collective-permute-start | bytes 98312 | tf_op jit(solution)/shard_map/ppermute | solution.py:413
  90.7 7.8 %collective-permute-start.10 = (bf16[128,128]{1,0:T(8,128)(2,1)S(1)}, bf16[128,128]{1,0:T(8,128)(2,1)S(1)}, u32[]{:S(2)}, u32[]{:S(2)}) collective-permute-start(bf16[128,128]{1,0:T(8,128)(2,1)S(1)} %responses.1.refs_0_), channel_id=1, source_target_pairs={{8,0},{16,8},{24,16},{9,1},{17,9},{25,17},{10,2},{18,10},{26,18},{... | collective-permute-start | bytes 98312 | tf_op jit(solution)/shard_map/ppermute | solution.py:413
  100.9 0.7 copy-start.4
  101.5 0.6 copy-start.5
  102.2 9.6 %all-to-all-start.2 = ((bf16[8,16,768]{2,1,0:T(8,128)(2,1)}), bf16[8,16,768]{2,1,0:T(8,128)(2,1)S(1)}, u32[]{:S(2)}, u32[]{:S(2)}) async-start(bf16[8,16,768]{2,1,0:T(8,128)(2,1)} %bitcast.20), calls=%async_computation.2 | async-start | bytes 393216 | tf_op jit(solution)/shard_map/all_to_all | solution.py:403
  111.7 0.7 copy-start.7
  121.0 37.0 %copy-start.9 = (f32[8,640]{1,0:T(8,128)S(1)}, f32[8,640]{1,0:T(8,128)}, u32[]{:S(2)}) copy-start(f32[8,640]{1,0:T(8,128)} %get-tuple-element.52) | copy-start | bytes 61444

commit v8 on v7

--- a/solution.py
+++ b/solution.py
@@ -80,7 +80,7 @@
     return one_hot(jnp.abs(dot(number, one_hot(owner)) - place) < 0.5)
 
 
-def prepare_kernel(logits_ref, routes_ref, grad_ref, state_ref, rows_ref, order_ref):
+def prepare_kernel(logits_ref, routes_ref, grad_ref, state_ref, rows_ref):
     tokens, routed = logits_ref.shape
     top = routes_ref.shape[1]
     width = grad_ref.shape[1]
@@ -104,6 +104,9 @@
     )
     rows_ref[:, :width] = dot_tn(select, grad_ref[...]).astype(BF16)
     rows_ref[:, width:] = jnp.broadcast_to(slot_gate, (rows, LANES)).astype(BF16)
+
+
+def order_kernel(after_ref, order_ref):
     span = order_ref.shape[0]
     row = iota((span, span), 0)
     source = (span // LANES) * (row & (LANES - 1)) + row // LANES
@@ -186,22 +189,18 @@
 def score_far_kernel(twist_ref, out_ref, router_ref, total_ref, base_ref, score_ref):
     rows = out_ref.shape[0]
     later_count, routed = router_ref.shape[1:3]
-    wide = later_count * WIDE
+    wide = later_count * routed
     total = add_products(1, twist_ref[0], out_ref, router_ref, total_ref[...])
-    score_ref[:, :wide] = jnp.zeros((rows, wide), BF16)
-    for s in range(later_count):
-        part = total[s * routed : (s + 1) * routed, :].T
-        score_ref[:, s * WIDE : s * WIDE + routed] = part.astype(BF16)
-    base = base_ref[...]
+    tail = jnp.zeros((score_ref.shape[1] - wide, rows), F32)
+    total = jnp.concatenate([total, tail], 0).T
+    base = base_ref[:, :1]
     high = base.astype(BF16).astype(F32)
     middle = (base - high).astype(BF16).astype(F32)
     low = base - high - middle
-    column = iota((rows, LANES), 1)
-    score_ref[:, wide:] = jnp.where(
-        column == 0,
-        high,
-        jnp.where(column == 1, middle, jnp.where(column == 2, low, 0.0)),
-    ).astype(BF16)
+    column = iota(total.shape, 1) - wide
+    for place, part in enumerate((high, middle, low)):
+        total = jnp.where(column == place, part, total)
+    score_ref[...] = total.astype(BF16)
 
 
 def response_kernel(routed, scores_ref, state_ref, *rest):
@@ -213,16 +212,20 @@
     column = iota((routed, width), 1)
     entry = iota((routed, width), 0)
     base_row, base_column = iota((LANES, width), 0), iota((LANES, width), 1)
+    last = scores_ref.shape[1] - LANES
+    base_row = base_row + last - later_count * routed
     total = dot(
-        scores_ref[:, later_count * WIDE :],
-        one_hot((base_column - later_count * experts == base_row) & (base_row < 3)),
+        scores_ref[:, last:],
+        one_hot(
+            (base_column - later_count * experts == base_row) & (base_row >= 0) & (base_row < 3)
+        ),
     )
     for s in range(later_count):
         probs = later_refs[s][:, :routed]
         high = probs.astype(BF16)
         low = (probs - high.astype(F32)).astype(BF16)
         picked = dot_tn(select, high) + dot_tn(select, low)
-        product = scores_ref[:, s * WIDE : s * WIDE + routed].astype(F32)
+        product = scores_ref[:, s * routed : (s + 1) * routed].astype(F32)
         mean = jnp.sum(picked * product, axis=1, keepdims=True)
         response = (ROUTE_SCALE * picked * (product - mean)).astype(BF16)
         total = total + dot(
@@ -470,18 +473,17 @@
     logits = dot(saved_inputs[0], router[0])
     state_width = -(-(routed + experts) // LANES) * LANES
     span = size * LANES
-    state, outgoing, order = pl.pallas_call(
+    state, outgoing = pl.pallas_call(
         prepare_kernel,
         out_shape=(
             jax.ShapeDtypeStruct((tokens, state_width), F32),
             jax.ShapeDtypeStruct((rows, width + LANES), BF16),
-            jax.ShapeDtypeStruct((span, span), BF16),
         ),
         compiler_params=params(20 + 6 * grow),
         name="prepare",
     )(logits, routes[0], out_grad)
     slots = exchange(outgoing)
-    hidden, outgoing, scale_split = lax.optimization_barrier((hidden, outgoing, scale_split))
+    hidden, outgoing = lax.optimization_barrier((hidden, outgoing))
 
     halves = entries // LANES
     table = codebook.transpose(0, 2, 1).reshape(books, size, halves, LANES)
@@ -492,6 +494,17 @@
 
     blocks = inner // block
 
+    later_states = pass_down(state, layers)
+    hidden, shares, farthest = lax.optimization_barrier((hidden, shares, later_states[-1]))
+    near = exchange_near(shares) if direct else None
+    states = [state] + later_states[:-1] + [farthest]
+    order = pl.pallas_call(
+        order_kernel,
+        in_specs=[pl.BlockSpec(memory_space=pl.ANY)],
+        out_shape=jax.ShapeDtypeStruct((span, span), BF16),
+        compiler_params=params(60),
+        name="order",
+    )(hidden)
     def decode():
         return pl.pallas_call(
             decode_kernel,
@@ -516,10 +529,6 @@
             name="decode",
         )(codes, table, hidden, scale_split, order)
 
-    later_states = pass_down(state, layers)
-    hidden, shares, farthest = lax.optimization_barrier((hidden, shares, later_states[-1]))
-    near = exchange_near(shares) if direct else None
-    states = [state] + later_states[:-1] + [farthest]
     plain_out, expert_out = decode()
     if direct:
         near = join(near)
@@ -570,6 +579,7 @@
             name="scores",
         )(twist, *operands)
 
+    score_width = -(-(later_count * routed + 3) // LANES) * LANES
     sums = [
         jax.ShapeDtypeStruct((later_count * routed, rows), F32),
         jax.ShapeDtypeStruct((rows, LANES), F32),
@@ -579,7 +589,7 @@
         score(
             score_far_kernel,
             [expert_out, far, *sums],
-            jax.ShapeDtypeStruct((rows, wide + LANES), BF16),
+            jax.ShapeDtypeStruct((rows, score_width), BF16),
         )
     )
 
@@ -597,7 +607,7 @@
             jax.ShapeDtypeStruct((tokens, wide), BF16),
             jax.ShapeDtypeStruct((rows, wide), BF16),
         ),
-        compiler_params=params(12 + 4 * grow),
+        compiler_params=params(60),
         name="chain",
     )(response, *pass_down(response, layers), *states)
 

time: 160 us -> 159 us (level)
  Pallas kernels: 94.5 us -> 96.9 us
  local copies, waits for them, and re-layouts: 12 us -> 10 us
    ppermute x4, waiting for transfers between devices: 7.76 us -> 3.41 us  [swap(): lax.ppermute(value, 'expert', [(i, i ^ distance) for i in range(count)])]
    ppermute x9, waiting for transfers between devices: 6.84 us -> 10.5 us  [pass_down(): lax.ppermute(value, 'pipe', [(p, p - s) for p in range(s, layers)])]
    unnamed x27 -> x37, local copies, waits for them, and re-layouts: 6.78 us -> 4.78 us
    pallas_call x0 -> x1, Pallas kernels: none -> 1.81 us  [on_device(): pl.pallas_call(order_kernel, in_specs=[pl.BlockSpec(memory_space=pl.ANY)]...]
  transfers between devices with their start and end apart: 15 -> 15, of which waited for: 4 -> 6; matrix products, arithmetic and copies ran while one was open for 3% -> 3% of each run, Pallas kernels for 27% -> 28%
where the time goes in v8:
time: 159 us; the launch traced here: 158 us
  Pallas kernels  96.9 us (61%)
  starting transfers between devices  24.7 us (16%)
  waiting for transfers between devices  13.9 us (9%)
  local copies, waits for them, and re-layouts  10 us (6%)
  blocking collectives  8.81 us (6%)
  matrix products  2.08 us (1%)
    pallas_call x1, Pallas kernels, on_device(): pl.pallas_call(functools.partial(book_kernel, unroll), grid=(inner // blo...  35.3 us
    pallas_call x1, Pallas kernels, decode(): pl.pallas_call(decode_kernel, grid=(blocks,), in_specs=[pl.BlockSpec((boo...  26.3 us
    ppermute x9, starting transfers between devices, pass_down(): lax.ppermute(value, 'pipe', [(p, p - s) for p in range(s, layers)])  12 us
    ppermute x9, waiting for transfers between devices, pass_down(): lax.ppermute(value, 'pipe', [(p, p - s) for p in range(s, layers)])  10.5 us
    all_to_all x1, blocking collectives, exchange(): lax.all_to_all(value, 'expert', split_axis=0, concat_axis=0, tiled=True)  8.81 us
    all_to_all x2, starting transfers between devices, exchange(): lax.all_to_all(value, 'expert', split_axis=0, concat_axis=0, tiled=True)  8.75 us
    pallas_call x1, Pallas kernels, on_device(): by_columns(slots_kernel, [columns(rows), pl.BlockSpec((rows, LANES), lamb...  8.6 us
    pallas_call x2, Pallas kernels, score(): pl.pallas_call(kernel, grid_spec=pltpu.PrefetchScalarGridSpec(num_scalar_...  7.88 us
  transfers between devices with their start and end apart: 15, of which 6 were waited for; matrix products, arithmetic and copies ran while one was open for 3% of the time, Pallas kernels for 28%

profile of v8, /device:TPU:0, one launch (start us, length us, event | category | flops | bytes accessed | tf_op | source)
XLA Modules:
  0.0 158.0 jit_solution(26908414996370466)
XLA Ops:
  0.6 1.7 %dynamic-slice_bitcast_fusion = bf16[160,640]{1,0:T(8,128)(2,1)} fusion(bf16[1,5120,160]{1,2,0:T(8,128)(2,1)} %param.10, s32[]{:T(128)S(6)} %select_n.11), kind=kLoop, calls=%fused_computation.4 | loop fusion | bytes 409604 | tf_op jit(solution)/shard_map/dynamic_slice | solution.py:465
  2.4 1.4 collective-permute-start.2
  3.8 1.3 collective-permute-start.1
  5.1 1.3 collective-permute-start
  6.4 2.1 %fusion.logits_ref = f32[128,160]{1,0:T(8,128)S(1)} fusion(bf16[1,5120,160]{1,2,0:T(8,128)(2,1)} %param.10, bf16[1,128,5120]{2,1,0:T(8,128)(2,1)S(1)} %copy-done), kind=kOutput, calls=%fused_computation | convolution fusion | flops 209715200 | bytes 3031040 | tf_op jit(solution)/shard_map/dot_general | solution.py:28
  8.6 1.1 prepare.1
  9.7 1.1 copy-done.2
  10.8 1.4 collective-permute-start.3
  12.2 1.3 collective-permute-start.8
  13.5 5.2 %all-to-all-start = ((bf16[8,16,5248]{2,1,0:T(8,128)(2,1)}), bf16[8,16,5248]{2,1,0:T(8,128)(2,1)S(1)}, u32[]{:S(2)}, u32[]{:S(2)}) async-start(bf16[8,16,5248]{2,1,0:T(8,128)(2,1)} %bitcast.34), calls=%async_computation | async-start | bytes 2686976 | tf_op jit(solution)/shard_map/all_to_all | solution.py:406
  20.9 1.4 collective-permute-start.7
  22.3 1.7 %collective-permute-done.1.refs_1_ = bf16[160,640]{1,0:T(8,128)(2,1)} collective-permute-done((bf16[160,640]{1,0:T(8,128)(2,1)}, bf16[160,640]{1,0:T(8,128)(2,1)}, u32[]{:S(2)}, u32[]{:S(2)}) %collective-permute-start.1) | collective-permute-done | bytes 204832 | tf_op jit(solution)/shard_map/ppermute | solution.py:416
  24.0 2.0 %join.2.refs_0_ = bf16[3,160,640]{2,1,0:T(8,128)(2,1)} custom-call(bf16[160,640]{1,0:T(8,128)(2,1)} %collective-permute-done.refs_0_, bf16[160,640]{1,0:T(8,128)(2,1)} %collective-permute-done.1.refs_1_, bf16[160,640]{1,0:T(8,128)(2,1)} %collective-permute-done.2.refs_2_), custom_call_target="tpu_custom_call" | custom-call | tf_op jit(solution)/shard_map/join/pallas_call | solution.py:428
  26.7 3.3 %collective-permute-start.6 = (bf16[3,160,640]{2,1,0:T(8,128)(2,1)}, bf16[3,160,640]{2,1,0:T(8,128)(2,1)}, u32[]{:S(2)}, u32[]{:S(2)}) collective-permute-start(bf16[3,160,640]{2,1,0:T(8,128)(2,1)} %join.2.refs_0_), channel_id=1, source_target_pairs={{0,6},{1,7},{2,4},{3,5},{4,2},{5,3},{6,0},{7,1},{8,14},{9,15},{10,... | collective-permute-start | bytes 1843208 | tf_op jit(solution)/shard_map/ppermute | solution.py:411
  30.6 1.8 %order.1.order_ref = bf16[1024,1024]{1,0:T(8,128)(2,1)} custom-call(bf16[72,768]{1,0:T(8,128)(2,1)} %bitcast.46), custom_call_target="tpu_custom_call" | custom-call | tf_op jit(solution)/shard_map/order/pallas_call | solution.py:501
  33.1 26.3 %decode.1 = (f32[8,128,640]{2,1,0:T(8,128)}, bf16[128,5120]{1,0:T(8,128)(2,1)}) custom-call(s32[2,768,640]{2,1,0:T(8,128)} %bitcast.41, bf16[2,2,8,16,128]{4,3,2,1,0:T(8,128)(2,1)} %broadcast_in_dim.16.table_ref, bf16[72,768]{1,0:T(8,128)(2,1)} %bitcast.47, f32[8,640]{1,0:T(8,128)} %bitcast.50, bf16[1024,1024]{1,0:T(8,128)(2,1)} %order.1.order_ref), custom_call_target="tpu_custom_call" | custom-call | flops 30000001024 | bytes 10000000 | tf_op jit(solution)/shard_map/decode/pallas_call | solution.py:509
  59.4 3.3 %collective-permute-done.5.refs_2_ = bf16[3,160,640]{2,1,0:T(8,128)(2,1)} collective-permute-done((bf16[3,160,640]{2,1,0:T(8,128)(2,1)}, bf16[3,160,640]{2,1,0:T(8,128)(2,1)}, u32[]{:S(2)}, u32[]{:S(2)}) %collective-permute-start.5) | collective-permute-done | bytes 614432 | tf_op jit(solution)/shard_map/ppermute | solution.py:411
  62.8 3.3 %join.3.router_ref.near_ref = bf16[4,3,160,640]{3,2,1,0:T(8,128)(2,1)} custom-call(bf16[3,160,640]{2,1,0:T(8,128)(2,1)} %join.2.refs_0_, bf16[3,160,640]{2,1,0:T(8,128)(2,1)} %collective-permute-done.4.refs_1_, bf16[3,160,640]{2,1,0:T(8,128)(2,1)} %collective-permute-done.5.refs_2_, bf16[3,160,640]{2,1,0:T(8,128)(2,1)} %collective-permute-done.6.refs_3_), custom_call_target="tpu_custom_call" | custom-call | tf_op jit(solution)/shard_map/join/pallas_call | solution.py:428
  67.3 4.2 %scores.2 = (f32[480,128]{1,0:T(8,128)}, f32[128,128]{1,0:T(8,128)}) custom-call(s32[1]{0:T(128)} %bitcast.twist_ref, bf16[128,5120]{1,0:T(8,128)(2,1)} %get-tuple-element.34.out_ref, bf16[128,5248]{1,0:T(8,128)(2,1)} %bitcast.37, bf16[4,3,160,640]{3,2,1,0:T(8,128)(2,1)} %join.3.router_ref.near_ref), custom_call_target="tpu_custom_call" | custom-call | tf_op jit(solution)/shard_map/scores/pallas_call | solution.py:569
  71.5 3.7 %scores.3 = bf16[128,512]{1,0:T(8,128)(2,1)} custom-call(s32[1]{0:T(128)} %bitcast.twist_ref, bf16[128,5120]{1,0:T(8,128)(2,1)} %get-tuple-element.34.out_ref, bf16[4,3,160,640]{3,2,1,0:T(8,128)(2,1)} %collective-permute-done.9.router_ref.far_ref, f32[480,128]{1,0:T(8,128)} %get-tuple-element.37.total_ref, f32[128,128]{1,0:T(8,128)} %get-tuple-element.38.base_ref), custom_call_target="tpu_custom_call" | custom-call | tf_op jit(solution)/shard_map/scores/pallas_call | solution.py:569
  75.2 8.8 %all_to_all.34 = bf16[8,16,512]{2,1,0:T(8,128)(2,1)S(1)} all-to-all(bf16[8,16,512]{2,1,0:T(8,128)(2,1)} %bitcast.45), channel_id=1, replica_groups=mesh['pipe'=4,'expert'=8] {'expert'}, dimensions={0} | all-to-all | bytes 262144 | tf_op jit(solution)/shard_map/all_to_all | solution.py:406
  84.0 1.1 responses.1.refs_0_
  85.1 1.3 collective-permute-start.12
  86.4 1.3 collective-permute-start.11
  87.7 1.3 collective-permute-start.10
  89.0 6.2 %collective-permute-done.12.refs_3_ = bf16[128,128]{1,0:T(8,128)(2,1)S(1)} collective-permute-done((bf16[128,128]{1,0:T(8,128)(2,1)S(1)}, bf16[128,128]{1,0:T(8,128)(2,1)S(1)}, u32[]{:S(2)}, u32[]{:S(2)}) %collective-permute-start.12) | collective-permute-done | bytes 32800 | tf_op jit(solution)/shard_map/ppermute | solution.py:416
  95.2 1.8 %collective-permute-done.10.refs_1_ = bf16[128,128]{1,0:T(8,128)(2,1)S(1)} collective-permute-done((bf16[128,128]{1,0:T(8,128)(2,1)S(1)}, bf16[128,128]{1,0:T(8,128)(2,1)S(1)}, u32[]{:S(2)}, u32[]{:S(2)}) %collective-permute-start.10) | collective-permute-done | bytes 32800 | tf_op jit(solution)/shard_map/ppermute | solution.py:416
  97.7 3.5 %chain.1 = (bf16[128,160]{1,0:T(8,128)(2,1)}, bf16[128,768]{1,0:T(8,128)(2,1)}, bf16[128,768]{1,0:T(8,128)(2,1)}) custom-call(bf16[128,128]{1,0:T(8,128)(2,1)} %copy-done.7, bf16[128,128]{1,0:T(8,128)(2,1)} %copy-done.12, bf16[128,128]{1,0:T(8,128)(2,1)} %copy-done.11, bf16[128,128]{1,0:T(8,128)(2,1)} %copy-done.10, f32[128,256]{1,0:T(8,128)} %copy-done.3, ...), custom_call_target="tpu_custom_call" | custom-call | tf_op jit(solution)/shard_map/chain/pallas_call | solution.py:603
  101.2 3.6 %all-to-all-start.2 = ((bf16[8,16,768]{2,1,0:T(8,128)(2,1)}), bf16[8,16,768]{2,1,0:T(8,128)(2,1)S(1)}, u32[]{:S(2)}, u32[]{:S(2)}) async-start(bf16[8,16,768]{2,1,0:T(8,128)(2,1)} %bitcast.49), calls=%async_computation.2 | async-start | bytes 393216 | tf_op jit(solution)/shard_map/all_to_all | solution.py:406
  104.8 6.0 %finish.1 = bf16[128,5120]{1,0:T(8,128)(2,1)} custom-call(s32[1]{0:T(128)} %bitcast.twist_ref, bf16[128,5120]{1,0:T(8,128)(2,1)} %grad_ref.3, bf16[128,768]{1,0:T(8,128)(2,1)} %get-tuple-element.43.later_ref, bf16[128,160]{1,0:T(8,128)(2,1)} %get-tuple-element.44.own_ref, bf16[160,5120]{1,0:T(8,128)(2,1)} %bitcast.40, ...), custom_call_target="tpu_custom_call" | custom-call | tf_op jit(solution)/shard_map/finish/pallas_call | solution.py:616
  111.5 8.6 %slot_grads.1 = (bf16[8,128,640]{2,1,0:T(8,128)(2,1)}, f32[8,640]{1,0:T(8,128)}) custom-call(s32[1]{0:T(128)} %bitcast.twist_ref, bf16[128,5248]{1,0:T(8,128)(2,1)} %bitcast.38, bf16[128,5248]{1,0:T(8,128)(2,1)} %bitcast.39, bf16[128,768]{1,0:T(8,128)(2,1)} %bitcast.44, bf16[4,3,160,640]{3,2,1,0:T(8,128)(2,1)} %join.3.router_ref.near_ref, ...), custom_call_target="tpu_custom_call" | custom-call | tf_op jit(solution)/shard_map/slot_grads/pallas_call | solution.py:632
  120.1 35.3 %book_grads.1 = f32[2,48,48]{2,1,0:T(8,128)} custom-call(bf16[72,768]{1,0:T(8,128)(2,1)} %bitcast.48, bf16[8,128,640]{2,1,0:T(8,128)(2,1)} %get-tuple-element.47.slots_ref, f32[8,640]{1,0:T(8,128)} %bitcast.51, s32[2,768,640]{2,1,0:T(8,128)} %bitcast.42), custom_call_target="tpu_custom_call" | custom-call | tf_op jit(solution)/shard_map/book_grads/pallas_call | solution.py:654
  (58 shorter events, 9.4 us)
Async XLA Ops:
  0.6 5.8 %copy-start = (bf16[1,128,5120]{2,1,0:T(8,128)(2,1)S(1)}, bf16[1,128,5120]{2,1,0:T(8,128)(2,1)}, u32[]{:S(2)}) copy-start(bf16[1,128,5120]{2,1,0:T(8,128)(2,1)} %param.9) | copy-start | bytes 3932164
  2.4 6.1 %copy-start.16 = (s32[1,128,6]{1,0,2:T(1,128)S(1)}, s32[1,128,6]{1,0,2:T(1,128)}, u32[]{:S(2)}) copy-start(s32[1,128,6]{1,0,2:T(1,128)} %param.11) | copy-start | bytes 9220
  2.4 6.2 %copy-start.1 = (bf16[128,5120]{1,0:T(8,128)(2,1)S(1)}, bf16[128,5120]{1,0:T(8,128)(2,1)}, u32[]{:S(2)}) copy-start(bf16[128,5120]{1,0:T(8,128)(2,1)} %grad_ref.3) | copy-start | bytes 3932164
  2.4 18.5 %collective-permute-start.2 = (bf16[160,640]{1,0:T(8,128)(2,1)}, bf16[160,640]{1,0:T(8,128)(2,1)}, u32[]{:S(2)}, u32[]{:S(2)}) collective-permute-start(bf16[160,640]{1,0:T(8,128)(2,1)} %dynamic-slice_bitcast_fusion), channel_id=1, source_target_pairs={{24,0},{25,1},{26,2},{27,3},{28,4},{29,5},{30,6},{31,7}} | collective-permute-start | bytes 614408 | tf_op jit(solution)/shard_map/ppermute | solution.py:416
  3.8 20.2 %collective-permute-start.1 = (bf16[160,640]{1,0:T(8,128)(2,1)}, bf16[160,640]{1,0:T(8,128)(2,1)}, u32[]{:S(2)}, u32[]{:S(2)}) collective-permute-start(bf16[160,640]{1,0:T(8,128)(2,1)} %dynamic-slice_bitcast_fusion), channel_id=1, source_target_pairs={{16,0},{24,8},{17,1},{25,9},{18,2},{26,10},{19,3},{27,11},{20,4},{... | collective-permute-start | bytes 614408 | tf_op jit(solution)/shard_map/ppermute | solution.py:416
  5.1 18.9 %collective-permute-start = (bf16[160,640]{1,0:T(8,128)(2,1)}, bf16[160,640]{1,0:T(8,128)(2,1)}, u32[]{:S(2)}, u32[]{:S(2)}) collective-permute-start(bf16[160,640]{1,0:T(8,128)(2,1)} %dynamic-slice_bitcast_fusion), channel_id=1, source_target_pairs={{8,0},{16,8},{24,16},{9,1},{17,9},{25,17},{10,2},{18,10},{26,18},{... | collective-permute-start | bytes 614408 | tf_op jit(solution)/shard_map/ppermute | solution.py:416
  9.7 1.1 copy-start.2
  10.8 73.2 %copy-start.3 = (f32[128,256]{1,0:T(8,128)}, f32[128,256]{1,0:T(8,128)S(1)}, u32[]{:S(2)}) copy-start(f32[128,256]{1,0:T(8,128)S(1)} %get-tuple-element.39.state_ref.refs_4_) | copy-start | bytes 393220
  10.8 8.4 %copy-start.13 = (f32[1,1,5120]{2,1,0:T(1,128)S(1)}, f32[1,1,5120]{2,1,0:T(1,128)}, u32[]{:S(2)}) copy-start(f32[1,1,5120]{2,1,0:T(1,128)} %param.15) | copy-start | bytes 61444
  10.8 15.9 %collective-permute-start.3 = (f32[128,256]{1,0:T(8,128)S(1)}, f32[128,256]{1,0:T(8,128)S(1)}, u32[]{:S(2)}, u32[]{:S(2)}) collective-permute-start(f32[128,256]{1,0:T(8,128)S(1)} %get-tuple-element.39.state_ref.refs_4_), channel_id=1, source_target_pairs={{24,0},{25,1},{26,2},{27,3},{28,4},{29,5},{30,6},{31,7}} | collective-permute-start | bytes 393224 | tf_op jit(solution)/shard_map/ppermute | solution.py:416
  12.2 54.0 %collective-permute-start.8 = (f32[128,256]{1,0:T(8,128)S(1)}, f32[128,256]{1,0:T(8,128)S(1)}, u32[]{:S(2)}, u32[]{:S(2)}) collective-permute-start(f32[128,256]{1,0:T(8,128)S(1)} %get-tuple-element.39.state_ref.refs_4_), channel_id=1, source_target_pairs={{16,0},{24,8},{17,1},{25,9},{18,2},{26,10},{19,3},{27,11},{20,4},{... | collective-permute-start | bytes 393224 | tf_op jit(solution)/shard_map/ppermute | solution.py:416
  13.5 52.7 %all-to-all-start = ((bf16[8,16,5248]{2,1,0:T(8,128)(2,1)}), bf16[8,16,5248]{2,1,0:T(8,128)(2,1)S(1)}, u32[]{:S(2)}, u32[]{:S(2)}) async-start(bf16[8,16,5248]{2,1,0:T(8,128)(2,1)} %bitcast.34), calls=%async_computation | async-start | bytes 2686976 | tf_op jit(solution)/shard_map/all_to_all | solution.py:406
  20.8 11.6 %copy-start.15 = (bf16[1,1,2,256,8]{3,4,2,1,0:T(8,128)(2,1)S(1)}, bf16[1,1,2,256,8]{3,4,2,1,0:T(8,128)(2,1)}, u32[]{:S(2)}) copy-start(bf16[1,1,2,256,8]{3,4,2,1,0:T(8,128)(2,1)} %param.14) | copy-start | bytes 24580
  20.9 45.3 %collective-permute-start.7 = (f32[128,256]{1,0:T(8,128)S(1)}, f32[128,256]{1,0:T(8,128)S(1)}, u32[]{:S(2)}, u32[]{:S(2)}) collective-permute-start(f32[128,256]{1,0:T(8,128)S(1)} %get-tuple-element.39.state_ref.refs_4_), channel_id=1, source_target_pairs={{8,0},{16,8},{24,16},{9,1},{17,9},{25,17},{10,2},{18,10},{26,18},{... | collective-permute-start | bytes 393224 | tf_op jit(solution)/shard_map/ppermute | solution.py:416
  26.7 57.3 %copy-start.4 = (f32[128,256]{1,0:T(8,128)}, f32[128,256]{1,0:T(8,128)S(1)}, u32[]{:S(2)}) copy-start(f32[128,256]{1,0:T(8,128)S(1)} %collective-permute-done.3.rest_2_.refs_7_) | copy-start | bytes 393220
  26.7 32.7 %collective-permute-start.6 = (bf16[3,160,640]{2,1,0:T(8,128)(2,1)}, bf16[3,160,640]{2,1,0:T(8,128)(2,1)}, u32[]{:S(2)}, u32[]{:S(2)}) collective-permute-start(bf16[3,160,640]{2,1,0:T(8,128)(2,1)} %join.2.refs_0_), channel_id=1, source_target_pairs={{0,6},{1,7},{2,4},{3,5},{4,2},{5,3},{6,0},{7,1},{8,14},{9,15},{10,... | collective-permute-start | bytes 1843208 | tf_op jit(solution)/shard_map/ppermute | solution.py:411
  30.0 32.7 %collective-permute-start.5 = (bf16[3,160,640]{2,1,0:T(8,128)(2,1)}, bf16[3,160,640]{2,1,0:T(8,128)(2,1)}, u32[]{:S(2)}, u32[]{:S(2)}) collective-permute-start(bf16[3,160,640]{2,1,0:T(8,128)(2,1)} %join.2.refs_0_), channel_id=1, source_target_pairs={{0,4},{1,5},{2,6},{3,7},{4,0},{5,1},{6,2},{7,3},{8,12},{9,13},{10,... | collective-permute-start | bytes 1843208 | tf_op jit(solution)/shard_map/ppermute | solution.py:411
  30.6 32.3 %collective-permute-start.4 = (bf16[3,160,640]{2,1,0:T(8,128)(2,1)}, bf16[3,160,640]{2,1,0:T(8,128)(2,1)}, u32[]{:S(2)}, u32[]{:S(2)}) collective-permute-start(bf16[3,160,640]{2,1,0:T(8,128)(2,1)} %join.2.refs_0_), channel_id=1, source_target_pairs={{0,2},{1,3},{2,0},{3,1},{4,6},{5,7},{6,4},{7,5},{8,10},{9,11},{10,... | collective-permute-start | bytes 1843208 | tf_op jit(solution)/shard_map/ppermute | solution.py:411
  66.2 17.8 %copy-start.5 = (f32[128,256]{1,0:T(8,128)}, f32[128,256]{1,0:T(8,128)S(1)}, u32[]{:S(2)}) copy-start(f32[128,256]{1,0:T(8,128)S(1)} %collective-permute-done.8.rest_1_.refs_6_) | copy-start | bytes 393220
  66.2 17.8 %copy-start.6 = (f32[128,256]{1,0:T(8,128)}, f32[128,256]{1,0:T(8,128)S(1)}, u32[]{:S(2)}) copy-start(f32[128,256]{1,0:T(8,128)S(1)} %collective-permute-done.7.rest_0_.refs_5_) | copy-start | bytes 393220
  66.2 1.1 copy-start.8
  66.2 5.3 %collective-permute-start.9 = (bf16[4,3,160,640]{3,2,1,0:T(8,128)(2,1)}, bf16[4,3,160,640]{3,2,1,0:T(8,128)(2,1)}, u32[]{:S(2)}, u32[]{:S(2)}) collective-permute-start(bf16[4,3,160,640]{3,2,1,0:T(8,128)(2,1)} %join.3.router_ref.near_ref), channel_id=1, source_target_pairs={{0,1},{1,0},{2,3},{3,2},{4,5},{5,4},{6,7},{7,6},{8,9},{9,8},{10,11... | collective-permute-start | bytes 7372808 | tf_op jit(solution)/shard_map/ppermute | solution.py:411
  85.1 12.0 %copy-start.7 = (bf16[128,128]{1,0:T(8,128)(2,1)}, bf16[128,128]{1,0:T(8,128)(2,1)S(1)}, u32[]{:S(2)}) copy-start(bf16[128,128]{1,0:T(8,128)(2,1)S(1)} %responses.1.refs_0_) | copy-start | bytes 98308
  85.1 10.1 %collective-permute-start.12 = (bf16[128,128]{1,0:T(8,128)(2,1)S(1)}, bf16[128,128]{1,0:T(8,128)(2,1)S(1)}, u32[]{:S(2)}, u32[]{:S(2)}) collective-permute-start(bf16[128,128]{1,0:T(8,128)(2,1)S(1)} %responses.1.refs_0_), channel_id=1, source_target_pairs={{24,0},{25,1},{26,2},{27,3},{28,4},{29,5},{30,6},{31,7}} | collective-permute-start | bytes 98312 | tf_op jit(solution)/shard_map/ppermute | solution.py:416
  86.4 8.8 %collective-permute-start.11 = (bf16[128,128]{1,0:T(8,128)(2,1)S(1)}, bf16[128,128]{1,0:T(8,128)(2,1)S(1)}, u32[]{:S(2)}, u32[]{:S(2)}) collective-permute-start(bf16[128,128]{1,0:T(8,128)(2,1)S(1)} %responses.1.refs_0_), channel_id=1, source_target_pairs={{16,0},{24,8},{17,1},{25,9},{18,2},{26,10},{19,3},{27,11},{20,4},{... | collective-permute-start | bytes 98312 | tf_op jit(solution)/shard_map/ppermute | solution.py:416
  87.7 9.3 %collective-permute-start.10 = (bf16[128,128]{1,0:T(8,128)(2,1)S(1)}, bf16[128,128]{1,0:T(8,128)(2,1)S(1)}, u32[]{:S(2)}, u32[]{:S(2)}) collective-permute-start(bf16[128,128]{1,0:T(8,128)(2,1)S(1)} %responses.1.refs_0_), channel_id=1, source_target_pairs={{8,0},{16,8},{24,16},{9,1},{17,9},{25,17},{10,2},{18,10},{26,18},{... | collective-permute-start | bytes 98312 | tf_op jit(solution)/shard_map/ppermute | solution.py:416
  95.2 1.8 %copy-start.10 = (bf16[128,128]{1,0:T(8,128)(2,1)}, bf16[128,128]{1,0:T(8,128)(2,1)S(1)}, u32[]{:S(2)}) copy-start(bf16[128,128]{1,0:T(8,128)(2,1)S(1)} %collective-permute-done.12.refs_3_) | copy-start | bytes 98308
  95.2 1.8 %copy-start.11 = (bf16[128,128]{1,0:T(8,128)(2,1)}, bf16[128,128]{1,0:T(8,128)(2,1)S(1)}, u32[]{:S(2)}) copy-start(bf16[128,128]{1,0:T(8,128)(2,1)S(1)} %collective-permute-done.11.refs_2_) | copy-start | bytes 98308
  97.1 0.6 copy-start.12
  101.2 9.6 %all-to-all-start.2 = ((bf16[8,16,768]{2,1,0:T(8,128)(2,1)}), bf16[8,16,768]{2,1,0:T(8,128)(2,1)S(1)}, u32[]{:S(2)}, u32[]{:S(2)}) async-start(bf16[8,16,768]{2,1,0:T(8,128)(2,1)} %bitcast.49), calls=%async_computation.2 | async-start | bytes 393216 | tf_op jit(solution)/shard_map/all_to_all | solution.py:406
  110.8 0.7 copy-start.9
  120.1 37.0 %copy-start.14 = (f32[8,640]{1,0:T(8,128)S(1)}, f32[8,640]{1,0:T(8,128)}, u32[]{:S(2)}) copy-start(f32[8,640]{1,0:T(8,128)} %get-tuple-element.48) | copy-start | bytes 61444

commit v9 on v8

--- a/solution.py
+++ b/solution.py
@@ -419,18 +419,59 @@
 
 
 def join_kernel(*refs):
-    *part_refs, out_ref = refs
-    for k, ref in enumerate(part_refs):
-        out_ref[k] = ref[...]
+    *part_refs, out_ref, held_ref, in_sems, out_sems = refs
+    count = len(part_refs)
+    into = [
+        pltpu.make_async_copy(part_refs[k], held_ref.at[k], in_sems.at[k]) for k in range(count)
+    ]
+    out = [
+        pltpu.make_async_copy(held_ref.at[k], out_ref.at[k], out_sems.at[k]) for k in range(count)
+    ]
+    for copy in into:
+        copy.start()
+    for k in range(count):
+        into[k].wait()
+        out[k].start()
+    for copy in out:
+        copy.wait()
 
 
 def join(parts):
+    count = len(parts)
+    joined = (count,) + parts[0].shape
+    anywhere = pl.BlockSpec(memory_space=pl.ANY)
     return pl.pallas_call(
         join_kernel,
-        out_shape=jax.ShapeDtypeStruct((len(parts),) + parts[0].shape, parts[0].dtype),
+        in_specs=[anywhere] * count,
+        out_specs=anywhere,
+        out_shape=jax.ShapeDtypeStruct(joined, parts[0].dtype),
+        scratch_shapes=[
+            pltpu.VMEM(joined, parts[0].dtype),
+            pltpu.SemaphoreType.DMA((count,)),
+            pltpu.SemaphoreType.DMA((count,)),
+        ],
         compiler_params=params(60),
         name="join",
     )(*parts)
+
+
+def take_kernel(place_ref, value_ref, out_ref):
+    out_ref[...] = value_ref[...]
+
+
+def take(value, row, column, shape):
+    return pl.pallas_call(
+        take_kernel,
+        grid_spec=pltpu.PrefetchScalarGridSpec(
+            num_scalar_prefetch=1,
+            grid=(1,),
+            in_specs=[pl.BlockSpec(shape, lambda i, t: (t[0], t[1]))],
+            out_specs=pl.BlockSpec(shape, lambda i, t: (0, 0)),
+        ),
+        out_shape=jax.ShapeDtypeStruct(shape, value.dtype),
+        compiler_params=params(60),
+        name="take",
+    )(jnp.stack([row, column]).astype(jnp.int32), value)
 
 
 def exchange_near(shares):
@@ -462,11 +503,7 @@
     sharers = experts // parts
     part_width = width // parts
     share_rows = routed // sharers
-    own_share = lax.dynamic_slice(
-        router_t,
-        ((place % sharers) * share_rows, (place // sharers) * part_width),
-        (share_rows, part_width),
-    )
+    own_share = take(router_t, place % sharers, place // sharers, (share_rows, part_width))
     shares = join(pass_down(own_share, layers))
     twist = jnp.full((1,), place if direct else 0, jnp.int32)
 

time: 159 us -> 160 us (level)
  local copies, waits for them, and re-layouts: 10 us -> 8.31 us
    dynamic_slice x1 -> x0, local copies, waits for them, and re-layouts: 1.73 us -> none  [on_device(): lax.dynamic_slice(router_t, (place % sharers * share_rows, place // share...]
    pallas_call x2 -> x3, Pallas kernels: 5.31 us -> 6.79 us  [the longest x2 4.5 us: join(): pl.pallas_call(join_kernel, in_specs=[anywhere] * count, out_specs=anywhe...]
    unnamed x37 -> x39, local copies, waits for them, and re-layouts: 4.78 us -> 4.78 us
where the time goes in v9:
time: 160 us; the launch traced here: 159 us
  Pallas kernels  98.4 us (62%)
  starting transfers between devices  24.4 us (15%)
  waiting for transfers between devices  15.1 us (9%)
  blocking collectives  8.81 us (6%)
  local copies, waits for them, and re-layouts  8.31 us (5%)
  matrix products  2.08 us (1%)
    pallas_call x1, Pallas kernels, on_device(): pl.pallas_call(functools.partial(book_kernel, unroll), grid=(inner // blo...  35.3 us
    pallas_call x1, Pallas kernels, decode(): pl.pallas_call(decode_kernel, grid=(blocks,), in_specs=[pl.BlockSpec((boo...  26.3 us
    ppermute x9, waiting for transfers between devices, pass_down(): lax.ppermute(value, 'pipe', [(p, p - s) for p in range(s, layers)])  11.8 us
    ppermute x9, starting transfers between devices, pass_down(): lax.ppermute(value, 'pipe', [(p, p - s) for p in range(s, layers)])  11.7 us
    all_to_all x1, blocking collectives, exchange(): lax.all_to_all(value, 'expert', split_axis=0, concat_axis=0, tiled=True)  8.81 us
    all_to_all x2, starting transfers between devices, exchange(): lax.all_to_all(value, 'expert', split_axis=0, concat_axis=0, tiled=True)  8.75 us
    pallas_call x1, Pallas kernels, on_device(): by_columns(slots_kernel, [columns(rows), pl.BlockSpec((rows, LANES), lamb...  8.64 us
    pallas_call x2, Pallas kernels, score(): pl.pallas_call(kernel, grid_spec=pltpu.PrefetchScalarGridSpec(num_scalar_...  7.86 us
  transfers between devices with their start and end apart: 15, of which 6 were waited for; matrix products, arithmetic and copies ran while one was open for 3% of the time, Pallas kernels for 28%

profile of v9, /device:TPU:0, one launch (start us, length us, event | category | flops | bytes accessed | tf_op | source)
XLA Modules:
  0.0 159.3 jit_solution(5852457629463484555)
XLA Ops:
  1.2 2.3 %take.1 = bf16[160,640]{1,0:T(8,128)(2,1)} custom-call(s32[2]{0:T(128)} %pad_add_fusion.place_ref, bf16[160,5120]{1,0:T(8,128)(2,1)} %bitcast.36), custom_call_target="tpu_custom_call" | custom-call | tf_op jit(solution)/shard_map/take/pallas_call | solution.py:463
  3.5 1.4 collective-permute-start.2
  5.0 1.3 collective-permute-start.1
  6.3 1.3 collective-permute-start
  7.6 2.1 %fusion.logits_ref = f32[128,160]{1,0:T(8,128)S(1)} fusion(bf16[1,5120,160]{1,2,0:T(8,128)(2,1)} %param.10, bf16[1,128,5120]{2,1,0:T(8,128)(2,1)S(1)} %copy-done), kind=kOutput, calls=%fused_computation | convolution fusion | flops 209715200 | bytes 3031040 | tf_op jit(solution)/shard_map/dot_general | solution.py:28
  9.8 1.1 prepare.1
  10.8 1.1 copy-done.2
  11.9 1.3 collective-permute-start.3
  13.2 1.3 collective-permute-start.8
  14.5 5.2 %all-to-all-start = ((bf16[8,16,5248]{2,1,0:T(8,128)(2,1)}), bf16[8,16,5248]{2,1,0:T(8,128)(2,1)S(1)}, u32[]{:S(2)}, u32[]{:S(2)}) async-start(bf16[8,16,5248]{2,1,0:T(8,128)(2,1)} %bitcast.30), calls=%async_computation | async-start | bytes 2686976 | tf_op jit(solution)/shard_map/all_to_all | solution.py:406
  21.9 1.3 collective-permute-start.7
  23.2 1.9 %collective-permute-done.1.refs_1_ = bf16[160,640]{1,0:T(8,128)(2,1)} collective-permute-done((bf16[160,640]{1,0:T(8,128)(2,1)}, bf16[160,640]{1,0:T(8,128)(2,1)}, u32[]{:S(2)}, u32[]{:S(2)}) %collective-permute-start.1) | collective-permute-done | bytes 204832 | tf_op jit(solution)/shard_map/ppermute | solution.py:416
  25.1 1.9 %join.2.refs_0_ = bf16[3,160,640]{2,1,0:T(8,128)(2,1)} custom-call(bf16[160,640]{1,0:T(8,128)(2,1)} %collective-permute-done.refs_0_, bf16[160,640]{1,0:T(8,128)(2,1)} %collective-permute-done.1.refs_1_, bf16[160,640]{1,0:T(8,128)(2,1)} %collective-permute-done.2.refs_2_), custom_call_target="tpu_custom_call" | custom-call | tf_op jit(solution)/shard_map/join/pallas_call | solution.py:443
  27.9 3.3 %collective-permute-start.6 = (bf16[3,160,640]{2,1,0:T(8,128)(2,1)}, bf16[3,160,640]{2,1,0:T(8,128)(2,1)S(1)}, u32[]{:S(2)}, u32[]{:S(2)}) collective-permute-start(bf16[3,160,640]{2,1,0:T(8,128)(2,1)} %join.2.refs_0_), channel_id=1, source_target_pairs={{0,6},{1,7},{2,4},{3,5},{4,2},{5,3},{6,0},{7,1},{8,14},{9,15},{10,... | collective-permute-start | bytes 1843208 | tf_op jit(solution)/shard_map/ppermute | solution.py:411
  31.8 1.8 %order.1.order_ref = bf16[1024,1024]{1,0:T(8,128)(2,1)} custom-call(bf16[72,768]{1,0:T(8,128)(2,1)} %bitcast.43), custom_call_target="tpu_custom_call" | custom-call | tf_op jit(solution)/shard_map/order/pallas_call | solution.py:538
  34.3 26.3 %decode.1 = (f32[8,128,640]{2,1,0:T(8,128)}, bf16[128,5120]{1,0:T(8,128)(2,1)}) custom-call(s32[2,768,640]{2,1,0:T(8,128)} %bitcast.38, bf16[2,2,8,16,128]{4,3,2,1,0:T(8,128)(2,1)} %broadcast_in_dim.16.table_ref, bf16[72,768]{1,0:T(8,128)(2,1)} %bitcast.44, f32[8,640]{1,0:T(8,128)} %bitcast.47, bf16[1024,1024]{1,0:T(8,128)(2,1)} %order.1.order_ref), custom_call_target="tpu_custom_call" | custom-call | flops 30000001024 | bytes 10000000 | tf_op jit(solution)/shard_map/decode/pallas_call | solution.py:546
  60.6 3.2 %collective-permute-done.5.refs_2_ = bf16[3,160,640]{2,1,0:T(8,128)(2,1)} collective-permute-done((bf16[3,160,640]{2,1,0:T(8,128)(2,1)}, bf16[3,160,640]{2,1,0:T(8,128)(2,1)}, u32[]{:S(2)}, u32[]{:S(2)}) %collective-permute-start.5) | collective-permute-done | bytes 614432 | tf_op jit(solution)/shard_map/ppermute | solution.py:411
  63.9 2.6 %join.3.router_ref.near_ref = bf16[4,3,160,640]{3,2,1,0:T(8,128)(2,1)} custom-call(bf16[3,160,640]{2,1,0:T(8,128)(2,1)} %join.2.refs_0_, bf16[3,160,640]{2,1,0:T(8,128)(2,1)} %collective-permute-done.4.refs_1_, bf16[3,160,640]{2,1,0:T(8,128)(2,1)} %collective-permute-done.5.refs_2_, bf16[3,160,640]{2,1,0:T(8,128)(2,1)} %copy-done.10), custom_call_target="tpu_custom_call" | custom-call | tf_op jit(solution)/shard_map/join/pallas_call | solution.py:443
  67.7 4.2 %scores.2 = (f32[480,128]{1,0:T(8,128)}, f32[128,128]{1,0:T(8,128)}) custom-call(s32[1]{0:T(128)} %bitcast.twist_ref, bf16[128,5120]{1,0:T(8,128)(2,1)} %get-tuple-element.34.out_ref, bf16[128,5248]{1,0:T(8,128)(2,1)} %bitcast.33, bf16[4,3,160,640]{3,2,1,0:T(8,128)(2,1)} %join.3.router_ref.near_ref), custom_call_target="tpu_custom_call" | custom-call | tf_op jit(solution)/shard_map/scores/pallas_call | solution.py:606
  71.9 3.7 %scores.3 = bf16[128,512]{1,0:T(8,128)(2,1)} custom-call(s32[1]{0:T(128)} %bitcast.twist_ref, bf16[128,5120]{1,0:T(8,128)(2,1)} %get-tuple-element.34.out_ref, bf16[4,3,160,640]{3,2,1,0:T(8,128)(2,1)} %collective-permute-done.9.router_ref.far_ref, f32[480,128]{1,0:T(8,128)} %get-tuple-element.37.total_ref, f32[128,128]{1,0:T(8,128)} %get-tuple-element.38.base_ref), custom_call_target="tpu_custom_call" | custom-call | tf_op jit(solution)/shard_map/scores/pallas_call | solution.py:606
  75.5 8.8 %all_to_all.34 = bf16[8,16,512]{2,1,0:T(8,128)(2,1)S(1)} all-to-all(bf16[8,16,512]{2,1,0:T(8,128)(2,1)} %bitcast.42), channel_id=1, replica_groups=mesh['pipe'=4,'expert'=8] {'expert'}, dimensions={0} | all-to-all | bytes 262144 | tf_op jit(solution)/shard_map/all_to_all | solution.py:406
  84.4 1.1 responses.1.refs_0_
  85.5 1.3 collective-permute-start.12
  86.8 1.3 collective-permute-start.11
  88.1 1.3 collective-permute-start.10
  89.4 6.3 %collective-permute-done.12.refs_3_ = bf16[128,128]{1,0:T(8,128)(2,1)S(1)} collective-permute-done((bf16[128,128]{1,0:T(8,128)(2,1)S(1)}, bf16[128,128]{1,0:T(8,128)(2,1)S(1)}, u32[]{:S(2)}, u32[]{:S(2)}) %collective-permute-start.12) | collective-permute-done | bytes 32800 | tf_op jit(solution)/shard_map/ppermute | solution.py:416
  95.7 2.6 %collective-permute-done.10.refs_1_ = bf16[128,128]{1,0:T(8,128)(2,1)S(1)} collective-permute-done((bf16[128,128]{1,0:T(8,128)(2,1)S(1)}, bf16[128,128]{1,0:T(8,128)(2,1)S(1)}, u32[]{:S(2)}, u32[]{:S(2)}) %collective-permute-start.10) | collective-permute-done | bytes 32800 | tf_op jit(solution)/shard_map/ppermute | solution.py:416
  98.9 3.5 %chain.1 = (bf16[128,160]{1,0:T(8,128)(2,1)}, bf16[128,768]{1,0:T(8,128)(2,1)}, bf16[128,768]{1,0:T(8,128)(2,1)}) custom-call(bf16[128,128]{1,0:T(8,128)(2,1)} %copy-done.7, bf16[128,128]{1,0:T(8,128)(2,1)} %copy-done.13, bf16[128,128]{1,0:T(8,128)(2,1)} %copy-done.12, bf16[128,128]{1,0:T(8,128)(2,1)} %copy-done.11, f32[128,256]{1,0:T(8,128)} %copy-done.3, ...), custom_call_target="tpu_custom_call" | custom-call | tf_op jit(solution)/shard_map/chain/pallas_call | solution.py:640
  102.5 3.6 %all-to-all-start.2 = ((bf16[8,16,768]{2,1,0:T(8,128)(2,1)}), bf16[8,16,768]{2,1,0:T(8,128)(2,1)S(1)}, u32[]{:S(2)}, u32[]{:S(2)}) async-start(bf16[8,16,768]{2,1,0:T(8,128)(2,1)} %bitcast.46), calls=%async_computation.2 | async-start | bytes 393216 | tf_op jit(solution)/shard_map/all_to_all | solution.py:406
  106.0 6.0 %finish.1 = bf16[128,5120]{1,0:T(8,128)(2,1)} custom-call(s32[1]{0:T(128)} %bitcast.twist_ref, bf16[128,5120]{1,0:T(8,128)(2,1)} %grad_ref.3, bf16[128,768]{1,0:T(8,128)(2,1)} %get-tuple-element.43.later_ref, bf16[128,160]{1,0:T(8,128)(2,1)} %get-tuple-element.44.own_ref, bf16[160,5120]{1,0:T(8,128)(2,1)} %bitcast.37, ...), custom_call_target="tpu_custom_call" | custom-call | tf_op jit(solution)/shard_map/finish/pallas_call | solution.py:653
  112.7 8.6 %slot_grads.1 = (bf16[8,128,640]{2,1,0:T(8,128)(2,1)}, f32[8,640]{1,0:T(8,128)}) custom-call(s32[1]{0:T(128)} %bitcast.twist_ref, bf16[128,5248]{1,0:T(8,128)(2,1)} %bitcast.34, bf16[128,5248]{1,0:T(8,128)(2,1)} %bitcast.35, bf16[128,768]{1,0:T(8,128)(2,1)} %bitcast.41, bf16[4,3,160,640]{3,2,1,0:T(8,128)(2,1)} %join.3.router_ref.near_ref, ...), custom_call_target="tpu_custom_call" | custom-call | tf_op jit(solution)/shard_map/slot_grads/pallas_call | solution.py:669
  121.4 35.3 %book_grads.1 = f32[2,48,48]{2,1,0:T(8,128)} custom-call(bf16[72,768]{1,0:T(8,128)(2,1)} %bitcast.45, bf16[8,128,640]{2,1,0:T(8,128)(2,1)} %get-tuple-element.47.slots_ref, f32[8,640]{1,0:T(8,128)} %bitcast.48, s32[2,768,640]{2,1,0:T(8,128)} %bitcast.39), custom_call_target="tpu_custom_call" | custom-call | tf_op jit(solution)/shard_map/book_grads/pallas_call | solution.py:691
  (61 shorter events, 10.2 us)
Async XLA Ops:
  0.6 6.9 %copy-start = (bf16[1,128,5120]{2,1,0:T(8,128)(2,1)S(1)}, bf16[1,128,5120]{2,1,0:T(8,128)(2,1)}, u32[]{:S(2)}) copy-start(bf16[1,128,5120]{2,1,0:T(8,128)(2,1)} %param.9) | copy-start | bytes 3932164
  3.5 6.1 %copy-start.17 = (s32[1,128,6]{1,0,2:T(1,128)S(1)}, s32[1,128,6]{1,0,2:T(1,128)}, u32[]{:S(2)}) copy-start(s32[1,128,6]{1,0,2:T(1,128)} %param.11) | copy-start | bytes 9220
  3.5 6.2 %copy-start.1 = (bf16[128,5120]{1,0:T(8,128)(2,1)S(1)}, bf16[128,5120]{1,0:T(8,128)(2,1)}, u32[]{:S(2)}) copy-start(bf16[128,5120]{1,0:T(8,128)(2,1)} %grad_ref.3) | copy-start | bytes 3932164
  3.5 18.3 %collective-permute-start.2 = (bf16[160,640]{1,0:T(8,128)(2,1)}, bf16[160,640]{1,0:T(8,128)(2,1)}, u32[]{:S(2)}, u32[]{:S(2)}) collective-permute-start(bf16[160,640]{1,0:T(8,128)(2,1)} %take.1), channel_id=1, source_target_pairs={{24,0},{25,1},{26,2},{27,3},{28,4},{29,5},{30,6},{31,7}} | collective-permute-start | bytes 614408 | tf_op jit(solution)/shard_map/ppermute | solution.py:416
  5.0 20.2 %collective-permute-start.1 = (bf16[160,640]{1,0:T(8,128)(2,1)}, bf16[160,640]{1,0:T(8,128)(2,1)}, u32[]{:S(2)}, u32[]{:S(2)}) collective-permute-start(bf16[160,640]{1,0:T(8,128)(2,1)} %take.1), channel_id=1, source_target_pairs={{16,0},{24,8},{17,1},{25,9},{18,2},{26,10},{19,3},{27,11},{20,4},{... | collective-permute-start | bytes 614408 | tf_op jit(solution)/shard_map/ppermute | solution.py:416
  6.3 18.9 %collective-permute-start = (bf16[160,640]{1,0:T(8,128)(2,1)}, bf16[160,640]{1,0:T(8,128)(2,1)}, u32[]{:S(2)}, u32[]{:S(2)}) collective-permute-start(bf16[160,640]{1,0:T(8,128)(2,1)} %take.1), channel_id=1, source_target_pairs={{8,0},{16,8},{24,16},{9,1},{17,9},{25,17},{10,2},{18,10},{26,18},{... | collective-permute-start | bytes 614408 | tf_op jit(solution)/shard_map/ppermute | solution.py:416
  10.8 1.1 copy-start.2
  11.9 72.4 %copy-start.3 = (f32[128,256]{1,0:T(8,128)}, f32[128,256]{1,0:T(8,128)S(1)}, u32[]{:S(2)}) copy-start(f32[128,256]{1,0:T(8,128)S(1)} %get-tuple-element.39.state_ref.refs_4_) | copy-start | bytes 393220
  11.9 15.9 %collective-permute-start.3 = (f32[128,256]{1,0:T(8,128)S(1)}, f32[128,256]{1,0:T(8,128)S(1)}, u32[]{:S(2)}, u32[]{:S(2)}) collective-permute-start(f32[128,256]{1,0:T(8,128)S(1)} %get-tuple-element.39.state_ref.refs_4_), channel_id=1, source_target_pairs={{24,0},{25,1},{26,2},{27,3},{28,4},{29,5},{30,6},{31,7}} | collective-permute-start | bytes 393224 | tf_op jit(solution)/shard_map/ppermute | solution.py:416
  13.2 53.3 %collective-permute-start.8 = (f32[128,256]{1,0:T(8,128)S(1)}, f32[128,256]{1,0:T(8,128)S(1)}, u32[]{:S(2)}, u32[]{:S(2)}) collective-permute-start(f32[128,256]{1,0:T(8,128)S(1)} %get-tuple-element.39.state_ref.refs_4_), channel_id=1, source_target_pairs={{16,0},{24,8},{17,1},{25,9},{18,2},{26,10},{19,3},{27,11},{20,4},{... | collective-permute-start | bytes 393224 | tf_op jit(solution)/shard_map/ppermute | solution.py:416
  14.5 5.7 %copy-start.14 = (f32[1,1,5120]{2,1,0:T(1,128)S(1)}, f32[1,1,5120]{2,1,0:T(1,128)}, u32[]{:S(2)}) copy-start(f32[1,1,5120]{2,1,0:T(1,128)} %param.15) | copy-start | bytes 61444
  14.5 52.0 %all-to-all-start = ((bf16[8,16,5248]{2,1,0:T(8,128)(2,1)}), bf16[8,16,5248]{2,1,0:T(8,128)(2,1)S(1)}, u32[]{:S(2)}, u32[]{:S(2)}) async-start(bf16[8,16,5248]{2,1,0:T(8,128)(2,1)} %bitcast.30), calls=%async_computation | async-start | bytes 2686976 | tf_op jit(solution)/shard_map/all_to_all | solution.py:406
  21.9 44.7 %collective-permute-start.7 = (f32[128,256]{1,0:T(8,128)S(1)}, f32[128,256]{1,0:T(8,128)S(1)}, u32[]{:S(2)}, u32[]{:S(2)}) collective-permute-start(f32[128,256]{1,0:T(8,128)S(1)} %get-tuple-element.39.state_ref.refs_4_), channel_id=1, source_target_pairs={{8,0},{16,8},{24,16},{9,1},{17,9},{25,17},{10,2},{18,10},{26,18},{... | collective-permute-start | bytes 393224 | tf_op jit(solution)/shard_map/ppermute | solution.py:416
  27.0 6.6 %copy-start.16 = (bf16[1,1,2,256,8]{3,4,2,1,0:T(8,128)(2,1)S(1)}, bf16[1,1,2,256,8]{3,4,2,1,0:T(8,128)(2,1)}, u32[]{:S(2)}) copy-start(bf16[1,1,2,256,8]{3,4,2,1,0:T(8,128)(2,1)} %param.14) | copy-start | bytes 24580
  27.9 56.5 %copy-start.4 = (f32[128,256]{1,0:T(8,128)}, f32[128,256]{1,0:T(8,128)S(1)}, u32[]{:S(2)}) copy-start(f32[128,256]{1,0:T(8,128)S(1)} %collective-permute-done.3.rest_2_.refs_7_) | copy-start | bytes 393220
  27.9 32.7 %collective-permute-start.6 = (bf16[3,160,640]{2,1,0:T(8,128)(2,1)}, bf16[3,160,640]{2,1,0:T(8,128)(2,1)S(1)}, u32[]{:S(2)}, u32[]{:S(2)}) collective-permute-start(bf16[3,160,640]{2,1,0:T(8,128)(2,1)} %join.2.refs_0_), channel_id=1, source_target_pairs={{0,6},{1,7},{2,4},{3,5},{4,2},{5,3},{6,0},{7,1},{8,14},{9,15},{10,... | collective-permute-start | bytes 1843208 | tf_op jit(solution)/shard_map/ppermute | solution.py:411
  31.2 32.6 %collective-permute-start.5 = (bf16[3,160,640]{2,1,0:T(8,128)(2,1)}, bf16[3,160,640]{2,1,0:T(8,128)(2,1)}, u32[]{:S(2)}, u32[]{:S(2)}) collective-permute-start(bf16[3,160,640]{2,1,0:T(8,128)(2,1)} %join.2.refs_0_), channel_id=1, source_target_pairs={{0,4},{1,5},{2,6},{3,7},{4,0},{5,1},{6,2},{7,3},{8,12},{9,13},{10,... | collective-permute-start | bytes 1843208 | tf_op jit(solution)/shard_map/ppermute | solution.py:411
  31.7 32.2 %collective-permute-start.4 = (bf16[3,160,640]{2,1,0:T(8,128)(2,1)}, bf16[3,160,640]{2,1,0:T(8,128)(2,1)}, u32[]{:S(2)}, u32[]{:S(2)}) collective-permute-start(bf16[3,160,640]{2,1,0:T(8,128)(2,1)} %join.2.refs_0_), channel_id=1, source_target_pairs={{0,2},{1,3},{2,0},{3,1},{4,6},{5,7},{6,4},{7,5},{8,10},{9,11},{10,... | collective-permute-start | bytes 1843208 | tf_op jit(solution)/shard_map/ppermute | solution.py:411
  60.6 3.3 %copy-start.10 = (bf16[3,160,640]{2,1,0:T(8,128)(2,1)}, bf16[3,160,640]{2,1,0:T(8,128)(2,1)S(1)}, u32[]{:S(2)}) copy-start(bf16[3,160,640]{2,1,0:T(8,128)(2,1)S(1)} %collective-permute-done.6.refs_3_) | copy-start | bytes 1843204
  66.5 17.8 %copy-start.5 = (f32[128,256]{1,0:T(8,128)}, f32[128,256]{1,0:T(8,128)S(1)}, u32[]{:S(2)}) copy-start(f32[128,256]{1,0:T(8,128)S(1)} %collective-permute-done.8.rest_1_.refs_6_) | copy-start | bytes 393220
  66.5 17.8 %copy-start.6 = (f32[128,256]{1,0:T(8,128)}, f32[128,256]{1,0:T(8,128)S(1)}, u32[]{:S(2)}) copy-start(f32[128,256]{1,0:T(8,128)S(1)} %collective-permute-done.7.rest_0_.refs_5_) | copy-start | bytes 393220
  66.6 1.1 copy-start.8
  66.6 5.3 %collective-permute-start.9 = (bf16[4,3,160,640]{3,2,1,0:T(8,128)(2,1)}, bf16[4,3,160,640]{3,2,1,0:T(8,128)(2,1)}, u32[]{:S(2)}, u32[]{:S(2)}) collective-permute-start(bf16[4,3,160,640]{3,2,1,0:T(8,128)(2,1)} %join.3.router_ref.near_ref), channel_id=1, source_target_pairs={{0,1},{1,0},{2,3},{3,2},{4,5},{5,4},{6,7},{7,6},{8,9},{9,8},{10,11... | collective-permute-start | bytes 7372808 | tf_op jit(solution)/shard_map/ppermute | solution.py:411
  85.4 12.9 %copy-start.7 = (bf16[128,128]{1,0:T(8,128)(2,1)}, bf16[128,128]{1,0:T(8,128)(2,1)S(1)}, u32[]{:S(2)}) copy-start(bf16[128,128]{1,0:T(8,128)(2,1)S(1)} %responses.1.refs_0_) | copy-start | bytes 98308
  85.5 10.2 %collective-permute-start.12 = (bf16[128,128]{1,0:T(8,128)(2,1)S(1)}, bf16[128,128]{1,0:T(8,128)(2,1)S(1)}, u32[]{:S(2)}, u32[]{:S(2)}) collective-permute-start(bf16[128,128]{1,0:T(8,128)(2,1)S(1)} %responses.1.refs_0_), channel_id=1, source_target_pairs={{24,0},{25,1},{26,2},{27,3},{28,4},{29,5},{30,6},{31,7}} | collective-permute-start | bytes 98312 | tf_op jit(solution)/shard_map/ppermute | solution.py:416
  86.8 9.0 %collective-permute-start.11 = (bf16[128,128]{1,0:T(8,128)(2,1)S(1)}, bf16[128,128]{1,0:T(8,128)(2,1)S(1)}, u32[]{:S(2)}, u32[]{:S(2)}) collective-permute-start(bf16[128,128]{1,0:T(8,128)(2,1)S(1)} %responses.1.refs_0_), channel_id=1, source_target_pairs={{16,0},{24,8},{17,1},{25,9},{18,2},{26,10},{19,3},{27,11},{20,4},{... | collective-permute-start | bytes 98312 | tf_op jit(solution)/shard_map/ppermute | solution.py:416
  88.1 10.3 %collective-permute-start.10 = (bf16[128,128]{1,0:T(8,128)(2,1)S(1)}, bf16[128,128]{1,0:T(8,128)(2,1)S(1)}, u32[]{:S(2)}, u32[]{:S(2)}) collective-permute-start(bf16[128,128]{1,0:T(8,128)(2,1)S(1)} %responses.1.refs_0_), channel_id=1, source_target_pairs={{8,0},{16,8},{24,16},{9,1},{17,9},{25,17},{10,2},{18,10},{26,18},{... | collective-permute-start | bytes 98312 | tf_op jit(solution)/shard_map/ppermute | solution.py:416
  95.7 2.6 %copy-start.11 = (bf16[128,128]{1,0:T(8,128)(2,1)}, bf16[128,128]{1,0:T(8,128)(2,1)S(1)}, u32[]{:S(2)}) copy-start(bf16[128,128]{1,0:T(8,128)(2,1)S(1)} %collective-permute-done.12.refs_3_) | copy-start | bytes 98308
  95.7 2.6 %copy-start.12 = (bf16[128,128]{1,0:T(8,128)(2,1)}, bf16[128,128]{1,0:T(8,128)(2,1)S(1)}, u32[]{:S(2)}) copy-start(bf16[128,128]{1,0:T(8,128)(2,1)S(1)} %collective-permute-done.11.refs_2_) | copy-start | bytes 98308
  102.5 9.6 %all-to-all-start.2 = ((bf16[8,16,768]{2,1,0:T(8,128)(2,1)}), bf16[8,16,768]{2,1,0:T(8,128)(2,1)S(1)}, u32[]{:S(2)}, u32[]{:S(2)}) async-start(bf16[8,16,768]{2,1,0:T(8,128)(2,1)} %bitcast.46), calls=%async_computation.2 | async-start | bytes 393216 | tf_op jit(solution)/shard_map/all_to_all | solution.py:406
  112.0 0.7 copy-start.9
  121.3 37.0 %copy-start.15 = (f32[8,640]{1,0:T(8,128)S(1)}, f32[8,640]{1,0:T(8,128)}, u32[]{:S(2)}) copy-start(f32[8,640]{1,0:T(8,128)} %get-tuple-element.48) | copy-start | bytes 61444
  (1 other events, 0.6 us)

commit v10 on v9

--- a/solution.py
+++ b/solution.py
@@ -455,25 +455,6 @@
     )(*parts)
 
 
-def take_kernel(place_ref, value_ref, out_ref):
-    out_ref[...] = value_ref[...]
-
-
-def take(value, row, column, shape):
-    return pl.pallas_call(
-        take_kernel,
-        grid_spec=pltpu.PrefetchScalarGridSpec(
-            num_scalar_prefetch=1,
-            grid=(1,),
-            in_specs=[pl.BlockSpec(shape, lambda i, t: (t[0], t[1]))],
-            out_specs=pl.BlockSpec(shape, lambda i, t: (0, 0)),
-        ),
-        out_shape=jax.ShapeDtypeStruct(shape, value.dtype),
-        compiler_params=params(60),
-        name="take",
-    )(jnp.stack([row, column]).astype(jnp.int32), value)
-
-
 def exchange_near(shares):
     count = lax.axis_size("expert")
     return [shares] + [swap(shares, d) for d in range(2, count, 2)]
@@ -503,7 +484,11 @@
     sharers = experts // parts
     part_width = width // parts
     share_rows = routed // sharers
-    own_share = take(router_t, place % sharers, place // sharers, (share_rows, part_width))
+    own_share = lax.dynamic_slice(
+        router_t,
+        ((place % sharers) * share_rows, (place // sharers) * part_width),
+        (share_rows, part_width),
+    )
     shares = join(pass_down(own_share, layers))
     twist = jnp.full((1,), place if direct else 0, jnp.int32)
 
@@ -644,7 +629,7 @@
             jax.ShapeDtypeStruct((tokens, wide), BF16),
             jax.ShapeDtypeStruct((rows, wide), BF16),
         ),
-        compiler_params=params(60),
+        compiler_params=params(12 + 4 * grow),
         name="chain",
     )(response, *pass_down(response, layers), *states)
 

time: 160 us -> 158 us (0.988)
  Pallas kernels: 98.4 us -> 94.8 us
  local copies, waits for them, and re-layouts: 8.31 us -> 10.7 us
    pallas_call x1 -> x0, Pallas kernels: 2.29 us -> none  [take(): pl.pallas_call(take_kernel, grid_spec=pltpu.PrefetchScalarGridSpec(num_sc...]
    dynamic_slice x0 -> x1, local copies, waits for them, and re-layouts: none -> 1.73 us  [on_device(): lax.dynamic_slice(router_t, (place % sharers * share_rows, place // share...]
    unnamed x39 -> x25, local copies, waits for them, and re-layouts: 4.78 us -> 5.43 us
where the time goes in v10:
time: 158 us; the launch traced here: 157 us
  Pallas kernels  94.8 us (60%)
  starting transfers between devices  24.7 us (16%)
  waiting for transfers between devices  14 us (9%)
  local copies, waits for them, and re-layouts  10.7 us (7%)
  blocking collectives  8.81 us (6%)
  matrix products  2.08 us (1%)
    pallas_call x1, Pallas kernels, on_device(): pl.pallas_call(functools.partial(book_kernel, unroll), grid=(inner // blo...  35.3 us
    pallas_call x1, Pallas kernels, decode(): pl.pallas_call(decode_kernel, grid=(blocks,), in_specs=[pl.BlockSpec((boo...  26.3 us
    ppermute x9, starting transfers between devices, pass_down(): lax.ppermute(value, 'pipe', [(p, p - s) for p in range(s, layers)])  12 us
    ppermute x9, waiting for transfers between devices, pass_down(): lax.ppermute(value, 'pipe', [(p, p - s) for p in range(s, layers)])  10.5 us
    all_to_all x1, blocking collectives, exchange(): lax.all_to_all(value, 'expert', split_axis=0, concat_axis=0, tiled=True)  8.81 us
    all_to_all x2, starting transfers between devices, exchange(): lax.all_to_all(value, 'expert', split_axis=0, concat_axis=0, tiled=True)  8.75 us
    pallas_call x1, Pallas kernels, on_device(): by_columns(slots_kernel, [columns(rows), pl.BlockSpec((rows, LANES), lamb...  8.6 us
    pallas_call x2, Pallas kernels, score(): pl.pallas_call(kernel, grid_spec=pltpu.PrefetchScalarGridSpec(num_scalar_...  7.86 us
  transfers between devices with their start and end apart: 15, of which 6 were waited for; matrix products, arithmetic and copies ran while one was open for 3% of the time, Pallas kernels for 28%

profile of v10, /device:TPU:0, one launch (start us, length us, event | category | flops | bytes accessed | tf_op | source)
XLA Modules:
  0.0 156.6 jit_solution(2426932867823383033)
XLA Ops:
  0.6 1.7 %dynamic-slice_bitcast_fusion = bf16[160,640]{1,0:T(8,128)(2,1)} fusion(bf16[1,5120,160]{1,2,0:T(8,128)(2,1)} %param.10, s32[]{:T(128)S(6)} %select_n.11), kind=kLoop, calls=%fused_computation.4 | loop fusion | bytes 409604 | tf_op jit(solution)/shard_map/dynamic_slice | solution.py:487
  2.4 1.4 collective-permute-start.2
  3.8 1.3 collective-permute-start.1
  5.1 1.3 collective-permute-start
  6.4 2.1 %fusion.logits_ref = f32[128,160]{1,0:T(8,128)S(1)} fusion(bf16[1,5120,160]{1,2,0:T(8,128)(2,1)} %param.10, bf16[1,128,5120]{2,1,0:T(8,128)(2,1)S(1)} %copy-done), kind=kOutput, calls=%fused_computation | convolution fusion | flops 209715200 | bytes 3031040 | tf_op jit(solution)/shard_map/dot_general | solution.py:28
  8.6 1.1 prepare.1
  9.7 1.1 copy-done.2
  10.8 1.4 collective-permute-start.3
  12.2 1.3 collective-permute-start.8
  13.5 5.2 %all-to-all-start = ((bf16[8,16,5248]{2,1,0:T(8,128)(2,1)}), bf16[8,16,5248]{2,1,0:T(8,128)(2,1)S(1)}, u32[]{:S(2)}, u32[]{:S(2)}) async-start(bf16[8,16,5248]{2,1,0:T(8,128)(2,1)} %bitcast.34), calls=%async_computation | async-start | bytes 2686976 | tf_op jit(solution)/shard_map/all_to_all | solution.py:406
  20.9 1.4 collective-permute-start.7
  22.3 1.7 %collective-permute-done.1.refs_1_ = bf16[160,640]{1,0:T(8,128)(2,1)} collective-permute-done((bf16[160,640]{1,0:T(8,128)(2,1)}, bf16[160,640]{1,0:T(8,128)(2,1)}, u32[]{:S(2)}, u32[]{:S(2)}) %collective-permute-start.1) | collective-permute-done | bytes 204832 | tf_op jit(solution)/shard_map/ppermute | solution.py:416
  24.0 1.9 %join.2.refs_0_ = bf16[3,160,640]{2,1,0:T(8,128)(2,1)} custom-call(bf16[160,640]{1,0:T(8,128)(2,1)} %collective-permute-done.refs_0_, bf16[160,640]{1,0:T(8,128)(2,1)} %collective-permute-done.1.refs_1_, bf16[160,640]{1,0:T(8,128)(2,1)} %collective-permute-done.2.refs_2_), custom_call_target="tpu_custom_call" | custom-call | tf_op jit(solution)/shard_map/join/pallas_call | solution.py:443
  26.7 3.3 %collective-permute-start.6 = (bf16[3,160,640]{2,1,0:T(8,128)(2,1)}, bf16[3,160,640]{2,1,0:T(8,128)(2,1)}, u32[]{:S(2)}, u32[]{:S(2)}) collective-permute-start(bf16[3,160,640]{2,1,0:T(8,128)(2,1)} %join.2.refs_0_), channel_id=1, source_target_pairs={{0,6},{1,7},{2,4},{3,5},{4,2},{5,3},{6,0},{7,1},{8,14},{9,15},{10,... | collective-permute-start | bytes 1843208 | tf_op jit(solution)/shard_map/ppermute | solution.py:411
  30.6 1.8 %order.1.order_ref = bf16[1024,1024]{1,0:T(8,128)(2,1)} custom-call(bf16[72,768]{1,0:T(8,128)(2,1)} %bitcast.46), custom_call_target="tpu_custom_call" | custom-call | tf_op jit(solution)/shard_map/order/pallas_call | solution.py:523
  33.1 26.3 %decode.1 = (f32[8,128,640]{2,1,0:T(8,128)}, bf16[128,5120]{1,0:T(8,128)(2,1)}) custom-call(s32[2,768,640]{2,1,0:T(8,128)} %bitcast.41, bf16[2,2,8,16,128]{4,3,2,1,0:T(8,128)(2,1)} %broadcast_in_dim.16.table_ref, bf16[72,768]{1,0:T(8,128)(2,1)} %bitcast.47, f32[8,640]{1,0:T(8,128)} %bitcast.49, bf16[1024,1024]{1,0:T(8,128)(2,1)} %order.1.order_ref), custom_call_target="tpu_custom_call" | custom-call | flops 30000001024 | bytes 10000000 | tf_op jit(solution)/shard_map/decode/pallas_call | solution.py:531
  59.4 3.3 %collective-permute-done.5.refs_2_ = bf16[3,160,640]{2,1,0:T(8,128)(2,1)} collective-permute-done((bf16[3,160,640]{2,1,0:T(8,128)(2,1)}, bf16[3,160,640]{2,1,0:T(8,128)(2,1)}, u32[]{:S(2)}, u32[]{:S(2)}) %collective-permute-start.5) | collective-permute-done | bytes 614432 | tf_op jit(solution)/shard_map/ppermute | solution.py:411
  62.9 2.6 %join.3.router_ref.near_ref = bf16[4,3,160,640]{3,2,1,0:T(8,128)(2,1)} custom-call(bf16[3,160,640]{2,1,0:T(8,128)(2,1)} %join.2.refs_0_, bf16[3,160,640]{2,1,0:T(8,128)(2,1)} %collective-permute-done.4.refs_1_, bf16[3,160,640]{2,1,0:T(8,128)(2,1)} %collective-permute-done.5.refs_2_, bf16[3,160,640]{2,1,0:T(8,128)(2,1)} %collective-permute-done.6.refs_3_), custom_call_target="tpu_custom_call" | custom-call | tf_op jit(solution)/shard_map/join/pallas_call | solution.py:443
  66.6 4.2 %scores.2 = (f32[480,128]{1,0:T(8,128)}, f32[128,128]{1,0:T(8,128)}) custom-call(s32[1]{0:T(128)} %bitcast.twist_ref, bf16[128,5120]{1,0:T(8,128)(2,1)} %get-tuple-element.34.out_ref, bf16[128,5248]{1,0:T(8,128)(2,1)} %bitcast.37, bf16[4,3,160,640]{3,2,1,0:T(8,128)(2,1)} %join.3.router_ref.near_ref), custom_call_target="tpu_custom_call" | custom-call | tf_op jit(solution)/shard_map/scores/pallas_call | solution.py:591
  70.8 3.6 %scores.3 = bf16[128,512]{1,0:T(8,128)(2,1)} custom-call(s32[1]{0:T(128)} %bitcast.twist_ref, bf16[128,5120]{1,0:T(8,128)(2,1)} %get-tuple-element.34.out_ref, bf16[4,3,160,640]{3,2,1,0:T(8,128)(2,1)} %collective-permute-done.9.router_ref.far_ref, f32[480,128]{1,0:T(8,128)} %get-tuple-element.37.total_ref, f32[128,128]{1,0:T(8,128)} %get-tuple-element.38.base_ref), custom_call_target="tpu_custom_call" | custom-call | tf_op jit(solution)/shard_map/scores/pallas_call | solution.py:591
  74.4 8.8 %all_to_all.34 = bf16[8,16,512]{2,1,0:T(8,128)(2,1)S(1)} all-to-all(bf16[8,16,512]{2,1,0:T(8,128)(2,1)} %bitcast.45), channel_id=1, replica_groups=mesh['pipe'=4,'expert'=8] {'expert'}, dimensions={0} | all-to-all | bytes 262144 | tf_op jit(solution)/shard_map/all_to_all | solution.py:406
  83.2 1.1 responses.1.refs_0_
  84.3 1.3 collective-permute-start.12
  85.6 1.3 collective-permute-start.11
  86.9 1.3 collective-permute-start.10
  88.2 6.2 %collective-permute-done.12.refs_3_ = bf16[128,128]{1,0:T(8,128)(2,1)S(1)} collective-permute-done((bf16[128,128]{1,0:T(8,128)(2,1)S(1)}, bf16[128,128]{1,0:T(8,128)(2,1)S(1)}, u32[]{:S(2)}, u32[]{:S(2)}) %collective-permute-start.12) | collective-permute-done | bytes 32800 | tf_op jit(solution)/shard_map/ppermute | solution.py:416
  94.5 1.7 %collective-permute-done.10.refs_1_ = bf16[128,128]{1,0:T(8,128)(2,1)S(1)} collective-permute-done((bf16[128,128]{1,0:T(8,128)(2,1)S(1)}, bf16[128,128]{1,0:T(8,128)(2,1)S(1)}, u32[]{:S(2)}, u32[]{:S(2)}) %collective-permute-start.10) | collective-permute-done | bytes 32800 | tf_op jit(solution)/shard_map/ppermute | solution.py:416
  96.2 2.3 %chain.1 = (bf16[128,160]{1,0:T(8,128)(2,1)S(1)}, bf16[128,768]{1,0:T(8,128)(2,1)S(1)}, bf16[128,768]{1,0:T(8,128)(2,1)}) custom-call(bf16[128,128]{1,0:T(8,128)(2,1)S(1)} %responses.1.refs_0_, bf16[128,128]{1,0:T(8,128)(2,1)S(1)} %collective-permute-done.10.refs_1_, bf16[128,128]{1,0:T(8,128)(2,1)S(1)} %collective-permute-done.11.refs_2_, ...), custom_call_target="tpu_custom_call" | custom-call | tf_op jit(solution)/shard_map/chain/pallas_call | solution.py:625
  99.8 3.6 %all-to-all-start.2 = ((bf16[8,16,768]{2,1,0:T(8,128)(2,1)}), bf16[8,16,768]{2,1,0:T(8,128)(2,1)S(1)}, u32[]{:S(2)}, u32[]{:S(2)}) async-start(bf16[8,16,768]{2,1,0:T(8,128)(2,1)} %bitcast.20), calls=%async_computation.2 | async-start | bytes 393216 | tf_op jit(solution)/shard_map/all_to_all | solution.py:406
  103.4 6.0 %finish.1 = bf16[128,5120]{1,0:T(8,128)(2,1)} custom-call(s32[1]{0:T(128)} %bitcast.twist_ref, bf16[128,5120]{1,0:T(8,128)(2,1)} %grad_ref.3, bf16[128,768]{1,0:T(8,128)(2,1)} %copy-done.3, bf16[128,160]{1,0:T(8,128)(2,1)} %copy-done.4, bf16[160,5120]{1,0:T(8,128)(2,1)} %bitcast.40, bf16[4,3,160,640]{3,2,1,0:T(8,128)(2,1)} %join.3.router_ref.near_ref, ...), custom_call_target="tpu_custom_call" | custom-call | tf_op jit(solution)/shard_map/finish/pallas_call | solution.py:638
  110.1 8.6 %slot_grads.1 = (bf16[8,128,640]{2,1,0:T(8,128)(2,1)}, f32[8,640]{1,0:T(8,128)}) custom-call(s32[1]{0:T(128)} %bitcast.twist_ref, bf16[128,5248]{1,0:T(8,128)(2,1)} %bitcast.38, bf16[128,5248]{1,0:T(8,128)(2,1)} %bitcast.39, bf16[128,768]{1,0:T(8,128)(2,1)} %bitcast.44, bf16[4,3,160,640]{3,2,1,0:T(8,128)(2,1)} %join.3.router_ref.near_ref, ...), custom_call_target="tpu_custom_call" | custom-call | tf_op jit(solution)/shard_map/slot_grads/pallas_call | solution.py:654
  118.7 35.3 %book_grads.1 = f32[2,48,48]{2,1,0:T(8,128)} custom-call(bf16[72,768]{1,0:T(8,128)(2,1)} %bitcast.48, bf16[8,128,640]{2,1,0:T(8,128)(2,1)} %get-tuple-element.47.slots_ref, f32[8,640]{1,0:T(8,128)} %bitcast.50, s32[2,768,640]{2,1,0:T(8,128)} %bitcast.42), custom_call_target="tpu_custom_call" | custom-call | tf_op jit(solution)/shard_map/book_grads/pallas_call | solution.py:676
  (46 shorter events, 10.2 us)
Async XLA Ops:
  0.6 5.8 %copy-start = (bf16[1,128,5120]{2,1,0:T(8,128)(2,1)S(1)}, bf16[1,128,5120]{2,1,0:T(8,128)(2,1)}, u32[]{:S(2)}) copy-start(bf16[1,128,5120]{2,1,0:T(8,128)(2,1)} %param.9) | copy-start | bytes 3932164
  2.4 6.1 %copy-start.10 = (s32[1,128,6]{1,0,2:T(1,128)S(1)}, s32[1,128,6]{1,0,2:T(1,128)}, u32[]{:S(2)}) copy-start(s32[1,128,6]{1,0,2:T(1,128)} %param.11) | copy-start | bytes 9220
  2.4 6.2 %copy-start.1 = (bf16[128,5120]{1,0:T(8,128)(2,1)S(1)}, bf16[128,5120]{1,0:T(8,128)(2,1)}, u32[]{:S(2)}) copy-start(bf16[128,5120]{1,0:T(8,128)(2,1)} %grad_ref.3) | copy-start | bytes 3932164
  2.4 18.5 %collective-permute-start.2 = (bf16[160,640]{1,0:T(8,128)(2,1)}, bf16[160,640]{1,0:T(8,128)(2,1)}, u32[]{:S(2)}, u32[]{:S(2)}) collective-permute-start(bf16[160,640]{1,0:T(8,128)(2,1)} %dynamic-slice_bitcast_fusion), channel_id=1, source_target_pairs={{24,0},{25,1},{26,2},{27,3},{28,4},{29,5},{30,6},{31,7}} | collective-permute-start | bytes 614408 | tf_op jit(solution)/shard_map/ppermute | solution.py:416
  3.8 20.2 %collective-permute-start.1 = (bf16[160,640]{1,0:T(8,128)(2,1)}, bf16[160,640]{1,0:T(8,128)(2,1)}, u32[]{:S(2)}, u32[]{:S(2)}) collective-permute-start(bf16[160,640]{1,0:T(8,128)(2,1)} %dynamic-slice_bitcast_fusion), channel_id=1, source_target_pairs={{16,0},{24,8},{17,1},{25,9},{18,2},{26,10},{19,3},{27,11},{20,4},{... | collective-permute-start | bytes 614408 | tf_op jit(solution)/shard_map/ppermute | solution.py:416
  5.1 18.9 %collective-permute-start = (bf16[160,640]{1,0:T(8,128)(2,1)}, bf16[160,640]{1,0:T(8,128)(2,1)}, u32[]{:S(2)}, u32[]{:S(2)}) collective-permute-start(bf16[160,640]{1,0:T(8,128)(2,1)} %dynamic-slice_bitcast_fusion), channel_id=1, source_target_pairs={{8,0},{16,8},{24,16},{9,1},{17,9},{25,17},{10,2},{18,10},{26,18},{... | collective-permute-start | bytes 614408 | tf_op jit(solution)/shard_map/ppermute | solution.py:416
  9.7 1.1 copy-start.2
  10.8 8.4 %copy-start.7 = (f32[1,1,5120]{2,1,0:T(1,128)S(1)}, f32[1,1,5120]{2,1,0:T(1,128)}, u32[]{:S(2)}) copy-start(f32[1,1,5120]{2,1,0:T(1,128)} %param.15) | copy-start | bytes 61444
  10.8 15.9 %collective-permute-start.3 = (f32[128,256]{1,0:T(8,128)S(1)}, f32[128,256]{1,0:T(8,128)S(1)}, u32[]{:S(2)}, u32[]{:S(2)}) collective-permute-start(f32[128,256]{1,0:T(8,128)S(1)} %get-tuple-element.39.state_ref.refs_4_), channel_id=1, source_target_pairs={{24,0},{25,1},{26,2},{27,3},{28,4},{29,5},{30,6},{31,7}} | collective-permute-start | bytes 393224 | tf_op jit(solution)/shard_map/ppermute | solution.py:416
  12.2 53.2 %collective-permute-start.8 = (f32[128,256]{1,0:T(8,128)S(1)}, f32[128,256]{1,0:T(8,128)S(1)}, u32[]{:S(2)}, u32[]{:S(2)}) collective-permute-start(f32[128,256]{1,0:T(8,128)S(1)} %get-tuple-element.39.state_ref.refs_4_), channel_id=1, source_target_pairs={{16,0},{24,8},{17,1},{25,9},{18,2},{26,10},{19,3},{27,11},{20,4},{... | collective-permute-start | bytes 393224 | tf_op jit(solution)/shard_map/ppermute | solution.py:416
  13.5 52.0 %all-to-all-start = ((bf16[8,16,5248]{2,1,0:T(8,128)(2,1)}), bf16[8,16,5248]{2,1,0:T(8,128)(2,1)S(1)}, u32[]{:S(2)}, u32[]{:S(2)}) async-start(bf16[8,16,5248]{2,1,0:T(8,128)(2,1)} %bitcast.34), calls=%async_computation | async-start | bytes 2686976 | tf_op jit(solution)/shard_map/all_to_all | solution.py:406
  20.9 11.5 %copy-start.9 = (bf16[1,1,2,256,8]{3,4,2,1,0:T(8,128)(2,1)S(1)}, bf16[1,1,2,256,8]{3,4,2,1,0:T(8,128)(2,1)}, u32[]{:S(2)}) copy-start(bf16[1,1,2,256,8]{3,4,2,1,0:T(8,128)(2,1)} %param.14) | copy-start | bytes 24580
  20.9 44.6 %collective-permute-start.7 = (f32[128,256]{1,0:T(8,128)S(1)}, f32[128,256]{1,0:T(8,128)S(1)}, u32[]{:S(2)}, u32[]{:S(2)}) collective-permute-start(f32[128,256]{1,0:T(8,128)S(1)} %get-tuple-element.39.state_ref.refs_4_), channel_id=1, source_target_pairs={{8,0},{16,8},{24,16},{9,1},{17,9},{25,17},{10,2},{18,10},{26,18},{... | collective-permute-start | bytes 393224 | tf_op jit(solution)/shard_map/ppermute | solution.py:416
  26.7 32.7 %collective-permute-start.6 = (bf16[3,160,640]{2,1,0:T(8,128)(2,1)}, bf16[3,160,640]{2,1,0:T(8,128)(2,1)}, u32[]{:S(2)}, u32[]{:S(2)}) collective-permute-start(bf16[3,160,640]{2,1,0:T(8,128)(2,1)} %join.2.refs_0_), channel_id=1, source_target_pairs={{0,6},{1,7},{2,4},{3,5},{4,2},{5,3},{6,0},{7,1},{8,14},{9,15},{10,... | collective-permute-start | bytes 1843208 | tf_op jit(solution)/shard_map/ppermute | solution.py:411
  30.0 32.7 %collective-permute-start.5 = (bf16[3,160,640]{2,1,0:T(8,128)(2,1)}, bf16[3,160,640]{2,1,0:T(8,128)(2,1)}, u32[]{:S(2)}, u32[]{:S(2)}) collective-permute-start(bf16[3,160,640]{2,1,0:T(8,128)(2,1)} %join.2.refs_0_), channel_id=1, source_target_pairs={{0,4},{1,5},{2,6},{3,7},{4,0},{5,1},{6,2},{7,3},{8,12},{9,13},{10,... | collective-permute-start | bytes 1843208 | tf_op jit(solution)/shard_map/ppermute | solution.py:411
  30.6 32.3 %collective-permute-start.4 = (bf16[3,160,640]{2,1,0:T(8,128)(2,1)}, bf16[3,160,640]{2,1,0:T(8,128)(2,1)}, u32[]{:S(2)}, u32[]{:S(2)}) collective-permute-start(bf16[3,160,640]{2,1,0:T(8,128)(2,1)} %join.2.refs_0_), channel_id=1, source_target_pairs={{0,2},{1,3},{2,0},{3,1},{4,6},{5,7},{6,4},{7,5},{8,10},{9,11},{10,... | collective-permute-start | bytes 1843208 | tf_op jit(solution)/shard_map/ppermute | solution.py:411
  65.5 1.1 copy-start.5
  65.5 5.3 %collective-permute-start.9 = (bf16[4,3,160,640]{3,2,1,0:T(8,128)(2,1)}, bf16[4,3,160,640]{3,2,1,0:T(8,128)(2,1)}, u32[]{:S(2)}, u32[]{:S(2)}) collective-permute-start(bf16[4,3,160,640]{3,2,1,0:T(8,128)(2,1)} %join.3.router_ref.near_ref), channel_id=1, source_target_pairs={{0,1},{1,0},{2,3},{3,2},{4,5},{5,4},{6,7},{7,6},{8,9},{9,8},{10,11... | collective-permute-start | bytes 7372808 | tf_op jit(solution)/shard_map/ppermute | solution.py:411
  84.3 10.1 %collective-permute-start.12 = (bf16[128,128]{1,0:T(8,128)(2,1)S(1)}, bf16[128,128]{1,0:T(8,128)(2,1)S(1)}, u32[]{:S(2)}, u32[]{:S(2)}) collective-permute-start(bf16[128,128]{1,0:T(8,128)(2,1)S(1)} %responses.1.refs_0_), channel_id=1, source_target_pairs={{24,0},{25,1},{26,2},{27,3},{28,4},{29,5},{30,6},{31,7}} | collective-permute-start | bytes 98312 | tf_op jit(solution)/shard_map/ppermute | solution.py:416
  85.6 8.8 %collective-permute-start.11 = (bf16[128,128]{1,0:T(8,128)(2,1)S(1)}, bf16[128,128]{1,0:T(8,128)(2,1)S(1)}, u32[]{:S(2)}, u32[]{:S(2)}) collective-permute-start(bf16[128,128]{1,0:T(8,128)(2,1)S(1)} %responses.1.refs_0_), channel_id=1, source_target_pairs={{16,0},{24,8},{17,1},{25,9},{18,2},{26,10},{19,3},{27,11},{20,4},{... | collective-permute-start | bytes 98312 | tf_op jit(solution)/shard_map/ppermute | solution.py:416
  86.9 9.3 %collective-permute-start.10 = (bf16[128,128]{1,0:T(8,128)(2,1)S(1)}, bf16[128,128]{1,0:T(8,128)(2,1)S(1)}, u32[]{:S(2)}, u32[]{:S(2)}) collective-permute-start(bf16[128,128]{1,0:T(8,128)(2,1)S(1)} %responses.1.refs_0_), channel_id=1, source_target_pairs={{8,0},{16,8},{24,16},{9,1},{17,9},{25,17},{10,2},{18,10},{26,18},{... | collective-permute-start | bytes 98312 | tf_op jit(solution)/shard_map/ppermute | solution.py:416
  98.5 0.7 copy-start.3
  99.2 0.6 copy-start.4
  99.8 9.6 %all-to-all-start.2 = ((bf16[8,16,768]{2,1,0:T(8,128)(2,1)}), bf16[8,16,768]{2,1,0:T(8,128)(2,1)S(1)}, u32[]{:S(2)}, u32[]{:S(2)}) async-start(bf16[8,16,768]{2,1,0:T(8,128)(2,1)} %bitcast.20), calls=%async_computation.2 | async-start | bytes 393216 | tf_op jit(solution)/shard_map/all_to_all | solution.py:406
  109.4 0.7 copy-start.6
  118.7 37.0 %copy-start.8 = (f32[8,640]{1,0:T(8,128)S(1)}, f32[8,640]{1,0:T(8,128)}, u32[]{:S(2)}) copy-start(f32[8,640]{1,0:T(8,128)} %get-tuple-element.48) | copy-start | bytes 61444
